TPU v7x, 32 devices: a whole 2x2x4 slice. The times are simulated.
32 devices in a mesh: page: 16 (over z, x, core), seq: 2 (over y).
Axes of the slice: x: 2, y: 2, z: 4, core: 2. Of those that a mesh axis runs over, the one named last changes fastest.
Arguments:
- tokens: bfloat16 [16, 1024, 1024], P('page', 'seq'), may hold values from -6 to 6
- patches: bfloat16 [16, 1088, 1024], P('page', 'seq'), may hold values from -6 to 6
- lengths: int32 [16], P('page'), may hold values from 513 to 1024, as said below
- blank_mask: int32 [16, 1088], P('page'), may hold values from 0 to 1, as said below
- cotangent: bfloat16 [16, 1024, 1024], P('page', 'seq'), may hold values from -6 to 6
- first_gain: bfloat16 [1024], P('seq'), may hold values from 0.25 to 1.75
- first_shift: bfloat16 [1024], P('seq'), may hold values from -1.25 to 1.25
- self_query: bfloat16 [1024, 1024], P('seq'), may hold values from -0.1875 to 0.1875
- self_query_bias: bfloat16 [1024], P('seq'), may hold values from -1.25 to 1.25
- self_key: bfloat16 [1024, 1024], P('seq'), may hold values from -0.1875 to 0.1875
- self_value: bfloat16 [1024, 1024], P('seq'), may hold values from -0.1875 to 0.1875
- self_value_bias: bfloat16 [1024], P('seq'), may hold values from -1.25 to 1.25
- self_output: bfloat16 [1024, 1024], P('seq'), may hold values from -3 to 3
- self_output_bias: bfloat16 [1024], P('seq'), may hold values from -1.25 to 1.25
- second_gain: bfloat16 [1024], P('seq'), may hold values from 0.25 to 1.75
- second_shift: bfloat16 [1024], P('seq'), may hold values from -1.25 to 1.25
- cross_query: bfloat16 [1024, 1024], P('seq'), may hold values from -0.1875 to 0.1875
- cross_query_bias: bfloat16 [1024], P('seq'), may hold values from -1.25 to 1.25
- cross_key: bfloat16 [1024, 1024], P('seq'), may hold values from -0.1875 to 0.1875
- cross_value: bfloat16 [1024, 1024], P('seq'), may hold values from -0.1875 to 0.1875
- cross_value_bias: bfloat16 [1024], P('seq'), may hold values from -1.25 to 1.25
- cross_output: bfloat16 [1024, 1024], P('seq'), may hold values from -3.5 to 3.5
- cross_output_bias: bfloat16 [1024], P('seq'), may hold values from -1.25 to 1.25
- third_gain: bfloat16 [1024], P('seq'), may hold values from 0.25 to 1.75
- third_shift: bfloat16 [1024], P('seq'), may hold values from -1.25 to 1.25
- ffn_inner: bfloat16 [1024, 4096], P('seq'), may hold values from -0.1875 to 0.1875
- ffn_inner_bias: bfloat16 [4096], P('seq'), may hold values from -1.25 to 1.25
- ffn_outer: bfloat16 [4096, 1024], P('seq'), may hold values from -0.09375 to 0.09375
- ffn_outer_bias: bfloat16 [1024], P('seq'), may hold values from -1.25 to 1.25
Outputs:
- outputs: bfloat16 [16, 1024, 1024], P('page', 'seq')
- grad_tokens: float32 [16, 1024, 1024], P('page', 'seq')
- grad_patches: float32 [16, 1088, 1024], P('page', 'seq')
- grad_first_gain: float32 [1024], P('seq')
- grad_first_shift: float32 [1024], P('seq')
- grad_self_query: float32 [1024, 1024], P('seq')
- grad_self_query_bias: float32 [1024], P('seq')
- grad_self_key: float32 [1024, 1024], P('seq')
- grad_self_value: float32 [1024, 1024], P('seq')
- grad_self_value_bias: float32 [1024], P('seq')
- grad_self_output: float32 [1024, 1024], P('seq')
- grad_self_output_bias: float32 [1024], P('seq')
- grad_second_gain: float32 [1024], P('seq')
- grad_second_shift: float32 [1024], P('seq')
- grad_cross_query: float32 [1024, 1024], P('seq')
- grad_cross_query_bias: float32 [1024], P('seq')
- grad_cross_key: float32 [1024, 1024], P('seq')
- grad_cross_value: float32 [1024, 1024], P('seq')
- grad_cross_value_bias: float32 [1024], P('seq')
- grad_cross_output: float32 [1024, 1024], P('seq')
- grad_cross_output_bias: float32 [1024], P('seq')
- grad_third_gain: float32 [1024], P('seq')
- grad_third_shift: float32 [1024], P('seq')
- grad_ffn_inner: float32 [1024, 4096], P('seq')
- grad_ffn_inner_bias: float32 [4096], P('seq')
- grad_ffn_outer: float32 [4096, 1024], P('seq')
- grad_ffn_outer_bias: float32 [1024], P('seq')
Inputs may be any that keep to these rules, and one draw needn't show every extreme that they name: `lengths`: in each group of 1 consecutive pages one page (which one is drawn) has more than 512 valid tokens. `blank_mask`: the first patch of every page is never blank.
All inputs are finite; a program needn't handle non-finite values.
Results may differ from a plain program's by a relative error of at most 0.024.
Values may be sent and summed in bfloat16 or wider, within the bound.
No kernel may reach another device: no remote copies, remote signals or barrier semaphores. Data moves between devices by JAX's collectives and lax.ppermute only.
A program may use at most 448 MiB of HBM per device.

v0:
```python
import math

import jax
import jax.numpy as jnp
from jax import lax
from jax.sharding import PartitionSpec as P

HEADS = 16
HEAD = 64


norm_epsilon = 1e-05
masked_score = -1000000000.0


def layer_norm(values, norm_gain, norm_shift):
    center = values - jnp.mean(values, axis=-1, keepdims=True)
    spread = jnp.mean(center * center, axis=-1, keepdims=True)
    return center * lax.rsqrt(spread + norm_epsilon) * norm_gain + norm_shift


def project(activations, weight):
    return jnp.einsum("ptd,de->pte", activations, weight, preferred_element_type=jnp.float32)


def project_back(gradient, weight):
    return jnp.einsum("pte,de->ptd", gradient, weight, preferred_element_type=jnp.float32)


def outer_sum(left_side, right_side):
    return jnp.einsum("ptd,pte->de", left_side, right_side, preferred_element_type=jnp.float32)


def column_sum(values):
    return jnp.sum(values.astype(jnp.float32), axis=(0, 1))


def split_heads(values):
    return values.reshape(values.shape[0], HEADS, HEAD)


def masked_scores(query_rows, key_rows, allowed):
    scores = jnp.einsum(
        "qhd,khd->hqk",
        split_heads(query_rows),
        split_heads(key_rows),
        preferred_element_type=jnp.float32,
    )
    return jnp.where(allowed[None], scores, masked_score)


def attend_page(page_item):
    query_rows, key_rows, value_rows, allowed, valid_rows = page_item
    scores = masked_scores(query_rows, key_rows, allowed)
    row_peak = jnp.max(scores, axis=-1, keepdims=True)
    weights = jnp.exp(scores - row_peak)
    row_total = jnp.sum(weights, axis=-1, keepdims=True)
    shares = (weights / row_total).astype(jnp.bfloat16)
    blended = jnp.einsum(
        "hqk,khd->qhd", shares, split_heads(value_rows), preferred_element_type=jnp.float32
    )
    blended = blended.reshape(query_rows.shape[0], -1) * valid_rows[:, None]
    return (blended.astype(jnp.bfloat16), (row_peak + jnp.log(row_total))[..., 0])


def attend_back(page_item):
    query_rows, key_rows, value_rows, allowed, log_total, grad_blended = page_item
    heads_grad = split_heads(grad_blended)
    scores = masked_scores(query_rows, key_rows, allowed)
    shares = jnp.exp(scores - log_total[..., None])
    grad_shares = jnp.einsum(
        "qhd,khd->hqk", heads_grad, split_heads(value_rows), preferred_element_type=jnp.float32
    )
    weighted = jnp.sum(shares * grad_shares, axis=-1, keepdims=True)
    grad_scores = (shares * (grad_shares - weighted)).astype(jnp.bfloat16)
    grad_query = jnp.einsum(
        "hqk,khd->qhd", grad_scores, split_heads(key_rows), preferred_element_type=jnp.float32
    )
    grad_key = jnp.einsum(
        "hqk,qhd->khd", grad_scores, split_heads(query_rows), preferred_element_type=jnp.float32
    )
    grad_value = jnp.einsum(
        "hqk,qhd->khd", shares.astype(jnp.bfloat16), heads_grad, preferred_element_type=jnp.float32
    )
    return (
        grad_query.reshape(query_rows.shape[0], -1).astype(jnp.bfloat16),
        grad_key.reshape(key_rows.shape[0], -1),
        grad_value.reshape(key_rows.shape[0], -1),
    )


def on_device(
    tokens,
    patches,
    lengths,
    blank_mask,
    cotangent,
    first_gain,
    first_shift,
    self_query,
    self_query_bias,
    self_key,
    self_value,
    self_value_bias,
    self_output,
    self_output_bias,
    second_gain,
    second_shift,
    cross_query,
    cross_query_bias,
    cross_key,
    cross_value,
    cross_value_bias,
    cross_output,
    cross_output_bias,
    third_gain,
    third_shift,
    ffn_inner,
    ffn_inner_bias,
    ffn_outer,
    ffn_outer_bias,
):
    seq_count = lax.axis_size("seq")
    seq_index = lax.axis_index("seq")
    (
        whole_first_gain,
        whole_first_shift,
        whole_self_query,
        whole_self_query_bias,
        whole_self_key,
        whole_self_value,
        whole_self_value_bias,
        whole_self_output,
        whole_self_output_bias,
        whole_second_gain,
        whole_second_shift,
        whole_cross_query,
        whole_cross_query_bias,
        whole_cross_key,
        whole_cross_value,
        whole_cross_value_bias,
        whole_cross_output,
        whole_cross_output_bias,
        whole_third_gain,
        whole_third_shift,
        whole_ffn_inner,
        whole_ffn_inner_bias,
        whole_ffn_outer,
        whole_ffn_outer_bias,
    ) = (
        lax.all_gather(first_gain, "seq", axis=0, tiled=True),
        lax.all_gather(first_shift, "seq", axis=0, tiled=True),
        lax.all_gather(self_query, "seq", axis=0, tiled=True),
        lax.all_gather(self_query_bias, "seq", axis=0, tiled=True),
        lax.all_gather(self_key, "seq", axis=0, tiled=True),
        lax.all_gather(self_value, "seq", axis=0, tiled=True),
        lax.all_gather(self_value_bias, "seq", axis=0, tiled=True),
        lax.all_gather(self_output, "seq", axis=0, tiled=True),
        lax.all_gather(self_output_bias, "seq", axis=0, tiled=True),
        lax.all_gather(second_gain, "seq", axis=0, tiled=True),
        lax.all_gather(second_shift, "seq", axis=0, tiled=True),
        lax.all_gather(cross_query, "seq", axis=0, tiled=True),
        lax.all_gather(cross_query_bias, "seq", axis=0, tiled=True),
        lax.all_gather(cross_key, "seq", axis=0, tiled=True),
        lax.all_gather(cross_value, "seq", axis=0, tiled=True),
        lax.all_gather(cross_value_bias, "seq", axis=0, tiled=True),
        lax.all_gather(cross_output, "seq", axis=0, tiled=True),
        lax.all_gather(cross_output_bias, "seq", axis=0, tiled=True),
        lax.all_gather(third_gain, "seq", axis=0, tiled=True),
        lax.all_gather(third_shift, "seq", axis=0, tiled=True),
        lax.all_gather(ffn_inner, "seq", axis=0, tiled=True),
        lax.all_gather(ffn_inner_bias, "seq", axis=0, tiled=True),
        lax.all_gather(ffn_outer, "seq", axis=0, tiled=True),
        lax.all_gather(ffn_outer_bias, "seq", axis=0, tiled=True),
    )
    gain_one = whole_first_gain.astype(jnp.float32)
    shift_one = whole_first_shift.astype(jnp.float32)
    gain_two = whole_second_gain.astype(jnp.float32)
    shift_two = whole_second_shift.astype(jnp.float32)
    gain_three = whole_third_gain.astype(jnp.float32)
    shift_three = whole_third_shift.astype(jnp.float32)
    bias_self_query = whole_self_query_bias.astype(jnp.float32)
    bias_self_value = whole_self_value_bias.astype(jnp.float32)
    bias_self_output = whole_self_output_bias.astype(jnp.float32)
    bias_cross_query = whole_cross_query_bias.astype(jnp.float32)
    bias_cross_value = whole_cross_value_bias.astype(jnp.float32)
    bias_cross_output = whole_cross_output_bias.astype(jnp.float32)
    bias_inner = whole_ffn_inner_bias.astype(jnp.float32)
    bias_outer = whole_ffn_outer_bias.astype(jnp.float32)
    page_count, tok_rows, width = tokens.shape
    query_scale = 1.0 / math.sqrt(HEAD)
    positions = seq_index * tok_rows + jnp.arange(tok_rows, dtype=jnp.int32)
    valid_rows = (positions[None, :] < lengths[:, None]).astype(jnp.float32)
    key_places = jnp.arange(tok_rows * seq_count, dtype=jnp.int32)
    self_allowed = (key_places[None, None, :] <= positions[None, :, None]) & (
        key_places[None, None, :] < lengths[:, None, None]
    )
    token_values = tokens.astype(jnp.float32)
    normed_one = layer_norm(token_values, gain_one, shift_one).astype(jnp.bfloat16)
    queries_self = ((project(normed_one, whole_self_query) + bias_self_query) * query_scale).astype(
        jnp.bfloat16
    )
    keys_self = project(normed_one, whole_self_key).astype(jnp.bfloat16)
    values_self = (project(normed_one, whole_self_value) + bias_self_value).astype(jnp.bfloat16)
    keys_all, values_all = (
        lax.all_gather(keys_self, "seq", axis=1, tiled=True),
        lax.all_gather(values_self, "seq", axis=1, tiled=True),
    )
    mixed_self, lse_self = lax.map(
        attend_page, (queries_self, keys_all, values_all, self_allowed, valid_rows)
    )
    hidden_one = token_values + project(mixed_self, whole_self_output) + bias_self_output
    normed_two = layer_norm(hidden_one, gain_two, shift_two).astype(jnp.bfloat16)
    queries_cross = (
        (project(normed_two, whole_cross_query) + bias_cross_query) * query_scale
    ).astype(jnp.bfloat16)
    keys_patch = project(patches, whole_cross_key).astype(jnp.bfloat16)
    values_patch = (project(patches, whole_cross_value) + bias_cross_value).astype(jnp.bfloat16)
    cross_allowed = jnp.broadcast_to(
        (blank_mask == 0)[:, None, :], (page_count, tok_rows, blank_mask.shape[1])
    )
    patch_keys_all, patch_values_all = (
        lax.all_gather(keys_patch, "seq", axis=1, tiled=True),
        lax.all_gather(values_patch, "seq", axis=1, tiled=True),
    )
    mixed_cross, lse_cross = lax.map(
        attend_page, (queries_cross, patch_keys_all, patch_values_all, cross_allowed, valid_rows)
    )
    hidden_two = hidden_one + project(mixed_cross, whole_cross_output) + bias_cross_output
    normed_three = layer_norm(hidden_two, gain_three, shift_three).astype(jnp.bfloat16)
    inner_sum = project(normed_three, whole_ffn_inner) + bias_inner
    active = jax.nn.gelu(inner_sum, approximate=False).astype(jnp.bfloat16)
    outputs = (hidden_two + project(active, whole_ffn_outer) + bias_outer).astype(jnp.bfloat16)
    grad_active = project_back(cotangent, whole_ffn_outer)
    gelu_pull = jax.vjp(lambda argument: jax.nn.gelu(argument, approximate=False), inner_sum)[1]
    grad_inner = gelu_pull(grad_active)[0].astype(jnp.bfloat16)
    norm_pull = jax.vjp(layer_norm, hidden_two, gain_three, shift_three)[1]
    back_two, grad_gain_three, grad_shift_three = norm_pull(
        project_back(grad_inner, whole_ffn_inner)
    )
    grad_hidden_two = cotangent.astype(jnp.float32) + back_two
    valid_low = valid_rows.astype(jnp.bfloat16)[:, :, None]
    branch_cross = grad_hidden_two.astype(jnp.bfloat16)
    grad_mixed_cross = (
        project_back(branch_cross, whole_cross_output).astype(jnp.bfloat16) * valid_low
    )
    grad_queries_cross, cross_key_terms, cross_value_terms = lax.map(
        attend_back,
        (
            queries_cross,
            patch_keys_all,
            patch_values_all,
            cross_allowed,
            lse_cross,
            grad_mixed_cross,
        ),
    )
    grad_keys_patch, grad_values_patch = (
        lax.psum_scatter(
            cross_key_terms.astype(jnp.bfloat16), "seq", scatter_dimension=1, tiled=True
        ).astype(jnp.float32),
        lax.psum_scatter(
            cross_value_terms.astype(jnp.bfloat16), "seq", scatter_dimension=1, tiled=True
        ).astype(jnp.float32),
    )
    grad_keys_patch = grad_keys_patch.astype(jnp.bfloat16)
    grad_values_patch = grad_values_patch.astype(jnp.bfloat16)
    grad_patches = project_back(grad_keys_patch, whole_cross_key) + project_back(
        grad_values_patch, whole_cross_value
    )
    scaled_cross = grad_queries_cross * query_scale
    norm_pull = jax.vjp(layer_norm, hidden_one, gain_two, shift_two)[1]
    back_one, grad_gain_two, grad_shift_two = norm_pull(
        project_back(scaled_cross, whole_cross_query)
    )
    grad_hidden_one = grad_hidden_two + back_one
    branch_self = grad_hidden_one.astype(jnp.bfloat16)
    grad_mixed_self = project_back(branch_self, whole_self_output).astype(jnp.bfloat16) * valid_low
    grad_queries_self, self_key_terms, self_value_terms = lax.map(
        attend_back, (queries_self, keys_all, values_all, self_allowed, lse_self, grad_mixed_self)
    )
    grad_keys_self, grad_values_self = (
        lax.psum_scatter(
            self_key_terms.astype(jnp.bfloat16), "seq", scatter_dimension=1, tiled=True
        ).astype(jnp.float32),
        lax.psum_scatter(
            self_value_terms.astype(jnp.bfloat16), "seq", scatter_dimension=1, tiled=True
        ).astype(jnp.float32),
    )
    grad_keys_self = grad_keys_self.astype(jnp.bfloat16)
    grad_values_self = grad_values_self.astype(jnp.bfloat16)
    scaled_self = grad_queries_self * query_scale
    grad_normed_one = (
        project_back(scaled_self, whole_self_query)
        + project_back(grad_keys_self, whole_self_key)
        + project_back(grad_values_self, whole_self_value)
    )
    norm_pull = jax.vjp(layer_norm, token_values, gain_one, shift_one)[1]
    back_zero, grad_gain_one, grad_shift_one = norm_pull(grad_normed_one)
    grad_tokens = grad_hidden_one + back_zero
    shard_sums = (
        lax.psum_scatter(
            grad_gain_one.astype(jnp.bfloat16), "seq", scatter_dimension=0, tiled=True
        ).astype(jnp.float32),
        lax.psum_scatter(
            grad_shift_one.astype(jnp.bfloat16), "seq", scatter_dimension=0, tiled=True
        ).astype(jnp.float32),
        lax.psum_scatter(
            outer_sum(normed_one, scaled_self).astype(jnp.bfloat16),
            "seq",
            scatter_dimension=0,
            tiled=True,
        ).astype(jnp.float32),
        lax.psum_scatter(
            column_sum(scaled_self).astype(jnp.bfloat16), "seq", scatter_dimension=0, tiled=True
        ).astype(jnp.float32),
        lax.psum_scatter(
            outer_sum(normed_one, grad_keys_self).astype(jnp.bfloat16),
            "seq",
            scatter_dimension=0,
            tiled=True,
        ).astype(jnp.float32),
        lax.psum_scatter(
            outer_sum(normed_one, grad_values_self).astype(jnp.bfloat16),
            "seq",
            scatter_dimension=0,
            tiled=True,
        ).astype(jnp.float32),
        lax.psum_scatter(
            column_sum(grad_values_self).astype(jnp.bfloat16),
            "seq",
            scatter_dimension=0,
            tiled=True,
        ).astype(jnp.float32),
        lax.psum_scatter(
            outer_sum(mixed_self, branch_self).astype(jnp.bfloat16),
            "seq",
            scatter_dimension=0,
            tiled=True,
        ).astype(jnp.float32),
        lax.psum_scatter(
            column_sum(branch_self).astype(jnp.bfloat16), "seq", scatter_dimension=0, tiled=True
        ).astype(jnp.float32),
        lax.psum_scatter(
            grad_gain_two.astype(jnp.bfloat16), "seq", scatter_dimension=0, tiled=True
        ).astype(jnp.float32),
        lax.psum_scatter(
            grad_shift_two.astype(jnp.bfloat16), "seq", scatter_dimension=0, tiled=True
        ).astype(jnp.float32),
        lax.psum_scatter(
            outer_sum(normed_two, scaled_cross).astype(jnp.bfloat16),
            "seq",
            scatter_dimension=0,
            tiled=True,
        ).astype(jnp.float32),
        lax.psum_scatter(
            column_sum(scaled_cross).astype(jnp.bfloat16), "seq", scatter_dimension=0, tiled=True
        ).astype(jnp.float32),
        lax.psum_scatter(
            outer_sum(patches, grad_keys_patch).astype(jnp.bfloat16),
            "seq",
            scatter_dimension=0,
            tiled=True,
        ).astype(jnp.float32),
        lax.psum_scatter(
            outer_sum(patches, grad_values_patch).astype(jnp.bfloat16),
            "seq",
            scatter_dimension=0,
            tiled=True,
        ).astype(jnp.float32),
        lax.psum_scatter(
            column_sum(grad_values_patch).astype(jnp.bfloat16),
            "seq",
            scatter_dimension=0,
            tiled=True,
        ).astype(jnp.float32),
        lax.psum_scatter(
            outer_sum(mixed_cross, branch_cross).astype(jnp.bfloat16),
            "seq",
            scatter_dimension=0,
            tiled=True,
        ).astype(jnp.float32),
        lax.psum_scatter(
            column_sum(branch_cross).astype(jnp.bfloat16), "seq", scatter_dimension=0, tiled=True
        ).astype(jnp.float32),
        lax.psum_scatter(
            grad_gain_three.astype(jnp.bfloat16), "seq", scatter_dimension=0, tiled=True
        ).astype(jnp.float32),
        lax.psum_scatter(
            grad_shift_three.astype(jnp.bfloat16), "seq", scatter_dimension=0, tiled=True
        ).astype(jnp.float32),
        lax.psum_scatter(
            outer_sum(normed_three, grad_inner).astype(jnp.bfloat16),
            "seq",
            scatter_dimension=0,
            tiled=True,
        ).astype(jnp.float32),
        lax.psum_scatter(
            column_sum(grad_inner).astype(jnp.bfloat16), "seq", scatter_dimension=0, tiled=True
        ).astype(jnp.float32),
        lax.psum_scatter(
            outer_sum(active, cotangent).astype(jnp.bfloat16),
            "seq",
            scatter_dimension=0,
            tiled=True,
        ).astype(jnp.float32),
        lax.psum_scatter(
            column_sum(cotangent).astype(jnp.bfloat16), "seq", scatter_dimension=0, tiled=True
        ).astype(jnp.float32),
    )
    totals = (
        lax.psum(shard_sums[0].astype(jnp.bfloat16), "page").astype(jnp.float32),
        lax.psum(shard_sums[1].astype(jnp.bfloat16), "page").astype(jnp.float32),
        lax.psum(shard_sums[2].astype(jnp.bfloat16), "page").astype(jnp.float32),
        lax.psum(shard_sums[3].astype(jnp.bfloat16), "page").astype(jnp.float32),
        lax.psum(shard_sums[4].astype(jnp.bfloat16), "page").astype(jnp.float32),
        lax.psum(shard_sums[5].astype(jnp.bfloat16), "page").astype(jnp.float32),
        lax.psum(shard_sums[6].astype(jnp.bfloat16), "page").astype(jnp.float32),
        lax.psum(shard_sums[7].astype(jnp.bfloat16), "page").astype(jnp.float32),
        lax.psum(shard_sums[8].astype(jnp.bfloat16), "page").astype(jnp.float32),
        lax.psum(shard_sums[9].astype(jnp.bfloat16), "page").astype(jnp.float32),
        lax.psum(shard_sums[10].astype(jnp.bfloat16), "page").astype(jnp.float32),
        lax.psum(shard_sums[11].astype(jnp.bfloat16), "page").astype(jnp.float32),
        lax.psum(shard_sums[12].astype(jnp.bfloat16), "page").astype(jnp.float32),
        lax.psum(shard_sums[13].astype(jnp.bfloat16), "page").astype(jnp.float32),
        lax.psum(shard_sums[14].astype(jnp.bfloat16), "page").astype(jnp.float32),
        lax.psum(shard_sums[15].astype(jnp.bfloat16), "page").astype(jnp.float32),
        lax.psum(shard_sums[16].astype(jnp.bfloat16), "page").astype(jnp.float32),
        lax.psum(shard_sums[17].astype(jnp.bfloat16), "page").astype(jnp.float32),
        lax.psum(shard_sums[18].astype(jnp.bfloat16), "page").astype(jnp.float32),
        lax.psum(shard_sums[19].astype(jnp.bfloat16), "page").astype(jnp.float32),
        lax.psum(shard_sums[20].astype(jnp.bfloat16), "page").astype(jnp.float32),
        lax.psum(shard_sums[21].astype(jnp.bfloat16), "page").astype(jnp.float32),
        lax.psum(shard_sums[22].astype(jnp.bfloat16), "page").astype(jnp.float32),
        lax.psum(shard_sums[23].astype(jnp.bfloat16), "page").astype(jnp.float32),
    )
    return (
        outputs,
        grad_tokens,
        grad_patches,
        totals[0],
        totals[1],
        totals[2],
        totals[3],
        totals[4],
        totals[5],
        totals[6],
        totals[7],
        totals[8],
        totals[9],
        totals[10],
        totals[11],
        totals[12],
        totals[13],
        totals[14],
        totals[15],
        totals[16],
        totals[17],
        totals[18],
        totals[19],
        totals[20],
        totals[21],
        totals[22],
        totals[23],
    )


def solution(mesh):
    placed = (
        P("page", "seq", None),
        P("page", "seq", None),
        P("page"),
        P("page", None),
        P("page", "seq", None),
        P("seq"),
        P("seq"),
        P("seq", None),
        P("seq"),
        P("seq", None),
        P("seq", None),
        P("seq"),
        P("seq", None),
        P("seq"),
        P("seq"),
        P("seq"),
        P("seq", None),
        P("seq"),
        P("seq", None),
        P("seq", None),
        P("seq"),
        P("seq", None),
        P("seq"),
        P("seq"),
        P("seq"),
        P("seq", None),
        P("seq"),
        P("seq", None),
        P("seq"),
    )
    return jax.shard_map(
        on_device,
        mesh=mesh,
        in_specs=placed,
        out_specs=(
            P("page", "seq", None),
            P("page", "seq", None),
            P("page", "seq", None),
            P("seq"),
            P("seq"),
            P("seq", None),
            P("seq"),
            P("seq", None),
            P("seq", None),
            P("seq"),
            P("seq", None),
            P("seq"),
            P("seq"),
            P("seq"),
            P("seq", None),
            P("seq"),
            P("seq", None),
            P("seq", None),
            P("seq"),
            P("seq", None),
            P("seq"),
            P("seq"),
            P("seq"),
            P("seq", None),
            P("seq"),
            P("seq", None),
            P("seq"),
        ),
        check_vma=False,
    )
```

profile of v0, /device:TPU:0, one launch (start us, length us, event | category | flops | bytes accessed | tf_op | source)
XLA Modules:
  0.0 1758.5 jit_solution(36208972090598465)
XLA Ops:
  21.0 24.4 %all-gather.36.cloned.1.call-done = bf16[1024,1024]{1,0:T(8,128)(2,1)} async-done(((bf16[512,1024]{1,0:T(8,128)(2,1)}), bf16[1024,1024]{1,0:T(8,128)(2,1)}) %all-gather.36.cloned.1.call-update) | async-done | bytes 2097168 | tf_op jit(solution)/shard_map/all_gather | solution.py:155
  53.8 26.4 %all-gather.32.cloned.1.call-done = bf16[1024,1024]{1,0:T(8,128)(2,1)} async-done(((bf16[512,1024]{1,0:T(8,128)(2,1)}), bf16[1024,1024]{1,0:T(8,128)(2,1)}) %all-gather.32.cloned.1.call-update) | async-done | bytes 2097168 | tf_op jit(solution)/shard_map/all_gather | solution.py:156
  85.6 29.3 %all-gather.44.cloned.1.call-done = bf16[1024,1024]{1,0:T(8,128)(2,1)} async-done(((bf16[512,1024]{1,0:T(8,128)(2,1)}), bf16[1024,1024]{1,0:T(8,128)(2,1)}) %all-gather.44.cloned.1.call-update) | async-done | bytes 2097168 | tf_op jit(solution)/shard_map/all_gather | solution.py:164
  123.2 26.2 %all-gather.40.cloned.1.call-done = bf16[1024,1024]{1,0:T(8,128)(2,1)} async-done(((bf16[512,1024]{1,0:T(8,128)(2,1)}), bf16[1024,1024]{1,0:T(8,128)(2,1)}) %all-gather.40.cloned.1.call-update) | async-done | bytes 2097168 | tf_op jit(solution)/shard_map/all_gather | solution.py:165
  205.3 14.1 all-gather.54.cloned.1.call-done
  223.3 18.0 %select_reduce_fusion = (f32[16,512]{1,0:T(8,128)S(1)}, f32[16,512,1024]{2,1,0:T(8,128)}) fusion(pred[512,1024]{1,0:T(8,128)(4,1)S(1)} %fusion.46, bf16[512,16,64]{0,2,1:T(8,128)(2,1)} %bitcast.265, bf16[1024,16,64]{0,2,1:T(8,128)(2,1)} %bitcast.255), kind=kOutput, calls=%fused_computation.13 | convolution fusion | flops 1090510848 | bytes 37257216 | tf_op jit(solution)/shard_map/while/body/eval_jaxpr/qhd,khd->hqk/dot_general | solution.py:43
  241.3 14.5 fusion.1
  260.4 15.0 fusion.13
  277.1 12.3 all-gather.38.cloned.1.call-done
  294.0 30.1 %all-gather.42.cloned.1.call-done = bf16[1024,1024]{1,0:T(8,128)(2,1)} async-done(((bf16[512,1024]{1,0:T(8,128)(2,1)}), bf16[1024,1024]{1,0:T(8,128)(2,1)}) %all-gather.42.cloned.1.call-update) | async-done | bytes 2097168 | tf_op jit(solution)/shard_map/all_gather | solution.py:162
  328.9 31.7 %all-gather.58.cloned.1.call-done = bf16[1088,1024]{1,0:T(8,128)(2,1)} async-done(((bf16[544,1024]{1,0:T(8,128)(2,1)}), bf16[1088,1024]{1,0:T(8,128)(2,1)}) %all-gather.58.cloned.1.call-update) | async-done | bytes 2228240 | tf_op jit(solution)/shard_map/all_gather | solution.py:223
  363.8 16.7 fusion.108
  380.5 13.6 fusion
  400.3 18.1 %fusion.44 = (bf16[512,16,64]{0,2,1:T(8,128)(2,1)}, bf16[512,16,64]{0,2,1:T(8,128)(2,1)}, f32[16,64,512]{2,1,0:T(8,128)}) fusion(f32[512]{0:T(512)S(1)} %compare_convert_fusion, f32[16,64,512]{2,1,0:T(8,128)} %copy-done.30, bf16[1088,16,64]{0,2,1:T(8,128)(2,1)S(1)} %bitcast.253, f32[16,512,1088]{1,2,0:T(8,128)} %get-tuple-element.280, ...), kind=kOutput, calls=%fused_computation.87 | convolution fusion | flops 1169686528 | bytes 44238848 | tf_op jit(solution)/shard_map/while/body/eval_jaxpr/hqk,khd->qhd/dot_general | solution.py:59
  421.3 10.6 all-gather.46.cloned.1.call-done
  437.5 100.0 %all-gather.48.cloned.1.call-done = bf16[1024,4096]{1,0:T(8,128)(2,1)} async-done(((bf16[512,4096]{1,0:T(8,128)(2,1)}), bf16[1024,4096]{1,0:T(8,128)(2,1)}) %all-gather.48.cloned.1.call-update) | async-done | bytes 8388624 | tf_op jit(solution)/shard_map/all_gather | solution.py:171
  537.5 28.4 %multiply_convert_fusion.2 = (bf16[512,4096]{1,0:T(8,128)(2,1)}, f32[512,4096]{1,0:T(8,128)}, f32[512,4096]{1,0:T(8,128)}) fusion(f32[4096]{0:T(1024)S(1)} %copy-done.64, bf16[1024,4096]{1,0:T(8,128)(2,1)} %all-gather.48.cloned.1.call-done, f32[1,512,1024]{2,1,0:T(8,128)} %copy-done.16, f32[1024]{0:T(1024)S(1)} %bitcast.303, f32[1024]{0:T(1024)S(1)} %bitcast.289, ...), kind=kOutput, calls=%fused_computation.27 | convolution fusion | flops 4436000768 | bytes 31485952 | tf_op jit(solution)/shard_map/ptd,de->pte/dot_general | solution.py:23
  565.9 77.0 %all-gather.50.cloned.1.call-done = bf16[4096,1024]{1,0:T(8,128)(2,1)} async-done(((bf16[2048,1024]{1,0:T(8,128)(2,1)}), bf16[4096,1024]{1,0:T(8,128)(2,1)}) %all-gather.50.cloned.1.call-update) | async-done | bytes 8388624 | tf_op jit(solution)/shard_map/all_gather | solution.py:173
  643.0 14.2 fusion.110
  657.2 9.6 fusion.37
  675.3 25.7 %multiply_reduce_fusion = (f32[16,512]{1,0:T(8,128)S(1)}, f32[16,512,1088]{1,2,0:T(8,128)}) fusion(f32[16,512,1088]{1,2,0:T(8,128)} %get-tuple-element.280, f32[16,512]{1,0:T(8,128)S(1)} %log_add_fusion.1, bf16[512,16,64]{0,2,1:T(8,128)(2,1)} %bitcast.259, bf16[1088,16,64]{0,2,1:T(8,128)(2,1)S(1)} %bitcast.254), kind=kOutput, calls=%fused_computation.1 | convolution fusion | flops 1167581184 | bytes 74645504 | tf_op jit(solution)/shard_map/while/body/eval_jaxpr/qhd,khd->hqk/dot_general | solution.py:71
  701.0 29.8 %multiply_convert_fusion = bf16[16,512,1088]{1,2,0:T(8,128)(2,1)} fusion(f32[16,512,1088]{1,2,0:T(8,128)} %get-tuple-element.286, f32[16,512,1088]{1,2,0:T(8,128)} %get-tuple-element.280, f32[16,512]{1,0:T(8,128)S(1)} %get-tuple-element.285, f32[16,512]{1,0:T(8,128)S(1)} %log_add_fusion.1), kind=kLoop, calls=%fused_computation | loop fusion | flops 35651584 | bytes 89194496 | tf_op jit(solution)/shard_map/while/body/eval_jaxpr/convert_element_type | solution.py:75
  730.9 10.1 bitcast_reduce_fusion.1
  752.5 15.4 fusion.47
  767.9 25.0 %multiply_reduce_fusion.1 = (f32[16,512]{1,0:T(8,128)S(1)}, f32[16,512,1024]{2,1,0:T(8,128)}) fusion(f32[16,512,1024]{2,1,0:T(8,128)} %get-tuple-element.276, f32[16,512]{1,0:T(8,128)S(1)} %copy-done.48, pred[512,1024]{1,0:T(8,128)(4,1)S(1)} %copy-done.7, bf16[512,16,64]{0,2,1:T(8,128)(2,1)S(1)} %bitcast.273, bf16[1024,16,64]{0,2,1:T(8,128)(2,1)} %bitcast.264), kind=kOutput, calls=%fused_computation.6 | convolution fusion | flops 1107288064 | bytes 70844416 | tf_op jit(solution)/shard_map/while/body/eval_jaxpr/qhd,khd->hqk/dot_general | solution.py:71
  793.0 28.7 %multiply_convert_fusion.1 = bf16[16,512,1024]{2,1,0:T(8,128)(2,1)} fusion(f32[16,512,1024]{2,1,0:T(8,128)} %get-tuple-element.289, f32[16,512,1024]{2,1,0:T(8,128)} %get-tuple-element.276, f32[16,512]{1,0:T(8,128)S(1)} %get-tuple-element.288, f32[16,512]{1,0:T(8,128)S(1)} %copy-done.48, pred[512,1024]{1,0:T(8,128)(4,1)S(1)} %copy-done.7), kind=kLoop, calls=%fused_computation.5 | loop fusion | flops 41943040 | bytes 84475904 | tf_op jit(solution)/shard_map/while/body/eval_jaxpr/convert_element_type | solution.py:75
  821.6 10.2 convolution_convert_fusion.9
  833.1 16.3 fusion.20
  849.3 11.2 copy.96
  866.3 12.8 convolution_convert_fusion.2
  879.1 11.2 copy.94
  910.2 11.7 bitcast_reduce_fusion
  933.8 5.6 fusion.103
  959.9 11.0 convolution_convert_fusion.1
  972.0 9.0 convolution_convert_fusion
  981.1 22.8 %reduce-scatter.31.cloned.1.call-done = bf16[512,1024]{1,0:T(8,128)(2,1)} async-done(((bf16[1024,1024]{1,0:T(8,128)(2,1)}), bf16[512,1024]{1,0:T(8,128)(2,1)}) %reduce-scatter.31.cloned.1.call-update) | async-done | bytes 1048592 | tf_op jit(solution)/shard_map/reduce_scatter | solution.py:350
  1004.0 34.1 %reduce-scatter.29.cloned.1.call-done = bf16[512,1024]{1,0:T(8,128)(2,1)} async-done(((bf16[1024,1024]{1,0:T(8,128)(2,1)}), bf16[512,1024]{1,0:T(8,128)(2,1)}) %reduce-scatter.29.cloned.1.call-update) | async-done | bytes 1048592 | tf_op jit(solution)/shard_map/reduce_scatter | solution.py:335
  1038.1 34.8 %reduce-scatter.23.cloned.1.call-done = bf16[512,1024]{1,0:T(8,128)(2,1)} async-done(((bf16[1024,1024]{1,0:T(8,128)(2,1)}), bf16[512,1024]{1,0:T(8,128)(2,1)}) %reduce-scatter.23.cloned.1.call-update) | async-done | bytes 1048592 | tf_op jit(solution)/shard_map/reduce_scatter | solution.py:308
  1072.8 34.7 %reduce-scatter.27.cloned.1.call-done = bf16[512,1024]{1,0:T(8,128)(2,1)} async-done(((bf16[1024,1024]{1,0:T(8,128)(2,1)}), bf16[512,1024]{1,0:T(8,128)(2,1)}) %reduce-scatter.27.cloned.1.call-update) | async-done | bytes 1048592 | tf_op jit(solution)/shard_map/reduce_scatter | solution.py:323
  1107.6 34.6 %reduce-scatter.25.cloned.1.call-done = bf16[512,1024]{1,0:T(8,128)(2,1)} async-done(((bf16[1024,1024]{1,0:T(8,128)(2,1)}), bf16[512,1024]{1,0:T(8,128)(2,1)}) %reduce-scatter.25.cloned.1.call-update) | async-done | bytes 1048592 | tf_op jit(solution)/shard_map/reduce_scatter | solution.py:317
  1142.2 34.7 %reduce-scatter.35.cloned.1.call-done = bf16[512,1024]{0,1:T(8,128)(2,1)} async-done(((bf16[1024,1024]{0,1:T(8,128)(2,1)}), bf16[512,1024]{0,1:T(8,128)(2,1)}) %reduce-scatter.35.cloned.1.call-update) | async-done | bytes 1048592 | tf_op jit(solution)/shard_map/reduce_scatter | solution.py:365
  1176.9 34.6 %reduce-scatter.33.cloned.1.call-done = bf16[512,1024]{0,1:T(8,128)(2,1)} async-done(((bf16[1024,1024]{0,1:T(8,128)(2,1)}), bf16[512,1024]{0,1:T(8,128)(2,1)}) %reduce-scatter.33.cloned.1.call-update) | async-done | bytes 1048592 | tf_op jit(solution)/shard_map/reduce_scatter | solution.py:359
  1211.5 102.0 %reduce-scatter.39.cloned.1.call-done = bf16[512,4096]{1,0:T(8,128)(2,1)} async-done(((bf16[1024,4096]{1,0:T(8,128)(2,1)}), bf16[512,4096]{1,0:T(8,128)(2,1)}) %reduce-scatter.39.cloned.1.call-update) | async-done | bytes 4194320 | tf_op jit(solution)/shard_map/reduce_scatter | solution.py:392
  1313.5 102.2 %reduce-scatter.41.cloned.1.call-done = bf16[2048,1024]{1,0:T(8,128)(2,1)} async-done(((bf16[4096,1024]{1,0:T(8,128)(2,1)}), bf16[2048,1024]{1,0:T(8,128)(2,1)}) %reduce-scatter.41.cloned.1.call-update) | async-done | bytes 4194320 | tf_op jit(solution)/shard_map/reduce_scatter | solution.py:401
  1430.9 9.2 fusion.42
  1453.8 7.0 all-reduce.16
  1461.8 63.1 %all-reduce.14 = (bf16[512]{0:T(512)(128)(2,1)S(1)}, bf16[512]{0:T(512)(128)(2,1)S(1)}, bf16[512]{0:T(512)(128)(2,1)S(1)}, bf16[512]{0:T(512)(128)(2,1)S(1)}, bf...) all-reduce(bf16[512]{0:T(512)(128)(2,1)S(1)} %dynamic-slice.1, ...), channel_id=1, replica_groups=mesh['page'=16,'seq'=2] {'page'}, use_global_device_ids=true, to_apply=%region_24.25 | all-reduce | flops 8704 | bytes 34816 | tf_op jit(solution)/shard_map/psum | solution.py:412
  1539.4 188.8 %all-reduce.19.cloned.1.call-done = (bf16[512,1024]{0,1:T(8,128)(2,1)}, bf16[512,1024]{0,1:T(8,128)(2,1)}, bf16[512,1024]{1,0:T(8,128)(2,1)}, bf16[512,1024]{1,0...) async-done(((bf16[512,1024]{0,1:T(8,128)(2,1)}, ...) | async-done | bytes 16777232 | tf_op jit(solution)/shard_map/psum | solution.py:425
  (445 shorter events, 274.4 us)
Async XLA Ops:
  7.2 107.6 %copy-start = (bf16[1,544,1024]{2,1,0:T(8,128)(2,1)S(1)}, bf16[1,544,1024]{2,1,0:T(8,128)(2,1)}, u32[]{:S(2)}) copy-start(bf16[1,544,1024]{2,1,0:T(8,128)(2,1)} %param.30) | copy-start | bytes 3342340
  7.2 38.2 %all-gather.36.cloned.1.call-start = ((), (), s32[]{:S(2)}) async-start(), calls=%async_computation.16 | async-start | bytes 3145728 | tf_op jit(solution)/shard_map/all_gather | solution.py:155
  8.0 72.2 %all-gather.32.cloned.1.call-start = ((), (), s32[]{:S(2)}) async-start(), calls=%async_computation.14 | async-start | bytes 3145728 | tf_op jit(solution)/shard_map/all_gather | solution.py:156
  8.7 106.1 %all-gather.44.cloned.1.call-start = ((), (), s32[]{:S(2)}) async-start(), calls=%async_computation.20 | async-start | bytes 3145728 | tf_op jit(solution)/shard_map/all_gather | solution.py:164
  9.5 139.9 %all-gather.40.cloned.1.call-start = ((), (), s32[]{:S(2)}) async-start(), calls=%async_computation.18 | async-start | bytes 3145728 | tf_op jit(solution)/shard_map/all_gather | solution.py:165
  10.0 188.7 %all-gather.34.cloned.1.call-start = ((), (), s32[]{:S(2)}) async-start(), calls=%async_computation.15 | async-start | bytes 3145728 | tf_op jit(solution)/shard_map/all_gather | solution.py:153
  10.6 208.7 %all-gather.54.cloned.1.call-start = ((), (), s32[]{:S(2)}) async-start(), calls=%async_computation.37 | async-start | bytes 3145728 | tf_op jit(solution)/shard_map/all_gather | solution.py:206
  16.0 182.8 %copy-start.50 = (f32[2,1,512]{2,1,0:T(1,128)}, f32[2,1,512]{2,1,0:T(1,128)S(1)}, u32[]{:S(2)}) copy-start(f32[2,1,512]{2,1,0:T(1,128)S(1)} %convert_element_type.581) | copy-start | bytes 12292
  20.3 178.5 %copy-start.80 = (f32[2,1,512]{2,1,0:T(1,128)}, f32[2,1,512]{2,1,0:T(1,128)S(1)}, u32[]{:S(2)}) copy-start(f32[2,1,512]{2,1,0:T(1,128)S(1)} %convert_element_type.582) | copy-start | bytes 12292
  20.6 178.2 %copy-start.52 = (f32[512]{0:T(512)}, f32[512]{0:T(512)S(1)}, u32[]{:S(2)}) copy-start(f32[512]{0:T(512)S(1)} %broadcast_multiply_fusion.2) | copy-start | bytes 6148
  21.0 177.8 %copy-start.54 = (f32[512]{0:T(512)}, f32[512]{0:T(512)S(1)}, u32[]{:S(2)}) copy-start(f32[512]{0:T(512)S(1)} %fusion.81) | copy-start | bytes 6148
  49.4 207.1 %all-gather.52.cloned.1.call-start = ((), (), s32[]{:S(2)}) async-start(), calls=%async_computation.36 | async-start | bytes 3145728 | tf_op jit(solution)/shard_map/all_gather | solution.py:207
  84.0 205.3 %all-gather.38.cloned.1.call-start = ((), (), s32[]{:S(2)}) async-start(), calls=%async_computation.17 | async-start | bytes 3145728 | tf_op jit(solution)/shard_map/all_gather | solution.py:158
  84.8 239.2 %all-gather.42.cloned.1.call-start = ((), (), s32[]{:S(2)}) async-start(), calls=%async_computation.19 | async-start | bytes 3145728 | tf_op jit(solution)/shard_map/all_gather | solution.py:162
  85.5 275.1 %all-gather.58.cloned.1.call-start = ((), (), s32[]{:S(2)}) async-start(), calls=%async_computation.39 | async-start | bytes 3342336 | tf_op jit(solution)/shard_map/all_gather | solution.py:223
  118.8 278.6 %all-gather.56.cloned.1.call-start = ((), (), s32[]{:S(2)}) async-start(), calls=%async_computation.38 | async-start | bytes 3342336 | tf_op jit(solution)/shard_map/all_gather | solution.py:224
  153.3 278.6 %all-gather.46.cloned.1.call-start = ((), (), s32[]{:S(2)}) async-start(), calls=%async_computation.21 | async-start | bytes 3145728 | tf_op jit(solution)/shard_map/all_gather | solution.py:167
  153.9 383.6 %all-gather.48.cloned.1.call-start = ((), (), s32[]{:S(2)}) async-start(), calls=%async_computation.22 | async-start | bytes 12582912 | tf_op jit(solution)/shard_map/all_gather | solution.py:171
  154.8 33.7 %copy-start.100 = (bf16[512]{0:T(512)(128)(2,1)S(1)}, bf16[512]{0:T(512)(128)(2,1)}, u32[]{:S(2)}) copy-start(bf16[512]{0:T(512)(128)(2,1)} %param.53) | copy-start | bytes 3076
  154.8 38.6 %copy-start.79 = (bf16[2048]{0:T(1024)(128)(2,1)S(1)}, bf16[2048]{0:T(1024)(128)(2,1)}, u32[]{:S(2)}) copy-start(bf16[2048]{0:T(1024)(128)(2,1)} %param.55) | copy-start | bytes 12292
  154.8 488.2 %all-gather.50.cloned.1.call-start = ((), (), s32[]{:S(2)}) async-start(), calls=%async_computation.23 | async-start | bytes 12582912 | tf_op jit(solution)/shard_map/all_gather | solution.py:173
  155.4 769.6 %reduce-scatter.21.cloned.1.call-start = ((), (), s32[]{:S(2)}) async-start(), calls=%async_computation.25 | async-start | bytes 3145728 | tf_op jit(solution)/shard_map/reduce_scatter | solution.py:286
  169.8 154.2 %copy-start.67 = (f32[2,1,512]{2,1,0:T(1,128)}, f32[2,1,512]{2,1,0:T(1,128)S(1)}, u32[]{:S(2)}) copy-start(f32[2,1,512]{2,1,0:T(1,128)S(1)} %convert_element_type.587) | copy-start | bytes 12292
  174.2 149.8 %copy-start.84 = (f32[2,1,512]{2,1,0:T(1,128)}, f32[2,1,512]{2,1,0:T(1,128)S(1)}, u32[]{:S(2)}) copy-start(f32[2,1,512]{2,1,0:T(1,128)S(1)} %convert_element_type.588) | copy-start | bytes 12292
  198.8 61.6 %copy-start.6 = (pred[512,1024]{1,0:T(8,128)(4,1)}, pred[512,1024]{1,0:T(8,128)(4,1)S(1)}, u32[]{:S(2)}) copy-start(pred[512,1024]{1,0:T(8,128)(4,1)S(1)} %fusion.46) | copy-start | bytes 1572868
  292.3 35.3 %copy-start.60 = (f32[512]{0:T(512)}, f32[512]{0:T(512)S(1)}, u32[]{:S(2)}) copy-start(f32[512]{0:T(512)S(1)} %broadcast_multiply_fusion.1) | copy-start | bytes 6148
  293.9 33.6 %copy-start.62 = (f32[512]{0:T(512)}, f32[512]{0:T(512)S(1)}, u32[]{:S(2)}) copy-start(f32[512]{0:T(512)S(1)} %multiply_reduce_fusion.3) | copy-start | bytes 6148
  294.0 33.6 %copy-start.75 = (f32[512]{0:T(512)}, f32[512]{0:T(512)S(1)}, u32[]{:S(2)}) copy-start(f32[512]{0:T(512)S(1)} %fusion.82) | copy-start | bytes 6148
  435.8 101.7 %copy-start.64 = (f32[4096]{0:T(1024)S(1)}, f32[4096]{0:T(1024)}, u32[]{:S(2)}) copy-start(f32[4096]{0:T(1024)} %convert_element_type.506) | copy-start | bytes 49156
  435.8 101.7 %copy-start.65 = (f32[2,1,512]{2,1,0:T(1,128)S(1)}, f32[2,1,512]{2,1,0:T(1,128)}, u32[]{:S(2)}) copy-start(f32[2,1,512]{2,1,0:T(1,128)} %convert_element_type.591) | copy-start | bytes 12292
  435.9 101.7 %copy-start.82 = (f32[2,1,512]{2,1,0:T(1,128)S(1)}, f32[2,1,512]{2,1,0:T(1,128)}, u32[]{:S(2)}) copy-start(f32[2,1,512]{2,1,0:T(1,128)} %convert_element_type.592) | copy-start | bytes 12292
  435.9 230.9 %copy-start.58 = (f32[512]{0:T(512)}, f32[512]{0:T(512)S(1)}, u32[]{:S(2)}) copy-start(f32[512]{0:T(512)S(1)} %broadcast_multiply_fusion) | copy-start | bytes 6148
  437.5 229.3 %copy-start.73 = (f32[512]{0:T(512)}, f32[512]{0:T(512)S(1)}, u32[]{:S(2)}) copy-start(f32[512]{0:T(512)S(1)} %fusion.83) | copy-start | bytes 6148
  792.9 136.3 %reduce-scatter.19.cloned.1.call-start = ((), (), s32[]{:S(2)}) async-start(), calls=%async_computation.24 | async-start | bytes 3145728 | tf_op jit(solution)/shard_map/reduce_scatter | solution.py:283
  831.9 101.9 %reduce-scatter.45.cloned.1.call-start = ((), (), s32[]{:S(2)}) async-start(), calls=%async_computation.41 | async-start | bytes 3342336
  865.1 82.3 %reduce-scatter.43.cloned.1.call-start = ((), (), s32[]{:S(2)}) async-start(), calls=%async_computation.40 | async-start | bytes 3342336
  894.8 86.3 %reduce-scatter.37.cloned.1.call-start = ((), (), s32[]{:S(2)}) async-start(), calls=%async_computation.33 | async-start | bytes 3145728 | tf_op jit(solution)/shard_map/reduce_scatter | solution.py:377
  898.9 105.1 %reduce-scatter.31.cloned.1.call-start = ((), (), s32[]{:S(2)}) async-start(), calls=%async_computation.30 | async-start | bytes 3145728 | tf_op jit(solution)/shard_map/reduce_scatter | solution.py:350
  904.8 133.3 %reduce-scatter.29.cloned.1.call-start = ((), (), s32[]{:S(2)}) async-start(), calls=%async_computation.29 | async-start | bytes 3145728 | tf_op jit(solution)/shard_map/reduce_scatter | solution.py:335
  910.2 162.7 %reduce-scatter.23.cloned.1.call-start = ((), (), s32[]{:S(2)}) async-start(), calls=%async_computation.26 | async-start | bytes 3145728 | tf_op jit(solution)/shard_map/reduce_scatter | solution.py:308
  924.9 182.6 %reduce-scatter.27.cloned.1.call-start = ((), (), s32[]{:S(2)}) async-start(), calls=%async_computation.28 | async-start | bytes 3145728 | tf_op jit(solution)/shard_map/reduce_scatter | solution.py:323
  929.1 213.1 %reduce-scatter.25.cloned.1.call-start = ((), (), s32[]{:S(2)}) async-start(), calls=%async_computation.27 | async-start | bytes 3145728 | tf_op jit(solution)/shard_map/reduce_scatter | solution.py:317
  933.3 243.6 %reduce-scatter.35.cloned.1.call-start = ((), (), s32[]{:S(2)}) async-start(), calls=%async_computation.32 | async-start | bytes 3145728 | tf_op jit(solution)/shard_map/reduce_scatter | solution.py:365
  947.4 264.1 %reduce-scatter.33.cloned.1.call-start = ((), (), s32[]{:S(2)}) async-start(), calls=%async_computation.31 | async-start | bytes 3145728 | tf_op jit(solution)/shard_map/reduce_scatter | solution.py:359
  959.2 354.3 %reduce-scatter.39.cloned.1.call-start = ((), (), s32[]{:S(2)}) async-start(), calls=%async_computation.34 | async-start | bytes 12582912 | tf_op jit(solution)/shard_map/reduce_scatter | solution.py:392
  970.8 444.9 %reduce-scatter.41.cloned.1.call-start = ((), (), s32[]{:S(2)}) async-start(), calls=%async_computation.35 | async-start | bytes 12582912 | tf_op jit(solution)/shard_map/reduce_scatter | solution.py:401
  981.0 747.2 %all-reduce.19.cloned.1.call-start = ((), (), s32[]{:S(2)}) async-start(), calls=%async_computation.42 | async-start | bytes 33554432 | tf_op jit(solution)/shard_map/psum | solution.py:425
  1449.9 83.1 %copy-start.36 = (bf16[1,544,1024]{1,2,0:T(8,128)(2,1)S(1)}, bf16[1,544,1024]{1,2,0:T(8,128)(2,1)}, u32[]{:S(2)}) copy-start(bf16[1,544,1024]{1,2,0:T(8,128)(2,1)} %copy-done.35) | copy-start | bytes 3342340
  (93 other events, 571.8 us)
Sparse Core Ops, SparseCore 0:
  9.6 35.8 all-gather.35
  47.0 33.1 all-gather.31
  81.7 33.1 all-gather.43
  116.2 33.1 all-gather.39
  150.8 33.3 all-gather.33
  186.2 33.1 all-gather.53
  221.5 33.1 all-gather.51
  256.2 33.1 all-gather.37
  290.9 33.1 all-gather.41
  326.0 34.5 all-gather.57
  362.7 34.5 all-gather.55
  398.8 33.1 all-gather.45
  433.5 103.9 all-gather.47
  538.9 103.9 all-gather.49
  793.0 31.8 reduce-scatter.20
  832.0 32.3 reduce-scatter.18
  866.4 33.2 reduce-scatter.44
  902.5 33.2 reduce-scatter.42
  938.1 31.8 reduce-scatter.36
  972.1 31.8 reduce-scatter.30
  1006.2 31.8 reduce-scatter.28
  1041.0 31.8 reduce-scatter.22
  1075.7 31.8 reduce-scatter.26
  1110.3 31.8 reduce-scatter.24
  1145.0 31.8 reduce-scatter.34
  1179.6 31.8 reduce-scatter.32
  1214.2 99.2 reduce-scatter.38
  1316.5 99.2 reduce-scatter.40
  1422.2 305.9 all-reduce.18
where the time goes:
time: 1770 us; the launch traced here: 1760 us
  waiting for transfers between devices  1010 us (57%)
  matrix products  355 us (20%)
  other arithmetic  143 us (8%)
  blocking collectives  132 us (7%)
  local copies, waits for them, and re-layouts  94.5 us (5%)
    psum x1, waiting for transfers between devices, on_device(): lax.psum(shard_sums[13].astype(jnp.bfloat16), 'page').astype(jnp.float32)  189 us
    reduce_scatter x1, waiting for transfers between devices, on_device(): lax.psum_scatter(outer_sum(active, cotangent).astype(jnp.bfloat16), 'seq'...  102 us
    reduce_scatter x1, waiting for transfers between devices, on_device(): lax.psum_scatter(outer_sum(normed_three, grad_inner).astype(jnp.bfloat16)...  102 us
    all_gather x1, waiting for transfers between devices, on_device(): lax.all_gather(ffn_inner, 'seq', axis=0, tiled=True)  100 us
    all_gather x1, waiting for transfers between devices, on_device(): lax.all_gather(ffn_outer, 'seq', axis=0, tiled=True)  77 us
    unnamed x261, local copies, waits for them, and re-layouts  72.8 us
    dot_general x10, matrix products, project(): jnp.einsum('ptd,de->pte', activations, weight, preferred_element_type=jnp...  67.5 us
    psum x1, blocking collectives, on_device(): lax.psum(shard_sums[0].astype(jnp.bfloat16), 'page').astype(jnp.float32)  63.1 us
  transfers between devices with their start and end apart: 29, of which 22 were waited for; matrix products, arithmetic and copies ran while one was open for 23% of the time, Pallas kernels for 0%

commit v1 on v0

v1 whole, which is shorter than its diff:
```python
import functools
import math

import jax
import jax.numpy as jnp
from jax import lax
from jax.experimental import pallas as pl
from jax.experimental.pallas import tpu as pltpu
from jax.sharding import Mesh
from jax.sharding import PartitionSpec as P

HEADS = 16
HEAD = 64


norm_epsilon = 1e-05
masked_score = -1000000000.0


def layer_norm(values, norm_gain, norm_shift):
    center = values - jnp.mean(values, axis=-1, keepdims=True)
    spread = jnp.mean(center * center, axis=-1, keepdims=True)
    return center * lax.rsqrt(spread + norm_epsilon) * norm_gain + norm_shift


pair_width = 2 * HEAD
vmem_bytes = 48 * 1024 * 1024


def dot_nt(left_side, right_side):
    return lax.dot_general(
        left_side, right_side, (((1,), (1,)), ((), ())), preferred_element_type=jnp.float32
    )


def dot_nn(left_side, right_side):
    return jnp.dot(left_side, right_side, preferred_element_type=jnp.float32)


def dot_tn(left_side, right_side):
    return lax.dot_general(
        left_side, right_side, (((0,), (0,)), ((), ())), preferred_element_type=jnp.float32
    )


def one_head(values, head):
    lane = lax.broadcasted_iota(jnp.int32, values.shape, 1)
    return jnp.where((lane >= head * HEAD) & (lane < (head + 1) * HEAD), values, 0)


class Plan:
    def __init__(self, kinds, key_rows, query_rows, chunk, causal):
        self.kinds = kinds
        self.key_rows = key_rows
        self.all_rows = key_rows * len(kinds)
        self.query_rows = query_rows
        self.chunk = min(chunk, query_rows)
        self.causal = causal

    def blocks(self, start, segments):
        found = []
        for segment in segments:
            rows = self.key_rows
            if self.causal and self.kinds[segment] == "limit":
                rows = min(rows, start + self.chunk)
            found.append((self.kinds[segment], pl.ds(segment * self.key_rows, rows)))
        return found


def query_limit(info_ref, start, chunk):
    lane = lax.broadcasted_iota(jnp.int32, (1, chunk), 1) + start
    place = info_ref[0] + lane
    return jnp.minimum(place, info_ref[1] - 1) - info_ref[2]


def masked_block(kind, scores, limit, bias_ref):
    if kind == "limit":
        key = lax.broadcasted_iota(jnp.int32, scores.shape, 0)
        return jnp.where(key <= limit, scores, masked_score)
    if kind == "bias":
        return scores + bias_ref[...]
    return scores


def run_segments(plan, info_ref, body):
    every = list(range(len(plan.kinds)))
    needed = [segment for segment in every if plan.kinds[segment] != "earlier"]
    if len(needed) == len(every):
        body(every)
        return
    pl.when(info_ref[3] == 1)(lambda: body(every))
    pl.when(info_ref[3] != 1)(lambda: body(needed))


def attend_kernel(plan, info_ref, query_ref, key_ref, value_ref, bias_ref, mixed_ref, log_ref):
    def body(segments):
        for start in range(0, plan.query_rows, plan.chunk):
            limit = query_limit(info_ref, start, plan.chunk)
            lane = lax.broadcasted_iota(jnp.int32, (1, plan.chunk), 1) + start
            valid = (info_ref[0] + lane < info_ref[1]).astype(jnp.float32)
            query = query_ref[pl.ds(start, plan.chunk), :]
            parts = []
            for head in range(2):
                head_query = one_head(query, head)
                blocks = plan.blocks(start, segments)
                scores = [
                    masked_block(kind, dot_nt(key_ref[rows, :], head_query), limit, bias_ref)
                    for kind, rows in blocks
                ]
                peak = jnp.max(scores[0], axis=0, keepdims=True)
                for block in scores[1:]:
                    peak = jnp.maximum(peak, jnp.max(block, axis=0, keepdims=True))
                total = jnp.zeros_like(peak)
                mixed = jnp.zeros((pair_width, plan.chunk), jnp.float32)
                for (kind, rows), block in zip(blocks, scores):
                    weights = jnp.exp(block - peak)
                    total = total + jnp.sum(weights, axis=0, keepdims=True)
                    mixed = mixed + dot_tn(value_ref[rows, :], weights.astype(jnp.bfloat16))
                parts.append(mixed[head * HEAD : (head + 1) * HEAD] * (valid / total))
                log_ref[0, pl.ds(head, 1), pl.ds(start, plan.chunk)] = peak + jnp.log(total)
            joined = jnp.concatenate(parts, axis=0)
            mixed_ref[pl.ds(start, plan.chunk), :] = joined.T.astype(jnp.bfloat16)

    run_segments(plan, info_ref, body)


def attend_back_kernel(
    plan,
    info_ref,
    query_ref,
    mixed_ref,
    grad_ref,
    log_ref,
    key_ref,
    value_ref,
    bias_ref,
    grad_query_ref,
    grad_key_ref,
    grad_value_ref,
    key_sum,
    value_sum,
):
    def body(segments):
        key_sum[...] = jnp.zeros_like(key_sum)
        value_sum[...] = jnp.zeros_like(value_sum)
        for start in range(0, plan.query_rows, plan.chunk):
            limit = query_limit(info_ref, start, plan.chunk)
            rows_here = pl.ds(start, plan.chunk)
            row = lax.broadcasted_iota(jnp.int32, (plan.chunk, 1), 0) + start
            valid = info_ref[0] + row < info_ref[1]
            query = query_ref[rows_here, :]
            grad = jnp.where(valid, grad_ref[rows_here, :], 0).astype(jnp.bfloat16)
            product = grad.astype(jnp.float32) * mixed_ref[rows_here, :].astype(jnp.float32)
            product = product.T
            parts = []
            for head in range(2):
                own = slice(head * HEAD, (head + 1) * HEAD)
                head_query, head_grad = one_head(query, head), one_head(grad, head)
                weighted = jnp.sum(product[own], axis=0, keepdims=True)
                log_total = log_ref[0, pl.ds(head, 1), rows_here]
                grad_query = jnp.zeros((pair_width, plan.chunk), jnp.float32)
                for kind, rows in plan.blocks(start, segments):
                    keys = key_ref[rows, :]
                    scores = masked_block(kind, dot_nt(keys, head_query), limit, bias_ref)
                    shares = jnp.exp(scores - log_total)
                    grad_shares = dot_nt(value_ref[rows, :], head_grad)
                    grad_scores = (shares * (grad_shares - weighted)).astype(jnp.bfloat16)
                    value_sum[rows, :] += dot_nn(shares.astype(jnp.bfloat16), head_grad)
                    key_sum[rows, :] += dot_nn(grad_scores, head_query)
                    grad_query = grad_query + dot_tn(keys, grad_scores)
                parts.append(grad_query[own])
            joined = jnp.concatenate(parts, axis=0) * (1.0 / math.sqrt(HEAD))
            grad_query_ref[rows_here, :] = joined.T.astype(jnp.bfloat16)
        grad_key_ref[...] = key_sum[...].astype(jnp.bfloat16)
        grad_value_ref[...] = value_sum[...].astype(jnp.bfloat16)

    run_segments(plan, info_ref, body)


def column_block(rows, first):
    return pl.BlockSpec((rows, pair_width), lambda step, info: (0, first + step))


def log_block(rows, first):
    return pl.BlockSpec((1, 2, rows), lambda step, info: (first + step, 0, 0))


def key_specs(plan, first):
    return [
        column_block(plan.all_rows, first),
        column_block(plan.all_rows, HEADS // 2 + first),
        pl.BlockSpec((plan.all_rows, 1), lambda step, info: (0, 0)),
    ]


any_block = pl.BlockSpec(memory_space=pl.ANY)


def skip_refs(kernel, place, count):
    def run(*refs):
        kernel(*refs[:place], *refs[place + count :])

    return run


def attend(plan, info, queries, key_values, bias, part, parts, into=()):
    pairs = HEADS // 2
    count, first = pairs // parts, part * (pairs // parts)
    rows, keys = plan.query_rows, plan.all_rows
    return pl.pallas_call(
        skip_refs(functools.partial(attend_kernel, plan), 5, len(into)),
        grid_spec=pltpu.PrefetchScalarGridSpec(
            num_scalar_prefetch=1,
            grid=(count,),
            in_specs=[column_block(rows, first)] + key_specs(plan, first) + [any_block] * len(into),
            out_specs=[column_block(rows, first), log_block(rows, first)],
        ),
        out_shape=[
            jax.ShapeDtypeStruct((rows, HEADS * HEAD), jnp.bfloat16),
            jax.ShapeDtypeStruct((pairs, 2, rows), jnp.float32),
        ],
        input_output_aliases={5 + index: index for index in range(len(into))},
        compiler_params=pltpu.CompilerParams(vmem_limit_bytes=vmem_bytes),
        cost_estimate=pl.CostEstimate(
            flops=4 * 4 * rows * keys * HEADS * HEAD // parts,
            bytes_accessed=4 * (rows + keys) * HEADS * HEAD // parts,
            transcendentals=rows * keys * HEADS // parts,
        ),
    )(info, queries, key_values, key_values, bias, *into)


def attend_back(
    plan, info, queries, mixed, grad_mixed, log_total, key_values, bias, part, parts, into=()
):
    pairs = HEADS // 2
    count, first = pairs // parts, part * (pairs // parts)
    rows, keys = plan.query_rows, plan.all_rows
    return pl.pallas_call(
        skip_refs(functools.partial(attend_back_kernel, plan), 8, len(into)),
        grid_spec=pltpu.PrefetchScalarGridSpec(
            num_scalar_prefetch=1,
            grid=(count,),
            in_specs=[column_block(rows, first)] * 3
            + [log_block(rows, first)]
            + key_specs(plan, first)
            + [any_block] * len(into),
            out_specs=[
                column_block(rows, first),
                column_block(keys, first),
                column_block(keys, first),
            ],
            scratch_shapes=[pltpu.VMEM((keys, pair_width), jnp.float32)] * 2,
        ),
        out_shape=[
            jax.ShapeDtypeStruct((rows, HEADS * HEAD), jnp.bfloat16),
            jax.ShapeDtypeStruct((keys, HEADS * HEAD), jnp.bfloat16),
            jax.ShapeDtypeStruct((keys, HEADS * HEAD), jnp.bfloat16),
        ],
        input_output_aliases={8 + index: index for index in range(len(into))},
        compiler_params=pltpu.CompilerParams(vmem_limit_bytes=vmem_bytes),
        cost_estimate=pl.CostEstimate(
            flops=4 * 10 * rows * keys * HEADS * HEAD // parts,
            bytes_accessed=8 * (rows + keys) * HEADS * HEAD // parts,
            transcendentals=rows * keys * HEADS // parts,
        ),
    )(info, queries, mixed, grad_mixed, log_total, key_values, key_values, bias, *into)


def copy_all(copies):
    for copy in copies:
        copy.start()
    for copy in copies:
        copy.wait()


def merge_kernel(place_ref, own_ref, other_ref, out_ref, sems):
    rows = own_ref.shape[0]
    copies = []
    for which, source in enumerate((own_ref, other_ref)):
        first = pl.multiple_of(place_ref[which] * rows, rows)
        copies.append(
            pltpu.make_async_copy(source, out_ref.at[pl.ds(first, rows), :], sems.at[which])
        )
    copy_all(copies)


def merge(index, own, other):
    rows, width = own.shape
    return pl.pallas_call(
        merge_kernel,
        grid_spec=pltpu.PrefetchScalarGridSpec(
            num_scalar_prefetch=1,
            grid=(),
            in_specs=[any_block, any_block],
            out_specs=any_block,
            scratch_shapes=[pltpu.SemaphoreType.DMA((2,))],
        ),
        out_shape=jax.ShapeDtypeStruct((2 * rows, width), own.dtype),
        compiler_params=pltpu.CompilerParams(vmem_limit_bytes=4 * 1024 * 1024),
        cost_estimate=pl.CostEstimate(
            flops=0, bytes_accessed=8 * rows * width, transcendentals=0
        ),
    )(jnp.stack([index, 1 - index]).astype(jnp.int32), own, other)


def assemble_kernel(count, place_ref, *refs):
    shards, (four_ref, came_ref, out_ref, sems) = refs[:count], refs[count:]
    rows, part = shards[0].shape[0], four_ref.shape[0]
    seq, core = place_ref[0], place_ref[1]
    copies, left = [], 0
    for index, shard in enumerate(shards):
        own = out_ref.at[
            pl.ds(pl.multiple_of(seq * rows, rows), rows), pl.ds(left, shard.shape[1])
        ]
        copies.append(pltpu.make_async_copy(shard, own, sems.at[index]))
        left += shard.shape[1]
    for index, (source, half) in enumerate(((four_ref, core), (came_ref, 1 - core))):
        first = pl.multiple_of((1 - seq) * rows + half * part, part)
        copies.append(
            pltpu.make_async_copy(source, out_ref.at[pl.ds(first, part), :], sems.at[count + index])
        )
    copy_all(copies)


def assemble(seq, core, shards, four, came):
    count, width = len(shards), four.shape[1]
    rows = shards[0].shape[0]
    return pl.pallas_call(
        functools.partial(assemble_kernel, count),
        grid_spec=pltpu.PrefetchScalarGridSpec(
            num_scalar_prefetch=1,
            grid=(),
            in_specs=[any_block] * (count + 2),
            out_specs=any_block,
            scratch_shapes=[pltpu.SemaphoreType.DMA((count + 2,))],
        ),
        out_shape=jax.ShapeDtypeStruct((2 * rows, width), four.dtype),
        compiler_params=pltpu.CompilerParams(vmem_limit_bytes=4 * 1024 * 1024),
        cost_estimate=pl.CostEstimate(
            flops=0, bytes_accessed=8 * rows * width, transcendentals=0
        ),
    )(jnp.stack([seq, core]).astype(jnp.int32), *shards, four, came)


def ffn_kernel(half_steps, place_ref, *refs):
    normed, inner = refs[0:4], refs[4:8]
    outer_own, outer_other, bias_ref, bias_outer_ref, hidden_ref, cotangent_ref = refs[8:14]
    out_ref, grad_ref, column_ref, kept_outer, sent_outer, kept_inner, sent_inner = refs[14:21]
    total_ref, turned_ref = refs[21], refs[22]
    grad_sums = refs[23:27]
    step = pl.program_id(0)
    quarter = normed[0].shape[1]

    @pl.when(step == 0)
    def start():
        for index in range(4):
            turned_ref[index] = normed[index][...].T
            grad_sums[index][...] = jnp.zeros_like(grad_sums[index])
        total_ref[...] = hidden_ref[...] + bias_outer_ref[...]

    def run(outer_ref):
        inner_sum = bias_ref[...] + dot_nn(normed[0][...], inner[0][...])
        for index in range(1, 4):
            inner_sum = inner_sum + dot_nn(normed[index][...], inner[index][...])
        part = 0.5 + 0.5 * lax.erf(inner_sum * math.sqrt(0.5))
        active = (inner_sum * part).astype(jnp.bfloat16)
        slope = part + inner_sum * (
            jnp.exp(-0.5 * inner_sum * inner_sum) * (1.0 / math.sqrt(2.0 * math.pi))
        )
        cotangent = cotangent_ref[...]
        total_ref[...] += dot_nn(active, outer_ref[...])
        grad_inner = (dot_nt(cotangent, outer_ref[...]) * slope).astype(jnp.bfloat16)
        column_ref[...] = jnp.sum(grad_inner.astype(jnp.float32), axis=0, keepdims=True)
        for index in range(4):
            grad_sums[index][...] += dot_nt(grad_inner, inner[index][...])
        grad_outer = dot_tn(active, cotangent).astype(jnp.bfloat16)
        for which, out in ((0, kept_outer), (1, sent_outer)):

            def store(out=out):
                out[0] = grad_outer

            pl.when(step % 2 == which)(store)
        for index, (out, seq_at) in enumerate(
            ((kept_inner, 0), (sent_inner, 0), (kept_inner, 1), (sent_inner, 1))
        ):
            out[pl.ds(place_ref[seq_at], 1)] = dot_nn(turned_ref[index], grad_inner).astype(
                jnp.bfloat16
            )[None]

    pl.when(step < half_steps)(lambda: run(outer_own))
    pl.when(step >= half_steps)(lambda: run(outer_other))

    @pl.when(step == 2 * half_steps - 1)
    def finish():
        out_ref[...] = total_ref[...].astype(jnp.bfloat16)
        for index in range(4):
            first = pl.multiple_of(place_ref[4 + index] * quarter, quarter)
            grad_ref[:, pl.ds(first, quarter)] = grad_sums[index][...]


def ffn_both_ways(
    seq, core, normed, hidden, cotangent, inner_own, inner_other, outer_own, outer_other, bias, last
):
    rows, width = normed.shape
    units = inner_own.shape[1]
    chunk, quarter = 512, width // 4
    steps = units // chunk
    half_steps = steps // 2
    run = half_steps // 2
    order = []
    for step in range(steps):
        which, at = (seq, step) if step < half_steps else (1 - seq, step - half_steps)
        side = core if at % 2 == 0 else 1 - core
        order.append((which, side * run + at // 2))
    local = [at for _, at in order]
    whole = [which * half_steps + at for which, at in order]
    out_at = [which * run + step % half_steps // 2 for step, (which, _) in enumerate(order)]
    quarters = [seq * 2 + core, seq * 2 + 1 - core, (1 - seq) * 2 + core, (1 - seq) * 2 + 1 - core]
    place = jnp.stack(
        [seq, 1 - seq, core, 1 - core] + quarters + whole + local + out_at
    ).astype(jnp.int32)
    at_whole, at_local, at_out = 8, 8 + steps, 8 + 2 * steps
    fixed = lambda shape: pl.BlockSpec(shape, lambda step, place: (0,) * len(shape))
    normed_specs = [
        pl.BlockSpec((rows, quarter), lambda step, place, i=i: (0, place[4 + i])) for i in range(4)
    ]
    inner_specs = [
        pl.BlockSpec(
            (quarter, chunk), lambda step, place, i=i: (place[2 + i % 2], place[at_whole + step])
        )
        for i in range(4)
    ]
    own_at = lambda step, place: place[at_local + jnp.minimum(step, half_steps - 1)]
    other_at = lambda step, place: place[at_local + jnp.maximum(step, half_steps)]
    outer_shape = jax.ShapeDtypeStruct((2 * run, chunk, width), jnp.bfloat16)
    inner_shape = jax.ShapeDtypeStruct((2, quarter, units), jnp.bfloat16)
    outer_spec = pl.BlockSpec((1, chunk, width), lambda step, place: (place[at_out + step], 0, 0))
    inner_spec = pl.BlockSpec(
        (2, quarter, chunk), lambda step, place: (0, 0, place[at_whole + step])
    )
    row_spec = pl.BlockSpec((1, chunk), lambda step, place: (0, place[at_whole + step]))
    out, grad, column, kept_outer, sent_outer, kept_inner, sent_inner = pl.pallas_call(
        functools.partial(ffn_kernel, half_steps),
        grid_spec=pltpu.PrefetchScalarGridSpec(
            num_scalar_prefetch=1,
            grid=(steps,),
            in_specs=normed_specs
            + inner_specs
            + [
                pl.BlockSpec((chunk, width), lambda step, place: (own_at(step, place), 0)),
                pl.BlockSpec((chunk, width), lambda step, place: (other_at(step, place), 0)),
                row_spec,
                fixed((1, width)),
                fixed((rows, width)),
                fixed((rows, width)),
            ],
            out_specs=[
                fixed((rows, width)),
                fixed((rows, width)),
                row_spec,
                outer_spec,
                outer_spec,
                inner_spec,
                inner_spec,
            ],
            scratch_shapes=[
                pltpu.VMEM((rows, width), jnp.float32),
                pltpu.VMEM((4, quarter, rows), jnp.bfloat16),
            ]
            + [pltpu.VMEM((rows, quarter), jnp.float32)] * 4,
        ),
        out_shape=[
            jax.ShapeDtypeStruct((rows, width), jnp.bfloat16),
            jax.ShapeDtypeStruct((rows, width), jnp.float32),
            jax.ShapeDtypeStruct((1, units), jnp.float32),
            outer_shape,
            outer_shape,
            inner_shape,
            inner_shape,
        ],
        compiler_params=pltpu.CompilerParams(vmem_limit_bytes=56 * 1024 * 1024),
        cost_estimate=pl.CostEstimate(
            flops=12 * rows * width * units,
            bytes_accessed=4 * 2 * width * units + 12 * rows * width,
            transcendentals=2 * rows * units,
        ),
    )(
        place,
        *[normed] * 4,
        inner_own,
        inner_own,
        inner_other,
        inner_other,
        outer_own,
        outer_other,
        bias[None],
        last[None],
        hidden,
        cotangent,
    )
    split = lambda kept, sent: (kept.reshape(2, -1, kept.shape[2]), sent.reshape(2, -1, kept.shape[2]))
    return out, grad, column[0], split(kept_outer, sent_outer), (kept_inner, sent_inner)


def outer_group_kernel(count, place_ref, *refs):
    lefts, rights = refs[:count], refs[count : 2 * count]
    kept_ref, sent_ref = refs[2 * count :]
    part = kept_ref.shape[1]
    matrix, seq = pl.program_id(0), pl.program_id(1)

    def one(left_ref, right_ref):
        for which, out_ref in ((0, kept_ref), (1, sent_ref)):
            first = pl.multiple_of((seq * 2 + place_ref[which]) * part, part)
            left = left_ref[:, pl.ds(first, part)]
            out_ref[0] = dot_tn(left, right_ref[...]).astype(jnp.bfloat16)

    for index in range(count):
        pl.when(matrix == index)(functools.partial(one, lefts[index], rights[index]))


def outer_group(core, pairs):
    count, width = len(pairs), pairs[0][0].shape[1]
    part = width // 4
    place = jnp.stack([core, 1 - core]).astype(jnp.int32)
    whole = lambda values: pl.BlockSpec(values.shape, lambda matrix, seq, place: (0, 0))
    out_spec = pl.BlockSpec((1, part, width), lambda matrix, seq, place: (seq, 0, matrix))
    shape = jax.ShapeDtypeStruct((2, part, count * width), jnp.bfloat16)
    lefts, rights = [pair[0] for pair in pairs], [pair[1] for pair in pairs]
    tokens = sum(left.shape[0] for left in lefts)
    return pl.pallas_call(
        functools.partial(outer_group_kernel, count),
        grid_spec=pltpu.PrefetchScalarGridSpec(
            num_scalar_prefetch=1,
            grid=(count, 2),
            in_specs=[whole(values) for values in lefts + rights],
            out_specs=[out_spec, out_spec],
        ),
        out_shape=[shape, shape],
        compiler_params=pltpu.CompilerParams(vmem_limit_bytes=vmem_bytes),
        cost_estimate=pl.CostEstimate(
            flops=2 * tokens * width * width,
            bytes_accessed=2 * (2 * tokens * width + count * width * width),
            transcendentals=0,
        ),
    )(place, *lefts, *rights)


def halve_kernel(place_ref, kept_a, came_a, kept_b, came_b, kept_ref, sent_ref):
    kept_ref[0] = (kept_a[0].astype(jnp.float32) + came_a[0].astype(jnp.float32)).astype(
        jnp.bfloat16
    )
    sent_ref[0] = (kept_b[0].astype(jnp.float32) + came_b[0].astype(jnp.float32)).astype(
        jnp.bfloat16
    )


def halve(keep_at, send_at, kept, came):
    blocks, rows, width = kept.shape
    count = blocks // 2
    place = jnp.stack(list(keep_at) + list(send_at)).astype(jnp.int32)
    spec = lambda first: pl.BlockSpec(
        (1, rows, width), lambda j, place: (place[first + j], 0, 0)
    )
    out_spec = pl.BlockSpec((1, rows, width), lambda j, place: (j, 0, 0))
    shape = jax.ShapeDtypeStruct((count, rows, width), jnp.bfloat16)
    return pl.pallas_call(
        halve_kernel,
        grid_spec=pltpu.PrefetchScalarGridSpec(
            num_scalar_prefetch=1,
            grid=(count,),
            in_specs=[spec(0), spec(0), spec(count), spec(count)],
            out_specs=[out_spec, out_spec],
        ),
        out_shape=[shape, shape],
        compiler_params=pltpu.CompilerParams(vmem_limit_bytes=vmem_bytes),
        cost_estimate=pl.CostEstimate(
            flops=blocks * rows * width,
            bytes_accessed=6 * blocks * rows * width,
            transcendentals=0,
        ),
    )(place, kept, came, kept, came)


def layer_norm_back(values, norm_gain, grad):
    center = values - jnp.mean(values, axis=-1, keepdims=True)
    inverse = lax.rsqrt(jnp.mean(center * center, axis=-1, keepdims=True) + norm_epsilon)
    unit = center * inverse
    scaled = grad * norm_gain
    back = scaled - jnp.mean(scaled, axis=-1, keepdims=True)
    back = back - unit * jnp.mean(scaled * unit, axis=-1, keepdims=True)
    return back * inverse, jnp.sum(grad * unit, axis=0), jnp.sum(grad, axis=0)


def dot_back(gradient, weight):
    return dot_nt(gradient, weight)


def column_sum(values):
    return jnp.sum(values.astype(jnp.float32), axis=0)


def swap(values, axis_name):
    return lax.ppermute(values, axis_name, [(0, 1), (1, 0)])


flips = {"x": 4, "y": 1, "z": 8}
square = ("zlo", "x", "core", "seq")


def exchange(values, axes):
    flip = [flips[axis] for axis in axes]
    return lax.ppermute(values, square, [(i, i ^ flip[i // 2 % 2]) for i in range(16)])


def square_bits(turned):
    core, x, zlo = lax.axis_index("core"), lax.axis_index("x"), lax.axis_index("zlo")
    first = 1 - core if turned else core
    return core, jnp.where(first == 1, x, zlo), jnp.where(first == 1, zlo, x)


def after(values, *others):
    return lax.optimization_barrier((values,) + others)[0]


def first_piece(shards):
    piece_rows = shards[0].shape[0] // 8
    core, high, low = square_bits(False)
    place = (core * 2 + high) * 2 + low
    piece = [
        lax.dynamic_slice_in_dim(shard, place * piece_rows, piece_rows, axis=0) for shard in shards
    ]
    return swap(piece[0] if len(piece) == 1 else jnp.concatenate(piece, axis=1), "seq")


def second_piece(piece):
    return merge(square_bits(False)[2], piece, exchange(piece, "xz"))


def third_piece(two):
    return merge(square_bits(False)[1], two, exchange(two, "zx"))


class Total:
    def __init__(self, split, steps, turned):
        self.kept, sent = split
        self.core, self.first, self.second = square_bits(turned)
        self.seq, self.zhi = lax.axis_index("seq"), lax.axis_index("zhi")
        self.steps = steps
        self.along = ("x", "z") if turned else ("z", "x")
        on_seq = [axes == "y" for axes in steps[0]]
        self.starts = jnp.where(self.core == 0, on_seq[0], on_seq[1])
        self.came = swap(self.blocks(sent, 4), "core")
        self.kept = self.blocks(self.kept, 4)
        self.stage = 0

    def blocks(self, values, count):
        return values.reshape(count, -1, values.shape[-1])

    def step(self):
        if self.stage == 0:
            seq, first = self.seq, self.first
            keep = [jnp.where(self.starts, seq * 2 + j, j * 2 + first) for j in range(2)]
            send = [jnp.where(self.starts, (1 - seq) * 2 + j, j * 2 + 1 - first) for j in range(2)]
        else:
            bit = (jnp.where(self.starts, self.first, self.seq), self.second, self.zhi)
            bit = bit[self.stage - 1]
            keep, send = [bit], [1 - bit]
            self.kept, self.came = self.blocks(self.kept, 2), self.blocks(self.came, 2)
        self.kept, sent = halve(keep, send, self.kept, self.came)
        if self.stage < 3:
            self.came = exchange(sent, self.steps[self.stage])
        else:
            self.came = swap(sent, "zhi")
        self.stage += 1
        return sent

    def gather(self):
        if self.stage == 4:
            piece = self.kept[0].astype(jnp.float32) + self.came[0].astype(jnp.float32)
            self.part = piece.astype(jnp.bfloat16)
            self.came = swap(self.part, "zhi")
        elif self.stage == 5:
            self.part = merge(self.zhi, self.part, self.came)
            self.came = exchange(self.part, self.along[::-1])
        elif self.stage == 6:
            self.part = merge(self.second, self.part, self.came)
            self.came = exchange(self.part, self.along)
        else:
            self.part = merge(self.first, self.part, self.came)
            self.came = swap(self.part, "core")
        self.stage += 1
        return self.part

    def result(self):
        first = jnp.where(self.core == 0, self.part, self.came)
        second = jnp.where(self.core == 0, self.came, self.part)
        return jnp.concatenate([first, second]).astype(jnp.float32)


def sum_plain(terms):
    terms = lax.psum_scatter(terms.astype(jnp.bfloat16), "seq", scatter_dimension=0, tiled=True)
    return lax.psum(terms, page_axes)


page_axes = ("zhi", "zlo", "x", "core")


def sum_vectors(vectors):
    seq_count = lax.axis_size("seq")
    joined = jnp.concatenate([vector.reshape(seq_count, -1) for vector in vectors], axis=1)
    joined = joined.reshape(seq_count, -1, 128)
    seq = lax.axis_index("seq")
    if seq_count == 2:
        for axis in page_axes:
            if lax.axis_size(axis) == 2:
                joined = joined + swap(joined, axis)
            else:
                joined = lax.psum(joined, axis)
        own = lax.dynamic_index_in_dim(joined, seq, 0, keepdims=False)
        own = own + swap(lax.dynamic_index_in_dim(joined, 1 - seq, 0, keepdims=False), "seq")
    else:
        joined = lax.psum(joined, page_axes + ("seq",))
        own = lax.dynamic_index_in_dim(joined, seq, 0, keepdims=False)
    own = own.reshape(-1)
    out, start = [], 0
    for vector in vectors:
        size = vector.shape[0] // seq_count
        out.append(own[start : start + size])
        start += size
    return out


def on_device(
    tokens,
    patches,
    lengths,
    blank_mask,
    cotangent,
    first_gain,
    first_shift,
    self_query,
    self_query_bias,
    self_key,
    self_value,
    self_value_bias,
    self_output,
    self_output_bias,
    second_gain,
    second_shift,
    cross_query,
    cross_query_bias,
    cross_key,
    cross_value,
    cross_value_bias,
    cross_output,
    cross_output_bias,
    third_gain,
    third_shift,
    ffn_inner,
    ffn_inner_bias,
    ffn_outer,
    ffn_outer_bias,
):
    seq_count = lax.axis_size("seq")
    seq_index = lax.axis_index("seq")
    vectors = (
        first_gain,
        first_shift,
        self_query_bias,
        self_value_bias,
        self_output_bias,
        second_gain,
        second_shift,
        cross_query_bias,
        cross_value_bias,
        cross_output_bias,
        third_gain,
        third_shift,
        ffn_inner_bias,
        ffn_outer_bias,
    )
    two = seq_count == 2 and lax.axis_size("zhi") == 2
    joined = jnp.concatenate(vectors).reshape(-1, 128)
    if two:
        joined_other = swap(joined, "seq")
        gathered = jnp.where(
            seq_index == 0,
            jnp.stack([joined, joined_other]),
            jnp.stack([joined_other, joined]),
        )
    else:
        gathered = lax.all_gather(joined, "seq", axis=0, tiled=False)
    gathered = gathered.reshape(seq_count, -1)
    whole_vectors, start = [], 0
    for vector in vectors:
        part = gathered[:, start : start + vector.shape[0]].reshape(-1)
        whole_vectors.append(part.astype(jnp.float32))
        start += vector.shape[0]
    (
        gain_one,
        shift_one,
        bias_self_query,
        bias_self_value,
        bias_self_output,
        gain_two,
        shift_two,
        bias_cross_query,
        bias_cross_value,
        bias_cross_output,
        gain_three,
        shift_three,
        bias_inner,
        bias_outer,
    ) = whole_vectors
    tokens, patches, cotangent = tokens[0], patches[0], cotangent[0]
    tok_rows, width = tokens.shape
    patch_rows = patches.shape[0]
    query_scale = 1.0 / math.sqrt(HEAD)

    core = lax.axis_index("core")
    self_shards = [self_query, self_key, self_value, self_output]
    cross_shards = [cross_key, cross_value, cross_query, cross_output]
    if two:
        piece = first_piece(self_shards)
        tokens_other = lax.ppermute(after(tokens, piece), "seq", [(0, 1)])
        part = third_piece(second_piece(piece))
        cross_piece = first_piece([after(cross_key, part)] + cross_shards[1:])
        whole_self = assemble(seq_index, core, self_shards, part, swap(part, "core"))
        patches_other = swap(after(patches, whole_self), "seq")
        tokens_all = jnp.concatenate([tokens, after(tokens_other, whole_self)])
    else:
        gather = lambda shard: lax.all_gather(shard, "seq", axis=0, tiled=True)
        whole_self = gather(jnp.concatenate(self_shards, axis=1))
        whole_cross = gather(jnp.concatenate(cross_shards, axis=1))
        whole_ffn_inner, whole_ffn_outer = gather(ffn_inner), gather(ffn_outer)
        tokens_all, patches_all = gather(tokens), gather(patches)

    first_place = seq_index * tok_rows
    key_start = first_place if two else 0
    info = jnp.stack([first_place, lengths[0], key_start, seq_index]).astype(jnp.int32)
    self_plan = Plan(
        ("limit", "earlier") if two else ("limit",),
        tok_rows if two else tok_rows * seq_count,
        tok_rows,
        256,
        two,
    )
    cross_plan = Plan(("bias",), patch_rows * seq_count, tok_rows, 256, False)
    blank_bias = jnp.where(blank_mask[0] == 0, 0.0, masked_score).astype(jnp.float32)
    if two:
        halves = blank_bias.reshape(2, patch_rows)
        blank_bias = jnp.where(seq_index == 0, halves, halves[::-1]).reshape(-1)
    blank_bias = blank_bias[:, None]
    no_bias = jnp.zeros((self_plan.all_rows, 1), jnp.float32)

    zeros = jnp.zeros_like(bias_self_value)
    token_values = tokens.astype(jnp.float32)
    normed_all = layer_norm(tokens_all.astype(jnp.float32), gain_one, shift_one).astype(
        jnp.bfloat16
    )
    if two:
        normed_one = normed_all[:tok_rows]
    else:
        normed_one = layer_norm(token_values, gain_one, shift_one).astype(jnp.bfloat16)
    queries_self = (
        (dot_nn(normed_one, whole_self[:, :width]) + bias_self_query) * query_scale
    ).astype(jnp.bfloat16)
    self_bias = jnp.concatenate([zeros, bias_self_value])
    self_pairs = (dot_nn(normed_all, whole_self[:, width : 3 * width]) + self_bias).astype(
        jnp.bfloat16
    )
    attend_self = functools.partial(attend, self_plan, info)
    if two:
        first_half = attend_self(after(queries_self, cross_piece), self_pairs, no_bias, 0, 2)
        cross_part = second_piece(cross_piece)
        inner_piece = first_piece([after(ffn_inner, first_half[0])])
        mixed_self, log_self = attend_self(
            after(queries_self, cross_part), self_pairs, no_bias, 1, 2, first_half
        )
        cross_part = third_piece(cross_part)
    else:
        mixed_self, log_self = attend_self(queries_self, self_pairs, no_bias, 0, 1)
    hidden_one = token_values + dot_nn(mixed_self, whole_self[:, 3 * width :]) + bias_self_output
    normed_two = layer_norm(hidden_one, gain_two, shift_two).astype(jnp.bfloat16)
    if two:
        outer_piece = first_piece([after(ffn_outer, normed_two)])
        cross_came = swap(cross_part, "core")
        whole_cross = assemble(seq_index, core, cross_shards, cross_part, cross_came)
        patches_all = jnp.concatenate([patches, after(patches_other, whole_cross)])
    patch_bias = jnp.concatenate([zeros, bias_cross_value])
    patch_pairs = (dot_nn(patches_all, whole_cross[:, : 2 * width]) + patch_bias).astype(
        jnp.bfloat16
    )
    queries_cross = (
        (dot_nn(normed_two, whole_cross[:, 2 * width : 3 * width]) + bias_cross_query) * query_scale
    ).astype(jnp.bfloat16)
    attend_cross = functools.partial(attend, cross_plan, info)
    if two:
        first_half = attend_cross(after(queries_cross, inner_piece), patch_pairs, blank_bias, 0, 2)
        inner_part = second_piece(inner_piece)
        mixed_cross, log_cross = attend_cross(
            after(queries_cross, inner_part, outer_piece), patch_pairs, blank_bias, 1, 2, first_half
        )
        outer_part = second_piece(outer_piece)
        inner_part = third_piece(inner_part)
        inner_other = merge(core, inner_part, swap(inner_part, "core"))
        outer_part = third_piece(outer_part)
        outer_other = merge(core, outer_part, swap(outer_part, "core"))
    else:
        mixed_cross, log_cross = attend_cross(queries_cross, patch_pairs, blank_bias, 0, 1)
    hidden_two = hidden_one + dot_nn(mixed_cross, whole_cross[:, 3 * width :]) + bias_cross_output
    normed_three = layer_norm(hidden_two, gain_three, shift_three).astype(jnp.bfloat16)
    if two:
        outputs, grad_normed_three, column_inner, split_outer, split_inner = ffn_both_ways(
            seq_index,
            core,
            normed_three,
            hidden_two,
            cotangent,
            ffn_inner,
            inner_other,
            ffn_outer,
            outer_other,
            bias_inner,
            bias_outer,
        )
        total_outer = Total(split_outer, ("xy", "yz", "zx"), True)
        total_inner = Total(split_inner, ("zx", "yy", "xz"), False)
    else:
        inner_sum = dot_nn(normed_three, whole_ffn_inner) + bias_inner
        active = jax.nn.gelu(inner_sum, approximate=False).astype(jnp.bfloat16)
        outputs = (hidden_two + dot_nn(active, whole_ffn_outer) + bias_outer).astype(jnp.bfloat16)
        grad_active = dot_back(cotangent, whole_ffn_outer)
        gelu_pull = jax.vjp(lambda u: jax.nn.gelu(u, approximate=False), inner_sum)[1]
        grad_inner = gelu_pull(grad_active)[0].astype(jnp.bfloat16)
        column_inner = column_sum(grad_inner)
        grad_normed_three = dot_back(grad_inner, whole_ffn_inner)
    back_two, grad_gain_three, grad_shift_three = layer_norm_back(
        hidden_two, gain_three, grad_normed_three
    )
    grad_hidden_two = cotangent.astype(jnp.float32) + back_two
    branch_cross = grad_hidden_two.astype(jnp.bfloat16)
    grad_mixed_cross = dot_back(branch_cross, whole_cross[:, 3 * width :]).astype(jnp.bfloat16)
    back_cross = functools.partial(
        attend_back, cross_plan, info, queries_cross, mixed_cross
    )
    cross_rest = (log_cross, patch_pairs, blank_bias)
    if two:
        sent = (total_outer.step(), total_inner.step())
        cross_back = back_cross(after(grad_mixed_cross, *sent), *cross_rest, 0, 1)
    else:
        cross_back = back_cross(grad_mixed_cross, *cross_rest, 0, 1)
    scaled_cross, grad_patch_keys, grad_patch_values = cross_back
    back_one, grad_gain_two, grad_shift_two = layer_norm_back(
        hidden_one, gain_two, dot_back(scaled_cross, whole_cross[:, 2 * width : 3 * width])
    )
    grad_hidden_one = grad_hidden_two + back_one
    branch_self = grad_hidden_one.astype(jnp.bfloat16)
    grad_mixed_self = dot_back(branch_self, whole_self[:, 3 * width :]).astype(jnp.bfloat16)
    cross_products = [
        (normed_two, scaled_cross),
        (patches_all, grad_patch_keys),
        (patches_all, grad_patch_values),
        (mixed_cross, branch_cross),
    ]
    back_self = functools.partial(attend_back, self_plan, info, queries_self, mixed_self)
    self_rest = (log_self, self_pairs, no_bias)
    if two:
        total_cross = Total(outer_group(core, cross_products), ("xy", "yz", "zx"), True)
        sent = (total_outer.step(), total_inner.step(), total_cross.kept)
        first_half = back_self(after(grad_mixed_self, *sent), *self_rest, 0, 2)
        held = after(grad_mixed_self, first_half[0])
        total_outer.kept, total_inner.kept, total_cross.kept = (
            after(total.kept, first_half[0]) for total in (total_outer, total_inner, total_cross)
        )
        sent = (total_cross.step(), total_outer.step(), total_inner.step())
        self_back = back_self(after(held, *sent), *self_rest, 1, 2, first_half)
    else:
        self_back = back_self(grad_mixed_self, *self_rest, 0, 1)
    scaled_self, grad_keys, grad_values = self_back
    self_products = [
        (normed_one, scaled_self),
        (normed_all, grad_keys),
        (normed_all, grad_values),
        (mixed_self, branch_self),
    ]
    if two:
        total_self = Total(outer_group(core, self_products), ("xy", "yz", "zx"), True)
        scaled_late = after(scaled_self, total_self.kept)
    else:
        scaled_late = scaled_self
    normed_terms = dot_back(grad_keys, whole_self[:, width : 2 * width]) + dot_back(
        grad_values, whole_self[:, 2 * width : 3 * width]
    )
    patch_terms = dot_back(grad_patch_keys, whole_cross[:, :width]) + dot_back(
        grad_patch_values, whole_cross[:, width : 2 * width]
    )
    if two:
        normed_sent = normed_terms[tok_rows:].astype(jnp.bfloat16)
        normed_came = lax.ppermute(normed_sent, "seq", [(1, 0)])
        grad_normed = normed_terms[:tok_rows] + normed_came.astype(jnp.float32)
        patch_sent = patch_terms[patch_rows:].astype(jnp.bfloat16)
        grad_patches = patch_terms[:patch_rows] + swap(patch_sent, "seq").astype(jnp.float32)
    else:
        grad_patches, grad_normed = (
            lax.psum_scatter(
                terms.astype(jnp.bfloat16), "seq", scatter_dimension=0, tiled=True
            ).astype(jnp.float32)
            for terms in (patch_terms, normed_terms)
        )
    grad_normed = grad_normed + dot_back(scaled_late, whole_self[:, :width])
    back_zero, grad_gain_one, grad_shift_one = layer_norm_back(token_values, gain_one, grad_normed)
    grad_tokens = grad_hidden_one + back_zero
    small = sum_vectors(
        (
            grad_gain_one,
            grad_shift_one,
            column_sum(scaled_self),
            column_sum(grad_values),
            column_sum(branch_self),
            grad_gain_two,
            grad_shift_two,
            column_sum(scaled_cross),
            column_sum(grad_patch_values),
            column_sum(branch_cross),
            grad_gain_three,
            grad_shift_three,
            column_inner,
            column_sum(cotangent),
        )
    )
    if two:
        totals = (total_outer, total_inner, total_cross, total_self)
        for turn in range(9):
            for total in totals:
                if total.stage < 4:
                    total.step()
                elif total.stage < 8:
                    total.gather()
        grad_outer, grad_ffn_in, grad_cross, grad_self = (total.result() for total in totals)
        wide_cross, wide_self = jnp.split(grad_cross, 4, axis=1), jnp.split(grad_self, 4, axis=1)
    else:
        grad_outer = sum_plain(dot_tn(active, cotangent)).astype(jnp.float32)
        grad_ffn_in = sum_plain(dot_tn(normed_three, grad_inner)).astype(jnp.float32)
        wide_cross = [sum_plain(dot_tn(*product)).astype(jnp.float32) for product in cross_products]
        wide_self = [sum_plain(dot_tn(*product)).astype(jnp.float32) for product in self_products]
    totals = (
        small[0],
        small[1],
        wide_self[0],
        small[2],
        wide_self[1],
        wide_self[2],
        small[3],
        wide_self[3],
        small[4],
        small[5],
        small[6],
        wide_cross[0],
        small[7],
        wide_cross[1],
        wide_cross[2],
        small[8],
        wide_cross[3],
        small[9],
        small[10],
        small[11],
        grad_ffn_in,
        small[12],
        grad_outer,
        small[13],
    )
    return (outputs[None], grad_tokens[None], grad_patches[None]) + totals


def solution(mesh):
    page_count, seq_count = mesh.devices.shape
    mesh = Mesh(
        mesh.devices.reshape(page_count // 8, 2, 2, 2, seq_count),
        ("zhi", "zlo", "x", "core", "seq"),
    )
    page = ("zhi", "zlo", "x", "core")
    pages = P(page, "seq", None)
    rows, vector = P("seq", None), P("seq")
    layer = (
        (vector, vector)
        + (rows, vector, rows, rows, vector, rows, vector)
        + (vector, vector)
        + (rows, vector, rows, rows, vector, rows, vector)
        + (vector, vector)
        + (rows, vector, rows, vector)
    )
    return jax.shard_map(
        on_device,
        mesh=mesh,
        in_specs=(pages, pages, P(page), P(page, None), pages) + layer,
        out_specs=(pages, pages, pages) + layer,
        check_vma=False,
    )
```

time: 1770 us -> 757 us (0.43)
  waiting for transfers between devices: 1010 us -> 257 us
  matrix products: 355 us -> 52 us
  Pallas kernels: 0 us -> 253 us
  blocking collectives: 132 us -> 0 us
  other arithmetic: 143 us -> 44.4 us
  starting transfers between devices: 1.92 us -> 83.2 us
  local copies, waits for them, and re-layouts: 94.5 us -> 58.4 us
    reduce_scatter x12 -> x0, waiting for transfers between devices: 435 us -> none  [the longest x1 102 us: on_device(): lax.psum_scatter(outer_sum(active, cotangent).astype(jnp.bfloat16), 'seq'...]
    all_gather x14 -> x0, waiting for transfers between devices: 385 us -> none  [the longest x1 100 us: on_device(): lax.all_gather(ffn_inner, 'seq', axis=0, tiled=True)]
    dot_general x42 -> x14, matrix products: 355 us -> 52 us  [the longest x8 30.9 us: dot_nt(): lax.dot_general(left_side, right_side, (((1,), (1,)), ((), ())), preferre...]
    ppermute x0 -> x62, waiting for transfers between devices: none -> 257 us  [the longest x28 144 us: exchange(): lax.ppermute(values, square, [(i, i ^ flip[i // 2 % 2]) for i in range(16)])]
    pallas_call x0 -> x50, Pallas kernels: none -> 253 us  [the longest x4 46.9 us: attend(): pl.pallas_call(skip_refs(functools.partial(attend_kernel, plan), 5, len(i...]
    psum x1 -> x0, waiting for transfers between devices: 189 us -> none  [on_device(): lax.psum(shard_sums[13].astype(jnp.bfloat16), 'page').astype(jnp.float32)]
    ppermute x0 -> x62, starting transfers between devices: none -> 83.2 us  [the longest x32 42.8 us: swap(): return lax.ppermute(values, axis_name, [(0, 1), (1, 0)])]
    convert_element_type x42 -> x11, other arithmetic: 91.1 us -> 15.7 us  [the longest x4 11.1 us: result(): return jnp.concatenate([first, second]).astype(jnp.float32)]
  transfers between devices with their start and end apart: 29 -> 62, of which waited for: 22 -> 24; matrix products, arithmetic and copies ran while one was open for 23% -> 17% of each run, Pallas kernels for 0% -> 17%
where the time goes in v1:
time: 757 us; the launch traced here: 751 us
  waiting for transfers between devices  257 us (34%)
  Pallas kernels  253 us (33%)
  starting transfers between devices  83.2 us (11%)
  local copies, waits for them, and re-layouts  58.4 us (8%)
  matrix products  52 us (7%)
  other arithmetic  44.4 us (6%)
    ppermute x28, waiting for transfers between devices, exchange(): lax.ppermute(values, square, [(i, i ^ flip[i // 2 % 2]) for i in range(16)])  144 us
    ppermute x32, waiting for transfers between devices, swap(): return lax.ppermute(values, axis_name, [(0, 1), (1, 0)])  93.5 us
    pallas_call x4, Pallas kernels, attend(): pl.pallas_call(skip_refs(functools.partial(attend_kernel, plan), 5, len(i...  46.9 us
    pallas_call x3, Pallas kernels, attend_back(): pl.pallas_call(skip_refs(functools.partial(attend_back_kernel, plan), 8,...  45.4 us
    pallas_call x22, Pallas kernels, merge(): pl.pallas_call(merge_kernel, grid_spec=pltpu.PrefetchScalarGridSpec(num_s...  43 us
    ppermute x32, starting transfers between devices, swap(): return lax.ppermute(values, axis_name, [(0, 1), (1, 0)])  42.8 us
    pallas_call x16, Pallas kernels, halve(): pl.pallas_call(halve_kernel, grid_spec=pltpu.PrefetchScalarGridSpec(num_s...  42.3 us
    pallas_call x1, Pallas kernels, ffn_both_ways(): pl.pallas_call(functools.partial(ffn_kernel, half_steps), grid_spec=pltpu...  40.1 us
  transfers between devices with their start and end apart: 62, of which 24 were waited for; matrix products, arithmetic and copies ran while one was open for 17% of the time, Pallas kernels for 17%

profile of v1, /device:TPU:0, one launch (start us, length us, event | category | flops | bytes accessed | tf_op | source)
XLA Modules:
  0.0 751.5 jit_solution(10506869237199336642)
XLA Ops:
  5.8 11.9 %collective-permute-done.own_ref = bf16[64,4096]{1,0:T(8,128)(2,1)S(1)} collective-permute-done((bf16[64,4096]{1,0:T(8,128)(2,1)S(1)}, bf16[64,4096]{1,0:T(8,128)(2,1)S(1)}, u32[]{:S(2)}, u32[]{:S(2)}) %collective-permute-start) | collective-permute-done | bytes 524320 | tf_op jit(solution)/shard_map/ppermute | solution.py:603
  19.5 7.4 collective-permute-done.2.other_ref
  31.4 11.0 %collective-permute-done.3.other_ref = bf16[128,4096]{1,0:T(8,128)(2,1)S(1)} collective-permute-done((bf16[128,4096]{1,0:T(8,128)(2,1)S(1)}, bf16[128,4096]{1,0:T(8,128)(2,1)S(1)}, u32[]{:S(2)}, u32[]{:S(2)}) %collective-permute-start.3) | collective-permute-done | bytes 1048608 | tf_op jit(solution)/shard_map/ppermute | solution.py:612
  52.9 9.3 %collective-permute-done.5 = bf16[68,128]{1,0:T(8,128)(2,1)S(1)} collective-permute-done((bf16[68,128]{1,0:T(8,128)(2,1)S(1)}, bf16[68,128]{1,0:T(8,128)(2,1)S(1)}, u32[]{:S(2)}, u32[]{:S(2)}) %collective-permute-start.5) | collective-permute-done | bytes 17440 | tf_op jit(solution)/shard_map/ppermute | solution.py:603
  68.0 7.6 %collective-permute-done.7.other_ref = bf16[64,4096]{1,0:T(8,128)(2,1)S(1)} collective-permute-done((bf16[64,4096]{1,0:T(8,128)(2,1)}, bf16[64,4096]{1,0:T(8,128)(2,1)S(1)}, u32[]{:S(2)}, u32[]{:S(2)}) %collective-permute-start.7) | collective-permute-done | bytes 524320 | tf_op jit(solution)/shard_map/ppermute | solution.py:612
  83.1 5.4 collective-permute-done.1
  92.7 6.1 add_convert_fusion.refs_2_.refs_3_.refs_5_.refs_6_
  98.9 8.6 %shard_map.488 = (bf16[512,1024]{1,0:T(8,128)(2,1)S(1)}, f32[8,2,512]{2,1,0:T(2,128)S(1)}) custom-call(s32[4]{0:T(128)S(1)} %pad_add_fusion.refs_0_, bf16[512,1024]{1,0:T(8,128)(2,1)S(1)} %multiply_convert_fusion.1.refs_1_, bf16[1024,2048]{1,0:T(8,128)(2,1)} %add_convert_fusion.refs_2_.refs_3_.refs_5_.refs_6_, ...), custom_call_target="tpu_custom_call" | custom-call | flops 4294967296 | bytes 3145728 | tf_op jit(solution)/shard_map/pallas_call | solution.py:210
  107.6 9.0 %shard_map.489 = (bf16[512,1024]{1,0:T(8,128)(2,1)S(1)}, f32[8,2,512]{2,1,0:T(2,128)S(1)}) custom-call(s32[4]{0:T(128)S(1)} %pad_add_fusion.refs_0_, bf16[512,1024]{1,0:T(8,128)(2,1)S(1)} %multiply_convert_fusion.1.refs_1_, bf16[1024,2048]{1,0:T(8,128)(2,1)} %add_convert_fusion.refs_2_.refs_3_.refs_5_.refs_6_, ...), custom_call_target="tpu_custom_call", output_to_operand_aliasing={{0}: (5, {}), {1}: (6, {})} | custom-call | flops 4294967296 | bytes 3145728 | tf_op jit(solution)/shard_map/pallas_call | solution.py:210
  121.4 8.8 %collective-permute-start.10 = (bf16[64,4096]{1,0:T(8,128)(2,1)S(1)}, bf16[64,4096]{1,0:T(8,128)(2,1)}, u32[]{:S(2)}, u32[]{:S(2)}) collective-permute-start(bf16[64,4096]{1,0:T(8,128)(2,1)S(1)} %constant_dynamic-slice_fusion.1), channel_id=1, source_target_pairs={{0,1},{1,0},{2,3},{3,2},{4,5},{5,4},{6,7},{7,6},{8,9},{9,8},{10,11... | collective-permute-start | bytes 1572872 | tf_op jit(solution)/shard_map/ppermute | solution.py:603
  131.8 11.3 %collective-permute-done.10.own_ref = bf16[64,4096]{1,0:T(8,128)(2,1)} collective-permute-done((bf16[64,4096]{1,0:T(8,128)(2,1)S(1)}, bf16[64,4096]{1,0:T(8,128)(2,1)}, u32[]{:S(2)}, u32[]{:S(2)}) %collective-permute-start.10) | collective-permute-done | bytes 524320 | tf_op jit(solution)/shard_map/ppermute | solution.py:603
  144.6 9.5 %collective-permute-done.12.own_ref = bf16[256,1024]{1,0:T(8,128)(2,1)} collective-permute-done((bf16[256,1024]{1,0:T(8,128)(2,1)S(1)}, bf16[256,1024]{1,0:T(8,128)(2,1)}, u32[]{:S(2)}, u32[]{:S(2)}) %collective-permute-start.12) | collective-permute-done | bytes 524320 | tf_op jit(solution)/shard_map/ppermute | solution.py:603
  173.7 8.7 %collective-permute-done.13 = bf16[544,1024]{1,0:T(8,128)(2,1)} collective-permute-done((bf16[544,1024]{1,0:T(8,128)(2,1)}, bf16[544,1024]{1,0:T(8,128)(2,1)}, u32[]{:S(2)}, u32[]{:S(2)}) %collective-permute-start.13) | collective-permute-done | bytes 1114144 | tf_op jit(solution)/shard_map/ppermute | solution.py:603
  183.2 4.4 collective-permute-done.17.other_ref
  188.5 7.8 %fusion.refs_2_.refs_3_.refs_5_.refs_6_ = bf16[1088,2048]{1,0:T(8,128)(2,1)} fusion(f32[2048]{0:T(1024)S(1)} %pad_convert_fusion, bf16[1024,4096]{1,0:T(8,128)(2,1)S(1)} %shard_map.491, bf16[544,1024]{1,0:T(8,128)(2,1)} %collective-permute-done.13, bf16[544,1024]{1,0:T(8,128)(2,1)S(1)} %bitcast.226), kind=kOutput, calls=%fused_computation.2 | convolution fusion | flops 4572315648 | bytes 10887168 | tf_op jit(solution)/shard_map/dot_general | solution.py:37
  196.2 14.5 %shard_map.493 = (bf16[512,1024]{1,0:T(8,128)(2,1)S(1)}, f32[8,2,512]{2,1,0:T(2,128)S(1)}) custom-call(s32[4]{0:T(128)S(1)} %pad_add_fusion.refs_0_, bf16[512,1024]{1,0:T(8,128)(2,1)S(1)} %multiply_convert_fusion.refs_1_, bf16[1088,2048]{1,0:T(8,128)(2,1)} %fusion.refs_2_.refs_3_.refs_5_.refs_6_, bf16[1088,2048]{1,0:T(8,128)(2,1)} %fusion.refs_2_.refs_3_.refs_5_.refs_6_, ...), custom_call_target="tpu_custom_call" | custom-call | flops 4563402752 | bytes 3276800 | tf_op jit(solution)/shard_map/pallas_call | solution.py:210
  210.8 14.7 %shard_map.494 = (bf16[512,1024]{1,0:T(8,128)(2,1)S(1)}, f32[8,2,512]{2,1,0:T(2,128)S(1)}) custom-call(s32[4]{0:T(128)S(1)} %pad_add_fusion.refs_0_, bf16[512,1024]{1,0:T(8,128)(2,1)S(1)} %multiply_convert_fusion.refs_1_, bf16[1088,2048]{1,0:T(8,128)(2,1)} %fusion.refs_2_.refs_3_.refs_5_.refs_6_, ...), custom_call_target="tpu_custom_call", output_to_operand_aliasing={{0}: (5, {}), {1}: (6, {})} | custom-call | flops 4563402752 | bytes 3276800 | tf_op jit(solution)/shard_map/pallas_call | solution.py:210
  239.3 40.1 %shard_map.500 = (bf16[512,1024]{1,0:T(8,128)(2,1)}, f32[512,1024]{1,0:T(8,128)}, f32[1,4096]{1,0:T(1,128)}, bf16[4,512,1024]{2,1,0:T(8,128)(2,1)}, bf16[4,512,1...) custom-call(s32[32]{0:T(128)} %stack.144.place_ref, ...), custom_call_target="tpu_custom_call" | custom-call | flops 25769803776 | bytes 39845888 | tf_op jit(solution)/shard_map/pallas_call | solution.py:442
  289.9 4.5 shard_map.501
  295.8 5.5 shard_map.502
  302.6 27.2 %shard_map.503 = (bf16[512,1024]{1,0:T(8,128)(2,1)S(1)}, bf16[1088,1024]{1,0:T(8,128)(2,1)}, bf16[1088,1024]{1,0:T(8,128)(2,1)}) custom-call(s32[4]{0:T(128)S(1)} %pad_add_fusion.refs_0_, bf16[512,1024]{1,0:T(8,128)(2,1)S(1)} %copy-done.48, bf16[512,1024]{1,0:T(8,128)(2,1)S(1)} %copy-done.37, bf16[512,1024]{1,0:T(8,128)(2,1)S(1)} %fusion.56.refs_3_, ...), custom_call_target="tpu_custom_call" | custom-call | flops 22817013760 | bytes 13107200 | tf_op jit(solution)/shard_map/pallas_call | solution.py:238
  329.8 15.5 %shard_map.506 = (bf16[2,256,4096]{2,1,0:T(8,128)(2,1)}, bf16[2,256,4096]{2,1,0:T(8,128)(2,1)}) custom-call(s32[2]{0:T(128)S(1)} %pad_add_fusion.4.place_ref, bf16[512,1024]{1,0:T(8,128)(2,1)S(1)} %add_convert_fusion.2.refs_0_, bf16[1088,1024]{1,0:T(8,128)(2,1)} %pad_maximum_fusion.refs_1_.refs_2_, bf16[1088,1024]{1,0:T(8,128)(2,1)} %pad_maximum_fusion.refs_1_.refs_2_, ...), custom_call_target="tpu_custom_call" | custom-call | flops 6710886400 | bytes 21495808 | tf_op jit(solution)/shard_map/pallas_call | solution.py:530
  353.9 4.1 multiply_reduce_fusion.1
  360.2 35.6 %collective-permute-done.21.came_a.came_b = bf16[2,512,1024]{2,1,0:T(8,128)(2,1)} collective-permute-done((bf16[2,512,1024]{2,1,0:T(8,128)(2,1)}, bf16[2,512,1024]{2,1,0:T(8,128)(2,1)}, u32[]{:S(2)}, u32[]{:S(2)}) %collective-permute-start.21) | collective-permute-done | bytes 2097184 | tf_op jit(solution)/shard_map/ppermute | solution.py:612
  406.1 8.8 %shard_map.507 = (bf16[512,1024]{1,0:T(8,128)(2,1)S(1)}, bf16[1024,1024]{1,0:T(8,128)(2,1)}, bf16[1024,1024]{1,0:T(8,128)(2,1)}) custom-call(s32[4]{0:T(128)S(1)} %pad_add_fusion.refs_0_, bf16[512,1024]{1,0:T(8,128)(2,1)S(1)} %copy-done.39, bf16[512,1024]{1,0:T(8,128)(2,1)S(1)} %copy-done.42, bf16[512,1024]{1,0:T(8,128)(2,1)S(1)} %fusion.53.refs_3_, ...), custom_call_target="tpu_custom_call" | custom-call | flops 10737418240 | bytes 6291456 | tf_op jit(solution)/shard_map/pallas_call | solution.py:238
  414.9 19.1 %collective-permute-done.25 = bf16[1,128,4096]{2,1,0:T(8,128)(2,1)S(1)} collective-permute-done((bf16[1,128,4096]{2,1,0:T(8,128)(2,1)S(1)}, bf16[1,128,4096]{2,1,0:T(8,128)(2,1)S(1)}, u32[]{:S(2)}, u32[]{:S(2)}) %collective-permute-start.25) | collective-permute-done | bytes 1048608 | tf_op jit(solution)/shard_map/ppermute | solution.py:612
  437.1 5.6 shard_map.508
  445.1 9.4 %shard_map.511 = (bf16[512,1024]{1,0:T(8,128)(2,1)S(1)}, bf16[1024,1024]{1,0:T(8,128)(2,1)}, bf16[1024,1024]{1,0:T(8,128)(2,1)}) custom-call(s32[4]{0:T(128)S(1)} %pad_add_fusion.refs_0_, bf16[512,1024]{1,0:T(8,128)(2,1)S(1)} %copy-done.40, bf16[512,1024]{1,0:T(8,128)(2,1)S(1)} %copy-done.43, ...), custom_call_target="tpu_custom_call", output_to_operand_aliasing={{0}: (8, {}), {1}: (9, {}), {2}: (10, {})} | custom-call | flops 10737418240 | bytes 6291456 | tf_op jit(solution)/shard_map/pallas_call | solution.py:238
  460.4 14.1 %shard_map.512 = (bf16[2,256,4096]{2,1,0:T(8,128)(2,1)}, bf16[2,256,4096]{2,1,0:T(8,128)(2,1)}) custom-call(s32[2]{0:T(128)S(1)} %pad_add_fusion.4.place_ref, bf16[512,1024]{1,0:T(8,128)(2,1)S(1)} %copy-done.22, bf16[1024,1024]{1,0:T(8,128)(2,1)} %copy-done.59, bf16[1024,1024]{1,0:T(8,128)(2,1)} %copy-done.59, bf16[512,1024]{1,0:T(8,128)(2,1)S(1)} %copy-done.44, ...), custom_call_target="tpu_custom_call" | custom-call | flops 6442450944 | bytes 20971520 | tf_op jit(solution)/shard_map/pallas_call | solution.py:530
  474.7 4.3 fusion.26
  487.7 6.0 collective-permute-start.27
  509.1 4.0 fusion.34
  514.2 4.6 collective-permute-done.51
  520.2 4.2 collective-permute-done.57
  525.4 5.6 shard_map.513
  534.0 13.9 %collective-permute-done.26 = bf16[512,1024]{1,0:T(8,128)(2,1)} collective-permute-done((bf16[512,1024]{1,0:T(8,128)(2,1)}, bf16[512,1024]{1,0:T(8,128)(2,1)}, u32[]{:S(2)}, u32[]{:S(2)}) %collective-permute-start.26) | collective-permute-done | bytes 1048608 | tf_op jit(solution)/shard_map/ppermute | solution.py:1000
  547.9 6.1 fusion.23
  563.7 20.1 %collective-permute-done.43 = bf16[1,128,4096]{2,1,0:T(8,128)(2,1)S(1)} collective-permute-done((bf16[1,128,4096]{2,1,0:T(8,128)(2,1)S(1)}, bf16[1,128,4096]{2,1,0:T(8,128)(2,1)S(1)}, u32[]{:S(2)}, u32[]{:S(2)}) %collective-permute-start.43) | collective-permute-done | bytes 1048608 | tf_op jit(solution)/shard_map/ppermute | solution.py:612
  594.4 9.6 %shard_map.527.own_ref = bf16[64,4096]{1,0:T(8,128)(2,1)} custom-call(s32[2]{0:T(128)S(1)} %pad_add_fusion.11.place_ref, bf16[32,4096]{1,0:T(8,128)(2,1)S(1)} %fusion.71.own_ref, bf16[32,4096]{1,0:T(8,128)(2,1)} %collective-permute-done.52.other_ref), custom_call_target="tpu_custom_call" | custom-call | bytes 1048576 | tf_op jit(solution)/shard_map/pallas_call | solution.py:289
  606.4 9.6 %shard_map.531.own_ref = bf16[256,1024]{1,0:T(8,128)(2,1)} custom-call(s32[2]{0:T(128)S(1)} %pad_add_fusion.11.place_ref, bf16[128,1024]{1,0:T(8,128)(2,1)S(1)} %copy-done.26, bf16[128,1024]{1,0:T(8,128)(2,1)} %collective-permute-done.58.other_ref), custom_call_target="tpu_custom_call" | custom-call | bytes 1048576 | tf_op jit(solution)/shard_map/pallas_call | solution.py:289
  629.0 4.8 collective-permute-done.59.other_ref
  637.8 22.9 %collective-permute-done.30 = f32[2,68,128]{2,1,0:T(8,128)S(1)} collective-permute-done((f32[2,68,128]{2,1,0:T(8,128)S(1)}, f32[2,68,128]{2,1,0:T(8,128)S(1)}, u32[]{:S(2)}, u32[]{:S(2)}) %collective-permute-start.30) | collective-permute-done | bytes 69664 | tf_op jit(solution)/shard_map/ppermute | solution.py:603
  669.1 11.0 %collective-permute-done.46.other_ref = bf16[32,4096]{1,0:T(8,128)(2,1)S(1)} collective-permute-done((bf16[32,4096]{1,0:T(8,128)(2,1)S(1)}, bf16[32,4096]{1,0:T(8,128)(2,1)S(1)}, u32[]{:S(2)}, u32[]{:S(2)}) %collective-permute-start.46) | collective-permute-done | bytes 262176 | tf_op jit(solution)/shard_map/ppermute | solution.py:603
  686.8 11.7 %collective-permute-done.47.other_ref = bf16[64,4096]{1,0:T(8,128)(2,1)S(1)} collective-permute-done((bf16[64,4096]{1,0:T(8,128)(2,1)S(1)}, bf16[64,4096]{1,0:T(8,128)(2,1)S(1)}, u32[]{:S(2)}, u32[]{:S(2)}) %collective-permute-start.47) | collective-permute-done | bytes 524320 | tf_op jit(solution)/shard_map/ppermute | solution.py:612
  704.2 9.9 %collective-permute-done.48.other_ref = bf16[128,4096]{1,0:T(8,128)(2,1)S(1)} collective-permute-done((bf16[128,4096]{1,0:T(8,128)(2,1)S(1)}, bf16[128,4096]{1,0:T(8,128)(2,1)S(1)}, u32[]{:S(2)}, u32[]{:S(2)}) %collective-permute-start.48) | collective-permute-done | bytes 1048608 | tf_op jit(solution)/shard_map/ppermute | solution.py:612
  716.6 8.1 %collective-permute-done.39.other_ref = bf16[64,4096]{1,0:T(8,128)(2,1)S(1)} collective-permute-done((bf16[64,4096]{1,0:T(8,128)(2,1)S(1)}, bf16[64,4096]{1,0:T(8,128)(2,1)S(1)}, u32[]{:S(2)}, u32[]{:S(2)}) %collective-permute-start.39) | collective-permute-done | bytes 524320 | tf_op jit(solution)/shard_map/ppermute | solution.py:612
  727.4 4.5 maximum_convert_fusion.3
  731.9 4.5 maximum_convert_fusion.2
  (476 shorter events, 237.0 us)
Async XLA Ops:
  45.4 33.5 %collective-permute-start.4 = (bf16[256,4096]{1,0:T(8,128)(2,1)S(1)}, bf16[256,4096]{1,0:T(8,128)(2,1)}, u32[]{:S(2)}, u32[]{:S(2)}) collective-permute-start(bf16[256,4096]{1,0:T(8,128)(2,1)S(1)} %shard_map.485.refs_4_), channel_id=1, source_target_pairs={{0,2},{2,0},{1,3},{3,1},{4,6},{6,4},{5,7},{7,5},{8,10},{10,8},{9,1... | collective-permute-start | bytes 6291464 | tf_op jit(solution)/shard_map/ppermute | solution.py:603
  47.3 18.8 %collective-permute-start.6 = (bf16[64,4096]{1,0:T(8,128)(2,1)}, bf16[64,4096]{1,0:T(8,128)(2,1)}, u32[]{:S(2)}, u32[]{:S(2)}) collective-permute-start(bf16[64,4096]{1,0:T(8,128)(2,1)} %pad_maximum_fusion.3), channel_id=1, source_target_pairs={{0,1},{1,0},{2,3},{3,2},{4,5},{5,4},{6,7},{7,6},{8,9},{9,8},{10,11... | collective-permute-start | bytes 1572872 | tf_op jit(solution)/shard_map/ppermute | solution.py:603
  62.2 26.3 %collective-permute-start.1 = (bf16[512,1024]{1,0:T(8,128)(2,1)}, bf16[512,1024]{1,0:T(8,128)(2,1)S(1)}, u32[]{:S(2)}, u32[]{:S(2)}) collective-permute-start(bf16[512,1024]{1,0:T(8,128)(2,1)} %bitcast.214), channel_id=1, source_target_pairs={{0,1},{2,3},{4,5},{6,7},{8,9},{10,11},{12,13},{14,15},{16,17},{18,... | collective-permute-start | bytes 3145736 | tf_op jit(solution)/shard_map/ppermute | solution.py:825
  77.2 41.1 %collective-permute-start.8 = (bf16[128,4096]{1,0:T(8,128)(2,1)S(1)}, bf16[128,4096]{1,0:T(8,128)(2,1)}, u32[]{:S(2)}, u32[]{:S(2)}) collective-permute-start(bf16[128,4096]{1,0:T(8,128)(2,1)S(1)} %shard_map.487.own_ref), channel_id=1, source_target_pairs={{0,8},{1,9},{2,6},{3,7},{4,12},{5,13},{6,2},{7,3},{8,0},{9,1},{10,... | collective-permute-start | bytes 3145736 | tf_op jit(solution)/shard_map/ppermute | solution.py:612
  120.2 49.2 %collective-permute-start.9 = (bf16[256,4096]{1,0:T(8,128)(2,1)S(1)}, bf16[256,4096]{1,0:T(8,128)(2,1)}, u32[]{:S(2)}, u32[]{:S(2)}) collective-permute-start(bf16[256,4096]{1,0:T(8,128)(2,1)S(1)} %shard_map.490.refs_4_), channel_id=1, source_target_pairs={{0,2},{2,0},{1,3},{3,1},{4,6},{6,4},{5,7},{7,5},{8,10},{10,8},{9,1... | collective-permute-start | bytes 6291464 | tf_op jit(solution)/shard_map/ppermute | solution.py:603
  121.4 21.6 %collective-permute-start.10 = (bf16[64,4096]{1,0:T(8,128)(2,1)S(1)}, bf16[64,4096]{1,0:T(8,128)(2,1)}, u32[]{:S(2)}, u32[]{:S(2)}) collective-permute-start(bf16[64,4096]{1,0:T(8,128)(2,1)S(1)} %constant_dynamic-slice_fusion.1), channel_id=1, source_target_pairs={{0,1},{1,0},{2,3},{3,2},{4,5},{5,4},{6,7},{7,6},{8,9},{9,8},{10,11... | collective-permute-start | bytes 1572872 | tf_op jit(solution)/shard_map/ppermute | solution.py:603
  131.7 22.4 %collective-permute-start.12 = (bf16[256,1024]{1,0:T(8,128)(2,1)S(1)}, bf16[256,1024]{1,0:T(8,128)(2,1)}, u32[]{:S(2)}, u32[]{:S(2)}) collective-permute-start(bf16[256,1024]{1,0:T(8,128)(2,1)S(1)} %constant_dynamic-slice_fusion), channel_id=1, source_target_pairs={{0,1},{1,0},{2,3},{3,2},{4,5},{5,4},{6,7},{7,6},{8,9},{9,8},{10,11... | collective-permute-start | bytes 1572872 | tf_op jit(solution)/shard_map/ppermute | solution.py:603
  143.1 16.4 %collective-permute-start.11 = (bf16[64,4096]{1,0:T(8,128)(2,1)}, bf16[64,4096]{1,0:T(8,128)(2,1)}, u32[]{:S(2)}, u32[]{:S(2)}) collective-permute-start(bf16[64,4096]{1,0:T(8,128)(2,1)} %collective-permute-done.10.own_ref), channel_id=1, source_target_pairs={{0,4},{1,5},{2,10},{3,11},{4,0},{5,1},{6,14},{7,15},{8,12},{9,13},... | collective-permute-start | bytes 1572872 | tf_op jit(solution)/shard_map/ppermute | solution.py:612
  155.8 26.6 %collective-permute-start.13 = (bf16[544,1024]{1,0:T(8,128)(2,1)}, bf16[544,1024]{1,0:T(8,128)(2,1)}, u32[]{:S(2)}, u32[]{:S(2)}) collective-permute-start(bf16[544,1024]{1,0:T(8,128)(2,1)} %bitcast.224), channel_id=1, source_target_pairs={{0,1},{1,0},{2,3},{3,2},{4,5},{5,4},{6,7},{7,6},{8,9},{9,8},{10,11... | collective-permute-start | bytes 3342344 | tf_op jit(solution)/shard_map/ppermute | solution.py:603
  161.5 20.8 %collective-permute-start.14 = (bf16[128,4096]{1,0:T(8,128)(2,1)S(1)}, bf16[128,4096]{1,0:T(8,128)(2,1)S(1)}, u32[]{:S(2)}, u32[]{:S(2)}) collective-permute-start(bf16[128,4096]{1,0:T(8,128)(2,1)S(1)} %shard_map.492.own_ref), channel_id=1, source_target_pairs={{0,8},{1,9},{2,6},{3,7},{4,12},{5,13},{6,2},{7,3},{8,0},{9,1},{10,... | collective-permute-start | bytes 3145736 | tf_op jit(solution)/shard_map/ppermute | solution.py:612
  165.4 22.3 %collective-permute-start.17 = (bf16[512,1024]{1,0:T(8,128)(2,1)S(1)}, bf16[512,1024]{1,0:T(8,128)(2,1)S(1)}, u32[]{:S(2)}, u32[]{:S(2)}) collective-permute-start(bf16[512,1024]{1,0:T(8,128)(2,1)S(1)} %shard_map.497.own_ref), channel_id=1, source_target_pairs={{0,8},{1,9},{2,6},{3,7},{4,12},{5,13},{6,2},{7,3},{8,0},{9,1},{10,... | collective-permute-start | bytes 3145736 | tf_op jit(solution)/shard_map/ppermute | solution.py:612
  183.1 47.5 %collective-permute-start.15 = (bf16[256,4096]{1,0:T(8,128)(2,1)S(1)}, bf16[256,4096]{1,0:T(8,128)(2,1)}, u32[]{:S(2)}, u32[]{:S(2)}) collective-permute-start(bf16[256,4096]{1,0:T(8,128)(2,1)S(1)} %shard_map.495.own_ref), channel_id=1, source_target_pairs={{0,2},{2,0},{1,3},{3,1},{4,6},{6,4},{5,7},{7,5},{8,10},{10,8},{9,1... | collective-permute-start | bytes 6291464 | tf_op jit(solution)/shard_map/ppermute | solution.py:603
  188.4 46.6 %collective-permute-start.18 = (bf16[1024,1024]{1,0:T(8,128)(2,1)S(1)}, bf16[1024,1024]{1,0:T(8,128)(2,1)}, u32[]{:S(2)}, u32[]{:S(2)}) collective-permute-start(bf16[1024,1024]{1,0:T(8,128)(2,1)S(1)} %shard_map.498.own_ref), channel_id=1, source_target_pairs={{0,2},{2,0},{1,3},{3,1},{4,6},{6,4},{5,7},{7,5},{8,10},{10,8},{9,1... | collective-permute-start | bytes 6291464 | tf_op jit(solution)/shard_map/ppermute | solution.py:603
  279.9 15.9 %collective-permute-start.20 = (bf16[4,128,4096]{2,1,0:T(8,128)(2,1)}, bf16[4,128,4096]{2,1,0:T(8,128)(2,1)}, u32[]{:S(2)}, u32[]{:S(2)}) collective-permute-start(bf16[4,128,4096]{2,1,0:T(8,128)(2,1)} %bitcast.253), channel_id=1, source_target_pairs={{0,2},{2,0},{1,3},{3,1},{4,6},{6,4},{5,7},{7,5},{8,10},{10,8},{9,1... | collective-permute-start | bytes 12582920 | tf_op jit(solution)/shard_map/ppermute | solution.py:603
  345.4 91.7 %collective-permute-start.23 = (bf16[4,128,4096]{2,1,0:T(8,128)(2,1)}, bf16[4,128,4096]{2,1,0:T(8,128)(2,1)}, u32[]{:S(2)}, u32[]{:S(2)}) collective-permute-start(bf16[4,128,4096]{2,1,0:T(8,128)(2,1)} %bitcast.251), channel_id=1, source_target_pairs={{0,2},{2,0},{1,3},{3,1},{4,6},{6,4},{5,7},{7,5},{8,10},{10,8},{9,1... | collective-permute-start | bytes 12582920 | tf_op jit(solution)/shard_map/ppermute | solution.py:603
  347.7 48.1 %collective-permute-start.21 = (bf16[2,512,1024]{2,1,0:T(8,128)(2,1)}, bf16[2,512,1024]{2,1,0:T(8,128)(2,1)}, u32[]{:S(2)}, u32[]{:S(2)}) collective-permute-start(bf16[2,512,1024]{2,1,0:T(8,128)(2,1)} %copy-done.35), channel_id=1, source_target_pairs={{0,4},{1,5},{2,3},{3,2},{4,0},{5,1},{6,7},{7,6},{8,12},{9,13},{10,... | collective-permute-start | bytes 6291464 | tf_op jit(solution)/shard_map/ppermute | solution.py:612
  348.3 50.6 %collective-permute-start.22 = (bf16[2,128,4096]{2,1,0:T(8,128)(2,1)}, bf16[2,128,4096]{2,1,0:T(8,128)(2,1)}, u32[]{:S(2)}, u32[]{:S(2)}) collective-permute-start(bf16[2,128,4096]{2,1,0:T(8,128)(2,1)} %copy-done.34), channel_id=1, source_target_pairs={{0,8},{1,9},{2,6},{3,7},{4,12},{5,13},{6,2},{7,3},{8,0},{9,1},{10,... | collective-permute-start | bytes 6291464 | tf_op jit(solution)/shard_map/ppermute | solution.py:612
  398.3 37.2 %collective-permute-start.24 = (bf16[1,512,1024]{2,1,0:T(8,128)(2,1)S(1)}, bf16[1,512,1024]{2,1,0:T(8,128)(2,1)S(1)}, u32[]{:S(2)}, u32[]{:S(2)}) collective-permute-start(bf16[1,512,1024]{2,1,0:T(8,128)(2,1)S(1)} %get-tuple-element.135), channel_id=1, source_target_pairs={{0,1},{1,0},{2,10},{3,11},{4,5},{5,4},{6,14},{7,15},{8,9},{9,8},{1... | collective-permute-start | bytes 3145736 | tf_op jit(solution)/shard_map/ppermute | solution.py:612
  401.5 32.5 %collective-permute-start.25 = (bf16[1,128,4096]{2,1,0:T(8,128)(2,1)S(1)}, bf16[1,128,4096]{2,1,0:T(8,128)(2,1)S(1)}, u32[]{:S(2)}, u32[]{:S(2)}) collective-permute-start(bf16[1,128,4096]{2,1,0:T(8,128)(2,1)S(1)} %get-tuple-element.137), channel_id=1, source_target_pairs={{0,1},{1,0},{2,3},{3,2},{4,5},{5,4},{6,7},{7,6},{8,9},{9,8},{10,11... | collective-permute-start | bytes 3145736 | tf_op jit(solution)/shard_map/ppermute | solution.py:612
  474.6 50.8 %collective-permute-start.33 = (bf16[4,128,4096]{2,1,0:T(8,128)(2,1)}, bf16[4,128,4096]{2,1,0:T(8,128)(2,1)}, u32[]{:S(2)}, u32[]{:S(2)}) collective-permute-start(bf16[4,128,4096]{2,1,0:T(8,128)(2,1)} %bitcast.252), channel_id=1, source_target_pairs={{0,2},{2,0},{1,3},{3,1},{4,6},{6,4},{5,7},{7,5},{8,10},{10,8},{9,1... | collective-permute-start | bytes 12582920 | tf_op jit(solution)/shard_map/ppermute | solution.py:603
  479.0 18.2 %collective-permute-start.50 = (bf16[1,64,4096]{2,1,0:T(8,128)(2,1)}, bf16[1,64,4096]{2,1,0:T(8,128)(2,1)}, u32[]{:S(2)}, u32[]{:S(2)}) collective-permute-start(bf16[1,64,4096]{2,1,0:T(8,128)(2,1)} %get-tuple-element.153), channel_id=1, source_target_pairs={{0,4},{1,5},{2,10},{3,11},{4,0},{5,1},{6,14},{7,15},{8,12},{9,13},... | collective-permute-start | bytes 1572872 | tf_op jit(solution)/shard_map/ppermute | solution.py:612
  480.4 21.2 %collective-permute-start.56 = (bf16[1,256,1024]{2,1,0:T(8,128)(2,1)}, bf16[1,256,1024]{2,1,0:T(8,128)(2,1)}, u32[]{:S(2)}, u32[]{:S(2)}) collective-permute-start(bf16[1,256,1024]{2,1,0:T(8,128)(2,1)} %get-tuple-element.150), channel_id=1, source_target_pairs={{0,8},{1,9},{2,6},{3,7},{4,12},{5,13},{6,2},{7,3},{8,0},{9,1},{10,... | collective-permute-start | bytes 1572872 | tf_op jit(solution)/shard_map/ppermute | solution.py:612
  487.7 132.6 %collective-permute-start.27 = (bf16[544,1024]{1,0:T(8,128)(2,1)}, bf16[544,1024]{1,0:T(8,128)(2,1)}, u32[]{:S(2)}, u32[]{:S(2)}) collective-permute-start(bf16[544,1024]{1,0:T(8,128)(2,1)} %slice.361), channel_id=1, source_target_pairs={{0,1},{1,0},{2,3},{3,2},{4,5},{5,4},{6,7},{7,6},{8,9},{9,8},{10,11... | collective-permute-start | bytes 3342344 | tf_op jit(solution)/shard_map/ppermute | solution.py:603
  499.0 19.9 %collective-permute-start.51 = (bf16[1,32,4096]{2,1,0:T(8,128)(2,1)S(1)}, bf16[1,32,4096]{2,1,0:T(8,128)(2,1)S(1)}, u32[]{:S(2)}, u32[]{:S(2)}) collective-permute-start(bf16[1,32,4096]{2,1,0:T(8,128)(2,1)S(1)} %get-tuple-element.181), channel_id=1, source_target_pairs={{0,16},{16,0},{1,17},{17,1},{2,18},{18,2},{3,19},{19,3},{4,20},{20... | collective-permute-start | bytes 786440 | tf_op jit(solution)/shard_map/ppermute | solution.py:603
  503.3 21.1 %collective-permute-start.57 = (bf16[1,128,1024]{2,1,0:T(8,128)(2,1)S(1)}, bf16[1,128,1024]{2,1,0:T(8,128)(2,1)S(1)}, u32[]{:S(2)}, u32[]{:S(2)}) collective-permute-start(bf16[1,128,1024]{2,1,0:T(8,128)(2,1)S(1)} %get-tuple-element.184), channel_id=1, source_target_pairs={{0,16},{16,0},{1,17},{17,1},{2,18},{18,2},{3,19},{19,3},{4,20},{20... | collective-permute-start | bytes 786440 | tf_op jit(solution)/shard_map/ppermute | solution.py:603
  503.7 51.4 %collective-permute-start.42 = (bf16[2,128,4096]{2,1,0:T(8,128)(2,1)}, bf16[2,128,4096]{2,1,0:T(8,128)(2,1)}, u32[]{:S(2)}, u32[]{:S(2)}) collective-permute-start(bf16[2,128,4096]{2,1,0:T(8,128)(2,1)} %get-tuple-element.147), channel_id=1, source_target_pairs={{0,4},{1,5},{2,3},{3,2},{4,0},{5,1},{6,7},{7,6},{8,12},{9,13},{10,... | collective-permute-start | bytes 6291464 | tf_op jit(solution)/shard_map/ppermute | solution.py:612
  518.8 29.0 %collective-permute-start.26 = (bf16[512,1024]{1,0:T(8,128)(2,1)}, bf16[512,1024]{1,0:T(8,128)(2,1)}, u32[]{:S(2)}, u32[]{:S(2)}) collective-permute-start(bf16[512,1024]{1,0:T(8,128)(2,1)} %slice.362), channel_id=1, source_target_pairs={{1,0},{3,2},{5,4},{7,6},{9,8},{11,10},{13,12},{15,14},{17,16},{19,... | collective-permute-start | bytes 3145736 | tf_op jit(solution)/shard_map/ppermute | solution.py:1000
  524.4 70.0 %collective-permute-start.52 = (bf16[32,4096]{1,0:T(8,128)(2,1)S(1)}, bf16[32,4096]{1,0:T(8,128)(2,1)}, u32[]{:S(2)}, u32[]{:S(2)}) collective-permute-start(bf16[32,4096]{1,0:T(8,128)(2,1)S(1)} %fusion.71.own_ref), channel_id=1, source_target_pairs={{0,16},{16,0},{1,17},{17,1},{2,18},{18,2},{3,19},{19,3},{4,20},{20... | collective-permute-start | bytes 786440 | tf_op jit(solution)/shard_map/ppermute | solution.py:603
  532.3 56.6 %collective-permute-start.34 = (bf16[2,128,4096]{2,1,0:T(8,128)(2,1)}, bf16[2,128,4096]{2,1,0:T(8,128)(2,1)}, u32[]{:S(2)}, u32[]{:S(2)}) collective-permute-start(bf16[2,128,4096]{2,1,0:T(8,128)(2,1)} %get-tuple-element.165), channel_id=1, source_target_pairs={{0,4},{1,5},{2,3},{3,2},{4,0},{5,1},{6,7},{7,6},{8,12},{9,13},{10,... | collective-permute-start | bytes 6291464 | tf_op jit(solution)/shard_map/ppermute | solution.py:612
  547.9 56.1 %collective-permute-start.58 = (bf16[128,1024]{1,0:T(8,128)(2,1)}, bf16[128,1024]{1,0:T(8,128)(2,1)}, u32[]{:S(2)}, u32[]{:S(2)}) collective-permute-start(bf16[128,1024]{1,0:T(8,128)(2,1)} %fusion.72.own_ref), channel_id=1, source_target_pairs={{0,16},{16,0},{1,17},{17,1},{2,18},{18,2},{3,19},{19,3},{4,20},{20... | collective-permute-start | bytes 786440 | tf_op jit(solution)/shard_map/ppermute | solution.py:603
  557.7 26.2 %collective-permute-start.43 = (bf16[1,128,4096]{2,1,0:T(8,128)(2,1)S(1)}, bf16[1,128,4096]{2,1,0:T(8,128)(2,1)S(1)}, u32[]{:S(2)}, u32[]{:S(2)}) collective-permute-start(bf16[1,128,4096]{2,1,0:T(8,128)(2,1)S(1)} %get-tuple-element.174), channel_id=1, source_target_pairs={{0,1},{1,0},{2,10},{3,11},{4,5},{5,4},{6,14},{7,15},{8,9},{9,8},{1... | collective-permute-start | bytes 3145736 | tf_op jit(solution)/shard_map/ppermute | solution.py:612
  585.4 32.9 %collective-permute-start.44 = (bf16[1,64,4096]{2,1,0:T(8,128)(2,1)}, bf16[1,64,4096]{2,1,0:T(8,128)(2,1)S(1)}, u32[]{:S(2)}, u32[]{:S(2)}) collective-permute-start(bf16[1,64,4096]{2,1,0:T(8,128)(2,1)} %get-tuple-element.176), channel_id=1, source_target_pairs={{0,8},{1,9},{2,6},{3,7},{4,12},{5,13},{6,2},{7,3},{8,0},{9,1},{10,... | collective-permute-start | bytes 1572872 | tf_op jit(solution)/shard_map/ppermute | solution.py:612
  592.2 71.2 %collective-permute-start.35 = (bf16[1,128,4096]{2,1,0:T(8,128)(2,1)}, bf16[1,128,4096]{2,1,0:T(8,128)(2,1)S(1)}, u32[]{:S(2)}, u32[]{:S(2)}) collective-permute-start(bf16[1,128,4096]{2,1,0:T(8,128)(2,1)} %get-tuple-element.167), channel_id=1, source_target_pairs={{0,1},{1,0},{2,10},{3,11},{4,5},{5,4},{6,14},{7,15},{8,9},{9,8},{1... | collective-permute-start | bytes 3145736 | tf_op jit(solution)/shard_map/ppermute | solution.py:612
  594.3 21.7 %collective-permute-start.28 = (f32[2,68,128]{2,1,0:T(8,128)S(1)}, f32[2,68,128]{2,1,0:T(8,128)S(1)}, u32[]{:S(2)}, u32[]{:S(2)}) collective-permute-start(f32[2,68,128]{2,1,0:T(8,128)S(1)} %reshape.421), channel_id=1, source_target_pairs={{0,16},{16,0},{1,17},{17,1},{2,18},{18,2},{3,19},{19,3},{4,20},{20... | collective-permute-start | bytes 208904 | tf_op jit(solution)/shard_map/ppermute | solution.py:603
  604.0 23.1 %collective-permute-start.53 = (bf16[64,4096]{1,0:T(8,128)(2,1)}, bf16[64,4096]{1,0:T(8,128)(2,1)}, u32[]{:S(2)}, u32[]{:S(2)}) collective-permute-start(bf16[64,4096]{1,0:T(8,128)(2,1)} %shard_map.527.own_ref), channel_id=1, source_target_pairs={{0,4},{1,5},{2,10},{3,11},{4,0},{5,1},{6,14},{7,15},{8,12},{9,13},... | collective-permute-start | bytes 1572872 | tf_op jit(solution)/shard_map/ppermute | solution.py:612
  616.6 17.2 %collective-permute-start.59 = (bf16[256,1024]{1,0:T(8,128)(2,1)}, bf16[256,1024]{1,0:T(8,128)(2,1)}, u32[]{:S(2)}, u32[]{:S(2)}) collective-permute-start(bf16[256,1024]{1,0:T(8,128)(2,1)} %shard_map.531.own_ref), channel_id=1, source_target_pairs={{0,8},{1,9},{2,6},{3,7},{4,12},{5,13},{6,2},{7,3},{8,0},{9,1},{10,... | collective-permute-start | bytes 1572872 | tf_op jit(solution)/shard_map/ppermute | solution.py:612
  618.3 17.4 %collective-permute-start.29 = (f32[2,68,128]{2,1,0:T(8,128)S(1)}, f32[2,68,128]{2,1,0:T(8,128)S(1)}, u32[]{:S(2)}, u32[]{:S(2)}) collective-permute-start(f32[2,68,128]{2,1,0:T(8,128)S(1)} %add.325), channel_id=1, source_target_pairs={{0,8},{8,0},{1,9},{9,1},{2,10},{10,2},{3,11},{11,3},{4,12},{12,4},... | collective-permute-start | bytes 208904 | tf_op jit(solution)/shard_map/ppermute | solution.py:603
  620.4 44.1 %collective-permute-start.45 = (bf16[1,32,4096]{2,1,0:T(8,128)(2,1)S(1)}, bf16[1,32,4096]{2,1,0:T(8,128)(2,1)S(1)}, u32[]{:S(2)}, u32[]{:S(2)}) collective-permute-start(bf16[1,32,4096]{2,1,0:T(8,128)(2,1)S(1)} %get-tuple-element.178), channel_id=1, source_target_pairs={{0,16},{16,0},{1,17},{17,1},{2,18},{18,2},{3,19},{19,3},{4,20},{20... | collective-permute-start | bytes 786440 | tf_op jit(solution)/shard_map/ppermute | solution.py:603
  628.9 39.0 %collective-permute-start.54 = (bf16[128,4096]{1,0:T(8,128)(2,1)S(1)}, bf16[128,4096]{1,0:T(8,128)(2,1)S(1)}, u32[]{:S(2)}, u32[]{:S(2)}) collective-permute-start(bf16[128,4096]{1,0:T(8,128)(2,1)S(1)} %shard_map.528.own_ref), channel_id=1, source_target_pairs={{0,8},{1,9},{2,6},{3,7},{4,12},{5,13},{6,2},{7,3},{8,0},{9,1},{10,... | collective-permute-start | bytes 3145736 | tf_op jit(solution)/shard_map/ppermute | solution.py:612
  635.6 50.3 %collective-permute-start.60 = (bf16[512,1024]{1,0:T(8,128)(2,1)S(1)}, bf16[512,1024]{1,0:T(8,128)(2,1)S(1)}, u32[]{:S(2)}, u32[]{:S(2)}) collective-permute-start(bf16[512,1024]{1,0:T(8,128)(2,1)S(1)} %shard_map.532.own_ref), channel_id=1, source_target_pairs={{0,4},{1,5},{2,10},{3,11},{4,0},{5,1},{6,14},{7,15},{8,12},{9,13},... | collective-permute-start | bytes 3145736 | tf_op jit(solution)/shard_map/ppermute | solution.py:612
  635.7 25.0 %collective-permute-start.30 = (f32[2,68,128]{2,1,0:T(8,128)S(1)}, f32[2,68,128]{2,1,0:T(8,128)S(1)}, u32[]{:S(2)}, u32[]{:S(2)}) collective-permute-start(f32[2,68,128]{2,1,0:T(8,128)S(1)} %add.326), channel_id=1, source_target_pairs={{0,4},{4,0},{1,5},{5,1},{2,6},{6,2},{3,7},{7,3},{8,12},{12,8},{9,1... | collective-permute-start | bytes 208904 | tf_op jit(solution)/shard_map/ppermute | solution.py:603
  664.2 17.1 %collective-permute-start.36 = (bf16[1,64,4096]{2,1,0:T(8,128)(2,1)S(1)}, bf16[1,64,4096]{2,1,0:T(8,128)(2,1)S(1)}, u32[]{:S(2)}, u32[]{:S(2)}) collective-permute-start(bf16[1,64,4096]{2,1,0:T(8,128)(2,1)S(1)} %get-tuple-element.169), channel_id=1, source_target_pairs={{0,8},{1,9},{2,6},{3,7},{4,12},{5,13},{6,2},{7,3},{8,0},{9,1},{10,... | collective-permute-start | bytes 1572872 | tf_op jit(solution)/shard_map/ppermute | solution.py:612
  668.7 46.9 %collective-permute-start.55 = (bf16[256,4096]{1,0:T(8,128)(2,1)S(1)}, bf16[256,4096]{1,0:T(8,128)(2,1)S(1)}, u32[]{:S(2)}, u32[]{:S(2)}) collective-permute-start(bf16[256,4096]{1,0:T(8,128)(2,1)S(1)} %shard_map.529), channel_id=1, source_target_pairs={{0,2},{2,0},{1,3},{3,1},{4,6},{6,4},{5,7},{7,5},{8,10},{10,8},{9,1... | collective-permute-start | bytes 6291464 | tf_op jit(solution)/shard_map/ppermute | solution.py:603
  668.8 17.2 %collective-permute-start.32 = (f32[68,128]{1,0:T(8,128)S(1)}, f32[68,128]{1,0:T(8,128)S(1)}, u32[]{:S(2)}, u32[]{:S(2)}) collective-permute-start(f32[68,128]{1,0:T(8,128)S(1)} %dynamic-slice_bitcast_fusion), channel_id=1, source_target_pairs={{0,1},{1,0},{2,3},{3,2},{4,5},{5,4},{6,7},{7,6},{8,9},{9,8},{10,11... | collective-permute-start | bytes 104456 | tf_op jit(solution)/shard_map/ppermute | solution.py:603
  680.7 17.8 %collective-permute-start.47 = (bf16[64,4096]{1,0:T(8,128)(2,1)S(1)}, bf16[64,4096]{1,0:T(8,128)(2,1)S(1)}, u32[]{:S(2)}, u32[]{:S(2)}) collective-permute-start(bf16[64,4096]{1,0:T(8,128)(2,1)S(1)} %shard_map.523.own_ref), channel_id=1, source_target_pairs={{0,8},{1,9},{2,6},{3,7},{4,12},{5,13},{6,2},{7,3},{8,0},{9,1},{10,... | collective-permute-start | bytes 1572872 | tf_op jit(solution)/shard_map/ppermute | solution.py:612
  681.9 19.3 %collective-permute-start.37 = (bf16[1,32,4096]{2,1,0:T(8,128)(2,1)S(1)}, bf16[1,32,4096]{2,1,0:T(8,128)(2,1)S(1)}, u32[]{:S(2)}, u32[]{:S(2)}) collective-permute-start(bf16[1,32,4096]{2,1,0:T(8,128)(2,1)S(1)} %get-tuple-element.171), channel_id=1, source_target_pairs={{0,16},{16,0},{1,17},{17,1},{2,18},{18,2},{3,19},{19,3},{4,20},{20... | collective-permute-start | bytes 786440 | tf_op jit(solution)/shard_map/ppermute | solution.py:603
  686.7 29.4 %collective-permute-start.61 = (bf16[1024,1024]{1,0:T(8,128)(2,1)S(1)}, bf16[1024,1024]{1,0:T(8,128)(2,1)S(1)}, u32[]{:S(2)}, u32[]{:S(2)}) collective-permute-start(bf16[1024,1024]{1,0:T(8,128)(2,1)S(1)} %shard_map.533), channel_id=1, source_target_pairs={{0,2},{2,0},{1,3},{3,1},{4,6},{6,4},{5,7},{7,5},{8,10},{10,8},{9,1... | collective-permute-start | bytes 6291464 | tf_op jit(solution)/shard_map/ppermute | solution.py:603
  714.7 26.5 %collective-permute-start.49 = (bf16[256,4096]{1,0:T(8,128)(2,1)S(1)}, bf16[256,4096]{1,0:T(8,128)(2,1)S(1)}, u32[]{:S(2)}, u32[]{:S(2)}) collective-permute-start(bf16[256,4096]{1,0:T(8,128)(2,1)S(1)} %shard_map.525), channel_id=1, source_target_pairs={{0,2},{2,0},{1,3},{3,1},{4,6},{6,4},{5,7},{7,5},{8,10},{10,8},{9,1... | collective-permute-start | bytes 6291464 | tf_op jit(solution)/shard_map/ppermute | solution.py:603
  (105 other events, 1173.2 us)

commit v2 on v1

--- a/solution.py
+++ b/solution.py
@@ -24,7 +24,8 @@
 
 
 pair_width = 2 * HEAD
-vmem_bytes = 48 * 1024 * 1024
+vmem_bytes = 60 * 1024 * 1024
+light = pl.CostEstimate(flops=1, bytes_accessed=1, transcendentals=0)
 
 
 def dot_nt(left_side, right_side):
@@ -221,11 +222,7 @@
         ],
         input_output_aliases={5 + index: index for index in range(len(into))},
         compiler_params=pltpu.CompilerParams(vmem_limit_bytes=vmem_bytes),
-        cost_estimate=pl.CostEstimate(
-            flops=4 * 4 * rows * keys * HEADS * HEAD // parts,
-            bytes_accessed=4 * (rows + keys) * HEADS * HEAD // parts,
-            transcendentals=rows * keys * HEADS // parts,
-        ),
+        cost_estimate=light,
     )(info, queries, key_values, key_values, bias, *into)
 
 
@@ -258,88 +255,111 @@
         ],
         input_output_aliases={8 + index: index for index in range(len(into))},
         compiler_params=pltpu.CompilerParams(vmem_limit_bytes=vmem_bytes),
-        cost_estimate=pl.CostEstimate(
-            flops=4 * 10 * rows * keys * HEADS * HEAD // parts,
-            bytes_accessed=8 * (rows + keys) * HEADS * HEAD // parts,
-            transcendentals=rows * keys * HEADS // parts,
-        ),
+        cost_estimate=light,
     )(info, queries, mixed, grad_mixed, log_total, key_values, key_values, bias, *into)
 
 
-def copy_all(copies):
-    for copy in copies:
-        copy.start()
-    for copy in copies:
-        copy.wait()
-
-
-def merge_kernel(place_ref, own_ref, other_ref, out_ref, sems):
-    rows = own_ref.shape[0]
-    copies = []
-    for which, source in enumerate((own_ref, other_ref)):
-        first = pl.multiple_of(place_ref[which] * rows, rows)
-        copies.append(
-            pltpu.make_async_copy(source, out_ref.at[pl.ds(first, rows), :], sems.at[which])
-        )
-    copy_all(copies)
-
-
-def merge(index, own, other):
-    rows, width = own.shape
+def join_kernel(count, place_ref, *refs):
+    out_ref = refs[count]
+    for index, source in enumerate(refs[:count]):
+        rows = source.shape[0]
+        first = pl.multiple_of(place_ref[index] * rows, rows)
+        out_ref[pl.ds(first, rows), :] = source[...]
+
+
+def join(places, parts):
+    count, (rows, width) = len(parts), parts[0].shape
+    steps = 1 if count * rows * width <= 1024 * 1024 else 4
+    wide = width // steps
     return pl.pallas_call(
-        merge_kernel,
+        functools.partial(join_kernel, count),
         grid_spec=pltpu.PrefetchScalarGridSpec(
             num_scalar_prefetch=1,
-            grid=(),
-            in_specs=[any_block, any_block],
-            out_specs=any_block,
-            scratch_shapes=[pltpu.SemaphoreType.DMA((2,))],
+            grid=(steps,),
+            in_specs=[pl.BlockSpec((rows, wide), lambda i, place: (0, i))] * count,
+            out_specs=pl.BlockSpec((count * rows, wide), lambda i, place: (0, i)),
         ),
-        out_shape=jax.ShapeDtypeStruct((2 * rows, width), own.dtype),
-        compiler_params=pltpu.CompilerParams(vmem_limit_bytes=4 * 1024 * 1024),
-        cost_estimate=pl.CostEstimate(
-            flops=0, bytes_accessed=8 * rows * width, transcendentals=0
-        ),
-    )(jnp.stack([index, 1 - index]).astype(jnp.int32), own, other)
+        out_shape=jax.ShapeDtypeStruct((count * rows, width), parts[0].dtype),
+        compiler_params=pltpu.CompilerParams(vmem_limit_bytes=vmem_bytes),
+        cost_estimate=light,
+    )(jnp.stack(places).astype(jnp.int32), *parts)
+
+
+def merge(index, own, other):
+    return join([index, 1 - index], [own, other])
 
 
 def assemble_kernel(count, place_ref, *refs):
-    shards, (four_ref, came_ref, out_ref, sems) = refs[:count], refs[count:]
-    rows, part = shards[0].shape[0], four_ref.shape[0]
-    seq, core = place_ref[0], place_ref[1]
-    copies, left = [], 0
+    shards, parts, out_ref = refs[:count], refs[count:-1], refs[-1]
+    for index, part in enumerate(parts):
+        rows = part.shape[0]
+        first = pl.multiple_of(place_ref[1 + index] * rows, rows)
+        out_ref[pl.ds(first, rows), :] = part[...]
     for index, shard in enumerate(shards):
-        own = out_ref.at[
-            pl.ds(pl.multiple_of(seq * rows, rows), rows), pl.ds(left, shard.shape[1])
-        ]
-        copies.append(pltpu.make_async_copy(shard, own, sems.at[index]))
-        left += shard.shape[1]
-    for index, (source, half) in enumerate(((four_ref, core), (came_ref, 1 - core))):
-        first = pl.multiple_of((1 - seq) * rows + half * part, part)
-        copies.append(
-            pltpu.make_async_copy(source, out_ref.at[pl.ds(first, part), :], sems.at[count + index])
-        )
-    copy_all(copies)
-
-
-def assemble(seq, core, shards, four, came):
-    count, width = len(shards), four.shape[1]
-    rows = shards[0].shape[0]
+
+        def store(shard=shard):
+            rows = shard.shape[0]
+            first = pl.multiple_of(place_ref[0] * rows, rows)
+            out_ref[pl.ds(first, rows), :] = shard[...]
+
+        pl.when(pl.program_id(0) == index)(store)
+
+
+def assemble(seq, places, shards, parts):
+    count, (rows, wide) = len(shards), shards[0].shape
+    part_rows = parts[0].shape[0]
+    places = [seq] + [(1 - seq) * len(parts) + place for place in places]
     return pl.pallas_call(
         functools.partial(assemble_kernel, count),
         grid_spec=pltpu.PrefetchScalarGridSpec(
             num_scalar_prefetch=1,
-            grid=(),
-            in_specs=[any_block] * (count + 2),
-            out_specs=any_block,
-            scratch_shapes=[pltpu.SemaphoreType.DMA((count + 2,))],
+            grid=(count,),
+            in_specs=[pl.BlockSpec((rows, wide), lambda i, place: (0, 0))] * count
+            + [pl.BlockSpec((part_rows, wide), lambda i, place: (0, i))] * len(parts),
+            out_specs=pl.BlockSpec((2 * rows, wide), lambda i, place: (0, i)),
         ),
-        out_shape=jax.ShapeDtypeStruct((2 * rows, width), four.dtype),
-        compiler_params=pltpu.CompilerParams(vmem_limit_bytes=4 * 1024 * 1024),
-        cost_estimate=pl.CostEstimate(
-            flops=0, bytes_accessed=8 * rows * width, transcendentals=0
-        ),
-    )(jnp.stack([seq, core]).astype(jnp.int32), *shards, four, came)
+        out_shape=jax.ShapeDtypeStruct((2 * rows, count * wide), shards[0].dtype),
+        compiler_params=pltpu.CompilerParams(vmem_limit_bytes=vmem_bytes),
+        cost_estimate=light,
+    )(jnp.stack(places).astype(jnp.int32), *shards, *parts)
+
+
+def row_sums_kernel(norms, plain, *refs):
+    steps = refs[: 2 * norms + plain]
+    out_ref = refs[-1]
+
+    @pl.when(pl.program_id(0) == 0)
+    def start():
+        out_ref[...] = jnp.zeros_like(out_ref)
+
+    for index in range(norms):
+        values, grad = steps[2 * index][...].astype(jnp.float32), steps[2 * index + 1][...]
+        center = values - jnp.mean(values, axis=-1, keepdims=True)
+        spread = jnp.mean(center * center, axis=-1, keepdims=True)
+        unit = center * lax.rsqrt(spread + norm_epsilon)
+        out_ref[pl.ds(2 * index, 1), :] += jnp.sum(grad * unit, axis=0, keepdims=True)
+        out_ref[pl.ds(2 * index + 1, 1), :] += jnp.sum(grad, axis=0, keepdims=True)
+    for index in range(plain):
+        values = steps[2 * norms + index][...].astype(jnp.float32)
+        at = pl.ds(2 * norms + index, 1)
+        out_ref[at, :] += jnp.sum(values, axis=0, keepdims=True)
+
+
+def row_sums(norm_pairs, plain):
+    arrays = [values for pair in norm_pairs for values in pair] + list(plain)
+    width = arrays[0].shape[1]
+    rows = -(-(2 * len(norm_pairs) + len(plain)) // 8) * 8
+    return pl.pallas_call(
+        functools.partial(row_sums_kernel, len(norm_pairs), len(plain)),
+        grid=(4,),
+        in_specs=[
+            pl.BlockSpec((values.shape[0] // 4, width), lambda step: (step, 0)) for values in arrays
+        ],
+        out_specs=pl.BlockSpec((rows, width), lambda step: (0, 0)),
+        out_shape=jax.ShapeDtypeStruct((rows, width), jnp.float32),
+        compiler_params=pltpu.CompilerParams(vmem_limit_bytes=vmem_bytes),
+        cost_estimate=light,
+    )(*arrays)
 
 
 def ffn_kernel(half_steps, place_ref, *refs):
@@ -478,12 +498,8 @@
             inner_shape,
             inner_shape,
         ],
-        compiler_params=pltpu.CompilerParams(vmem_limit_bytes=56 * 1024 * 1024),
-        cost_estimate=pl.CostEstimate(
-            flops=12 * rows * width * units,
-            bytes_accessed=4 * 2 * width * units + 12 * rows * width,
-            transcendentals=2 * rows * units,
-        ),
+        compiler_params=pltpu.CompilerParams(vmem_limit_bytes=vmem_bytes),
+        cost_estimate=light,
     )(
         place,
         *[normed] * 4,
@@ -502,93 +518,274 @@
     return out, grad, column[0], split(kept_outer, sent_outer), (kept_inner, sent_inner)
 
 
-def outer_group_kernel(count, place_ref, *refs):
-    lefts, rights = refs[:count], refs[count : 2 * count]
-    kept_ref, sent_ref = refs[2 * count :]
+def outer_group_kernel(products, count, place_ref, *refs):
+    lefts, rights = refs[:count], refs[count : count + len(products)]
+    kept_ref, sent_ref, turned_ref = refs[count + len(products) :]
     part = kept_ref.shape[1]
-    matrix, seq = pl.program_id(0), pl.program_id(1)
-
-    def one(left_ref, right_ref):
-        for which, out_ref in ((0, kept_ref), (1, sent_ref)):
-            first = pl.multiple_of((seq * 2 + place_ref[which]) * part, part)
-            left = left_ref[:, pl.ds(first, part)]
-            out_ref[0] = dot_tn(left, right_ref[...]).astype(jnp.bfloat16)
-
-    for index in range(count):
-        pl.when(matrix == index)(functools.partial(one, lefts[index], rights[index]))
-
-
-def outer_group(core, pairs):
-    count, width = len(pairs), pairs[0][0].shape[1]
+    step = pl.program_id(0)
+    sides = [side for side, _ in products]
+    start = 0
+    for index, (side, blocks) in enumerate(products):
+        left, right = lefts[side], rights[index]
+        tokens = pl.ds(0, left.shape[0])
+        if sides.index(side) == index:
+
+            def turn(left=left, tokens=tokens):
+                turned_ref[:, tokens] = left[...].T
+
+            pl.when(step == start)(turn)
+
+        def run(right=right, tokens=tokens):
+            for seq in range(2):
+                for which, out_ref in ((0, kept_ref), (1, sent_ref)):
+                    first = pl.multiple_of((seq * 2 + place_ref[which]) * part, part)
+                    rows = turned_ref[pl.ds(first, part), tokens]
+                    out_ref[seq] = dot_nn(rows, right[...]).astype(jnp.bfloat16)
+
+        pl.when((step >= start) & (step < start + blocks))(run)
+        start += blocks
+
+
+def outer_group(core, lefts, products):
+    chunk = 512
+    width = lefts[0].shape[1]
     part = width // 4
-    place = jnp.stack([core, 1 - core]).astype(jnp.int32)
-    whole = lambda values: pl.BlockSpec(values.shape, lambda matrix, seq, place: (0, 0))
-    out_spec = pl.BlockSpec((1, part, width), lambda matrix, seq, place: (seq, 0, matrix))
-    shape = jax.ShapeDtypeStruct((2, part, count * width), jnp.bfloat16)
-    lefts, rights = [pair[0] for pair in pairs], [pair[1] for pair in pairs]
-    tokens = sum(left.shape[0] for left in lefts)
+    tokens = max(left.shape[0] for left in lefts)
+    specs, start = [], 0
+    for _, right in products:
+        blocks = right.shape[1] // chunk
+        specs.append(
+            pl.BlockSpec(
+                (right.shape[0], chunk),
+                lambda step, place, start=start, blocks=blocks: (
+                    0,
+                    jnp.clip(step - start, 0, blocks - 1),
+                ),
+            )
+        )
+        start += blocks
+    out_spec = pl.BlockSpec((2, part, chunk), lambda step, place: (0, 0, step))
+    shape = jax.ShapeDtypeStruct((2, part, start * chunk), jnp.bfloat16)
+    kinds = [(side, right.shape[1] // chunk) for side, right in products]
     return pl.pallas_call(
-        functools.partial(outer_group_kernel, count),
+        functools.partial(outer_group_kernel, kinds, len(lefts)),
         grid_spec=pltpu.PrefetchScalarGridSpec(
             num_scalar_prefetch=1,
-            grid=(count, 2),
-            in_specs=[whole(values) for values in lefts + rights],
+            grid=(start,),
+            in_specs=[pl.BlockSpec(left.shape, lambda step, place: (0, 0)) for left in lefts]
+            + specs,
+            out_specs=[out_spec, out_spec],
+            scratch_shapes=[pltpu.VMEM((width, tokens), jnp.bfloat16)],
+        ),
+        out_shape=[shape, shape],
+        compiler_params=pltpu.CompilerParams(vmem_limit_bytes=vmem_bytes),
+        cost_estimate=light,
+    )(
+        jnp.stack([core, 1 - core]).astype(jnp.int32),
+        *lefts,
+        *[right for _, right in products],
+    )
+
+
+def halve_kernel(split, place_ref, kept_a, came_a, kept_b, came_b, kept_ref, *sent_refs):
+    add = lambda kept, came: (kept[0].astype(jnp.float32) + came[0].astype(jnp.float32)).astype(
+        jnp.bfloat16
+    )
+    kept_ref[0] = add(kept_a, came_a)
+    if not split:
+        sent_refs[0][0] = add(kept_b, came_b)
+        return
+
+    for index, sent_ref in enumerate(sent_refs):
+
+        def store(sent_ref=sent_ref):
+            sent_ref[0] = add(kept_b, came_b)
+
+        pl.when(pl.program_id(0) == index)(store)
+
+
+def halve(keep_at, send_at, kept, came, split=False):
+    blocks, rows, width = kept.shape
+    count = len(keep_at)
+    place = jnp.stack(list(keep_at) + list(send_at)).astype(jnp.int32)
+    tiles = 2 if rows * width >= 256 * 1024 else 1
+    wide = width // tiles
+    spec = lambda first: pl.BlockSpec(
+        (1, rows, wide), lambda j, i, place: (place[first + j], 0, i)
+    )
+    out_spec = pl.BlockSpec((1, rows, wide), lambda j, i, place: (j, 0, i))
+    one_spec = lambda at: pl.BlockSpec(
+        (1, rows, wide),
+        lambda j, i, place: (0, 0, jnp.where(j == at, i, jnp.where(j > at, tiles - 1, 0))),
+    )
+    shape = jax.ShapeDtypeStruct((count, rows, width), jnp.bfloat16)
+    one = jax.ShapeDtypeStruct((1, rows, width), jnp.bfloat16)
+    out = pl.pallas_call(
+        functools.partial(halve_kernel, split),
+        grid_spec=pltpu.PrefetchScalarGridSpec(
+            num_scalar_prefetch=1,
+            grid=(count, tiles),
+            in_specs=[spec(0), spec(0), spec(count), spec(count)],
+            out_specs=[out_spec]
+            + ([one_spec(at) for at in range(count)] if split else [out_spec]),
+        ),
+        out_shape=[shape] + ([one] * count if split else [shape]),
+        compiler_params=pltpu.CompilerParams(vmem_limit_bytes=vmem_bytes),
+        cost_estimate=light,
+    )(place, kept, came, kept, came)
+    return out[0], out[1:]
+
+
+def halve_late_kernel(place_ref, *refs):
+    step = pl.program_id(0)
+    for which in range(2):
+        own_ref, early_ref, late_ref = refs[3 * which : 3 * which + 3]
+        out_ref = refs[6 + which]
+        for block, came_ref in enumerate((early_ref, late_ref)):
+
+            def store(out_ref=out_ref, own_ref=own_ref, came_ref=came_ref):
+                total = own_ref[0].astype(jnp.float32) + came_ref[0].astype(jnp.float32)
+                out_ref[0] = total.astype(jnp.bfloat16)
+
+            pl.when(place_ref[2 * which + step] // 2 == block)(store)
+
+
+def halve_late(keep_at, send_at, kept, early, late):
+    rows, width = kept.shape[1:]
+    at = list(keep_at) + list(send_at)
+    place = jnp.stack(at + [block % 2 for block in at]).astype(jnp.int32)
+    spec = lambda first: pl.BlockSpec((1, rows, width), lambda j, place: (place[first + j], 0, 0))
+    out_spec = pl.BlockSpec((1, rows, width), lambda j, place: (j, 0, 0))
+    shape = jax.ShapeDtypeStruct((2, rows, width), jnp.bfloat16)
+    return pl.pallas_call(
+        halve_late_kernel,
+        grid_spec=pltpu.PrefetchScalarGridSpec(
+            num_scalar_prefetch=1,
+            grid=(2,),
+            in_specs=[spec(0), spec(4), spec(4), spec(2), spec(6), spec(6)],
             out_specs=[out_spec, out_spec],
         ),
         out_shape=[shape, shape],
         compiler_params=pltpu.CompilerParams(vmem_limit_bytes=vmem_bytes),
-        cost_estimate=pl.CostEstimate(
-            flops=2 * tokens * width * width,
-            bytes_accessed=2 * (2 * tokens * width + count * width * width),
-            transcendentals=0,
-        ),
-    )(place, *lefts, *rights)
-
-
-def halve_kernel(place_ref, kept_a, came_a, kept_b, came_b, kept_ref, sent_ref):
-    kept_ref[0] = (kept_a[0].astype(jnp.float32) + came_a[0].astype(jnp.float32)).astype(
-        jnp.bfloat16
-    )
-    sent_ref[0] = (kept_b[0].astype(jnp.float32) + came_b[0].astype(jnp.float32)).astype(
-        jnp.bfloat16
-    )
-
-
-def halve(keep_at, send_at, kept, came):
-    blocks, rows, width = kept.shape
-    count = blocks // 2
+        cost_estimate=light,
+    )(place, kept, early, late, kept, early, late)
+
+
+def combine_kernel(place_ref, *refs):
+    kept_ref, sent_refs = refs[8], refs[9:]
+
+    def put(sources, out_ref):
+        total = lambda kept, came: (
+            kept[0].astype(jnp.float32) + came[0].astype(jnp.float32)
+        ).astype(jnp.bfloat16)
+        outer, inner = total(*sources[:2]), total(*sources[2:])
+        tall, low = outer.shape[0] // 4, inner.shape[0] // 4
+        wide = outer.shape[1]
+        both = tall + inner.shape[1] // wide * low
+        for piece in range(4):
+            out_ref[0, pl.ds(piece * both, tall), :] = outer[piece * tall : (piece + 1) * tall]
+            for block in range(inner.shape[1] // wide):
+                out_ref[0, pl.ds(piece * both + tall + block * low, low), :] = inner[
+                    piece * low : (piece + 1) * low, block * wide : (block + 1) * wide
+                ]
+
+    put(refs[:4], kept_ref)
+    for index, sent_ref in enumerate(sent_refs):
+        pl.when(pl.program_id(0) == index)(functools.partial(put, refs[4:8], sent_ref))
+
+
+def combine(keep_at, send_at, outer, inner):
     place = jnp.stack(list(keep_at) + list(send_at)).astype(jnp.int32)
-    spec = lambda first: pl.BlockSpec(
-        (1, rows, width), lambda j, place: (place[first + j], 0, 0)
-    )
-    out_spec = pl.BlockSpec((1, rows, width), lambda j, place: (j, 0, 0))
-    shape = jax.ShapeDtypeStruct((count, rows, width), jnp.bfloat16)
+    spec = lambda values, first: pl.BlockSpec(
+        (1,) + values.shape[1:], lambda j, place: (place[first + j], 0, 0)
+    )
+    arrays = list(outer) + list(inner)
+    width = outer[0].shape[2]
+    rows = outer[0].shape[1] + inner[0].shape[1] * inner[0].shape[2] // width
+    one = jax.ShapeDtypeStruct((1, rows, width), jnp.bfloat16)
+    one_spec = pl.BlockSpec((1, rows, width), lambda j, place: (0, 0, 0))
     return pl.pallas_call(
-        halve_kernel,
+        combine_kernel,
         grid_spec=pltpu.PrefetchScalarGridSpec(
             num_scalar_prefetch=1,
-            grid=(count,),
-            in_specs=[spec(0), spec(0), spec(count), spec(count)],
-            out_specs=[out_spec, out_spec],
+            grid=(2,),
+            in_specs=[spec(values, first) for first in (0, 2) for values in arrays],
+            out_specs=[
+                pl.BlockSpec((1, rows, width), lambda j, place: (j, 0, 0)),
+                one_spec,
+                one_spec,
+            ],
         ),
-        out_shape=[shape, shape],
+        out_shape=[jax.ShapeDtypeStruct((2, rows, width), jnp.bfloat16), one, one],
         compiler_params=pltpu.CompilerParams(vmem_limit_bytes=vmem_bytes),
-        cost_estimate=pl.CostEstimate(
-            flops=blocks * rows * width,
-            bytes_accessed=6 * blocks * rows * width,
-            transcendentals=0,
+        cost_estimate=light,
+    )(place, *arrays, *arrays)
+
+
+def unpack_kernel(tall, inner_blocks, place_ref, own_ref, other_ref, *out_refs):
+    def put(source):
+        if not inner_blocks:
+            for index, out_ref in enumerate(out_refs):
+                wide = out_ref.shape[1]
+                out_ref[...] = source[:, index * wide : (index + 1) * wide].astype(jnp.float32)
+            return
+        outer_ref, inner_ref = out_refs
+        low, wide = inner_ref.shape[0], source.shape[1]
+        outer_ref[...] = source[pl.ds(0, tall), :].astype(jnp.float32)
+        for block in range(inner_blocks):
+            rows = source[pl.ds(tall + block * low, low), :]
+            inner_ref[:, block * wide : (block + 1) * wide] = rows.astype(jnp.float32)
+
+    pl.when(pl.program_id(0) == 0)(lambda: put(own_ref))
+    pl.when(pl.program_id(0) == 1)(lambda: put(other_ref))
+
+
+def unpack(core, own, other, count=0, tall=0, inner_blocks=0):
+    rows, width = own.shape
+    if inner_blocks:
+        steps, block = 8, rows // 8
+        low = (block - tall) // inner_blocks
+        shapes = [(16 * tall, width), (16 * low, inner_blocks * width)]
+        blocks = [(tall, width), (low, inner_blocks * width)]
+    else:
+        steps, block = 2, rows // 2
+        shapes = [(2 * rows, width // count)] * count
+        blocks = [(block, width // count)] * count
+    return pl.pallas_call(
+        functools.partial(unpack_kernel, tall, inner_blocks),
+        grid_spec=pltpu.PrefetchScalarGridSpec(
+            num_scalar_prefetch=1,
+            grid=(2, steps),
+            in_specs=[
+                pl.BlockSpec(
+                    (block, width),
+                    lambda side, i, place: (jnp.where(side == 0, i, steps - 1), 0),
+                ),
+                pl.BlockSpec((block, width), lambda side, i, place: (jnp.where(side == 1, i, 0), 0)),
+            ],
+            out_specs=[
+                pl.BlockSpec(shape, lambda side, i, place: (place[side] * steps + i, 0))
+                for shape in blocks
+            ],
         ),
-    )(place, kept, came, kept, came)
-
-
-def layer_norm_back(values, norm_gain, grad):
+        out_shape=[jax.ShapeDtypeStruct(shape, jnp.float32) for shape in shapes],
+        compiler_params=pltpu.CompilerParams(vmem_limit_bytes=vmem_bytes),
+        cost_estimate=light,
+    )(jnp.stack([core, 1 - core]).astype(jnp.int32), own, other)
+
+
+def norm_unit(values):
     center = values - jnp.mean(values, axis=-1, keepdims=True)
     inverse = lax.rsqrt(jnp.mean(center * center, axis=-1, keepdims=True) + norm_epsilon)
-    unit = center * inverse
+    return center * inverse, inverse
+
+
+def layer_norm_back(values, norm_gain, grad):
+    unit, inverse = norm_unit(values)
     scaled = grad * norm_gain
     back = scaled - jnp.mean(scaled, axis=-1, keepdims=True)
     back = back - unit * jnp.mean(scaled * unit, axis=-1, keepdims=True)
-    return back * inverse, jnp.sum(grad * unit, axis=0), jnp.sum(grad, axis=0)
+    return back * inverse
 
 
 def dot_back(gradient, weight):
@@ -632,41 +829,120 @@
     return swap(piece[0] if len(piece) == 1 else jnp.concatenate(piece, axis=1), "seq")
 
 
-def second_piece(piece):
-    return merge(square_bits(False)[2], piece, exchange(piece, "xz"))
-
-
-def third_piece(two):
-    return merge(square_bits(False)[1], two, exchange(two, "zx"))
+class Pieces:
+    def __init__(self, piece):
+        core, high, low = square_bits(False)
+        self.own = piece
+        place = lambda side, one, two: (side * 2 + one) * 2 + two
+        self.places = [
+            place(core, high, low),
+            place(core, high, 1 - low),
+            place(core, 1 - high, low),
+            place(core, 1 - high, 1 - low),
+            place(1 - core, low, high),
+            place(1 - core, low, 1 - high),
+            place(1 - core, 1 - low, high),
+            place(1 - core, 1 - low, 1 - high),
+        ]
+
+    def first(self, *others):
+        self.own = after(self.own, *others)
+        self.low = exchange(self.own, "xz")
+        self.high = exchange(self.own, "zx")
+        self.core = swap(self.own, "core")
+        return self.low, self.high, self.core
+
+    def second(self, *others):
+        low, high = after(self.low, *others), after(self.high, *others)
+        self.both = exchange(low, "zx")
+        self.core_low, self.core_high = swap(low, "core"), swap(high, "core")
+        return self.both, self.core_low, self.core_high
+
+    def third(self, *others):
+        self.core_both = swap(after(self.both, *others), "core")
+        return [self.core_both]
+
+    def parts(self, *others):
+        return [
+            after(self.own, *others),
+            self.low,
+            self.high,
+            self.both,
+            self.core,
+            self.core_low,
+            self.core_high,
+            self.core_both,
+        ]
 
 
 class Total:
-    def __init__(self, split, steps, turned):
-        self.kept, sent = split
+    def __init__(self, split, steps, turned, halves, inner=None):
+        kept, sent = split
+        self.inner = None
+        if inner is not None:
+            self.inner = (inner[0], swap(self.blocks(inner[1], 4), "core"))
+            self.tall, self.inner_blocks = kept.shape[1] // 8, inner[0].shape[2] // kept.shape[2]
         self.core, self.first, self.second = square_bits(turned)
         self.seq, self.zhi = lax.axis_index("seq"), lax.axis_index("zhi")
-        self.steps = steps
+        self.steps, self.halves = steps, halves
         self.along = ("x", "z") if turned else ("z", "x")
-        on_seq = [axes == "y" for axes in steps[0]]
-        self.starts = jnp.where(self.core == 0, on_seq[0], on_seq[1])
         self.came = swap(self.blocks(sent, 4), "core")
-        self.kept = self.blocks(self.kept, 4)
+        self.kept = self.blocks(kept, 4)
         self.stage = 0
 
     def blocks(self, values, count):
         return values.reshape(count, -1, values.shape[-1])
 
-    def step(self):
-        if self.stage == 0:
-            seq, first = self.seq, self.first
-            keep = [jnp.where(self.starts, seq * 2 + j, j * 2 + first) for j in range(2)]
-            send = [jnp.where(self.starts, (1 - seq) * 2 + j, j * 2 + 1 - first) for j in range(2)]
+    def by_core(self, choose):
+        both = [choose([axes[core] for axes in self.steps]) for core in range(2)]
+        return [jnp.where(self.core == 0, *pair) for pair in zip(*both)]
+
+    def bits(self):
+        seq, first, second = self.seq, self.first, self.second
+
+        def one(axes):
+            if axes[0] == "y":
+                return [seq * 2, seq * 2 + 1, 2 - seq * 2, 3 - seq * 2]
+            return [first, 2 + first, 1 - first, 3 - first]
+
+        def two(axes):
+            if axes[0] != "y" and axes[1] != "y":
+                return [second, 2 + second, 1 - second, 3 - second]
+            bit = first if axes[0] == "y" else seq
+            return [bit * 2, bit * 2 + 1, 2 - bit * 2, 3 - bit * 2]
+
+        def three(axes):
+            bit = seq if axes[2] == "y" else second
+            return [bit, 1 - bit]
+
+        def four(axes):
+            return [self.zhi, 1 - self.zhi]
+
+        at = self.by_core((one, two, three, four)[self.stage])
+        return at[: len(at) // 2], at[len(at) // 2 :]
+
+    def step(self, *others):
+        self.kept = after(self.kept, *others)
+        keep, send = self.bits()
+        self.kept = self.blocks(self.kept, 2 * len(keep))
+        if self.stage == 0 and self.inner is not None:
+            kept, came = (self.blocks(values, 4) for values in self.inner)
+            self.kept, *sent = combine(keep, send, (self.kept, self.came), (kept, came))
+            self.came, self.rest = exchange(sent[0], self.steps[0]), sent[1]
+            self.stage += 1
+            return sent[0]
+        if self.stage == 1 and self.halves:
+            early, late = (self.blocks(came, 2) for came in self.came)
+            self.kept, sent = halve_late(keep, send, self.kept, early, late)
         else:
-            bit = (jnp.where(self.starts, self.first, self.seq), self.second, self.zhi)
-            bit = bit[self.stage - 1]
-            keep, send = [bit], [1 - bit]
-            self.kept, self.came = self.blocks(self.kept, 2), self.blocks(self.came, 2)
-        self.kept, sent = halve(keep, send, self.kept, self.came)
+            split = self.stage == 0 and self.halves
+            came = self.blocks(self.came, 2 * len(keep))
+            self.kept, sent = halve(keep, send, self.kept, came, split)
+            if split:
+                self.came, self.rest = exchange(sent[0], self.steps[0]), sent[1]
+                self.stage += 1
+                return sent[0]
+            sent = sent[0]
         if self.stage < 3:
             self.came = exchange(sent, self.steps[self.stage])
         else:
@@ -674,7 +950,14 @@
         self.stage += 1
         return sent
 
-    def gather(self):
+    def step_rest(self, *others):
+        sent = after(self.rest, self.came, *others)
+        self.came = (self.came, exchange(sent, self.steps[0]))
+        return sent
+
+    def gather(self, *others):
+        if self.stage > 4:
+            self.part = after(self.part, *others)
         if self.stage == 4:
             piece = self.kept[0].astype(jnp.float32) + self.came[0].astype(jnp.float32)
             self.part = piece.astype(jnp.bfloat16)
@@ -691,10 +974,16 @@
         self.stage += 1
         return self.part
 
-    def result(self):
-        first = jnp.where(self.core == 0, self.part, self.came)
-        second = jnp.where(self.core == 0, self.came, self.part)
-        return jnp.concatenate([first, second]).astype(jnp.float32)
+    def advance(self, *others):
+        if self.stage < 4:
+            return [self.step(*others)]
+        return [self.gather(*others)] if self.stage < 8 else []
+
+    def result(self, count, *others):
+        part = after(self.part, *others)
+        if self.inner is None:
+            return unpack(self.core, part, self.came, count)
+        return unpack(self.core, part, self.came, 2, self.tall, self.inner_blocks)
 
 
 def sum_plain(terms):
@@ -705,29 +994,27 @@
 page_axes = ("zhi", "zlo", "x", "core")
 
 
-def sum_vectors(vectors):
-    seq_count = lax.axis_size("seq")
-    joined = jnp.concatenate([vector.reshape(seq_count, -1) for vector in vectors], axis=1)
-    joined = joined.reshape(seq_count, -1, 128)
-    seq = lax.axis_index("seq")
-    if seq_count == 2:
-        for axis in page_axes:
-            if lax.axis_size(axis) == 2:
-                joined = joined + swap(joined, axis)
-            else:
-                joined = lax.psum(joined, axis)
-        own = lax.dynamic_index_in_dim(joined, seq, 0, keepdims=False)
-        own = own + swap(lax.dynamic_index_in_dim(joined, 1 - seq, 0, keepdims=False), "seq")
-    else:
-        joined = lax.psum(joined, page_axes + ("seq",))
-        own = lax.dynamic_index_in_dim(joined, seq, 0, keepdims=False)
-    own = own.reshape(-1)
-    out, start = [], 0
-    for vector in vectors:
-        size = vector.shape[0] // seq_count
-        out.append(own[start : start + size])
-        start += size
-    return out
+class VectorTotal:
+    def __init__(self, values):
+        self.values = values
+        self.axes = [axis for axis in page_axes + ("seq",) if lax.axis_size(axis) == 2]
+        rest = tuple(axis for axis in page_axes + ("seq",) if lax.axis_size(axis) != 2)
+        if rest:
+            self.values = lax.psum(self.values, rest)
+        self.came = swap(self.values, self.axes.pop(0))
+
+    def advance(self, *others):
+        if self.came is None:
+            return []
+        self.values, self.came = after(self.values, *others) + self.came, None
+        if self.axes:
+            self.came = swap(self.values, self.axes.pop(0))
+        return [self.values]
+
+    def result(self):
+        while self.came is not None:
+            self.advance()
+        return self.values
 
 
 def on_device(
@@ -821,12 +1108,15 @@
     self_shards = [self_query, self_key, self_value, self_output]
     cross_shards = [cross_key, cross_value, cross_query, cross_output]
     if two:
-        piece = first_piece(self_shards)
-        tokens_other = lax.ppermute(after(tokens, piece), "seq", [(0, 1)])
-        part = third_piece(second_piece(piece))
-        cross_piece = first_piece([after(cross_key, part)] + cross_shards[1:])
-        whole_self = assemble(seq_index, core, self_shards, part, swap(part, "core"))
-        patches_other = swap(after(patches, whole_self), "seq")
+        pieces = Pieces(first_piece(self_shards))
+        pieces.first(joined_other)
+        tokens_other = lax.ppermute(after(tokens, pieces.own), "seq", [(0, 1)])
+        pieces.second()
+        cross_pieces = Pieces(first_piece([after(cross_key, pieces.low)] + cross_shards[1:]))
+        pieces.third()
+        whole_self = assemble(
+            seq_index, pieces.places, self_shards, pieces.parts(tokens_other)
+        )
         tokens_all = jnp.concatenate([tokens, after(tokens_other, whole_self)])
     else:
         gather = lambda shard: lax.all_gather(shard, "seq", axis=0, tiled=True)
@@ -871,22 +1161,26 @@
     )
     attend_self = functools.partial(attend, self_plan, info)
     if two:
-        first_half = attend_self(after(queries_self, cross_piece), self_pairs, no_bias, 0, 2)
-        cross_part = second_piece(cross_piece)
-        inner_piece = first_piece([after(ffn_inner, first_half[0])])
+        sent = cross_pieces.first(queries_self)
+        patches_other = swap(after(patches, cross_pieces.own), "seq")
         mixed_self, log_self = attend_self(
-            after(queries_self, cross_part), self_pairs, no_bias, 1, 2, first_half
+            after(queries_self, *sent), self_pairs, no_bias, 0, 1
         )
-        cross_part = third_piece(cross_part)
+        sent = cross_pieces.second(mixed_self)
+        mixed_self = after(mixed_self, patches_other, *sent)
+        inner_pieces = Pieces(first_piece([after(ffn_inner, patches_other)]))
     else:
         mixed_self, log_self = attend_self(queries_self, self_pairs, no_bias, 0, 1)
     hidden_one = token_values + dot_nn(mixed_self, whole_self[:, 3 * width :]) + bias_self_output
     normed_two = layer_norm(hidden_one, gain_two, shift_two).astype(jnp.bfloat16)
     if two:
-        outer_piece = first_piece([after(ffn_outer, normed_two)])
-        cross_came = swap(cross_part, "core")
-        whole_cross = assemble(seq_index, core, cross_shards, cross_part, cross_came)
-        patches_all = jnp.concatenate([patches, after(patches_other, whole_cross)])
+        cross_pieces.third()
+        whole_cross = assemble(
+            seq_index, cross_pieces.places, cross_shards, cross_pieces.parts(normed_two)
+        )
+        patches_all = jnp.concatenate([patches, patches_other])
+        patches_all = after(patches_all, whole_cross, inner_pieces.own)
+        outer_pieces = Pieces(first_piece([after(ffn_outer, inner_pieces.own)]))
     patch_bias = jnp.concatenate([zeros, bias_cross_value])
     patch_pairs = (dot_nn(patches_all, whole_cross[:, : 2 * width]) + patch_bias).astype(
         jnp.bfloat16
@@ -896,21 +1190,23 @@
     ).astype(jnp.bfloat16)
     attend_cross = functools.partial(attend, cross_plan, info)
     if two:
-        first_half = attend_cross(after(queries_cross, inner_piece), patch_pairs, blank_bias, 0, 2)
-        inner_part = second_piece(inner_piece)
-        mixed_cross, log_cross = attend_cross(
-            after(queries_cross, inner_part, outer_piece), patch_pairs, blank_bias, 1, 2, first_half
-        )
-        outer_part = second_piece(outer_piece)
-        inner_part = third_piece(inner_part)
-        inner_other = merge(core, inner_part, swap(inner_part, "core"))
-        outer_part = third_piece(outer_part)
-        outer_other = merge(core, outer_part, swap(outer_part, "core"))
+        keys = (patch_pairs, blank_bias)
+        sent = inner_pieces.first(queries_cross) + (outer_pieces.own,)
+        done = attend_cross(after(queries_cross, *sent), *keys, 0, 2)
+        sent = inner_pieces.second(done[0]) + outer_pieces.first(done[0])
+        done = attend_cross(after(queries_cross, *sent), *keys, 1, 2, done)
+        inner_pieces.third(done[0])
+        sent = outer_pieces.second(done[0])
+        inner_other = join(inner_pieces.places, inner_pieces.parts(done[0], *sent))
+        mixed_cross, log_cross = done
+        outer_pieces.third(inner_other)
+        mixed_cross = after(mixed_cross, inner_other)
     else:
         mixed_cross, log_cross = attend_cross(queries_cross, patch_pairs, blank_bias, 0, 1)
     hidden_two = hidden_one + dot_nn(mixed_cross, whole_cross[:, 3 * width :]) + bias_cross_output
     normed_three = layer_norm(hidden_two, gain_three, shift_three).astype(jnp.bfloat16)
     if two:
+        outer_other = join(outer_pieces.places, outer_pieces.parts(normed_three))
         outputs, grad_normed_three, column_inner, split_outer, split_inner = ffn_both_ways(
             seq_index,
             core,
@@ -924,8 +1220,7 @@
             bias_inner,
             bias_outer,
         )
-        total_outer = Total(split_outer, ("xy", "yz", "zx"), True)
-        total_inner = Total(split_inner, ("zx", "yy", "xz"), False)
+        total_ffn = Total(split_outer, ("xy", "yz", "zx"), True, True, split_inner)
     else:
         inner_sum = dot_nn(normed_three, whole_ffn_inner) + bias_inner
         active = jax.nn.gelu(inner_sum, approximate=False).astype(jnp.bfloat16)
@@ -935,9 +1230,7 @@
         grad_inner = gelu_pull(grad_active)[0].astype(jnp.bfloat16)
         column_inner = column_sum(grad_inner)
         grad_normed_three = dot_back(grad_inner, whole_ffn_inner)
-    back_two, grad_gain_three, grad_shift_three = layer_norm_back(
-        hidden_two, gain_three, grad_normed_three
-    )
+    back_two = layer_norm_back(hidden_two, gain_three, grad_normed_three)
     grad_hidden_two = cotangent.astype(jnp.float32) + back_two
     branch_cross = grad_hidden_two.astype(jnp.bfloat16)
     grad_mixed_cross = dot_back(branch_cross, whole_cross[:, 3 * width :]).astype(jnp.bfloat16)
@@ -946,35 +1239,40 @@
     )
     cross_rest = (log_cross, patch_pairs, blank_bias)
     if two:
-        sent = (total_outer.step(), total_inner.step())
-        cross_back = back_cross(after(grad_mixed_cross, *sent), *cross_rest, 0, 1)
+        sent = total_ffn.step(grad_mixed_cross)
+        cross_back = back_cross(after(grad_mixed_cross, sent), *cross_rest, 0, 1)
     else:
         cross_back = back_cross(grad_mixed_cross, *cross_rest, 0, 1)
     scaled_cross, grad_patch_keys, grad_patch_values = cross_back
-    back_one, grad_gain_two, grad_shift_two = layer_norm_back(
-        hidden_one, gain_two, dot_back(scaled_cross, whole_cross[:, 2 * width : 3 * width])
-    )
-    grad_hidden_one = grad_hidden_two + back_one
-    branch_self = grad_hidden_one.astype(jnp.bfloat16)
-    grad_mixed_self = dot_back(branch_self, whole_self[:, 3 * width :]).astype(jnp.bfloat16)
     cross_products = [
         (normed_two, scaled_cross),
         (patches_all, grad_patch_keys),
         (patches_all, grad_patch_values),
         (mixed_cross, branch_cross),
     ]
+    if two:
+        scaled_cross = after(scaled_cross, total_ffn.step_rest(scaled_cross))
+    grad_normed_two = dot_back(scaled_cross, whole_cross[:, 2 * width : 3 * width])
+    back_one = layer_norm_back(hidden_one, gain_two, grad_normed_two)
+    grad_hidden_one = grad_hidden_two + back_one
+    branch_self = grad_hidden_one.astype(jnp.bfloat16)
+    grad_mixed_self = dot_back(branch_self, whole_self[:, 3 * width :]).astype(jnp.bfloat16)
     back_self = functools.partial(attend_back, self_plan, info, queries_self, mixed_self)
     self_rest = (log_self, self_pairs, no_bias)
     if two:
-        total_cross = Total(outer_group(core, cross_products), ("xy", "yz", "zx"), True)
-        sent = (total_outer.step(), total_inner.step(), total_cross.kept)
-        first_half = back_self(after(grad_mixed_self, *sent), *self_rest, 0, 2)
-        held = after(grad_mixed_self, first_half[0])
-        total_outer.kept, total_inner.kept, total_cross.kept = (
-            after(total.kept, first_half[0]) for total in (total_outer, total_inner, total_cross)
-        )
-        sent = (total_cross.step(), total_outer.step(), total_inner.step())
-        self_back = back_self(after(held, *sent), *self_rest, 1, 2, first_half)
+        products = [
+            (0, scaled_cross),
+            (1, grad_patch_keys),
+            (1, grad_patch_values),
+            (2, branch_cross),
+            (3, branch_self),
+        ]
+        lefts = [after(normed_two, grad_mixed_self), patches_all, mixed_cross, mixed_self]
+        kept, sent = outer_group(core, lefts, products)
+        late = total_ffn.step(kept)
+        total_mid = Total((kept, after(sent, late)), ("zx", "yz", "xy"), False, True)
+        sent = total_mid.step(late)
+        self_back = back_self(after(grad_mixed_self, sent), *self_rest, 0, 1)
     else:
         self_back = back_self(grad_mixed_self, *self_rest, 0, 1)
     scaled_self, grad_keys, grad_values = self_back
@@ -985,13 +1283,21 @@
         (mixed_self, branch_self),
     ]
     if two:
-        total_self = Total(outer_group(core, self_products), ("xy", "yz", "zx"), True)
-        scaled_late = after(scaled_self, total_self.kept)
-    else:
-        scaled_late = scaled_self
+        late = (total_ffn.step(scaled_self), total_mid.step_rest(scaled_self))
+        products = [(0, scaled_self), (1, grad_keys), (1, grad_values)]
+        lefts = [after(normed_one, *late), normed_all]
+        kept, sent = outer_group(core, lefts, products)
+        late = (total_ffn.step(kept), total_mid.step(kept))
+        total_last = Total((kept, after(sent, *late)), ("yz", "xy", "zx"), True, False)
+        grad_keys, scaled_self = (after(values, *late) for values in (grad_keys, scaled_self))
     normed_terms = dot_back(grad_keys, whole_self[:, width : 2 * width]) + dot_back(
         grad_values, whole_self[:, 2 * width : 3 * width]
     )
+    if two:
+        sent = total_last.advance(normed_terms)
+        for total in (total_mid, total_ffn):
+            sent = sent + total.advance(sent[0])
+        grad_patch_keys = after(grad_patch_keys, *sent)
     patch_terms = dot_back(grad_patch_keys, whole_cross[:, :width]) + dot_back(
         grad_patch_values, whole_cross[:, width : 2 * width]
     )
@@ -1008,42 +1314,59 @@
             ).astype(jnp.float32)
             for terms in (patch_terms, normed_terms)
         )
-    grad_normed = grad_normed + dot_back(scaled_late, whole_self[:, :width])
-    back_zero, grad_gain_one, grad_shift_one = layer_norm_back(token_values, gain_one, grad_normed)
-    grad_tokens = grad_hidden_one + back_zero
-    small = sum_vectors(
-        (
-            grad_gain_one,
-            grad_shift_one,
-            column_sum(scaled_self),
-            column_sum(grad_values),
-            column_sum(branch_self),
-            grad_gain_two,
-            grad_shift_two,
-            column_sum(scaled_cross),
-            column_sum(grad_patch_values),
-            column_sum(branch_cross),
-            grad_gain_three,
-            grad_shift_three,
-            column_inner,
-            column_sum(cotangent),
-        )
-    )
-    if two:
-        totals = (total_outer, total_inner, total_cross, total_self)
-        for turn in range(9):
-            for total in totals:
-                if total.stage < 4:
-                    total.step()
-                elif total.stage < 8:
-                    total.gather()
-        grad_outer, grad_ffn_in, grad_cross, grad_self = (total.result() for total in totals)
-        wide_cross, wide_self = jnp.split(grad_cross, 4, axis=1), jnp.split(grad_self, 4, axis=1)
+    grad_normed = grad_normed + dot_back(scaled_self, whole_self[:, :width])
+    grad_tokens = grad_hidden_one + layer_norm_back(token_values, gain_one, grad_normed)
+    norm_pairs = (
+        (token_values, grad_normed),
+        (hidden_one, grad_normed_two),
+        (hidden_two, grad_normed_three),
+    )
+    plain = (
+        scaled_self,
+        grad_values,
+        branch_self,
+        scaled_cross,
+        grad_patch_values,
+        branch_cross,
+        cotangent,
+    )
+    if two:
+        late = total_last.advance(patch_terms)
+        for total in (total_mid, total_ffn):
+            late = late + total.advance(late[0])
+        norm_pairs = ((after(token_values, *late), grad_normed),) + norm_pairs[1:]
+    sums = row_sums(norm_pairs, plain)
+    vector_sums = jnp.concatenate([sums, column_inner.reshape(-1, width)])
+    if two:
+        totals = (total_mid, total_ffn, total_last)
+        late = [vector_sums]
+        while any(total.stage < 8 for total in totals):
+            ahead = total_last.advance(*late)
+            late = ahead
+            for total in totals[:-1]:
+                late = late + total.advance(*ahead)
+        vector_total = VectorTotal(after(vector_sums, *late))
+        grad_outer, grad_ffn_in = total_ffn.result(2, *late)
+        late = vector_total.advance(grad_outer)
+        *wide_cross, wide_output = total_mid.result(5, *late)
+        late = vector_total.advance(wide_output)
+        wide_self = [*total_last.result(3, *late), wide_output]
     else:
         grad_outer = sum_plain(dot_tn(active, cotangent)).astype(jnp.float32)
         grad_ffn_in = sum_plain(dot_tn(normed_three, grad_inner)).astype(jnp.float32)
-        wide_cross = [sum_plain(dot_tn(*product)).astype(jnp.float32) for product in cross_products]
+        wide_cross = [
+            sum_plain(dot_tn(*product)).astype(jnp.float32) for product in cross_products
+        ]
         wide_self = [sum_plain(dot_tn(*product)).astype(jnp.float32) for product in self_products]
+        vector_total = VectorTotal(vector_sums)
+    sums = vector_total.result()
+    small_width = width // seq_count
+    own_sums = lax.dynamic_slice_in_dim(sums[:-4], seq_index * small_width, small_width, axis=1)
+    inner_rows = sums[-(column_inner.shape[0] // width) :].reshape(-1)
+    inner_width = column_inner.shape[0] // seq_count
+    own_inner = lax.dynamic_slice_in_dim(inner_rows, seq_index * inner_width, inner_width, axis=0)
+    order = (0, 1, 6, 7, 8, 2, 3, 9, 10, 11, 4, 5, None, 12)
+    small = [own_inner if at is None else own_sums[at] for at in order]
     totals = (
         small[0],
         small[1],

time: 757 us -> 730 us (0.964)
  waiting for transfers between devices: 257 us -> 154 us
  Pallas kernels: 253 us -> 321 us
  local copies, waits for them, and re-layouts: 58.4 us -> 42.7 us
  matrix products: 52 us -> 67.2 us
  starting transfers between devices: 83.2 us -> 98.2 us
    ppermute x28 -> x29, waiting for transfers between devices: 144 us -> 74.8 us  [exchange(): lax.ppermute(values, square, [(i, i ^ flip[i // 2 % 2]) for i in range(16)])]
    pallas_call x40 -> x29, Pallas kernels: 115 us -> 174 us  [the longest x11 42.2 us: join(): pl.pallas_call(functools.partial(join_kernel, count), grid_spec=pltpu.Pre...]
    ppermute x32 -> x41, waiting for transfers between devices: 93.5 us -> 67.7 us  [swap(): return lax.ppermute(values, axis_name, [(0, 1), (1, 0)])]
    unnamed x223 -> x184, local copies, waits for them, and re-layouts: 35.5 us -> 19.6 us
    ppermute x32 -> x41, starting transfers between devices: 42.8 us -> 58.4 us  [swap(): return lax.ppermute(values, axis_name, [(0, 1), (1, 0)])]
    pallas_call x2, Pallas kernels: 5.87 us -> 17.1 us  [assemble(): pl.pallas_call(functools.partial(assemble_kernel, count), grid_spec=pltpu...]
    ppermute x1, waiting for transfers between devices: 13.9 us -> 2.82 us  [on_device(): normed_came = lax.ppermute(normed_sent, 'seq', [(1, 0)])]
    dot_general x8, matrix products: 30.9 us -> 41.5 us  [dot_nt(): lax.dot_general(left_side, right_side, (((1,), (1,)), ((), ())), preferre...]
  transfers between devices with their start and end apart: 62 -> 72, of which waited for: 24 -> 26; matrix products, arithmetic and copies ran while one was open for 17% -> 17% of each run, Pallas kernels for 17% -> 29%
where the time goes in v2:
time: 730 us; the launch traced here: 723 us
  Pallas kernels  321 us (44%)
  waiting for transfers between devices  154 us (21%)
  starting transfers between devices  98.2 us (13%)
  matrix products  67.2 us (9%)
  local copies, waits for them, and re-layouts  42.7 us (6%)
  other arithmetic  37.5 us (5%)
    ppermute x29, waiting for transfers between devices, exchange(): lax.ppermute(values, square, [(i, i ^ flip[i // 2 % 2]) for i in range(16)])  74.8 us
    ppermute x41, waiting for transfers between devices, swap(): return lax.ppermute(values, axis_name, [(0, 1), (1, 0)])  67.7 us
    ppermute x41, starting transfers between devices, swap(): return lax.ppermute(values, axis_name, [(0, 1), (1, 0)])  58.4 us
    pallas_call x3, Pallas kernels, attend(): pl.pallas_call(skip_refs(functools.partial(attend_kernel, plan), 5, len(i...  47.7 us
    pallas_call x11, Pallas kernels, join(): pl.pallas_call(functools.partial(join_kernel, count), grid_spec=pltpu.Pre...  42.2 us
    pallas_call x2, Pallas kernels, attend_back(): pl.pallas_call(skip_refs(functools.partial(attend_back_kernel, plan), 8,...  41.9 us
    dot_general x8, matrix products, dot_nt(): lax.dot_general(left_side, right_side, (((1,), (1,)), ((), ())), preferre...  41.5 us
    pallas_call x1, Pallas kernels, ffn_both_ways(): pl.pallas_call(functools.partial(ffn_kernel, half_steps), grid_spec=pltpu...  40.2 us
  transfers between devices with their start and end apart: 72, of which 26 were waited for; matrix products, arithmetic and copies ran while one was open for 17% of the time, Pallas kernels for 29%

profile of v2, /device:TPU:0, one launch (start us, length us, event | category | flops | bytes accessed | tf_op | source)
XLA Modules:
  0.0 723.4 jit_solution(13951543259281475578)
XLA Ops:
  8.8 9.5 %collective-permute-done.1 = bf16[68,128]{1,0:T(8,128)(2,1)S(1)} collective-permute-done((bf16[68,128]{1,0:T(8,128)(2,1)S(1)}, bf16[68,128]{1,0:T(8,128)(2,1)S(1)}, u32[]{:S(2)}, u32[]{:S(2)}) %collective-permute-start.1) | collective-permute-done | bytes 17440 | tf_op jit(solution)/shard_map/ppermute | solution.py:800
  33.5 6.2 collective-permute-done.5.refs_7_
  41.6 8.4 %collective-permute-done.2 = bf16[512,1024]{1,0:T(8,128)(2,1)S(1)} collective-permute-done((bf16[512,1024]{1,0:T(8,128)(2,1)S(1)}, bf16[512,1024]{1,0:T(8,128)(2,1)S(1)}, u32[]{:S(2)}, u32[]{:S(2)}) %collective-permute-start.2) | collective-permute-done | bytes 1048608 | tf_op jit(solution)/shard_map/ppermute | solution.py:1113
  54.3 8.7 %shard_map.484 = bf16[1024,4096]{1,0:T(8,128)(2,1)} custom-call(s32[9]{0:T(128)} %stack.420.place_ref, bf16[512,1024]{1,0:T(8,128)(2,1)} %refs_0_.2, bf16[512,1024]{1,0:T(8,128)(2,1)} %refs_1_.2, bf16[512,1024]{1,0:T(8,128)(2,1)} %refs_2_.2, bf16[512,1024]{1,0:T(8,128)(2,1)} %refs_3_.2, bf16[64,4096]{1,0:T(8,128)(2,1)} %copy-done.37, ...), custom_call_target="tpu_custom_call" | custom-call | flops 1 | bytes 1 | tf_op jit(solution)/shard_map/pallas_call | solution.py:312
  69.7 6.1 add_convert_fusion.refs_2_.refs_3_.refs_5_.refs_6_
  75.8 4.4 collective-permute-done.11.refs_5_
  81.1 16.6 %shard_map.485 = (bf16[512,1024]{1,0:T(8,128)(2,1)}, f32[8,2,512]{2,1,0:T(2,128)}) custom-call(s32[4]{0:T(128)} %pad_add_fusion.refs_0_, bf16[512,1024]{1,0:T(8,128)(2,1)} %multiply_convert_fusion.1.refs_1_, bf16[1024,2048]{1,0:T(8,128)(2,1)} %add_convert_fusion.refs_2_.refs_3_.refs_5_.refs_6_, ...), custom_call_target="tpu_custom_call" | custom-call | flops 1 | bytes 1 | tf_op jit(solution)/shard_map/pallas_call | solution.py:211
  101.2 5.9 collective-permute-done.15.refs_7_
  113.9 6.7 collective-permute-start.19
  123.9 8.4 %shard_map.486 = bf16[1024,4096]{1,0:T(8,128)(2,1)} custom-call(s32[9]{0:T(128)} %stack.420.place_ref, bf16[512,1024]{1,0:T(8,128)(2,1)} %refs_0_.3, bf16[512,1024]{1,0:T(8,128)(2,1)} %refs_1_.3, bf16[512,1024]{1,0:T(8,128)(2,1)} %refs_2_.3, bf16[512,1024]{1,0:T(8,128)(2,1)} %refs_3_.3, bf16[64,4096]{1,0:T(8,128)(2,1)} %collective-permute-done.10.refs_4_, ...), custom_call_target="tpu_custom_call" | custom-call | flops 1 | bytes 1 | tf_op jit(solution)/shard_map/pallas_call | solution.py:312
  139.9 6.5 fusion.refs_2_.refs_3_.refs_5_.refs_6_
  146.4 4.5 collective-permute-done.20.refs_1_
  154.4 15.6 %shard_map.487 = (bf16[512,1024]{1,0:T(8,128)(2,1)}, f32[8,2,512]{2,1,0:T(2,128)}) custom-call(s32[4]{0:T(128)} %pad_add_fusion.refs_0_, bf16[512,1024]{1,0:T(8,128)(2,1)} %multiply_convert_fusion.refs_1_, bf16[1088,2048]{1,0:T(8,128)(2,1)} %fusion.refs_2_.refs_3_.refs_5_.refs_6_, bf16[1088,2048]{1,0:T(8,128)(2,1)} %fusion.refs_2_.refs_3_.refs_5_.refs_6_, ...), custom_call_target="tpu_custom_call" | custom-call | flops 1 | bytes 1 | tf_op jit(solution)/shard_map/pallas_call | solution.py:211
  174.1 10.2 %collective-permute-done.24.refs_3_ = bf16[64,4096]{1,0:T(8,128)(2,1)} collective-permute-done((bf16[64,4096]{1,0:T(8,128)(2,1)S(1)}, bf16[64,4096]{1,0:T(8,128)(2,1)}, u32[]{:S(2)}, u32[]{:S(2)}) %collective-permute-start.24) | collective-permute-done | bytes 524320 | tf_op jit(solution)/shard_map/ppermute | solution.py:809
  186.2 4.4 collective-permute-done.28.refs_2_
  190.6 15.5 %shard_map.488 = (bf16[512,1024]{1,0:T(8,128)(2,1)}, f32[8,2,512]{2,1,0:T(2,128)}) custom-call(s32[4]{0:T(128)} %pad_add_fusion.refs_0_, bf16[512,1024]{1,0:T(8,128)(2,1)} %multiply_convert_fusion.refs_1_, bf16[1088,2048]{1,0:T(8,128)(2,1)} %fusion.refs_2_.refs_3_.refs_5_.refs_6_, ...), custom_call_target="tpu_custom_call", output_to_operand_aliasing={{0}: (5, {}), {1}: (6, {})} | custom-call | flops 1 | bytes 1 | tf_op jit(solution)/shard_map/pallas_call | solution.py:211
  209.6 6.0 collective-permute-done.30.refs_3_
  215.6 5.7 shard_map.489.refs_6_.refs_7_
  227.6 5.5 shard_map.490.refs_9_
  233.1 40.2 %shard_map.491 = (bf16[512,1024]{1,0:T(8,128)(2,1)}, f32[512,1024]{1,0:T(8,128)}, f32[1,4096]{1,0:T(1,128)}, bf16[4,512,1024]{2,1,0:T(8,128)(2,1)}, bf16[4,512,1...) custom-call(s32[32]{0:T(128)} %stack.409.place_ref, ...), custom_call_target="tpu_custom_call" | custom-call | flops 1 | bytes 1 | tf_op jit(solution)/shard_map/pallas_call | solution.py:462
  286.9 11.3 %shard_map.492 = (bf16[2,1024,1024]{2,1,0:T(8,128)(2,1)}, bf16[1,1024,1024]{2,1,0:T(8,128)(2,1)}, bf16[1,1024,1024]{2,1,0:T(8,128)(2,1)}) custom-call(s32[4]{0:T(128)} %pad_add_fusion.1.place_ref, bf16[4,512,1024]{2,1,0:T(8,128)(2,1)} %get-tuple-element.189.refs_0_.refs_4_, bf16[4,512,1024]{2,1,0:T(8,128)(2,1)} %collective-permute-done.35.refs_1_.refs_5_, ...), custom_call_target="tpu_custom_call" | custom-call | flops 1 | bytes 1 | tf_op jit(solution)/shard_map/pallas_call | solution.py:707
  299.8 26.9 %shard_map.493 = (bf16[512,1024]{1,0:T(8,128)(2,1)}, bf16[1088,1024]{1,0:T(8,128)(2,1)}, bf16[1088,1024]{1,0:T(8,128)(2,1)}) custom-call(s32[4]{0:T(128)} %pad_add_fusion.refs_0_, bf16[512,1024]{1,0:T(8,128)(2,1)} %multiply_convert_fusion.refs_1_, bf16[512,1024]{1,0:T(8,128)(2,1)} %get-tuple-element.183.refs_2_, bf16[512,1024]{1,0:T(8,128)(2,1)} %fusion.43.refs_3_, ...), custom_call_target="tpu_custom_call" | custom-call | flops 1 | bytes 1 | tf_op jit(solution)/shard_map/pallas_call | solution.py:235
  338.4 19.3 %shard_map.494 = (bf16[2,256,5120]{2,1,0:T(8,128)(2,1)}, bf16[2,256,5120]{2,1,0:T(8,128)(2,1)}) custom-call(s32[2]{0:T(128)} %pad_add_fusion.3.place_ref, bf16[512,1024]{1,0:T(8,128)(2,1)} %add_convert_fusion.2.refs_0_, bf16[1088,1024]{1,0:T(8,128)(2,1)} %pad_maximum_fusion.refs_1_, bf16[512,1024]{1,0:T(8,128)(2,1)} %get-tuple-element.183.refs_2_, ...), custom_call_target="tpu_custom_call" | custom-call | flops 1 | bytes 1 | tf_op jit(solution)/shard_map/pallas_call | solution.py:570
  357.7 7.8 %shard_map.495 = (bf16[2,512,1024]{2,1,0:T(8,128)(2,1)}, bf16[2,512,1024]{2,1,0:T(8,128)(2,1)}) custom-call(s32[8]{0:T(128)} %stack.453.place_ref, bf16[4,512,1024]{2,1,0:T(8,128)(2,1)} %bitcast.212, bf16[2,512,1024]{2,1,0:T(8,128)(2,1)} %bitcast.66.refs_1_.refs_4_, bf16[2,512,1024]{2,1,0:T(8,128)(2,1)} %bitcast.67.refs_2_.refs_5_, ...), custom_call_target="tpu_custom_call" | custom-call | flops 1 | bytes 1 | tf_op jit(solution)/shard_map/pallas_call | solution.py:660
  366.3 8.2 %collective-permute-done.39.came_a.came_b = bf16[4,128,5120]{2,1,0:T(8,128)(2,1)} collective-permute-done((bf16[4,128,5120]{2,1,0:T(8,128)(2,1)}, bf16[4,128,5120]{2,1,0:T(8,128)(2,1)}, u32[]{:S(2)}, u32[]{:S(2)}) %collective-permute-start.39) | collective-permute-done | bytes 5242912 | tf_op jit(solution)/shard_map/ppermute | solution.py:800
  374.5 7.7 %shard_map.496 = (bf16[2,128,5120]{2,1,0:T(8,128)(2,1)}, bf16[1,128,5120]{2,1,0:T(8,128)(2,1)}, bf16[1,128,5120]{2,1,0:T(8,128)(2,1)}) custom-call(s32[4]{0:T(128)} %pad_add_fusion.2.place_ref, bf16[4,128,5120]{2,1,0:T(8,128)(2,1)} %bitcast.210, bf16[4,128,5120]{2,1,0:T(8,128)(2,1)} %collective-permute-done.39.came_a.came_b, ...), custom_call_target="tpu_custom_call" | custom-call | flops 1 | bytes 1 | tf_op jit(solution)/shard_map/pallas_call | solution.py:623
  382.7 15.0 %shard_map.497 = (bf16[512,1024]{1,0:T(8,128)(2,1)}, bf16[1024,1024]{1,0:T(8,128)(2,1)}, bf16[1024,1024]{1,0:T(8,128)(2,1)}) custom-call(s32[4]{0:T(128)} %pad_add_fusion.refs_0_, bf16[512,1024]{1,0:T(8,128)(2,1)} %multiply_convert_fusion.1.refs_1_, bf16[512,1024]{1,0:T(8,128)(2,1)} %get-tuple-element.165.refs_3_.refs_2_, bf16[512,1024]{1,0:T(8,128)(2,1)} %fusion.40.refs_3_, ...), custom_call_target="tpu_custom_call" | custom-call | flops 1 | bytes 1 | tf_op jit(solution)/shard_map/pallas_call | solution.py:235
  397.7 7.8 %collective-permute-done.41 = bf16[1,128,5120]{2,1,0:T(8,128)(2,1)} collective-permute-done((bf16[1,128,5120]{2,1,0:T(8,128)(2,1)}, bf16[1,128,5120]{2,1,0:T(8,128)(2,1)}, u32[]{:S(2)}, u32[]{:S(2)}) %collective-permute-start.41) | collective-permute-done | bytes 1310752 | tf_op jit(solution)/shard_map/ppermute | solution.py:809
  414.5 12.9 %shard_map.499 = (bf16[2,256,3072]{2,1,0:T(8,128)(2,1)}, bf16[2,256,3072]{2,1,0:T(8,128)(2,1)}) custom-call(s32[2]{0:T(128)} %pad_add_fusion.3.place_ref, bf16[512,1024]{1,0:T(8,128)(2,1)} %slice.184.refs_0_, bf16[1024,1024]{1,0:T(8,128)(2,1)} %copy-done.6, bf16[512,1024]{1,0:T(8,128)(2,1)} %get-tuple-element.230.refs_2_.refs_6_, ...), custom_call_target="tpu_custom_call" | custom-call | flops 1 | bytes 1 | tf_op jit(solution)/shard_map/pallas_call | solution.py:570
  427.4 7.2 collective-permute-done.42
  437.7 5.8 shard_map.501
  456.7 6.0 fusion.21
  462.7 5.7 shard_map.502
  468.4 6.3 fusion.13
  486.3 7.5 %convolution_add_fusion.1 = f32[1088,1024]{1,0:T(8,128)} fusion(f32[1088,1024]{1,0:T(8,128)} %fusion.13, bf16[1088,1024]{1,0:T(8,128)(2,1)S(1)} %copy-done.22, bf16[1024,4096]{1,0:T(8,128)(2,1)} %shard_map.486), kind=kOutput, calls=%fused_computation.7 | convolution fusion | flops 2282815488 | bytes 13238272 | tf_op jit(solution)/shard_map/dot_general | solution.py:32
  511.9 5.4 multiply_reduce_fusion.6
  521.1 9.6 %shard_map.507 = f32[16,1024]{1,0:T(8,128)} custom-call(f32[512,1024]{1,0:T(8,128)} %bitcast_convert_fusion.refs_0_, f32[512,1024]{1,0:T(8,128)} %get-tuple-element.322.refs_1_, f32[512,1024]{1,0:T(8,128)} %copy-done.3, f32[512,1024]{1,0:T(8,128)} %copy-done.17, f32[512,1024]{1,0:T(8,128)} %copy-done, f32[512,1024]{1,0:T(8,128)} %get-tuple-element.187.refs_5_, ...), custom_call_target="tpu_custom_call" | custom-call | flops 1 | bytes 1 | tf_op jit(solution)/shard_map/pallas_call | solution.py:352
  542.6 9.7 %collective-permute-done.53 = bf16[1,32,5120]{2,1,0:T(8,128)(2,1)S(1)} collective-permute-done((bf16[1,32,5120]{2,1,0:T(8,128)(2,1)S(1)}, bf16[1,32,5120]{2,1,0:T(8,128)(2,1)S(1)}, u32[]{:S(2)}, u32[]{:S(2)}) %collective-permute-start.53) | collective-permute-done | bytes 327712 | tf_op jit(solution)/shard_map/ppermute | solution.py:800
  561.0 7.9 %collective-permute-done.57.refs_1_ = bf16[32,5120]{1,0:T(8,128)(2,1)} collective-permute-done((bf16[32,5120]{1,0:T(8,128)(2,1)S(1)}, bf16[32,5120]{1,0:T(8,128)(2,1)}, u32[]{:S(2)}, u32[]{:S(2)}) %collective-permute-start.57) | collective-permute-done | bytes 327712 | tf_op jit(solution)/shard_map/ppermute | solution.py:800
  573.3 5.5 shard_map.517.own_ref
  578.8 31.0 %collective-permute-start.64 = (bf16[2048,1024]{1,0:T(8,128)(2,1)}, bf16[2048,1024]{1,0:T(8,128)(2,1)}, u32[]{:S(2)}, u32[]{:S(2)}) collective-permute-start(bf16[2048,1024]{1,0:T(8,128)(2,1)} %shard_map.517.own_ref), channel_id=1, source_target_pairs={{0,2},{2,0},{1,3},{3,1},{4,6},{6,4},{5,7},{7,5},{8,10},{10,8},{9,1... | collective-permute-start | bytes 12582920 | tf_op jit(solution)/shard_map/ppermute | solution.py:800
  617.2 18.3 %collective-permute-done.59.refs_1_ = bf16[32,3072]{1,0:T(8,128)(2,1)S(1)} collective-permute-done((bf16[32,3072]{1,0:T(8,128)(2,1)S(1)}, bf16[32,3072]{1,0:T(8,128)(2,1)S(1)}, u32[]{:S(2)}, u32[]{:S(2)}) %collective-permute-start.59) | collective-permute-done | bytes 196640 | tf_op jit(solution)/shard_map/ppermute | solution.py:800
  639.7 4.7 shard_map.514.own_ref
  647.3 5.8 collective-permute-done.61.refs_1_
  657.1 11.7 %collective-permute-done.62.refs_1_ = bf16[128,3072]{1,0:T(8,128)(2,1)S(1)} collective-permute-done((bf16[128,3072]{1,0:T(8,128)(2,1)}, bf16[128,3072]{1,0:T(8,128)(2,1)S(1)}, u32[]{:S(2)}, u32[]{:S(2)}) %collective-permute-start.62) | collective-permute-done | bytes 786464 | tf_op jit(solution)/shard_map/ppermute | solution.py:809
  679.6 14.7 %shard_map.518 = (f32[2048,1024]{1,0:T(8,128)}, f32[512,4096]{1,0:T(8,128)}) custom-call(s32[2]{0:T(128)} %pad_add_fusion.3.place_ref, bf16[2048,1024]{1,0:T(8,128)(2,1)} %shard_map.517.own_ref, bf16[2048,1024]{1,0:T(8,128)(2,1)} %collective-permute-done.64.other_ref), custom_call_target="tpu_custom_call" | custom-call | flops 1 | bytes 1 | tf_op jit(solution)/shard_map/pallas_call | solution.py:754
  694.4 8.1 %shard_map.519 = (f32[512,1024]{1,0:T(8,128)}, f32[512,1024]{1,0:T(8,128)}, f32[512,1024]{1,0:T(8,128)}, f32[512,1024]{1,0:T(8,128)}, f32[512,1024]{1,0:T(8,128)}) custom-call(s32[2]{0:T(128)} %pad_add_fusion.3.place_ref, bf16[256,5120]{1,0:T(8,128)(2,1)} %shard_map.514.own_ref, bf16[256,5120]{1,0:T(8,128)(2,1)} %collective-permute-done.66.other_ref), custom_call_target="tpu_custom_call" | custom-call | flops 1 | bytes 1 | tf_op jit(solution)/shard_map/pallas_call | solution.py:754
  715.5 6.0 shard_map.520
  (419 shorter events, 231.6 us)
Async XLA Ops:
  3.0 15.4 %collective-permute-start = (bf16[64,4096]{1,0:T(8,128)(2,1)S(1)}, bf16[64,4096]{1,0:T(8,128)(2,1)S(1)}, u32[]{:S(2)}, u32[]{:S(2)}) collective-permute-start(bf16[64,4096]{1,0:T(8,128)(2,1)S(1)} %pad_maximum_fusion.2), channel_id=1, source_target_pairs={{0,1},{1,0},{2,3},{3,2},{4,5},{5,4},{6,7},{7,6},{8,9},{9,8},{10,11... | collective-permute-start | bytes 1572872 | tf_op jit(solution)/shard_map/ppermute | solution.py:800
  25.6 24.4 %collective-permute-start.2 = (bf16[512,1024]{1,0:T(8,128)(2,1)S(1)}, bf16[512,1024]{1,0:T(8,128)(2,1)S(1)}, u32[]{:S(2)}, u32[]{:S(2)}) collective-permute-start(bf16[512,1024]{1,0:T(8,128)(2,1)S(1)} %bitcast.206), channel_id=1, source_target_pairs={{0,1},{2,3},{4,5},{6,7},{8,9},{10,11},{12,13},{14,15},{16,17},{18,... | collective-permute-start | bytes 3145736 | tf_op jit(solution)/shard_map/ppermute | solution.py:1113
  32.9 19.7 %collective-permute-start.6 = (bf16[64,4096]{1,0:T(8,128)(2,1)S(1)}, bf16[64,4096]{1,0:T(8,128)(2,1)S(1)}, u32[]{:S(2)}, u32[]{:S(2)}) collective-permute-start(bf16[64,4096]{1,0:T(8,128)(2,1)S(1)} %collective-permute-done.refs_4_), channel_id=1, source_target_pairs={{0,2},{2,0},{1,3},{3,1},{4,6},{6,4},{5,7},{7,5},{8,10},{10,8},{9,1... | collective-permute-start | bytes 1572872 | tf_op jit(solution)/shard_map/ppermute | solution.py:800
  32.9 19.6 %collective-permute-start.7 = (bf16[64,4096]{1,0:T(8,128)(2,1)S(1)}, bf16[64,4096]{1,0:T(8,128)(2,1)S(1)}, u32[]{:S(2)}, u32[]{:S(2)}) collective-permute-start(bf16[64,4096]{1,0:T(8,128)(2,1)S(1)} %collective-permute-done.3.refs_5_), channel_id=1, source_target_pairs={{0,2},{2,0},{1,3},{3,1},{4,6},{6,4},{5,7},{7,5},{8,10},{10,8},{9,1... | collective-permute-start | bytes 1572872 | tf_op jit(solution)/shard_map/ppermute | solution.py:800
  33.4 19.1 %collective-permute-start.8 = (bf16[64,4096]{1,0:T(8,128)(2,1)S(1)}, bf16[64,4096]{1,0:T(8,128)(2,1)S(1)}, u32[]{:S(2)}, u32[]{:S(2)}) collective-permute-start(bf16[64,4096]{1,0:T(8,128)(2,1)S(1)} %collective-permute-done.4.refs_6_), channel_id=1, source_target_pairs={{0,2},{2,0},{1,3},{3,1},{4,6},{6,4},{5,7},{7,5},{8,10},{10,8},{9,1... | collective-permute-start | bytes 1572872 | tf_op jit(solution)/shard_map/ppermute | solution.py:800
  39.8 14.5 %collective-permute-start.9 = (bf16[64,4096]{1,0:T(8,128)(2,1)S(1)}, bf16[64,4096]{1,0:T(8,128)(2,1)}, u32[]{:S(2)}, u32[]{:S(2)}) collective-permute-start(bf16[64,4096]{1,0:T(8,128)(2,1)S(1)} %collective-permute-done.5.refs_7_), channel_id=1, source_target_pairs={{0,2},{2,0},{1,3},{3,1},{4,6},{6,4},{5,7},{7,5},{8,10},{10,8},{9,1... | collective-permute-start | bytes 1572872 | tf_op jit(solution)/shard_map/ppermute | solution.py:800
  50.0 18.7 %collective-permute-start.10 = (bf16[64,4096]{1,0:T(8,128)(2,1)}, bf16[64,4096]{1,0:T(8,128)(2,1)}, u32[]{:S(2)}, u32[]{:S(2)}) collective-permute-start(bf16[64,4096]{1,0:T(8,128)(2,1)} %pad_maximum_fusion.3), channel_id=1, source_target_pairs={{0,1},{1,0},{2,3},{3,2},{4,5},{5,4},{6,7},{7,6},{8,9},{9,8},{10,11... | collective-permute-start | bytes 1572872 | tf_op jit(solution)/shard_map/ppermute | solution.py:800
  69.7 37.5 %collective-permute-start.14 = (bf16[544,1024]{1,0:T(8,128)(2,1)S(1)}, bf16[544,1024]{1,0:T(8,128)(2,1)S(1)}, u32[]{:S(2)}, u32[]{:S(2)}) collective-permute-start(bf16[544,1024]{1,0:T(8,128)(2,1)S(1)} %bitcast.234), channel_id=1, source_target_pairs={{0,1},{1,0},{2,3},{3,2},{4,5},{5,4},{6,7},{7,6},{8,9},{9,8},{10,11... | collective-permute-start | bytes 3342344 | tf_op jit(solution)/shard_map/ppermute | solution.py:800
  107.2 16.8 %collective-permute-start.18 = (bf16[64,4096]{1,0:T(8,128)(2,1)}, bf16[64,4096]{1,0:T(8,128)(2,1)}, u32[]{:S(2)}, u32[]{:S(2)}) collective-permute-start(bf16[64,4096]{1,0:T(8,128)(2,1)} %collective-permute-done.15.refs_7_), channel_id=1, source_target_pairs={{0,2},{2,0},{1,3},{3,1},{4,6},{6,4},{5,7},{7,5},{8,10},{10,8},{9,1... | collective-permute-start | bytes 1572872 | tf_op jit(solution)/shard_map/ppermute | solution.py:800
  113.9 22.7 %collective-permute-start.19 = (bf16[64,4096]{1,0:T(8,128)(2,1)}, bf16[64,4096]{1,0:T(8,128)(2,1)S(1)}, u32[]{:S(2)}, u32[]{:S(2)}) collective-permute-start(bf16[64,4096]{1,0:T(8,128)(2,1)} %constant_dynamic-slice_fusion.2), channel_id=1, source_target_pairs={{0,1},{1,0},{2,3},{3,2},{4,5},{5,4},{6,7},{7,6},{8,9},{9,8},{10,11... | collective-permute-start | bytes 1572872 | tf_op jit(solution)/shard_map/ppermute | solution.py:800
  136.7 14.3 %collective-permute-start.20 = (bf16[64,4096]{1,0:T(8,128)(2,1)S(1)}, bf16[64,4096]{1,0:T(8,128)(2,1)S(1)}, u32[]{:S(2)}, u32[]{:S(2)}) collective-permute-start(bf16[64,4096]{1,0:T(8,128)(2,1)S(1)} %collective-permute-done.19.refs_0_), channel_id=1, source_target_pairs={{0,4},{1,5},{2,10},{3,11},{4,0},{5,1},{6,14},{7,15},{8,12},{9,13},... | collective-permute-start | bytes 1572872 | tf_op jit(solution)/shard_map/ppermute | solution.py:809
  137.2 13.8 %collective-permute-start.21 = (bf16[64,4096]{1,0:T(8,128)(2,1)S(1)}, bf16[64,4096]{1,0:T(8,128)(2,1)S(1)}, u32[]{:S(2)}, u32[]{:S(2)}) collective-permute-start(bf16[64,4096]{1,0:T(8,128)(2,1)S(1)} %collective-permute-done.19.refs_0_), channel_id=1, source_target_pairs={{0,8},{1,9},{2,6},{3,7},{4,12},{5,13},{6,2},{7,3},{8,0},{9,1},{10,... | collective-permute-start | bytes 1572872 | tf_op jit(solution)/shard_map/ppermute | solution.py:809
  138.8 12.2 %collective-permute-start.22 = (bf16[64,4096]{1,0:T(8,128)(2,1)S(1)}, bf16[64,4096]{1,0:T(8,128)(2,1)S(1)}, u32[]{:S(2)}, u32[]{:S(2)}) collective-permute-start(bf16[64,4096]{1,0:T(8,128)(2,1)S(1)} %collective-permute-done.19.refs_0_), channel_id=1, source_target_pairs={{0,2},{2,0},{1,3},{3,1},{4,6},{6,4},{5,7},{7,5},{8,10},{10,8},{9,1... | collective-permute-start | bytes 1572872 | tf_op jit(solution)/shard_map/ppermute | solution.py:800
  139.8 14.5 %collective-permute-start.23 = (bf16[256,1024]{1,0:T(8,128)(2,1)S(1)}, bf16[256,1024]{1,0:T(8,128)(2,1)}, u32[]{:S(2)}, u32[]{:S(2)}) collective-permute-start(bf16[256,1024]{1,0:T(8,128)(2,1)S(1)} %constant_dynamic-slice_fusion.1), channel_id=1, source_target_pairs={{0,1},{1,0},{2,3},{3,2},{4,5},{5,4},{6,7},{7,6},{8,9},{9,8},{10,11... | collective-permute-start | bytes 1572872 | tf_op jit(solution)/shard_map/ppermute | solution.py:800
  170.0 14.3 %collective-permute-start.24 = (bf16[64,4096]{1,0:T(8,128)(2,1)S(1)}, bf16[64,4096]{1,0:T(8,128)(2,1)}, u32[]{:S(2)}, u32[]{:S(2)}) collective-permute-start(bf16[64,4096]{1,0:T(8,128)(2,1)S(1)} %copy-done.40), channel_id=1, source_target_pairs={{0,8},{1,9},{2,6},{3,7},{4,12},{5,13},{6,2},{7,3},{8,0},{9,1},{10,... | collective-permute-start | bytes 1572872 | tf_op jit(solution)/shard_map/ppermute | solution.py:809
  170.5 13.8 %collective-permute-start.25 = (bf16[64,4096]{1,0:T(8,128)(2,1)S(1)}, bf16[64,4096]{1,0:T(8,128)(2,1)S(1)}, u32[]{:S(2)}, u32[]{:S(2)}) collective-permute-start(bf16[64,4096]{1,0:T(8,128)(2,1)S(1)} %copy-done.40), channel_id=1, source_target_pairs={{0,2},{2,0},{1,3},{3,1},{4,6},{6,4},{5,7},{7,5},{8,10},{10,8},{9,1... | collective-permute-start | bytes 1572872 | tf_op jit(solution)/shard_map/ppermute | solution.py:800
  171.0 14.1 %collective-permute-start.26 = (bf16[64,4096]{1,0:T(8,128)(2,1)}, bf16[64,4096]{1,0:T(8,128)(2,1)S(1)}, u32[]{:S(2)}, u32[]{:S(2)}) collective-permute-start(bf16[64,4096]{1,0:T(8,128)(2,1)} %copy-done.41), channel_id=1, source_target_pairs={{0,2},{2,0},{1,3},{3,1},{4,6},{6,4},{5,7},{7,5},{8,10},{10,8},{9,1... | collective-permute-start | bytes 1572872 | tf_op jit(solution)/shard_map/ppermute | solution.py:800
  171.0 15.2 %collective-permute-start.27 = (bf16[256,1024]{1,0:T(8,128)(2,1)}, bf16[256,1024]{1,0:T(8,128)(2,1)}, u32[]{:S(2)}, u32[]{:S(2)}) collective-permute-start(bf16[256,1024]{1,0:T(8,128)(2,1)} %collective-permute-done.23.refs_0_), channel_id=1, source_target_pairs={{0,4},{1,5},{2,10},{3,11},{4,0},{5,1},{6,14},{7,15},{8,12},{9,13},... | collective-permute-start | bytes 1572872 | tf_op jit(solution)/shard_map/ppermute | solution.py:809
  172.5 18.1 %collective-permute-start.28 = (bf16[256,1024]{1,0:T(8,128)(2,1)}, bf16[256,1024]{1,0:T(8,128)(2,1)}, u32[]{:S(2)}, u32[]{:S(2)}) collective-permute-start(bf16[256,1024]{1,0:T(8,128)(2,1)} %collective-permute-done.23.refs_0_), channel_id=1, source_target_pairs={{0,8},{1,9},{2,6},{3,7},{4,12},{5,13},{6,2},{7,3},{8,0},{9,1},{10,... | collective-permute-start | bytes 1572872 | tf_op jit(solution)/shard_map/ppermute | solution.py:809
  273.7 13.2 %collective-permute-start.36 = (bf16[4,128,4096]{2,1,0:T(8,128)(2,1)}, bf16[4,128,4096]{2,1,0:T(8,128)(2,1)}, u32[]{:S(2)}, u32[]{:S(2)}) collective-permute-start(bf16[4,128,4096]{2,1,0:T(8,128)(2,1)} %bitcast.274), channel_id=1, source_target_pairs={{0,2},{2,0},{1,3},{3,1},{4,6},{6,4},{5,7},{7,5},{8,10},{10,8},{9,1... | collective-permute-start | bytes 12582920 | tf_op jit(solution)/shard_map/ppermute | solution.py:800
  298.2 28.4 %collective-permute-start.37 = (bf16[1,1024,1024]{2,1,0:T(8,128)(2,1)}, bf16[1,1024,1024]{2,1,0:T(8,128)(2,1)}, u32[]{:S(2)}, u32[]{:S(2)}) collective-permute-start(bf16[1,1024,1024]{2,1,0:T(8,128)(2,1)} %get-tuple-element.193), channel_id=1, source_target_pairs={{0,4},{1,5},{2,3},{3,2},{4,0},{5,1},{6,7},{7,6},{8,12},{9,13},{10,... | collective-permute-start | bytes 6291464 | tf_op jit(solution)/shard_map/ppermute | solution.py:809
  326.7 31.0 %collective-permute-start.38 = (bf16[1,1024,1024]{2,1,0:T(8,128)(2,1)}, bf16[1,1024,1024]{2,1,0:T(8,128)(2,1)}, u32[]{:S(2)}, u32[]{:S(2)}) collective-permute-start(bf16[1,1024,1024]{2,1,0:T(8,128)(2,1)} %get-tuple-element.198), channel_id=1, source_target_pairs={{0,4},{1,5},{2,3},{3,2},{4,0},{5,1},{6,7},{7,6},{8,12},{9,13},{10,... | collective-permute-start | bytes 6291464 | tf_op jit(solution)/shard_map/ppermute | solution.py:809
  365.5 41.0 %collective-permute-start.40 = (bf16[2,512,1024]{2,1,0:T(8,128)(2,1)}, bf16[2,512,1024]{2,1,0:T(8,128)(2,1)}, u32[]{:S(2)}, u32[]{:S(2)}) collective-permute-start(bf16[2,512,1024]{2,1,0:T(8,128)(2,1)} %get-tuple-element.206), channel_id=1, source_target_pairs={{0,1},{1,0},{2,10},{3,11},{4,5},{5,4},{6,14},{7,15},{8,9},{9,8},{1... | collective-permute-start | bytes 6291464 | tf_op jit(solution)/shard_map/ppermute | solution.py:809
  382.2 23.3 %collective-permute-start.41 = (bf16[1,128,5120]{2,1,0:T(8,128)(2,1)}, bf16[1,128,5120]{2,1,0:T(8,128)(2,1)}, u32[]{:S(2)}, u32[]{:S(2)}) collective-permute-start(bf16[1,128,5120]{2,1,0:T(8,128)(2,1)} %get-tuple-element.210), channel_id=1, source_target_pairs={{0,8},{1,9},{2,6},{3,7},{4,12},{5,13},{6,2},{7,3},{8,0},{9,1},{10,... | collective-permute-start | bytes 3932168 | tf_op jit(solution)/shard_map/ppermute | solution.py:809
  405.4 32.2 %collective-permute-start.43 = (bf16[1,128,5120]{2,1,0:T(8,128)(2,1)}, bf16[1,128,5120]{2,1,0:T(8,128)(2,1)}, u32[]{:S(2)}, u32[]{:S(2)}) collective-permute-start(bf16[1,128,5120]{2,1,0:T(8,128)(2,1)} %get-tuple-element.220), channel_id=1, source_target_pairs={{0,8},{1,9},{2,6},{3,7},{4,12},{5,13},{6,2},{7,3},{8,0},{9,1},{10,... | collective-permute-start | bytes 3932168 | tf_op jit(solution)/shard_map/ppermute | solution.py:809
  410.7 23.9 %collective-permute-start.42 = (bf16[1,512,1024]{2,1,0:T(8,128)(2,1)}, bf16[1,512,1024]{2,1,0:T(8,128)(2,1)}, u32[]{:S(2)}, u32[]{:S(2)}) collective-permute-start(bf16[1,512,1024]{2,1,0:T(8,128)(2,1)} %get-tuple-element.218), channel_id=1, source_target_pairs={{0,8},{1,9},{2,6},{3,7},{4,12},{5,13},{6,2},{7,3},{8,0},{9,1},{10,... | collective-permute-start | bytes 3145736 | tf_op jit(solution)/shard_map/ppermute | solution.py:809
  443.5 19.2 %collective-permute-start.45 = (bf16[4,128,3072]{2,1,0:T(8,128)(2,1)}, bf16[4,128,3072]{2,1,0:T(8,128)(2,1)}, u32[]{:S(2)}, u32[]{:S(2)}) collective-permute-start(bf16[4,128,3072]{2,1,0:T(8,128)(2,1)} %bitcast.275), channel_id=1, source_target_pairs={{0,2},{2,0},{1,3},{3,1},{4,6},{6,4},{5,7},{7,5},{8,10},{10,8},{9,1... | collective-permute-start | bytes 9437192 | tf_op jit(solution)/shard_map/ppermute | solution.py:800
  451.4 26.7 %collective-permute-start.47 = (bf16[1,256,1024]{2,1,0:T(8,128)(2,1)}, bf16[1,256,1024]{2,1,0:T(8,128)(2,1)S(1)}, u32[]{:S(2)}, u32[]{:S(2)}) collective-permute-start(bf16[1,256,1024]{2,1,0:T(8,128)(2,1)} %get-tuple-element.225), channel_id=1, source_target_pairs={{0,16},{16,0},{1,17},{17,1},{2,18},{18,2},{3,19},{19,3},{4,20},{20... | collective-permute-start | bytes 1572872 | tf_op jit(solution)/shard_map/ppermute | solution.py:800
  454.1 28.5 %collective-permute-start.46 = (bf16[2,64,5120]{2,1,0:T(8,128)(2,1)}, bf16[2,64,5120]{2,1,0:T(8,128)(2,1)}, u32[]{:S(2)}, u32[]{:S(2)}) collective-permute-start(bf16[2,64,5120]{2,1,0:T(8,128)(2,1)} %get-tuple-element.228), channel_id=1, source_target_pairs={{0,1},{1,0},{2,10},{3,11},{4,5},{5,4},{6,14},{7,15},{8,9},{9,8},{1... | collective-permute-start | bytes 3932168 | tf_op jit(solution)/shard_map/ppermute | solution.py:809
  468.4 25.4 %collective-permute-start.49 = (bf16[2,128,3072]{2,1,0:T(8,128)(2,1)}, bf16[2,128,3072]{2,1,0:T(8,128)(2,1)}, u32[]{:S(2)}, u32[]{:S(2)}) collective-permute-start(bf16[2,128,3072]{2,1,0:T(8,128)(2,1)} %get-tuple-element.234), channel_id=1, source_target_pairs={{0,1},{1,0},{2,10},{3,11},{4,5},{5,4},{6,14},{7,15},{8,9},{9,8},{1... | collective-permute-start | bytes 4718600 | tf_op jit(solution)/shard_map/ppermute | solution.py:809
  478.4 20.6 %collective-permute-start.51 = (bf16[256,1024]{1,0:T(8,128)(2,1)S(1)}, bf16[256,1024]{1,0:T(8,128)(2,1)}, u32[]{:S(2)}, u32[]{:S(2)}) collective-permute-start(bf16[256,1024]{1,0:T(8,128)(2,1)S(1)} %fusion.56.refs_0_), channel_id=1, source_target_pairs={{0,16},{16,0},{1,17},{17,1},{2,18},{18,2},{3,19},{19,3},{4,20},{20... | collective-permute-start | bytes 1572872 | tf_op jit(solution)/shard_map/ppermute | solution.py:800
  481.3 30.6 %collective-permute-start.44 = (bf16[512,1024]{1,0:T(8,128)(2,1)}, bf16[512,1024]{1,0:T(8,128)(2,1)}, u32[]{:S(2)}, u32[]{:S(2)}) collective-permute-start(bf16[512,1024]{1,0:T(8,128)(2,1)} %slice.285), channel_id=1, source_target_pairs={{1,0},{3,2},{5,4},{7,6},{9,8},{11,10},{13,12},{15,14},{17,16},{19,... | collective-permute-start | bytes 3145736 | tf_op jit(solution)/shard_map/ppermute | solution.py:1306
  501.8 33.5 %collective-permute-start.54 = (bf16[512,1024]{1,0:T(8,128)(2,1)}, bf16[512,1024]{1,0:T(8,128)(2,1)}, u32[]{:S(2)}, u32[]{:S(2)}) collective-permute-start(bf16[512,1024]{1,0:T(8,128)(2,1)} %shard_map.506.refs_0_), channel_id=1, source_target_pairs={{0,8},{1,9},{2,6},{3,7},{4,12},{5,13},{6,2},{7,3},{8,0},{9,1},{10,... | collective-permute-start | bytes 3145736 | tf_op jit(solution)/shard_map/ppermute | solution.py:809
  503.9 13.4 %collective-permute-start.50 = (bf16[1,64,5120]{2,1,0:T(8,128)(2,1)}, bf16[1,64,5120]{2,1,0:T(8,128)(2,1)S(1)}, u32[]{:S(2)}, u32[]{:S(2)}) collective-permute-start(bf16[1,64,5120]{2,1,0:T(8,128)(2,1)} %get-tuple-element.237), channel_id=1, source_target_pairs={{0,4},{1,5},{2,3},{3,2},{4,0},{5,1},{6,7},{7,6},{8,12},{9,13},{10,... | collective-permute-start | bytes 1966088 | tf_op jit(solution)/shard_map/ppermute | solution.py:809
  505.4 26.1 %collective-permute-start.52 = (bf16[2,64,3072]{2,1,0:T(8,128)(2,1)}, bf16[2,64,3072]{2,1,0:T(8,128)(2,1)S(1)}, u32[]{:S(2)}, u32[]{:S(2)}) collective-permute-start(bf16[2,64,3072]{2,1,0:T(8,128)(2,1)} %get-tuple-element.242), channel_id=1, source_target_pairs={{0,4},{1,5},{2,3},{3,2},{4,0},{5,1},{6,7},{7,6},{8,12},{9,13},{10,... | collective-permute-start | bytes 2359304 | tf_op jit(solution)/shard_map/ppermute | solution.py:809
  539.2 32.8 %collective-permute-start.63 = (bf16[1024,1024]{1,0:T(8,128)(2,1)}, bf16[1024,1024]{1,0:T(8,128)(2,1)S(1)}, u32[]{:S(2)}, u32[]{:S(2)}) collective-permute-start(bf16[1024,1024]{1,0:T(8,128)(2,1)} %shard_map.509.refs_0_), channel_id=1, source_target_pairs={{0,4},{1,5},{2,10},{3,11},{4,0},{5,1},{6,14},{7,15},{8,12},{9,13},... | collective-permute-start | bytes 6291464 | tf_op jit(solution)/shard_map/ppermute | solution.py:809
  541.0 12.5 %collective-permute-start.55 = (bf16[1,64,3072]{2,1,0:T(8,128)(2,1)}, bf16[1,64,3072]{2,1,0:T(8,128)(2,1)S(1)}, u32[]{:S(2)}, u32[]{:S(2)}) collective-permute-start(bf16[1,64,3072]{2,1,0:T(8,128)(2,1)} %get-tuple-element.252), channel_id=1, source_target_pairs={{0,8},{1,9},{2,6},{3,7},{4,12},{5,13},{6,2},{7,3},{8,0},{9,1},{10,... | collective-permute-start | bytes 1179656 | tf_op jit(solution)/shard_map/ppermute | solution.py:809
  553.4 15.5 %collective-permute-start.57 = (bf16[32,5120]{1,0:T(8,128)(2,1)S(1)}, bf16[32,5120]{1,0:T(8,128)(2,1)}, u32[]{:S(2)}, u32[]{:S(2)}) collective-permute-start(bf16[32,5120]{1,0:T(8,128)(2,1)S(1)} %fusion.57.refs_0_), channel_id=1, source_target_pairs={{0,16},{16,0},{1,17},{17,1},{2,18},{18,2},{3,19},{19,3},{4,20},{20... | collective-permute-start | bytes 983048 | tf_op jit(solution)/shard_map/ppermute | solution.py:800
  556.9 52.9 %collective-permute-start.56 = (bf16[1,32,3072]{2,1,0:T(8,128)(2,1)}, bf16[1,32,3072]{2,1,0:T(8,128)(2,1)}, u32[]{:S(2)}, u32[]{:S(2)}) collective-permute-start(bf16[1,32,3072]{2,1,0:T(8,128)(2,1)} %get-tuple-element.257), channel_id=1, source_target_pairs={{0,16},{16,0},{1,17},{17,1},{2,18},{18,2},{3,19},{19,3},{4,20},{20... | collective-permute-start | bytes 589832 | tf_op jit(solution)/shard_map/ppermute | solution.py:800
  571.5 39.4 %collective-permute-start.58 = (bf16[64,5120]{1,0:T(8,128)(2,1)}, bf16[64,5120]{1,0:T(8,128)(2,1)S(1)}, u32[]{:S(2)}, u32[]{:S(2)}) collective-permute-start(bf16[64,5120]{1,0:T(8,128)(2,1)} %shard_map.511.refs_0_), channel_id=1, source_target_pairs={{0,4},{1,5},{2,10},{3,11},{4,0},{5,1},{6,14},{7,15},{8,12},{9,13},... | collective-permute-start | bytes 1966088 | tf_op jit(solution)/shard_map/ppermute | solution.py:809
  578.8 100.8 %collective-permute-start.64 = (bf16[2048,1024]{1,0:T(8,128)(2,1)}, bf16[2048,1024]{1,0:T(8,128)(2,1)}, u32[]{:S(2)}, u32[]{:S(2)}) collective-permute-start(bf16[2048,1024]{1,0:T(8,128)(2,1)} %shard_map.517.own_ref), channel_id=1, source_target_pairs={{0,2},{2,0},{1,3},{3,1},{4,6},{6,4},{5,7},{7,5},{8,10},{10,8},{9,1... | collective-permute-start | bytes 12582920 | tf_op jit(solution)/shard_map/ppermute | solution.py:800
  614.9 23.7 %collective-permute-start.60 = (bf16[128,5120]{1,0:T(8,128)(2,1)}, bf16[128,5120]{1,0:T(8,128)(2,1)S(1)}, u32[]{:S(2)}, u32[]{:S(2)}) collective-permute-start(bf16[128,5120]{1,0:T(8,128)(2,1)} %shard_map.512.refs_0_), channel_id=1, source_target_pairs={{0,8},{1,9},{2,6},{3,7},{4,12},{5,13},{6,2},{7,3},{8,0},{9,1},{10,... | collective-permute-start | bytes 3932168 | tf_op jit(solution)/shard_map/ppermute | solution.py:809
  616.6 18.9 %collective-permute-start.59 = (bf16[32,3072]{1,0:T(8,128)(2,1)S(1)}, bf16[32,3072]{1,0:T(8,128)(2,1)S(1)}, u32[]{:S(2)}, u32[]{:S(2)}) collective-permute-start(bf16[32,3072]{1,0:T(8,128)(2,1)S(1)} %fusion.58.refs_0_), channel_id=1, source_target_pairs={{0,16},{16,0},{1,17},{17,1},{2,18},{18,2},{3,19},{19,3},{4,20},{20... | collective-permute-start | bytes 589832 | tf_op jit(solution)/shard_map/ppermute | solution.py:800
  644.4 50.0 %collective-permute-start.66 = (bf16[256,5120]{1,0:T(8,128)(2,1)}, bf16[256,5120]{1,0:T(8,128)(2,1)}, u32[]{:S(2)}, u32[]{:S(2)}) collective-permute-start(bf16[256,5120]{1,0:T(8,128)(2,1)} %shard_map.514.own_ref), channel_id=1, source_target_pairs={{0,2},{2,0},{1,3},{3,1},{4,6},{6,4},{5,7},{7,5},{8,10},{10,8},{9,1... | collective-permute-start | bytes 7864328 | tf_op jit(solution)/shard_map/ppermute | solution.py:800
  656.5 12.2 %collective-permute-start.62 = (bf16[128,3072]{1,0:T(8,128)(2,1)}, bf16[128,3072]{1,0:T(8,128)(2,1)S(1)}, u32[]{:S(2)}, u32[]{:S(2)}) collective-permute-start(bf16[128,3072]{1,0:T(8,128)(2,1)} %shard_map.515.refs_0_), channel_id=1, source_target_pairs={{0,4},{1,5},{2,10},{3,11},{4,0},{5,1},{6,14},{7,15},{8,12},{9,13},... | collective-permute-start | bytes 2359304 | tf_op jit(solution)/shard_map/ppermute | solution.py:809
  672.9 42.6 %collective-permute-start.71 = (bf16[256,3072]{1,0:T(8,128)(2,1)}, bf16[256,3072]{1,0:T(8,128)(2,1)}, u32[]{:S(2)}, u32[]{:S(2)}) collective-permute-start(bf16[256,3072]{1,0:T(8,128)(2,1)} %shard_map.516.own_ref), channel_id=1, source_target_pairs={{0,2},{2,0},{1,3},{3,1},{4,6},{6,4},{5,7},{7,5},{8,10},{10,8},{9,1... | collective-permute-start | bytes 4718600 | tf_op jit(solution)/shard_map/ppermute | solution.py:800
  675.7 36.1 %collective-permute-start.48 = (bf16[544,1024]{1,0:T(8,128)(2,1)}, bf16[544,1024]{1,0:T(8,128)(2,1)}, u32[]{:S(2)}, u32[]{:S(2)}) collective-permute-start(bf16[544,1024]{1,0:T(8,128)(2,1)} %slice.284), channel_id=1, source_target_pairs={{0,1},{1,0},{2,3},{3,2},{4,5},{5,4},{6,7},{7,6},{8,9},{9,8},{10,11... | collective-permute-start | bytes 3342344 | tf_op jit(solution)/shard_map/ppermute | solution.py:800
  676.7 17.5 %collective-permute-start.65 = (f32[20,1024]{1,0:T(8,128)S(1)}, f32[20,1024]{1,0:T(8,128)S(1)}, u32[]{:S(2)}, u32[]{:S(2)}) collective-permute-start(f32[20,1024]{1,0:T(8,128)S(1)} %pad_maximum_fusion.4), channel_id=1, source_target_pairs={{0,16},{16,0},{1,17},{17,1},{2,18},{18,2},{3,19},{19,3},{4,20},{20... | collective-permute-start | bytes 245768 | tf_op jit(solution)/shard_map/ppermute | solution.py:800
  (101 other events, 990.6 us)

commit v3 on v2

--- a/solution.py
+++ b/solution.py
@@ -423,7 +423,7 @@
 ):
     rows, width = normed.shape
     units = inner_own.shape[1]
-    chunk, quarter = 512, width // 4
+    chunk, quarter = units // 4, width // 4
     steps = units // chunk
     half_steps = steps // 2
     run = half_steps // 2
@@ -1166,8 +1166,7 @@
         mixed_self, log_self = attend_self(
             after(queries_self, *sent), self_pairs, no_bias, 0, 1
         )
-        sent = cross_pieces.second(mixed_self)
-        mixed_self = after(mixed_self, patches_other, *sent)
+        mixed_self = after(mixed_self, patches_other, *cross_pieces.second())
         inner_pieces = Pieces(first_piece([after(ffn_inner, patches_other)]))
     else:
         mixed_self, log_self = attend_self(queries_self, self_pairs, no_bias, 0, 1)
@@ -1193,13 +1192,18 @@
         keys = (patch_pairs, blank_bias)
         sent = inner_pieces.first(queries_cross) + (outer_pieces.own,)
         done = attend_cross(after(queries_cross, *sent), *keys, 0, 2)
-        sent = inner_pieces.second(done[0]) + outer_pieces.first(done[0])
+        sent = inner_pieces.second() + outer_pieces.first()
+        sent = [after(values, done[0]) for values in sent]
+        inner_pieces.both, inner_pieces.core_low, inner_pieces.core_high = sent[:3]
+        outer_pieces.low, outer_pieces.high, outer_pieces.core = sent[3:]
+        inner_pieces.third()
+        outer_pieces.second()
         done = attend_cross(after(queries_cross, *sent), *keys, 1, 2, done)
-        inner_pieces.third(done[0])
-        sent = outer_pieces.second(done[0])
-        inner_other = join(inner_pieces.places, inner_pieces.parts(done[0], *sent))
+        late = [after(values, done[0]) for values in (outer_pieces.both, inner_pieces.core_both)]
+        outer_pieces.both, inner_pieces.core_both = late
+        inner_other = join(inner_pieces.places, inner_pieces.parts(done[0]))
         mixed_cross, log_cross = done
-        outer_pieces.third(inner_other)
+        outer_pieces.third()
         mixed_cross = after(mixed_cross, inner_other)
     else:
         mixed_cross, log_cross = attend_cross(queries_cross, patch_pairs, blank_bias, 0, 1)

time: 730 us -> 724 us (level)
  waiting for transfers between devices: 154 us -> 142 us
    unnamed x184 -> x166, local copies, waits for them, and re-layouts: 19.6 us -> 15.6 us
  transfers between devices with their start and end apart: 72 -> 72, of which waited for: 26 -> 21; matrix products, arithmetic and copies ran while one was open for 17% -> 19% of each run, Pallas kernels for 29% -> 34%
where the time goes in v3:
time: 724 us; the launch traced here: 717 us
  Pallas kernels  321 us (44%)
  waiting for transfers between devices  142 us (20%)
  starting transfers between devices  101 us (14%)
  matrix products  73.5 us (10%)
  local copies, waits for them, and re-layouts  39.4 us (5%)
  other arithmetic  38 us (5%)
    ppermute x29, waiting for transfers between devices, exchange(): lax.ppermute(values, square, [(i, i ^ flip[i // 2 % 2]) for i in range(16)])  68.3 us
    ppermute x41, waiting for transfers between devices, swap(): return lax.ppermute(values, axis_name, [(0, 1), (1, 0)])  64.8 us
    ppermute x41, starting transfers between devices, swap(): return lax.ppermute(values, axis_name, [(0, 1), (1, 0)])  60.2 us
    pallas_call x3, Pallas kernels, attend(): pl.pallas_call(skip_refs(functools.partial(attend_kernel, plan), 5, len(i...  47.5 us
    pallas_call x11, Pallas kernels, join(): pl.pallas_call(functools.partial(join_kernel, count), grid_spec=pltpu.Pre...  42 us
    pallas_call x2, Pallas kernels, attend_back(): pl.pallas_call(skip_refs(functools.partial(attend_back_kernel, plan), 8,...  41.8 us
    dot_general x8, matrix products, dot_nt(): lax.dot_general(left_side, right_side, (((1,), (1,)), ((), ())), preferre...  41.4 us
    pallas_call x1, Pallas kernels, ffn_both_ways(): pl.pallas_call(functools.partial(ffn_kernel, half_steps), grid_spec=pltpu...  40.5 us
  transfers between devices with their start and end apart: 72, of which 21 were waited for; matrix products, arithmetic and copies ran while one was open for 19% of the time, Pallas kernels for 34%

profile of v3, /device:TPU:0, one launch (start us, length us, event | category | flops | bytes accessed | tf_op | source)
XLA Modules:
  0.0 717.1 jit_solution(11027450491859858099)
XLA Ops:
  8.8 9.5 %collective-permute-done.1 = bf16[68,128]{1,0:T(8,128)(2,1)S(1)} collective-permute-done((bf16[68,128]{1,0:T(8,128)(2,1)S(1)}, bf16[68,128]{1,0:T(8,128)(2,1)S(1)}, u32[]{:S(2)}, u32[]{:S(2)}) %collective-permute-start.1) | collective-permute-done | bytes 17440 | tf_op jit(solution)/shard_map/ppermute | solution.py:800
  34.8 6.3 collective-permute-done.5.refs_7_
  42.9 5.8 collective-permute-done.2
  53.0 8.7 %shard_map.484 = bf16[1024,4096]{1,0:T(8,128)(2,1)} custom-call(s32[9]{0:T(128)} %stack.366.place_ref, bf16[512,1024]{1,0:T(8,128)(2,1)} %refs_0_.2, bf16[512,1024]{1,0:T(8,128)(2,1)} %refs_1_.2, bf16[512,1024]{1,0:T(8,128)(2,1)} %refs_2_.2, bf16[512,1024]{1,0:T(8,128)(2,1)} %refs_3_.2, bf16[64,4096]{1,0:T(8,128)(2,1)} %copy-done.32, ...), custom_call_target="tpu_custom_call" | custom-call | flops 1 | bytes 1 | tf_op jit(solution)/shard_map/pallas_call | solution.py:312
  65.0 4.6 multiply_convert_fusion.1.refs_1_
  72.0 10.5 %collective-permute-done.11.refs_5_ = bf16[64,4096]{1,0:T(8,128)(2,1)} collective-permute-done((bf16[64,4096]{1,0:T(8,128)(2,1)}, bf16[64,4096]{1,0:T(8,128)(2,1)}, u32[]{:S(2)}, u32[]{:S(2)}) %collective-permute-start.11) | collective-permute-done | bytes 524320 | tf_op jit(solution)/shard_map/ppermute | solution.py:809
  85.7 8.2 %add_convert_fusion.refs_2_.refs_3_.refs_5_.refs_6_ = bf16[1024,2048]{1,0:T(8,128)(2,1)} fusion(f32[2048]{0:T(1024)S(1)} %pad_convert_fusion.1, bf16[1024,1024]{1,0:T(8,128)(2,1)S(1)} %fusion.6.refs_1_, bf16[1024,4096]{1,0:T(8,128)(2,1)} %shard_map.484), kind=kOutput, calls=%fused_computation.1 | convolution fusion | flops 4299161600 | bytes 10493952 | tf_op jit(solution)/shard_map/dot_general | solution.py:38
  94.8 16.4 %shard_map.485 = (bf16[512,1024]{1,0:T(8,128)(2,1)}, f32[8,2,512]{2,1,0:T(2,128)}) custom-call(s32[4]{0:T(128)} %pad_add_fusion.refs_0_, bf16[512,1024]{1,0:T(8,128)(2,1)} %multiply_convert_fusion.1.refs_1_, bf16[1024,2048]{1,0:T(8,128)(2,1)} %add_convert_fusion.refs_2_.refs_3_.refs_5_.refs_6_, ...), custom_call_target="tpu_custom_call" | custom-call | flops 1 | bytes 1 | tf_op jit(solution)/shard_map/pallas_call | solution.py:211
  117.0 6.5 collective-permute-start.19
  126.0 8.4 %shard_map.486 = bf16[1024,4096]{1,0:T(8,128)(2,1)} custom-call(s32[9]{0:T(128)} %stack.366.place_ref, bf16[512,1024]{1,0:T(8,128)(2,1)} %refs_0_.3, bf16[512,1024]{1,0:T(8,128)(2,1)} %refs_1_.3, bf16[512,1024]{1,0:T(8,128)(2,1)} %refs_2_.3, bf16[512,1024]{1,0:T(8,128)(2,1)} %refs_3_.3, bf16[64,4096]{1,0:T(8,128)(2,1)} %collective-permute-done.10.refs_4_, ...), custom_call_target="tpu_custom_call" | custom-call | flops 1 | bytes 1 | tf_op jit(solution)/shard_map/pallas_call | solution.py:312
  141.6 11.7 %collective-permute-done.20.refs_1_ = bf16[64,4096]{1,0:T(8,128)(2,1)} collective-permute-done((bf16[64,4096]{1,0:T(8,128)(2,1)}, bf16[64,4096]{1,0:T(8,128)(2,1)}, u32[]{:S(2)}, u32[]{:S(2)}) %collective-permute-start.20) | collective-permute-done | bytes 524320 | tf_op jit(solution)/shard_map/ppermute | solution.py:809
  159.5 5.9 collective-permute-done.21.refs_3_
  165.4 8.6 %fusion.refs_2_.refs_3_.refs_5_.refs_6_ = bf16[1088,2048]{1,0:T(8,128)(2,1)} fusion(bf16[1088,1024]{1,0:T(8,128)(2,1)S(1)} %pad_maximum_fusion.refs_1_, f32[2048]{0:T(1024)S(1)} %pad_convert_fusion, bf16[1024,4096]{1,0:T(8,128)(2,1)} %shard_map.486), kind=kOutput, calls=%fused_computation.2 | convolution fusion | flops 4567859200 | bytes 10887168 | tf_op jit(solution)/shard_map/dot_general | solution.py:38
  174.0 15.5 %shard_map.487 = (bf16[512,1024]{1,0:T(8,128)(2,1)}, f32[8,2,512]{2,1,0:T(2,128)}) custom-call(s32[4]{0:T(128)} %pad_add_fusion.refs_0_, bf16[512,1024]{1,0:T(8,128)(2,1)} %multiply_convert_fusion.refs_1_, bf16[1088,2048]{1,0:T(8,128)(2,1)} %fusion.refs_2_.refs_3_.refs_5_.refs_6_, bf16[1088,2048]{1,0:T(8,128)(2,1)} %fusion.refs_2_.refs_3_.refs_5_.refs_6_, ...), custom_call_target="tpu_custom_call" | custom-call | flops 1 | bytes 1 | tf_op jit(solution)/shard_map/pallas_call | solution.py:211
  192.8 15.5 %shard_map.488 = (bf16[512,1024]{1,0:T(8,128)(2,1)}, f32[8,2,512]{2,1,0:T(2,128)}) custom-call(s32[4]{0:T(128)} %pad_add_fusion.refs_0_, bf16[512,1024]{1,0:T(8,128)(2,1)} %multiply_convert_fusion.refs_1_, bf16[1088,2048]{1,0:T(8,128)(2,1)} %fusion.refs_2_.refs_3_.refs_5_.refs_6_, ...), custom_call_target="tpu_custom_call", output_to_operand_aliasing={{0}: (5, {}), {1}: (6, {})} | custom-call | flops 1 | bytes 1 | tf_op jit(solution)/shard_map/pallas_call | solution.py:211
  208.6 5.5 shard_map.489.refs_6_.refs_7_
  220.3 5.5 shard_map.490.refs_9_
  225.8 40.5 %shard_map.491 = (bf16[512,1024]{1,0:T(8,128)(2,1)}, f32[512,1024]{1,0:T(8,128)}, f32[1,4096]{1,0:T(1,128)}, bf16[2,1024,1024]{2,1,0:T(8,128)(2,1)}, bf16[2,1024...) custom-call(s32[20]{0:T(128)} %stack.355.place_ref, ...), custom_call_target="tpu_custom_call" | custom-call | flops 1 | bytes 1 | tf_op jit(solution)/shard_map/pallas_call | solution.py:462
  272.1 4.2 fusion.43.refs_3_
  279.9 10.9 %shard_map.492 = (bf16[2,1024,1024]{2,1,0:T(8,128)(2,1)}, bf16[1,1024,1024]{2,1,0:T(8,128)(2,1)}, bf16[1,1024,1024]{2,1,0:T(8,128)(2,1)}) custom-call(s32[4]{0:T(128)} %pad_add_fusion.1.place_ref, bf16[4,512,1024]{2,1,0:T(8,128)(2,1)} %bitcast.202, bf16[4,512,1024]{2,1,0:T(8,128)(2,1)} %collective-permute-done.35.refs_1_.refs_5_, ...), custom_call_target="tpu_custom_call" | custom-call | flops 1 | bytes 1 | tf_op jit(solution)/shard_map/pallas_call | solution.py:707
  292.4 26.8 %shard_map.493 = (bf16[512,1024]{1,0:T(8,128)(2,1)}, bf16[1088,1024]{1,0:T(8,128)(2,1)}, bf16[1088,1024]{1,0:T(8,128)(2,1)}) custom-call(s32[4]{0:T(128)} %pad_add_fusion.refs_0_, bf16[512,1024]{1,0:T(8,128)(2,1)} %multiply_convert_fusion.refs_1_, bf16[512,1024]{1,0:T(8,128)(2,1)} %get-tuple-element.181.refs_2_, bf16[512,1024]{1,0:T(8,128)(2,1)} %fusion.43.refs_3_, ...), custom_call_target="tpu_custom_call" | custom-call | flops 1 | bytes 1 | tf_op jit(solution)/shard_map/pallas_call | solution.py:235
  326.7 4.2 fusion.40.refs_3_
  330.9 19.3 %shard_map.494 = (bf16[2,256,5120]{2,1,0:T(8,128)(2,1)}, bf16[2,256,5120]{2,1,0:T(8,128)(2,1)}) custom-call(s32[2]{0:T(128)} %pad_add_fusion.3.place_ref, bf16[512,1024]{1,0:T(8,128)(2,1)} %add_convert_fusion.2.refs_0_, bf16[1088,1024]{1,0:T(8,128)(2,1)} %copy-done.12, bf16[512,1024]{1,0:T(8,128)(2,1)} %get-tuple-element.181.refs_2_, ...), custom_call_target="tpu_custom_call" | custom-call | flops 1 | bytes 1 | tf_op jit(solution)/shard_map/pallas_call | solution.py:570
  350.2 7.9 %shard_map.495 = (bf16[2,512,1024]{2,1,0:T(8,128)(2,1)}, bf16[2,512,1024]{2,1,0:T(8,128)(2,1)}) custom-call(s32[8]{0:T(128)} %stack.399.place_ref, bf16[4,512,1024]{2,1,0:T(8,128)(2,1)} %bitcast.200, bf16[2,512,1024]{2,1,0:T(8,128)(2,1)} %bitcast.54.refs_1_.refs_4_, bf16[2,512,1024]{2,1,0:T(8,128)(2,1)} %bitcast.55.refs_2_.refs_5_, ...), custom_call_target="tpu_custom_call" | custom-call | flops 1 | bytes 1 | tf_op jit(solution)/shard_map/pallas_call | solution.py:660
  359.0 8.1 %collective-permute-done.39.came_a.came_b = bf16[4,128,5120]{2,1,0:T(8,128)(2,1)} collective-permute-done((bf16[4,128,5120]{2,1,0:T(8,128)(2,1)}, bf16[4,128,5120]{2,1,0:T(8,128)(2,1)}, u32[]{:S(2)}, u32[]{:S(2)}) %collective-permute-start.39) | collective-permute-done | bytes 5242912 | tf_op jit(solution)/shard_map/ppermute | solution.py:800
  367.2 7.6 %shard_map.496 = (bf16[2,128,5120]{2,1,0:T(8,128)(2,1)}, bf16[1,128,5120]{2,1,0:T(8,128)(2,1)}, bf16[1,128,5120]{2,1,0:T(8,128)(2,1)}) custom-call(s32[4]{0:T(128)} %pad_add_fusion.2.place_ref, bf16[4,128,5120]{2,1,0:T(8,128)(2,1)} %bitcast.198, bf16[4,128,5120]{2,1,0:T(8,128)(2,1)} %collective-permute-done.39.came_a.came_b, ...), custom_call_target="tpu_custom_call" | custom-call | flops 1 | bytes 1 | tf_op jit(solution)/shard_map/pallas_call | solution.py:623
  376.7 15.0 %shard_map.497 = (bf16[512,1024]{1,0:T(8,128)(2,1)}, bf16[1024,1024]{1,0:T(8,128)(2,1)}, bf16[1024,1024]{1,0:T(8,128)(2,1)}) custom-call(s32[4]{0:T(128)} %pad_add_fusion.refs_0_, bf16[512,1024]{1,0:T(8,128)(2,1)} %multiply_convert_fusion.1.refs_1_, bf16[512,1024]{1,0:T(8,128)(2,1)} %get-tuple-element.162.refs_3_.refs_2_, bf16[512,1024]{1,0:T(8,128)(2,1)} %fusion.40.refs_3_, ...), custom_call_target="tpu_custom_call" | custom-call | flops 1 | bytes 1 | tf_op jit(solution)/shard_map/pallas_call | solution.py:235
  391.7 6.6 collective-permute-done.41
  407.3 12.9 %shard_map.499 = (bf16[2,256,3072]{2,1,0:T(8,128)(2,1)}, bf16[2,256,3072]{2,1,0:T(8,128)(2,1)}) custom-call(s32[2]{0:T(128)} %pad_add_fusion.3.place_ref, bf16[512,1024]{1,0:T(8,128)(2,1)} %slice.184.refs_0_, bf16[1024,1024]{1,0:T(8,128)(2,1)} %copy-done.6, bf16[512,1024]{1,0:T(8,128)(2,1)} %get-tuple-element.228.refs_2_.refs_6_, ...), custom_call_target="tpu_custom_call" | custom-call | flops 1 | bytes 1 | tf_op jit(solution)/shard_map/pallas_call | solution.py:570
  420.2 7.2 %collective-permute-done.42 = bf16[1,512,1024]{2,1,0:T(8,128)(2,1)} collective-permute-done((bf16[1,512,1024]{2,1,0:T(8,128)(2,1)}, bf16[1,512,1024]{2,1,0:T(8,128)(2,1)}, u32[]{:S(2)}, u32[]{:S(2)}) %collective-permute-start.42) | collective-permute-done | bytes 1048608 | tf_op jit(solution)/shard_map/ppermute | solution.py:809
  430.5 5.8 shard_map.501
  450.9 6.0 fusion.21
  456.9 5.7 shard_map.502
  462.6 6.3 fusion.13
  479.4 7.5 %convolution_add_fusion.1 = f32[1088,1024]{1,0:T(8,128)} fusion(f32[1088,1024]{1,0:T(8,128)} %fusion.13, bf16[1088,1024]{1,0:T(8,128)(2,1)S(1)} %copy-done.21, bf16[1024,4096]{1,0:T(8,128)(2,1)} %shard_map.486), kind=kOutput, calls=%fused_computation.7 | convolution fusion | flops 2282815488 | bytes 13238272 | tf_op jit(solution)/shard_map/dot_general | solution.py:32
  506.1 5.4 multiply_reduce_fusion.6
  515.3 9.6 %shard_map.507 = f32[16,1024]{1,0:T(8,128)} custom-call(f32[512,1024]{1,0:T(8,128)} %bitcast_convert_fusion.refs_0_, f32[512,1024]{1,0:T(8,128)} %get-tuple-element.320.refs_1_, f32[512,1024]{1,0:T(8,128)} %copy-done.3, f32[512,1024]{1,0:T(8,128)} %copy-done.16, f32[512,1024]{1,0:T(8,128)} %copy-done, f32[512,1024]{1,0:T(8,128)} %get-tuple-element.185.refs_5_, ...), custom_call_target="tpu_custom_call" | custom-call | flops 1 | bytes 1 | tf_op jit(solution)/shard_map/pallas_call | solution.py:352
  535.3 10.2 %collective-permute-done.53 = bf16[1,32,5120]{2,1,0:T(8,128)(2,1)S(1)} collective-permute-done((bf16[1,32,5120]{2,1,0:T(8,128)(2,1)S(1)}, bf16[1,32,5120]{2,1,0:T(8,128)(2,1)S(1)}, u32[]{:S(2)}, u32[]{:S(2)}) %collective-permute-start.53) | collective-permute-done | bytes 327712 | tf_op jit(solution)/shard_map/ppermute | solution.py:800
  554.2 7.7 %collective-permute-done.57.refs_1_ = bf16[32,5120]{1,0:T(8,128)(2,1)} collective-permute-done((bf16[32,5120]{1,0:T(8,128)(2,1)S(1)}, bf16[32,5120]{1,0:T(8,128)(2,1)}, u32[]{:S(2)}, u32[]{:S(2)}) %collective-permute-start.57) | collective-permute-done | bytes 327712 | tf_op jit(solution)/shard_map/ppermute | solution.py:800
  566.0 5.5 shard_map.517.own_ref
  571.4 31.6 %collective-permute-start.64 = (bf16[2048,1024]{1,0:T(8,128)(2,1)}, bf16[2048,1024]{1,0:T(8,128)(2,1)}, u32[]{:S(2)}, u32[]{:S(2)}) collective-permute-start(bf16[2048,1024]{1,0:T(8,128)(2,1)} %shard_map.517.own_ref), channel_id=1, source_target_pairs={{0,2},{2,0},{1,3},{3,1},{4,6},{6,4},{5,7},{7,5},{8,10},{10,8},{9,1... | collective-permute-start | bytes 12582920 | tf_op jit(solution)/shard_map/ppermute | solution.py:800
  610.4 18.8 %collective-permute-done.59.refs_1_ = bf16[32,3072]{1,0:T(8,128)(2,1)S(1)} collective-permute-done((bf16[32,3072]{1,0:T(8,128)(2,1)S(1)}, bf16[32,3072]{1,0:T(8,128)(2,1)S(1)}, u32[]{:S(2)}, u32[]{:S(2)}) %collective-permute-start.59) | collective-permute-done | bytes 196640 | tf_op jit(solution)/shard_map/ppermute | solution.py:800
  633.4 4.7 shard_map.514.own_ref
  640.1 5.8 collective-permute-done.61.refs_1_
  650.4 11.2 %collective-permute-done.62.refs_1_ = bf16[128,3072]{1,0:T(8,128)(2,1)S(1)} collective-permute-done((bf16[128,3072]{1,0:T(8,128)(2,1)}, bf16[128,3072]{1,0:T(8,128)(2,1)S(1)}, u32[]{:S(2)}, u32[]{:S(2)}) %collective-permute-start.62) | collective-permute-done | bytes 786464 | tf_op jit(solution)/shard_map/ppermute | solution.py:809
  672.7 14.7 %shard_map.518 = (f32[2048,1024]{1,0:T(8,128)}, f32[512,4096]{1,0:T(8,128)}) custom-call(s32[2]{0:T(128)} %pad_add_fusion.3.place_ref, bf16[2048,1024]{1,0:T(8,128)(2,1)} %shard_map.517.own_ref, bf16[2048,1024]{1,0:T(8,128)(2,1)} %collective-permute-done.64.other_ref), custom_call_target="tpu_custom_call" | custom-call | flops 1 | bytes 1 | tf_op jit(solution)/shard_map/pallas_call | solution.py:754
  687.5 8.1 %shard_map.519 = (f32[512,1024]{1,0:T(8,128)}, f32[512,1024]{1,0:T(8,128)}, f32[512,1024]{1,0:T(8,128)}, f32[512,1024]{1,0:T(8,128)}, f32[512,1024]{1,0:T(8,128)}) custom-call(s32[2]{0:T(128)} %pad_add_fusion.3.place_ref, bf16[256,5120]{1,0:T(8,128)(2,1)} %shard_map.514.own_ref, bf16[256,5120]{1,0:T(8,128)(2,1)} %collective-permute-done.66.other_ref), custom_call_target="tpu_custom_call" | custom-call | flops 1 | bytes 1 | tf_op jit(solution)/shard_map/pallas_call | solution.py:754
  709.3 6.0 shard_map.520
  (401 shorter events, 219.0 us)
Async XLA Ops:
  3.0 15.4 %collective-permute-start = (bf16[64,4096]{1,0:T(8,128)(2,1)S(1)}, bf16[64,4096]{1,0:T(8,128)(2,1)S(1)}, u32[]{:S(2)}, u32[]{:S(2)}) collective-permute-start(bf16[64,4096]{1,0:T(8,128)(2,1)S(1)} %pad_maximum_fusion.2), channel_id=1, source_target_pairs={{0,1},{1,0},{2,3},{3,2},{4,5},{5,4},{6,7},{7,6},{8,9},{9,8},{10,11... | collective-permute-start | bytes 1572872 | tf_op jit(solution)/shard_map/ppermute | solution.py:800
  24.4 24.4 %collective-permute-start.2 = (bf16[512,1024]{1,0:T(8,128)(2,1)S(1)}, bf16[512,1024]{1,0:T(8,128)(2,1)S(1)}, u32[]{:S(2)}, u32[]{:S(2)}) collective-permute-start(bf16[512,1024]{1,0:T(8,128)(2,1)S(1)} %bitcast.194), channel_id=1, source_target_pairs={{0,1},{2,3},{4,5},{6,7},{8,9},{10,11},{12,13},{14,15},{16,17},{18,... | collective-permute-start | bytes 3145736 | tf_op jit(solution)/shard_map/ppermute | solution.py:1113
  34.1 17.1 %collective-permute-start.6 = (bf16[64,4096]{1,0:T(8,128)(2,1)S(1)}, bf16[64,4096]{1,0:T(8,128)(2,1)S(1)}, u32[]{:S(2)}, u32[]{:S(2)}) collective-permute-start(bf16[64,4096]{1,0:T(8,128)(2,1)S(1)} %collective-permute-done.refs_4_), channel_id=1, source_target_pairs={{0,2},{2,0},{1,3},{3,1},{4,6},{6,4},{5,7},{7,5},{8,10},{10,8},{9,1... | collective-permute-start | bytes 1572872 | tf_op jit(solution)/shard_map/ppermute | solution.py:800
  34.2 17.0 %collective-permute-start.7 = (bf16[64,4096]{1,0:T(8,128)(2,1)S(1)}, bf16[64,4096]{1,0:T(8,128)(2,1)S(1)}, u32[]{:S(2)}, u32[]{:S(2)}) collective-permute-start(bf16[64,4096]{1,0:T(8,128)(2,1)S(1)} %collective-permute-done.3.refs_5_), channel_id=1, source_target_pairs={{0,2},{2,0},{1,3},{3,1},{4,6},{6,4},{5,7},{7,5},{8,10},{10,8},{9,1... | collective-permute-start | bytes 1572872 | tf_op jit(solution)/shard_map/ppermute | solution.py:800
  34.7 16.6 %collective-permute-start.8 = (bf16[64,4096]{1,0:T(8,128)(2,1)S(1)}, bf16[64,4096]{1,0:T(8,128)(2,1)S(1)}, u32[]{:S(2)}, u32[]{:S(2)}) collective-permute-start(bf16[64,4096]{1,0:T(8,128)(2,1)S(1)} %collective-permute-done.4.refs_6_), channel_id=1, source_target_pairs={{0,2},{2,0},{1,3},{3,1},{4,6},{6,4},{5,7},{7,5},{8,10},{10,8},{9,1... | collective-permute-start | bytes 1572872 | tf_op jit(solution)/shard_map/ppermute | solution.py:800
  48.8 20.8 %collective-permute-start.10 = (bf16[64,4096]{1,0:T(8,128)(2,1)}, bf16[64,4096]{1,0:T(8,128)(2,1)}, u32[]{:S(2)}, u32[]{:S(2)}) collective-permute-start(bf16[64,4096]{1,0:T(8,128)(2,1)} %pad_maximum_fusion.3), channel_id=1, source_target_pairs={{0,1},{1,0},{2,3},{3,2},{4,5},{5,4},{6,7},{7,6},{8,9},{9,8},{10,11... | collective-permute-start | bytes 1572872 | tf_op jit(solution)/shard_map/ppermute | solution.py:800
  70.1 15.1 %collective-permute-start.12 = (bf16[64,4096]{1,0:T(8,128)(2,1)}, bf16[64,4096]{1,0:T(8,128)(2,1)}, u32[]{:S(2)}, u32[]{:S(2)}) collective-permute-start(bf16[64,4096]{1,0:T(8,128)(2,1)} %collective-permute-done.10.refs_4_), channel_id=1, source_target_pairs={{0,8},{1,9},{2,6},{3,7},{4,12},{5,13},{6,2},{7,3},{8,0},{9,1},{10,... | collective-permute-start | bytes 1572872 | tf_op jit(solution)/shard_map/ppermute | solution.py:809
  71.8 39.6 %collective-permute-start.14 = (bf16[544,1024]{1,0:T(8,128)(2,1)}, bf16[544,1024]{1,0:T(8,128)(2,1)}, u32[]{:S(2)}, u32[]{:S(2)}) collective-permute-start(bf16[544,1024]{1,0:T(8,128)(2,1)} %bitcast.224), channel_id=1, source_target_pairs={{0,1},{1,0},{2,3},{3,2},{4,5},{5,4},{6,7},{7,6},{8,9},{9,8},{10,11... | collective-permute-start | bytes 3342344 | tf_op jit(solution)/shard_map/ppermute | solution.py:800
  71.9 22.1 %collective-permute-start.13 = (bf16[64,4096]{1,0:T(8,128)(2,1)}, bf16[64,4096]{1,0:T(8,128)(2,1)S(1)}, u32[]{:S(2)}, u32[]{:S(2)}) collective-permute-start(bf16[64,4096]{1,0:T(8,128)(2,1)} %collective-permute-done.10.refs_4_), channel_id=1, source_target_pairs={{0,2},{2,0},{1,3},{3,1},{4,6},{6,4},{5,7},{7,5},{8,10},{10,8},{9,1... | collective-permute-start | bytes 1572872 | tf_op jit(solution)/shard_map/ppermute | solution.py:800
  82.5 28.8 %collective-permute-start.15 = (bf16[64,4096]{1,0:T(8,128)(2,1)}, bf16[64,4096]{1,0:T(8,128)(2,1)}, u32[]{:S(2)}, u32[]{:S(2)}) collective-permute-start(bf16[64,4096]{1,0:T(8,128)(2,1)} %collective-permute-done.11.refs_5_), channel_id=1, source_target_pairs={{0,8},{1,9},{2,6},{3,7},{4,12},{5,13},{6,2},{7,3},{8,0},{9,1},{10,... | collective-permute-start | bytes 1572872 | tf_op jit(solution)/shard_map/ppermute | solution.py:809
  85.2 26.2 %collective-permute-start.16 = (bf16[64,4096]{1,0:T(8,128)(2,1)}, bf16[64,4096]{1,0:T(8,128)(2,1)}, u32[]{:S(2)}, u32[]{:S(2)}) collective-permute-start(bf16[64,4096]{1,0:T(8,128)(2,1)} %collective-permute-done.11.refs_5_), channel_id=1, source_target_pairs={{0,2},{2,0},{1,3},{3,1},{4,6},{6,4},{5,7},{7,5},{8,10},{10,8},{9,1... | collective-permute-start | bytes 1572872 | tf_op jit(solution)/shard_map/ppermute | solution.py:800
  85.2 26.2 %collective-permute-start.17 = (bf16[64,4096]{1,0:T(8,128)(2,1)}, bf16[64,4096]{1,0:T(8,128)(2,1)}, u32[]{:S(2)}, u32[]{:S(2)}) collective-permute-start(bf16[64,4096]{1,0:T(8,128)(2,1)} %collective-permute-done.12.refs_6_), channel_id=1, source_target_pairs={{0,2},{2,0},{1,3},{3,1},{4,6},{6,4},{5,7},{7,5},{8,10},{10,8},{9,1... | collective-permute-start | bytes 1572872 | tf_op jit(solution)/shard_map/ppermute | solution.py:800
  117.0 21.7 %collective-permute-start.19 = (bf16[64,4096]{1,0:T(8,128)(2,1)}, bf16[64,4096]{1,0:T(8,128)(2,1)}, u32[]{:S(2)}, u32[]{:S(2)}) collective-permute-start(bf16[64,4096]{1,0:T(8,128)(2,1)} %constant_dynamic-slice_fusion.2), channel_id=1, source_target_pairs={{0,1},{1,0},{2,3},{3,2},{4,5},{5,4},{6,7},{7,6},{8,9},{9,8},{10,11... | collective-permute-start | bytes 1572872 | tf_op jit(solution)/shard_map/ppermute | solution.py:800
  139.4 18.2 %collective-permute-start.22 = (bf16[64,4096]{1,0:T(8,128)(2,1)}, bf16[64,4096]{1,0:T(8,128)(2,1)}, u32[]{:S(2)}, u32[]{:S(2)}) collective-permute-start(bf16[64,4096]{1,0:T(8,128)(2,1)} %collective-permute-done.19.refs_0_), channel_id=1, source_target_pairs={{0,8},{1,9},{2,6},{3,7},{4,12},{5,13},{6,2},{7,3},{8,0},{9,1},{10,... | collective-permute-start | bytes 1572872 | tf_op jit(solution)/shard_map/ppermute | solution.py:809
  139.5 20.0 %collective-permute-start.23 = (bf16[64,4096]{1,0:T(8,128)(2,1)}, bf16[64,4096]{1,0:T(8,128)(2,1)}, u32[]{:S(2)}, u32[]{:S(2)}) collective-permute-start(bf16[64,4096]{1,0:T(8,128)(2,1)} %collective-permute-done.19.refs_0_), channel_id=1, source_target_pairs={{0,2},{2,0},{1,3},{3,1},{4,6},{6,4},{5,7},{7,5},{8,10},{10,8},{9,1... | collective-permute-start | bytes 1572872 | tf_op jit(solution)/shard_map/ppermute | solution.py:800
  156.3 33.2 %collective-permute-start.25 = (bf16[64,4096]{1,0:T(8,128)(2,1)}, bf16[64,4096]{1,0:T(8,128)(2,1)}, u32[]{:S(2)}, u32[]{:S(2)}) collective-permute-start(bf16[64,4096]{1,0:T(8,128)(2,1)} %collective-permute-done.20.refs_1_), channel_id=1, source_target_pairs={{0,2},{2,0},{1,3},{3,1},{4,6},{6,4},{5,7},{7,5},{8,10},{10,8},{9,1... | collective-permute-start | bytes 1572872 | tf_op jit(solution)/shard_map/ppermute | solution.py:800
  156.4 36.1 %collective-permute-start.27 = (bf16[256,1024]{1,0:T(8,128)(2,1)}, bf16[256,1024]{1,0:T(8,128)(2,1)}, u32[]{:S(2)}, u32[]{:S(2)}) collective-permute-start(bf16[256,1024]{1,0:T(8,128)(2,1)} %collective-permute-done.24.refs_0_), channel_id=1, source_target_pairs={{0,4},{1,5},{2,10},{3,11},{4,0},{5,1},{6,14},{7,15},{8,12},{9,13},... | collective-permute-start | bytes 1572872 | tf_op jit(solution)/shard_map/ppermute | solution.py:809
  157.6 35.2 %collective-permute-start.28 = (bf16[256,1024]{1,0:T(8,128)(2,1)}, bf16[256,1024]{1,0:T(8,128)(2,1)}, u32[]{:S(2)}, u32[]{:S(2)}) collective-permute-start(bf16[256,1024]{1,0:T(8,128)(2,1)} %collective-permute-done.24.refs_0_), channel_id=1, source_target_pairs={{0,8},{1,9},{2,6},{3,7},{4,12},{5,13},{6,2},{7,3},{8,0},{9,1},{10,... | collective-permute-start | bytes 1572872 | tf_op jit(solution)/shard_map/ppermute | solution.py:809
  159.5 33.3 %collective-permute-start.29 = (bf16[256,1024]{1,0:T(8,128)(2,1)}, bf16[256,1024]{1,0:T(8,128)(2,1)}, u32[]{:S(2)}, u32[]{:S(2)}) collective-permute-start(bf16[256,1024]{1,0:T(8,128)(2,1)} %collective-permute-done.24.refs_0_), channel_id=1, source_target_pairs={{0,2},{2,0},{1,3},{3,1},{4,6},{6,4},{5,7},{7,5},{8,10},{10,8},{9,1... | collective-permute-start | bytes 1572872 | tf_op jit(solution)/shard_map/ppermute | solution.py:800
  165.4 27.1 %collective-permute-start.26 = (bf16[64,4096]{1,0:T(8,128)(2,1)}, bf16[64,4096]{1,0:T(8,128)(2,1)}, u32[]{:S(2)}, u32[]{:S(2)}) collective-permute-start(bf16[64,4096]{1,0:T(8,128)(2,1)} %collective-permute-done.22.refs_2_), channel_id=1, source_target_pairs={{0,2},{2,0},{1,3},{3,1},{4,6},{6,4},{5,7},{7,5},{8,10},{10,8},{9,1... | collective-permute-start | bytes 1572872 | tf_op jit(solution)/shard_map/ppermute | solution.py:800
  189.5 19.1 %collective-permute-start.30 = (bf16[64,4096]{1,0:T(8,128)(2,1)}, bf16[64,4096]{1,0:T(8,128)(2,1)}, u32[]{:S(2)}, u32[]{:S(2)}) collective-permute-start(bf16[64,4096]{1,0:T(8,128)(2,1)} %collective-permute-done.21.refs_3_), channel_id=1, source_target_pairs={{0,2},{2,0},{1,3},{3,1},{4,6},{6,4},{5,7},{7,5},{8,10},{10,8},{9,1... | collective-permute-start | bytes 1572872 | tf_op jit(solution)/shard_map/ppermute | solution.py:800
  192.5 24.9 %collective-permute-start.31 = (bf16[256,1024]{1,0:T(8,128)(2,1)}, bf16[256,1024]{1,0:T(8,128)(2,1)S(1)}, u32[]{:S(2)}, u32[]{:S(2)}) collective-permute-start(bf16[256,1024]{1,0:T(8,128)(2,1)} %collective-permute-done.27.refs_1_), channel_id=1, source_target_pairs={{0,8},{1,9},{2,6},{3,7},{4,12},{5,13},{6,2},{7,3},{8,0},{9,1},{10,... | collective-permute-start | bytes 1572872 | tf_op jit(solution)/shard_map/ppermute | solution.py:809
  192.5 27.0 %collective-permute-start.32 = (bf16[256,1024]{1,0:T(8,128)(2,1)}, bf16[256,1024]{1,0:T(8,128)(2,1)}, u32[]{:S(2)}, u32[]{:S(2)}) collective-permute-start(bf16[256,1024]{1,0:T(8,128)(2,1)} %collective-permute-done.27.refs_1_), channel_id=1, source_target_pairs={{0,2},{2,0},{1,3},{3,1},{4,6},{6,4},{5,7},{7,5},{8,10},{10,8},{9,1... | collective-permute-start | bytes 1572872 | tf_op jit(solution)/shard_map/ppermute | solution.py:800
  290.9 28.4 %collective-permute-start.37 = (bf16[1,1024,1024]{2,1,0:T(8,128)(2,1)}, bf16[1,1024,1024]{2,1,0:T(8,128)(2,1)}, u32[]{:S(2)}, u32[]{:S(2)}) collective-permute-start(bf16[1,1024,1024]{2,1,0:T(8,128)(2,1)} %get-tuple-element.191), channel_id=1, source_target_pairs={{0,4},{1,5},{2,3},{3,2},{4,0},{5,1},{6,7},{7,6},{8,12},{9,13},{10,... | collective-permute-start | bytes 6291464 | tf_op jit(solution)/shard_map/ppermute | solution.py:809
  319.2 31.0 %collective-permute-start.38 = (bf16[1,1024,1024]{2,1,0:T(8,128)(2,1)}, bf16[1,1024,1024]{2,1,0:T(8,128)(2,1)}, u32[]{:S(2)}, u32[]{:S(2)}) collective-permute-start(bf16[1,1024,1024]{2,1,0:T(8,128)(2,1)} %get-tuple-element.196), channel_id=1, source_target_pairs={{0,4},{1,5},{2,3},{3,2},{4,0},{5,1},{6,7},{7,6},{8,12},{9,13},{10,... | collective-permute-start | bytes 6291464 | tf_op jit(solution)/shard_map/ppermute | solution.py:809
  358.2 42.4 %collective-permute-start.40 = (bf16[2,512,1024]{2,1,0:T(8,128)(2,1)}, bf16[2,512,1024]{2,1,0:T(8,128)(2,1)}, u32[]{:S(2)}, u32[]{:S(2)}) collective-permute-start(bf16[2,512,1024]{2,1,0:T(8,128)(2,1)} %get-tuple-element.204), channel_id=1, source_target_pairs={{0,1},{1,0},{2,10},{3,11},{4,5},{5,4},{6,14},{7,15},{8,9},{9,8},{1... | collective-permute-start | bytes 6291464 | tf_op jit(solution)/shard_map/ppermute | solution.py:809
  374.8 23.5 %collective-permute-start.41 = (bf16[1,128,5120]{2,1,0:T(8,128)(2,1)}, bf16[1,128,5120]{2,1,0:T(8,128)(2,1)}, u32[]{:S(2)}, u32[]{:S(2)}) collective-permute-start(bf16[1,128,5120]{2,1,0:T(8,128)(2,1)} %get-tuple-element.208), channel_id=1, source_target_pairs={{0,8},{1,9},{2,6},{3,7},{4,12},{5,13},{6,2},{7,3},{8,0},{9,1},{10,... | collective-permute-start | bytes 3932168 | tf_op jit(solution)/shard_map/ppermute | solution.py:809
  398.2 32.3 %collective-permute-start.43 = (bf16[1,128,5120]{2,1,0:T(8,128)(2,1)}, bf16[1,128,5120]{2,1,0:T(8,128)(2,1)}, u32[]{:S(2)}, u32[]{:S(2)}) collective-permute-start(bf16[1,128,5120]{2,1,0:T(8,128)(2,1)} %get-tuple-element.218), channel_id=1, source_target_pairs={{0,8},{1,9},{2,6},{3,7},{4,12},{5,13},{6,2},{7,3},{8,0},{9,1},{10,... | collective-permute-start | bytes 3932168 | tf_op jit(solution)/shard_map/ppermute | solution.py:809
  404.8 22.6 %collective-permute-start.42 = (bf16[1,512,1024]{2,1,0:T(8,128)(2,1)}, bf16[1,512,1024]{2,1,0:T(8,128)(2,1)}, u32[]{:S(2)}, u32[]{:S(2)}) collective-permute-start(bf16[1,512,1024]{2,1,0:T(8,128)(2,1)} %get-tuple-element.216), channel_id=1, source_target_pairs={{0,8},{1,9},{2,6},{3,7},{4,12},{5,13},{6,2},{7,3},{8,0},{9,1},{10,... | collective-permute-start | bytes 3145736 | tf_op jit(solution)/shard_map/ppermute | solution.py:809
  436.3 20.6 %collective-permute-start.45 = (bf16[4,128,3072]{2,1,0:T(8,128)(2,1)}, bf16[4,128,3072]{2,1,0:T(8,128)(2,1)}, u32[]{:S(2)}, u32[]{:S(2)}) collective-permute-start(bf16[4,128,3072]{2,1,0:T(8,128)(2,1)} %bitcast.266), channel_id=1, source_target_pairs={{0,2},{2,0},{1,3},{3,1},{4,6},{6,4},{5,7},{7,5},{8,10},{10,8},{9,1... | collective-permute-start | bytes 9437192 | tf_op jit(solution)/shard_map/ppermute | solution.py:800
  444.3 26.8 %collective-permute-start.47 = (bf16[1,256,1024]{2,1,0:T(8,128)(2,1)}, bf16[1,256,1024]{2,1,0:T(8,128)(2,1)S(1)}, u32[]{:S(2)}, u32[]{:S(2)}) collective-permute-start(bf16[1,256,1024]{2,1,0:T(8,128)(2,1)} %get-tuple-element.223), channel_id=1, source_target_pairs={{0,16},{16,0},{1,17},{17,1},{2,18},{18,2},{3,19},{19,3},{4,20},{20... | collective-permute-start | bytes 1572872 | tf_op jit(solution)/shard_map/ppermute | solution.py:800
  447.0 28.7 %collective-permute-start.46 = (bf16[2,64,5120]{2,1,0:T(8,128)(2,1)}, bf16[2,64,5120]{2,1,0:T(8,128)(2,1)}, u32[]{:S(2)}, u32[]{:S(2)}) collective-permute-start(bf16[2,64,5120]{2,1,0:T(8,128)(2,1)} %get-tuple-element.226), channel_id=1, source_target_pairs={{0,1},{1,0},{2,10},{3,11},{4,5},{5,4},{6,14},{7,15},{8,9},{9,8},{1... | collective-permute-start | bytes 3932168 | tf_op jit(solution)/shard_map/ppermute | solution.py:809
  462.6 24.4 %collective-permute-start.49 = (bf16[2,128,3072]{2,1,0:T(8,128)(2,1)}, bf16[2,128,3072]{2,1,0:T(8,128)(2,1)}, u32[]{:S(2)}, u32[]{:S(2)}) collective-permute-start(bf16[2,128,3072]{2,1,0:T(8,128)(2,1)} %get-tuple-element.232), channel_id=1, source_target_pairs={{0,1},{1,0},{2,10},{3,11},{4,5},{5,4},{6,14},{7,15},{8,9},{9,8},{1... | collective-permute-start | bytes 4718600 | tf_op jit(solution)/shard_map/ppermute | solution.py:809
  471.4 20.2 %collective-permute-start.51 = (bf16[256,1024]{1,0:T(8,128)(2,1)S(1)}, bf16[256,1024]{1,0:T(8,128)(2,1)}, u32[]{:S(2)}, u32[]{:S(2)}) collective-permute-start(bf16[256,1024]{1,0:T(8,128)(2,1)S(1)} %fusion.56.refs_0_), channel_id=1, source_target_pairs={{0,16},{16,0},{1,17},{17,1},{2,18},{18,2},{3,19},{19,3},{4,20},{20... | collective-permute-start | bytes 1572872 | tf_op jit(solution)/shard_map/ppermute | solution.py:800
  474.3 31.8 %collective-permute-start.44 = (bf16[512,1024]{1,0:T(8,128)(2,1)}, bf16[512,1024]{1,0:T(8,128)(2,1)}, u32[]{:S(2)}, u32[]{:S(2)}) collective-permute-start(bf16[512,1024]{1,0:T(8,128)(2,1)} %slice.285), channel_id=1, source_target_pairs={{1,0},{3,2},{5,4},{7,6},{9,8},{11,10},{13,12},{15,14},{17,16},{19,... | collective-permute-start | bytes 3145736 | tf_op jit(solution)/shard_map/ppermute | solution.py:1310
  494.5 35.1 %collective-permute-start.54 = (bf16[512,1024]{1,0:T(8,128)(2,1)}, bf16[512,1024]{1,0:T(8,128)(2,1)}, u32[]{:S(2)}, u32[]{:S(2)}) collective-permute-start(bf16[512,1024]{1,0:T(8,128)(2,1)} %shard_map.506.refs_0_), channel_id=1, source_target_pairs={{0,8},{1,9},{2,6},{3,7},{4,12},{5,13},{6,2},{7,3},{8,0},{9,1},{10,... | collective-permute-start | bytes 3145736 | tf_op jit(solution)/shard_map/ppermute | solution.py:809
  498.7 27.0 %collective-permute-start.52 = (bf16[2,64,3072]{2,1,0:T(8,128)(2,1)}, bf16[2,64,3072]{2,1,0:T(8,128)(2,1)S(1)}, u32[]{:S(2)}, u32[]{:S(2)}) collective-permute-start(bf16[2,64,3072]{2,1,0:T(8,128)(2,1)} %get-tuple-element.240), channel_id=1, source_target_pairs={{0,4},{1,5},{2,3},{3,2},{4,0},{5,1},{6,7},{7,6},{8,12},{9,13},{10,... | collective-permute-start | bytes 2359304 | tf_op jit(solution)/shard_map/ppermute | solution.py:809
  533.4 31.3 %collective-permute-start.63 = (bf16[1024,1024]{1,0:T(8,128)(2,1)}, bf16[1024,1024]{1,0:T(8,128)(2,1)S(1)}, u32[]{:S(2)}, u32[]{:S(2)}) collective-permute-start(bf16[1024,1024]{1,0:T(8,128)(2,1)} %shard_map.509.refs_0_), channel_id=1, source_target_pairs={{0,4},{1,5},{2,10},{3,11},{4,0},{5,1},{6,14},{7,15},{8,12},{9,13},... | collective-permute-start | bytes 6291464 | tf_op jit(solution)/shard_map/ppermute | solution.py:809
  546.6 15.2 %collective-permute-start.57 = (bf16[32,5120]{1,0:T(8,128)(2,1)S(1)}, bf16[32,5120]{1,0:T(8,128)(2,1)}, u32[]{:S(2)}, u32[]{:S(2)}) collective-permute-start(bf16[32,5120]{1,0:T(8,128)(2,1)S(1)} %fusion.57.refs_0_), channel_id=1, source_target_pairs={{0,16},{16,0},{1,17},{17,1},{2,18},{18,2},{3,19},{19,3},{4,20},{20... | collective-permute-start | bytes 983048 | tf_op jit(solution)/shard_map/ppermute | solution.py:800
  550.1 52.9 %collective-permute-start.56 = (bf16[1,32,3072]{2,1,0:T(8,128)(2,1)}, bf16[1,32,3072]{2,1,0:T(8,128)(2,1)}, u32[]{:S(2)}, u32[]{:S(2)}) collective-permute-start(bf16[1,32,3072]{2,1,0:T(8,128)(2,1)} %get-tuple-element.255), channel_id=1, source_target_pairs={{0,16},{16,0},{1,17},{17,1},{2,18},{18,2},{3,19},{19,3},{4,20},{20... | collective-permute-start | bytes 589832 | tf_op jit(solution)/shard_map/ppermute | solution.py:800
  564.4 39.7 %collective-permute-start.58 = (bf16[64,5120]{1,0:T(8,128)(2,1)}, bf16[64,5120]{1,0:T(8,128)(2,1)S(1)}, u32[]{:S(2)}, u32[]{:S(2)}) collective-permute-start(bf16[64,5120]{1,0:T(8,128)(2,1)} %shard_map.511.refs_0_), channel_id=1, source_target_pairs={{0,4},{1,5},{2,10},{3,11},{4,0},{5,1},{6,14},{7,15},{8,12},{9,13},... | collective-permute-start | bytes 1966088 | tf_op jit(solution)/shard_map/ppermute | solution.py:809
  571.4 101.3 %collective-permute-start.64 = (bf16[2048,1024]{1,0:T(8,128)(2,1)}, bf16[2048,1024]{1,0:T(8,128)(2,1)}, u32[]{:S(2)}, u32[]{:S(2)}) collective-permute-start(bf16[2048,1024]{1,0:T(8,128)(2,1)} %shard_map.517.own_ref), channel_id=1, source_target_pairs={{0,2},{2,0},{1,3},{3,1},{4,6},{6,4},{5,7},{7,5},{8,10},{10,8},{9,1... | collective-permute-start | bytes 12582920 | tf_op jit(solution)/shard_map/ppermute | solution.py:800
  608.1 24.2 %collective-permute-start.60 = (bf16[128,5120]{1,0:T(8,128)(2,1)}, bf16[128,5120]{1,0:T(8,128)(2,1)S(1)}, u32[]{:S(2)}, u32[]{:S(2)}) collective-permute-start(bf16[128,5120]{1,0:T(8,128)(2,1)} %shard_map.512.refs_0_), channel_id=1, source_target_pairs={{0,8},{1,9},{2,6},{3,7},{4,12},{5,13},{6,2},{7,3},{8,0},{9,1},{10,... | collective-permute-start | bytes 3932168 | tf_op jit(solution)/shard_map/ppermute | solution.py:809
  609.8 19.4 %collective-permute-start.59 = (bf16[32,3072]{1,0:T(8,128)(2,1)S(1)}, bf16[32,3072]{1,0:T(8,128)(2,1)S(1)}, u32[]{:S(2)}, u32[]{:S(2)}) collective-permute-start(bf16[32,3072]{1,0:T(8,128)(2,1)S(1)} %fusion.58.refs_0_), channel_id=1, source_target_pairs={{0,16},{16,0},{1,17},{17,1},{2,18},{18,2},{3,19},{19,3},{4,20},{20... | collective-permute-start | bytes 589832 | tf_op jit(solution)/shard_map/ppermute | solution.py:800
  638.1 49.4 %collective-permute-start.66 = (bf16[256,5120]{1,0:T(8,128)(2,1)}, bf16[256,5120]{1,0:T(8,128)(2,1)}, u32[]{:S(2)}, u32[]{:S(2)}) collective-permute-start(bf16[256,5120]{1,0:T(8,128)(2,1)} %shard_map.514.own_ref), channel_id=1, source_target_pairs={{0,2},{2,0},{1,3},{3,1},{4,6},{6,4},{5,7},{7,5},{8,10},{10,8},{9,1... | collective-permute-start | bytes 7864328 | tf_op jit(solution)/shard_map/ppermute | solution.py:800
  665.8 43.5 %collective-permute-start.71 = (bf16[256,3072]{1,0:T(8,128)(2,1)}, bf16[256,3072]{1,0:T(8,128)(2,1)}, u32[]{:S(2)}, u32[]{:S(2)}) collective-permute-start(bf16[256,3072]{1,0:T(8,128)(2,1)} %shard_map.516.own_ref), channel_id=1, source_target_pairs={{0,2},{2,0},{1,3},{3,1},{4,6},{6,4},{5,7},{7,5},{8,10},{10,8},{9,1... | collective-permute-start | bytes 4718600 | tf_op jit(solution)/shard_map/ppermute | solution.py:800
  668.5 36.9 %collective-permute-start.48 = (bf16[544,1024]{1,0:T(8,128)(2,1)}, bf16[544,1024]{1,0:T(8,128)(2,1)}, u32[]{:S(2)}, u32[]{:S(2)}) collective-permute-start(bf16[544,1024]{1,0:T(8,128)(2,1)} %slice.284), channel_id=1, source_target_pairs={{0,1},{1,0},{2,3},{3,2},{4,5},{5,4},{6,7},{7,6},{8,9},{9,8},{10,11... | collective-permute-start | bytes 3342344 | tf_op jit(solution)/shard_map/ppermute | solution.py:800
  670.0 17.3 %collective-permute-start.65 = (f32[20,1024]{1,0:T(8,128)S(1)}, f32[20,1024]{1,0:T(8,128)S(1)}, u32[]{:S(2)}, u32[]{:S(2)}) collective-permute-start(f32[20,1024]{1,0:T(8,128)S(1)} %pad_maximum_fusion.4), channel_id=1, source_target_pairs={{0,16},{16,0},{1,17},{17,1},{2,18},{18,2},{3,19},{19,3},{4,20},{20... | collective-permute-start | bytes 245768 | tf_op jit(solution)/shard_map/ppermute | solution.py:800
  (92 other events, 988.5 us)

commit v4 on v3

--- a/solution.py
+++ b/solution.py
@@ -958,6 +958,8 @@
     def gather(self, *others):
         if self.stage > 4:
             self.part = after(self.part, *others)
+        else:
+            self.kept = after(self.kept, *others)
         if self.stage == 4:
             piece = self.kept[0].astype(jnp.float32) + self.came[0].astype(jnp.float32)
             self.part = piece.astype(jnp.bfloat16)
@@ -1293,14 +1295,15 @@
         kept, sent = outer_group(core, lefts, products)
         late = (total_ffn.step(kept), total_mid.step(kept))
         total_last = Total((kept, after(sent, *late)), ("yz", "xy", "zx"), True, False)
+        late = total_last.advance(*late)
+        late = late + total_ffn.advance(*late)
         grad_keys, scaled_self = (after(values, *late) for values in (grad_keys, scaled_self))
     normed_terms = dot_back(grad_keys, whole_self[:, width : 2 * width]) + dot_back(
         grad_values, whole_self[:, 2 * width : 3 * width]
     )
     if two:
-        sent = total_last.advance(normed_terms)
-        for total in (total_mid, total_ffn):
-            sent = sent + total.advance(sent[0])
+        sent = total_mid.advance(normed_terms)
+        sent = sent + total_ffn.advance(*sent)
         grad_patch_keys = after(grad_patch_keys, *sent)
     patch_terms = dot_back(grad_patch_keys, whole_cross[:, :width]) + dot_back(
         grad_patch_values, whole_cross[:, width : 2 * width]
@@ -1336,22 +1339,22 @@
     )
     if two:
         late = total_last.advance(patch_terms)
-        for total in (total_mid, total_ffn):
-            late = late + total.advance(late[0])
+        late = late + total_ffn.advance(*late)
         norm_pairs = ((after(token_values, *late), grad_normed),) + norm_pairs[1:]
     sums = row_sums(norm_pairs, plain)
     vector_sums = jnp.concatenate([sums, column_inner.reshape(-1, width)])
     if two:
         totals = (total_mid, total_ffn, total_last)
-        late = [vector_sums]
+        late = total_mid.advance(vector_sums)
+        late = late + total_ffn.advance(*late)
+        late = total_last.advance(*late)
+        grad_outer, grad_ffn_in = total_ffn.result(2, *late)
+        late = total_mid.advance(grad_outer)
         while any(total.stage < 8 for total in totals):
-            ahead = total_last.advance(*late)
-            late = ahead
-            for total in totals[:-1]:
-                late = late + total.advance(*ahead)
+            late = total_last.advance(*late) or late
+            late = total_mid.advance(*late) or late
         vector_total = VectorTotal(after(vector_sums, *late))
-        grad_outer, grad_ffn_in = total_ffn.result(2, *late)
-        late = vector_total.advance(grad_outer)
+        late = vector_total.advance(*late)
         *wide_cross, wide_output = total_mid.result(5, *late)
         late = vector_total.advance(wide_output)
         wide_self = [*total_last.result(3, *late), wide_output]

time: 724 us -> 748 us (1.033)
  waiting for transfers between devices: 142 us -> 198 us
  starting transfers between devices: 101 us -> 72.2 us
    ppermute x41, starting transfers between devices: 60.2 us -> 31.2 us  [swap(): return lax.ppermute(values, axis_name, [(0, 1), (1, 0)])]
    ppermute x29, waiting for transfers between devices: 68.3 us -> 88.1 us  [exchange(): lax.ppermute(values, square, [(i, i ^ flip[i // 2 % 2]) for i in range(16)])]
    ppermute x1, waiting for transfers between devices: 3.09 us -> 22.8 us  [on_device(): normed_came = lax.ppermute(normed_sent, 'seq', [(1, 0)])]
    ppermute x41, waiting for transfers between devices: 64.8 us -> 80.8 us  [swap(): return lax.ppermute(values, axis_name, [(0, 1), (1, 0)])]
    unnamed x166 -> x164, local copies, waits for them, and re-layouts: 15.6 us -> 14.8 us
  transfers between devices with their start and end apart: 72 -> 72, of which waited for: 21 -> 25; matrix products, arithmetic and copies ran while one was open for 19% -> 18% of each run, Pallas kernels for 34% -> 31%
where the time goes in v4:
time: 748 us; the launch traced here: 742 us
  Pallas kernels  321 us (43%)
  waiting for transfers between devices  198 us (26%)
  matrix products  73.2 us (10%)
  starting transfers between devices  72.2 us (10%)
  local copies, waits for them, and re-layouts  37.8 us (5%)
  other arithmetic  36.8 us (5%)
    ppermute x29, waiting for transfers between devices, exchange(): lax.ppermute(values, square, [(i, i ^ flip[i // 2 % 2]) for i in range(16)])  88.1 us
    ppermute x41, waiting for transfers between devices, swap(): return lax.ppermute(values, axis_name, [(0, 1), (1, 0)])  80.8 us
    pallas_call x3, Pallas kernels, attend(): pl.pallas_call(skip_refs(functools.partial(attend_kernel, plan), 5, len(i...  47.4 us
    pallas_call x11, Pallas kernels, join(): pl.pallas_call(functools.partial(join_kernel, count), grid_spec=pltpu.Pre...  42.2 us
    pallas_call x2, Pallas kernels, attend_back(): pl.pallas_call(skip_refs(functools.partial(attend_back_kernel, plan), 8,...  41.8 us
    dot_general x8, matrix products, dot_nt(): lax.dot_general(left_side, right_side, (((1,), (1,)), ((), ())), preferre...  41.1 us
    pallas_call x1, Pallas kernels, ffn_both_ways(): pl.pallas_call(functools.partial(ffn_kernel, half_steps), grid_spec=pltpu...  40.5 us
    pallas_call x9, Pallas kernels, halve(): pl.pallas_call(functools.partial(halve_kernel, split), grid_spec=pltpu.Pr...  36.4 us
  transfers between devices with their start and end apart: 72, of which 25 were waited for; matrix products, arithmetic and copies ran while one was open for 18% of the time, Pallas kernels for 31%

profile of v4, /device:TPU:0, one launch (start us, length us, event | category | flops | bytes accessed | tf_op | source)
XLA Modules:
  0.0 741.6 jit_solution(16330111583414828350)
XLA Ops:
  8.8 9.5 %collective-permute-done.1 = bf16[68,128]{1,0:T(8,128)(2,1)S(1)} collective-permute-done((bf16[68,128]{1,0:T(8,128)(2,1)S(1)}, bf16[68,128]{1,0:T(8,128)(2,1)S(1)}, u32[]{:S(2)}, u32[]{:S(2)}) %collective-permute-start.1) | collective-permute-done | bytes 17440 | tf_op jit(solution)/shard_map/ppermute | solution.py:800
  34.8 6.3 collective-permute-done.5.refs_7_
  42.9 5.8 collective-permute-done.2
  53.1 8.8 %shard_map.484 = bf16[1024,4096]{1,0:T(8,128)(2,1)} custom-call(s32[9]{0:T(128)} %stack.366.place_ref, bf16[512,1024]{1,0:T(8,128)(2,1)} %refs_0_.2, bf16[512,1024]{1,0:T(8,128)(2,1)} %refs_1_.2, bf16[512,1024]{1,0:T(8,128)(2,1)} %refs_2_.2, bf16[512,1024]{1,0:T(8,128)(2,1)} %refs_3_.2, bf16[64,4096]{1,0:T(8,128)(2,1)} %copy-done.31, ...), custom_call_target="tpu_custom_call" | custom-call | flops 1 | bytes 1 | tf_op jit(solution)/shard_map/pallas_call | solution.py:312
  72.0 10.5 %collective-permute-done.11.refs_5_ = bf16[64,4096]{1,0:T(8,128)(2,1)} collective-permute-done((bf16[64,4096]{1,0:T(8,128)(2,1)}, bf16[64,4096]{1,0:T(8,128)(2,1)}, u32[]{:S(2)}, u32[]{:S(2)}) %collective-permute-start.11) | collective-permute-done | bytes 524320 | tf_op jit(solution)/shard_map/ppermute | solution.py:809
  85.7 8.2 %add_convert_fusion.refs_2_.refs_3_.refs_5_.refs_6_ = bf16[1024,2048]{1,0:T(8,128)(2,1)} fusion(f32[2048]{0:T(1024)S(1)} %pad_convert_fusion.1, bf16[1024,1024]{1,0:T(8,128)(2,1)S(1)} %fusion.6.refs_1_, bf16[1024,4096]{1,0:T(8,128)(2,1)} %shard_map.484), kind=kOutput, calls=%fused_computation.1 | convolution fusion | flops 4299161600 | bytes 10493952 | tf_op jit(solution)/shard_map/dot_general | solution.py:38
  94.9 16.4 %shard_map.485 = (bf16[512,1024]{1,0:T(8,128)(2,1)}, f32[8,2,512]{2,1,0:T(2,128)}) custom-call(s32[4]{0:T(128)} %pad_add_fusion.refs_0_, bf16[512,1024]{1,0:T(8,128)(2,1)} %multiply_convert_fusion.1.refs_1_, bf16[1024,2048]{1,0:T(8,128)(2,1)} %add_convert_fusion.refs_2_.refs_3_.refs_5_.refs_6_, ...), custom_call_target="tpu_custom_call" | custom-call | flops 1 | bytes 1 | tf_op jit(solution)/shard_map/pallas_call | solution.py:211
  117.0 6.5 collective-permute-start.19
  126.1 8.4 %shard_map.486 = bf16[1024,4096]{1,0:T(8,128)(2,1)} custom-call(s32[9]{0:T(128)} %stack.366.place_ref, bf16[512,1024]{1,0:T(8,128)(2,1)} %refs_0_.3, bf16[512,1024]{1,0:T(8,128)(2,1)} %refs_1_.3, bf16[512,1024]{1,0:T(8,128)(2,1)} %refs_2_.3, bf16[512,1024]{1,0:T(8,128)(2,1)} %refs_3_.3, bf16[64,4096]{1,0:T(8,128)(2,1)} %collective-permute-done.10.refs_4_, ...), custom_call_target="tpu_custom_call" | custom-call | flops 1 | bytes 1 | tf_op jit(solution)/shard_map/pallas_call | solution.py:312
  141.6 11.7 %collective-permute-done.20.refs_1_ = bf16[64,4096]{1,0:T(8,128)(2,1)} collective-permute-done((bf16[64,4096]{1,0:T(8,128)(2,1)}, bf16[64,4096]{1,0:T(8,128)(2,1)}, u32[]{:S(2)}, u32[]{:S(2)}) %collective-permute-start.20) | collective-permute-done | bytes 524320 | tf_op jit(solution)/shard_map/ppermute | solution.py:809
  159.5 5.9 collective-permute-done.21.refs_3_
  165.4 8.6 %fusion.refs_2_.refs_3_.refs_5_.refs_6_ = bf16[1088,2048]{1,0:T(8,128)(2,1)} fusion(bf16[1088,1024]{1,0:T(8,128)(2,1)S(1)} %pad_maximum_fusion.refs_1_, f32[2048]{0:T(1024)S(1)} %pad_convert_fusion, bf16[1024,4096]{1,0:T(8,128)(2,1)} %shard_map.486), kind=kOutput, calls=%fused_computation.2 | convolution fusion | flops 4567859200 | bytes 10887168 | tf_op jit(solution)/shard_map/dot_general | solution.py:38
  174.0 15.5 %shard_map.487 = (bf16[512,1024]{1,0:T(8,128)(2,1)}, f32[8,2,512]{2,1,0:T(2,128)}) custom-call(s32[4]{0:T(128)} %pad_add_fusion.refs_0_, bf16[512,1024]{1,0:T(8,128)(2,1)} %multiply_convert_fusion.refs_1_, bf16[1088,2048]{1,0:T(8,128)(2,1)} %fusion.refs_2_.refs_3_.refs_5_.refs_6_, bf16[1088,2048]{1,0:T(8,128)(2,1)} %fusion.refs_2_.refs_3_.refs_5_.refs_6_, ...), custom_call_target="tpu_custom_call" | custom-call | flops 1 | bytes 1 | tf_op jit(solution)/shard_map/pallas_call | solution.py:211
  192.8 15.5 %shard_map.488 = (bf16[512,1024]{1,0:T(8,128)(2,1)}, f32[8,2,512]{2,1,0:T(2,128)}) custom-call(s32[4]{0:T(128)} %pad_add_fusion.refs_0_, bf16[512,1024]{1,0:T(8,128)(2,1)} %multiply_convert_fusion.refs_1_, bf16[1088,2048]{1,0:T(8,128)(2,1)} %fusion.refs_2_.refs_3_.refs_5_.refs_6_, ...), custom_call_target="tpu_custom_call", output_to_operand_aliasing={{0}: (5, {}), {1}: (6, {})} | custom-call | flops 1 | bytes 1 | tf_op jit(solution)/shard_map/pallas_call | solution.py:211
  208.6 5.5 shard_map.489.refs_6_.refs_7_
  220.3 5.5 shard_map.490.refs_9_
  225.8 40.5 %shard_map.491 = (bf16[512,1024]{1,0:T(8,128)(2,1)}, f32[512,1024]{1,0:T(8,128)}, f32[1,4096]{1,0:T(1,128)}, bf16[2,1024,1024]{2,1,0:T(8,128)(2,1)}, bf16[2,1024...) custom-call(s32[20]{0:T(128)} %stack.355.place_ref, ...), custom_call_target="tpu_custom_call" | custom-call | flops 1 | bytes 1 | tf_op jit(solution)/shard_map/pallas_call | solution.py:462
  280.0 10.9 %shard_map.492 = (bf16[2,1024,1024]{2,1,0:T(8,128)(2,1)}, bf16[1,1024,1024]{2,1,0:T(8,128)(2,1)}, bf16[1,1024,1024]{2,1,0:T(8,128)(2,1)}) custom-call(s32[4]{0:T(128)} %pad_add_fusion.1.place_ref, bf16[4,512,1024]{2,1,0:T(8,128)(2,1)} %bitcast.202, bf16[4,512,1024]{2,1,0:T(8,128)(2,1)} %collective-permute-done.35.refs_1_.refs_5_, ...), custom_call_target="tpu_custom_call" | custom-call | flops 1 | bytes 1 | tf_op jit(solution)/shard_map/pallas_call | solution.py:707
  292.4 26.8 %shard_map.493 = (bf16[512,1024]{1,0:T(8,128)(2,1)}, bf16[1088,1024]{1,0:T(8,128)(2,1)}, bf16[1088,1024]{1,0:T(8,128)(2,1)}) custom-call(s32[4]{0:T(128)} %pad_add_fusion.refs_0_, bf16[512,1024]{1,0:T(8,128)(2,1)} %multiply_convert_fusion.refs_1_, bf16[512,1024]{1,0:T(8,128)(2,1)} %get-tuple-element.184.refs_2_, bf16[512,1024]{1,0:T(8,128)(2,1)} %fusion.43.refs_3_, ...), custom_call_target="tpu_custom_call" | custom-call | flops 1 | bytes 1 | tf_op jit(solution)/shard_map/pallas_call | solution.py:235
  331.0 19.3 %shard_map.494 = (bf16[2,256,5120]{2,1,0:T(8,128)(2,1)}, bf16[2,256,5120]{2,1,0:T(8,128)(2,1)}) custom-call(s32[2]{0:T(128)} %pad_add_fusion.3.place_ref, bf16[512,1024]{1,0:T(8,128)(2,1)} %add_convert_fusion.2.refs_0_, bf16[1088,1024]{1,0:T(8,128)(2,1)} %copy-done.12, bf16[512,1024]{1,0:T(8,128)(2,1)} %get-tuple-element.184.refs_2_, ...), custom_call_target="tpu_custom_call" | custom-call | flops 1 | bytes 1 | tf_op jit(solution)/shard_map/pallas_call | solution.py:570
  350.3 7.9 %shard_map.495 = (bf16[2,512,1024]{2,1,0:T(8,128)(2,1)}, bf16[2,512,1024]{2,1,0:T(8,128)(2,1)}) custom-call(s32[8]{0:T(128)} %stack.399.place_ref, bf16[4,512,1024]{2,1,0:T(8,128)(2,1)} %bitcast.200, bf16[2,512,1024]{2,1,0:T(8,128)(2,1)} %bitcast.54.refs_1_.refs_4_, bf16[2,512,1024]{2,1,0:T(8,128)(2,1)} %bitcast.55.refs_2_.refs_5_, ...), custom_call_target="tpu_custom_call" | custom-call | flops 1 | bytes 1 | tf_op jit(solution)/shard_map/pallas_call | solution.py:660
  359.0 8.2 %collective-permute-done.39.came_a.came_b = bf16[4,128,5120]{2,1,0:T(8,128)(2,1)} collective-permute-done((bf16[4,128,5120]{2,1,0:T(8,128)(2,1)}, bf16[4,128,5120]{2,1,0:T(8,128)(2,1)}, u32[]{:S(2)}, u32[]{:S(2)}) %collective-permute-start.39) | collective-permute-done | bytes 5242912 | tf_op jit(solution)/shard_map/ppermute | solution.py:800
  367.2 7.7 %shard_map.496 = (bf16[2,128,5120]{2,1,0:T(8,128)(2,1)}, bf16[1,128,5120]{2,1,0:T(8,128)(2,1)}, bf16[1,128,5120]{2,1,0:T(8,128)(2,1)}) custom-call(s32[4]{0:T(128)} %pad_add_fusion.2.place_ref, bf16[4,128,5120]{2,1,0:T(8,128)(2,1)} %bitcast.198, bf16[4,128,5120]{2,1,0:T(8,128)(2,1)} %collective-permute-done.39.came_a.came_b, ...), custom_call_target="tpu_custom_call" | custom-call | flops 1 | bytes 1 | tf_op jit(solution)/shard_map/pallas_call | solution.py:623
  376.8 15.0 %shard_map.497 = (bf16[512,1024]{1,0:T(8,128)(2,1)}, bf16[1024,1024]{1,0:T(8,128)(2,1)}, bf16[1024,1024]{1,0:T(8,128)(2,1)}) custom-call(s32[4]{0:T(128)} %pad_add_fusion.refs_0_, bf16[512,1024]{1,0:T(8,128)(2,1)} %multiply_convert_fusion.1.refs_1_, bf16[512,1024]{1,0:T(8,128)(2,1)} %get-tuple-element.165.refs_3_.refs_2_, bf16[512,1024]{1,0:T(8,128)(2,1)} %fusion.40.refs_3_, ...), custom_call_target="tpu_custom_call" | custom-call | flops 1 | bytes 1 | tf_op jit(solution)/shard_map/pallas_call | solution.py:235
  391.8 6.5 collective-permute-done.41
  407.4 12.8 %shard_map.499 = (bf16[2,256,3072]{2,1,0:T(8,128)(2,1)}, bf16[2,256,3072]{2,1,0:T(8,128)(2,1)}) custom-call(s32[2]{0:T(128)} %pad_add_fusion.3.place_ref, bf16[512,1024]{1,0:T(8,128)(2,1)} %slice.184.refs_0_, bf16[1024,1024]{1,0:T(8,128)(2,1)} %copy-done.6, bf16[512,1024]{1,0:T(8,128)(2,1)} %get-tuple-element.237.refs_2_.refs_6_, ...), custom_call_target="tpu_custom_call" | custom-call | flops 1 | bytes 1 | tf_op jit(solution)/shard_map/pallas_call | solution.py:570
  420.2 7.3 collective-permute-done.42
  430.6 5.9 shard_map.501
  444.9 6.0 fusion.17
  450.9 5.7 shard_map.502
  456.6 8.7 %collective-permute-done.45 = bf16[1,256,1024]{2,1,0:T(8,128)(2,1)} collective-permute-done((bf16[1,256,1024]{2,1,0:T(8,128)(2,1)}, bf16[1,256,1024]{2,1,0:T(8,128)(2,1)}, u32[]{:S(2)}, u32[]{:S(2)}) %collective-permute-start.45) | collective-permute-done | bytes 524320 | tf_op jit(solution)/shard_map/ppermute | solution.py:800
  470.2 7.2 fusion.21
  481.1 11.4 %collective-permute-done.48.refs_1_ = bf16[256,1024]{1,0:T(8,128)(2,1)} collective-permute-done((bf16[256,1024]{1,0:T(8,128)(2,1)S(1)}, bf16[256,1024]{1,0:T(8,128)(2,1)}, u32[]{:S(2)}, u32[]{:S(2)}) %collective-permute-start.48) | collective-permute-done | bytes 524320 | tf_op jit(solution)/shard_map/ppermute | solution.py:800
  499.7 6.2 convolution_add_fusion.1
  524.4 22.8 %collective-permute-done.46 = bf16[512,1024]{1,0:T(8,128)(2,1)} collective-permute-done((bf16[512,1024]{1,0:T(8,128)(2,1)}, bf16[512,1024]{1,0:T(8,128)(2,1)}, u32[]{:S(2)}, u32[]{:S(2)}) %collective-permute-start.46) | collective-permute-done | bytes 1048608 | tf_op jit(solution)/shard_map/ppermute | solution.py:1313
  547.2 5.4 multiply_reduce_fusion.6
  552.6 9.9 %shard_map.507 = f32[16,1024]{1,0:T(8,128)} custom-call(f32[512,1024]{1,0:T(8,128)} %bitcast_convert_fusion.refs_0_, f32[512,1024]{1,0:T(8,128)} %get-tuple-element.326.refs_1_, f32[512,1024]{1,0:T(8,128)} %copy-done.3, f32[512,1024]{1,0:T(8,128)} %copy-done.16, f32[512,1024]{1,0:T(8,128)} %copy-done, f32[512,1024]{1,0:T(8,128)} %get-tuple-element.188.refs_5_, ...), custom_call_target="tpu_custom_call" | custom-call | flops 1 | bytes 1 | tf_op jit(solution)/shard_map/pallas_call | solution.py:352
  567.0 5.6 shard_map.509.own_ref
  575.0 9.7 %collective-permute-done.54.came_a.came_b = bf16[2,64,3072]{2,1,0:T(8,128)(2,1)S(1)} collective-permute-done((bf16[2,64,3072]{2,1,0:T(8,128)(2,1)S(1)}, bf16[2,64,3072]{2,1,0:T(8,128)(2,1)S(1)}, u32[]{:S(2)}, u32[]{:S(2)}) %collective-permute-start.54) | collective-permute-done | bytes 786464 | tf_op jit(solution)/shard_map/ppermute | solution.py:809
  589.3 14.7 %shard_map.511 = (f32[2048,1024]{1,0:T(8,128)}, f32[512,4096]{1,0:T(8,128)}) custom-call(s32[2]{0:T(128)} %pad_add_fusion.3.place_ref, bf16[2048,1024]{1,0:T(8,128)(2,1)} %shard_map.509.own_ref, bf16[2048,1024]{1,0:T(8,128)(2,1)} %collective-permute-done.55.other_ref), custom_call_target="tpu_custom_call" | custom-call | flops 1 | bytes 1 | tf_op jit(solution)/shard_map/pallas_call | solution.py:754
  611.1 14.6 %collective-permute-done.58.refs_1_ = bf16[32,5120]{1,0:T(8,128)(2,1)S(1)} collective-permute-done((bf16[32,5120]{1,0:T(8,128)(2,1)S(1)}, bf16[32,5120]{1,0:T(8,128)(2,1)S(1)}, u32[]{:S(2)}, u32[]{:S(2)}) %collective-permute-start.58) | collective-permute-done | bytes 327712 | tf_op jit(solution)/shard_map/ppermute | solution.py:800
  631.1 8.7 %collective-permute-done.60.refs_1_ = bf16[64,5120]{1,0:T(8,128)(2,1)S(1)} collective-permute-done((bf16[64,5120]{1,0:T(8,128)(2,1)}, bf16[64,5120]{1,0:T(8,128)(2,1)S(1)}, u32[]{:S(2)}, u32[]{:S(2)}) %collective-permute-start.60) | collective-permute-done | bytes 655392 | tf_op jit(solution)/shard_map/ppermute | solution.py:809
  647.0 15.0 %collective-permute-done.61.refs_1_ = bf16[32,3072]{1,0:T(8,128)(2,1)S(1)} collective-permute-done((bf16[32,3072]{1,0:T(8,128)(2,1)S(1)}, bf16[32,3072]{1,0:T(8,128)(2,1)S(1)}, u32[]{:S(2)}, u32[]{:S(2)}) %collective-permute-start.61) | collective-permute-done | bytes 196640 | tf_op jit(solution)/shard_map/ppermute | solution.py:800
  674.2 5.8 collective-permute-done.63.refs_1_
  684.6 11.1 %collective-permute-done.64.refs_1_ = bf16[128,3072]{1,0:T(8,128)(2,1)S(1)} collective-permute-done((bf16[128,3072]{1,0:T(8,128)(2,1)}, bf16[128,3072]{1,0:T(8,128)(2,1)S(1)}, u32[]{:S(2)}, u32[]{:S(2)}) %collective-permute-start.64) | collective-permute-done | bytes 786464 | tf_op jit(solution)/shard_map/ppermute | solution.py:809
  705.3 5.6 collective-permute-done.65
  711.1 8.1 %shard_map.519 = (f32[512,1024]{1,0:T(8,128)}, f32[512,1024]{1,0:T(8,128)}, f32[512,1024]{1,0:T(8,128)}, f32[512,1024]{1,0:T(8,128)}, f32[512,1024]{1,0:T(8,128)}) custom-call(s32[2]{0:T(128)} %pad_add_fusion.3.place_ref, bf16[256,5120]{1,0:T(8,128)(2,1)} %shard_map.516.own_ref, bf16[256,5120]{1,0:T(8,128)(2,1)} %collective-permute-done.66.other_ref), custom_call_target="tpu_custom_call" | custom-call | flops 1 | bytes 1 | tf_op jit(solution)/shard_map/pallas_call | solution.py:754
  733.7 6.0 shard_map.520
  (399 shorter events, 232.9 us)
Async XLA Ops:
  3.0 15.4 %collective-permute-start = (bf16[64,4096]{1,0:T(8,128)(2,1)S(1)}, bf16[64,4096]{1,0:T(8,128)(2,1)S(1)}, u32[]{:S(2)}, u32[]{:S(2)}) collective-permute-start(bf16[64,4096]{1,0:T(8,128)(2,1)S(1)} %pad_maximum_fusion.2), channel_id=1, source_target_pairs={{0,1},{1,0},{2,3},{3,2},{4,5},{5,4},{6,7},{7,6},{8,9},{9,8},{10,11... | collective-permute-start | bytes 1572872 | tf_op jit(solution)/shard_map/ppermute | solution.py:800
  24.4 24.4 %collective-permute-start.2 = (bf16[512,1024]{1,0:T(8,128)(2,1)S(1)}, bf16[512,1024]{1,0:T(8,128)(2,1)S(1)}, u32[]{:S(2)}, u32[]{:S(2)}) collective-permute-start(bf16[512,1024]{1,0:T(8,128)(2,1)S(1)} %bitcast.194), channel_id=1, source_target_pairs={{0,1},{2,3},{4,5},{6,7},{8,9},{10,11},{12,13},{14,15},{16,17},{18,... | collective-permute-start | bytes 3145736 | tf_op jit(solution)/shard_map/ppermute | solution.py:1115
  34.1 17.1 %collective-permute-start.6 = (bf16[64,4096]{1,0:T(8,128)(2,1)S(1)}, bf16[64,4096]{1,0:T(8,128)(2,1)S(1)}, u32[]{:S(2)}, u32[]{:S(2)}) collective-permute-start(bf16[64,4096]{1,0:T(8,128)(2,1)S(1)} %collective-permute-done.refs_4_), channel_id=1, source_target_pairs={{0,2},{2,0},{1,3},{3,1},{4,6},{6,4},{5,7},{7,5},{8,10},{10,8},{9,1... | collective-permute-start | bytes 1572872 | tf_op jit(solution)/shard_map/ppermute | solution.py:800
  34.2 17.0 %collective-permute-start.7 = (bf16[64,4096]{1,0:T(8,128)(2,1)S(1)}, bf16[64,4096]{1,0:T(8,128)(2,1)S(1)}, u32[]{:S(2)}, u32[]{:S(2)}) collective-permute-start(bf16[64,4096]{1,0:T(8,128)(2,1)S(1)} %collective-permute-done.3.refs_5_), channel_id=1, source_target_pairs={{0,2},{2,0},{1,3},{3,1},{4,6},{6,4},{5,7},{7,5},{8,10},{10,8},{9,1... | collective-permute-start | bytes 1572872 | tf_op jit(solution)/shard_map/ppermute | solution.py:800
  34.7 16.6 %collective-permute-start.8 = (bf16[64,4096]{1,0:T(8,128)(2,1)S(1)}, bf16[64,4096]{1,0:T(8,128)(2,1)S(1)}, u32[]{:S(2)}, u32[]{:S(2)}) collective-permute-start(bf16[64,4096]{1,0:T(8,128)(2,1)S(1)} %collective-permute-done.4.refs_6_), channel_id=1, source_target_pairs={{0,2},{2,0},{1,3},{3,1},{4,6},{6,4},{5,7},{7,5},{8,10},{10,8},{9,1... | collective-permute-start | bytes 1572872 | tf_op jit(solution)/shard_map/ppermute | solution.py:800
  48.8 20.8 %collective-permute-start.10 = (bf16[64,4096]{1,0:T(8,128)(2,1)}, bf16[64,4096]{1,0:T(8,128)(2,1)}, u32[]{:S(2)}, u32[]{:S(2)}) collective-permute-start(bf16[64,4096]{1,0:T(8,128)(2,1)} %pad_maximum_fusion.3), channel_id=1, source_target_pairs={{0,1},{1,0},{2,3},{3,2},{4,5},{5,4},{6,7},{7,6},{8,9},{9,8},{10,11... | collective-permute-start | bytes 1572872 | tf_op jit(solution)/shard_map/ppermute | solution.py:800
  70.1 15.1 %collective-permute-start.12 = (bf16[64,4096]{1,0:T(8,128)(2,1)}, bf16[64,4096]{1,0:T(8,128)(2,1)}, u32[]{:S(2)}, u32[]{:S(2)}) collective-permute-start(bf16[64,4096]{1,0:T(8,128)(2,1)} %collective-permute-done.10.refs_4_), channel_id=1, source_target_pairs={{0,8},{1,9},{2,6},{3,7},{4,12},{5,13},{6,2},{7,3},{8,0},{9,1},{10,... | collective-permute-start | bytes 1572872 | tf_op jit(solution)/shard_map/ppermute | solution.py:809
  71.8 39.6 %collective-permute-start.14 = (bf16[544,1024]{1,0:T(8,128)(2,1)}, bf16[544,1024]{1,0:T(8,128)(2,1)}, u32[]{:S(2)}, u32[]{:S(2)}) collective-permute-start(bf16[544,1024]{1,0:T(8,128)(2,1)} %bitcast.224), channel_id=1, source_target_pairs={{0,1},{1,0},{2,3},{3,2},{4,5},{5,4},{6,7},{7,6},{8,9},{9,8},{10,11... | collective-permute-start | bytes 3342344 | tf_op jit(solution)/shard_map/ppermute | solution.py:800
  71.9 22.0 %collective-permute-start.13 = (bf16[64,4096]{1,0:T(8,128)(2,1)}, bf16[64,4096]{1,0:T(8,128)(2,1)S(1)}, u32[]{:S(2)}, u32[]{:S(2)}) collective-permute-start(bf16[64,4096]{1,0:T(8,128)(2,1)} %collective-permute-done.10.refs_4_), channel_id=1, source_target_pairs={{0,2},{2,0},{1,3},{3,1},{4,6},{6,4},{5,7},{7,5},{8,10},{10,8},{9,1... | collective-permute-start | bytes 1572872 | tf_op jit(solution)/shard_map/ppermute | solution.py:800
  82.6 28.7 %collective-permute-start.15 = (bf16[64,4096]{1,0:T(8,128)(2,1)}, bf16[64,4096]{1,0:T(8,128)(2,1)}, u32[]{:S(2)}, u32[]{:S(2)}) collective-permute-start(bf16[64,4096]{1,0:T(8,128)(2,1)} %collective-permute-done.11.refs_5_), channel_id=1, source_target_pairs={{0,8},{1,9},{2,6},{3,7},{4,12},{5,13},{6,2},{7,3},{8,0},{9,1},{10,... | collective-permute-start | bytes 1572872 | tf_op jit(solution)/shard_map/ppermute | solution.py:809
  85.2 26.2 %collective-permute-start.16 = (bf16[64,4096]{1,0:T(8,128)(2,1)}, bf16[64,4096]{1,0:T(8,128)(2,1)}, u32[]{:S(2)}, u32[]{:S(2)}) collective-permute-start(bf16[64,4096]{1,0:T(8,128)(2,1)} %collective-permute-done.11.refs_5_), channel_id=1, source_target_pairs={{0,2},{2,0},{1,3},{3,1},{4,6},{6,4},{5,7},{7,5},{8,10},{10,8},{9,1... | collective-permute-start | bytes 1572872 | tf_op jit(solution)/shard_map/ppermute | solution.py:800
  85.2 26.2 %collective-permute-start.17 = (bf16[64,4096]{1,0:T(8,128)(2,1)}, bf16[64,4096]{1,0:T(8,128)(2,1)}, u32[]{:S(2)}, u32[]{:S(2)}) collective-permute-start(bf16[64,4096]{1,0:T(8,128)(2,1)} %collective-permute-done.12.refs_6_), channel_id=1, source_target_pairs={{0,2},{2,0},{1,3},{3,1},{4,6},{6,4},{5,7},{7,5},{8,10},{10,8},{9,1... | collective-permute-start | bytes 1572872 | tf_op jit(solution)/shard_map/ppermute | solution.py:800
  117.0 21.7 %collective-permute-start.19 = (bf16[64,4096]{1,0:T(8,128)(2,1)}, bf16[64,4096]{1,0:T(8,128)(2,1)}, u32[]{:S(2)}, u32[]{:S(2)}) collective-permute-start(bf16[64,4096]{1,0:T(8,128)(2,1)} %constant_dynamic-slice_fusion.2), channel_id=1, source_target_pairs={{0,1},{1,0},{2,3},{3,2},{4,5},{5,4},{6,7},{7,6},{8,9},{9,8},{10,11... | collective-permute-start | bytes 1572872 | tf_op jit(solution)/shard_map/ppermute | solution.py:800
  139.4 18.2 %collective-permute-start.22 = (bf16[64,4096]{1,0:T(8,128)(2,1)}, bf16[64,4096]{1,0:T(8,128)(2,1)}, u32[]{:S(2)}, u32[]{:S(2)}) collective-permute-start(bf16[64,4096]{1,0:T(8,128)(2,1)} %collective-permute-done.19.refs_0_), channel_id=1, source_target_pairs={{0,8},{1,9},{2,6},{3,7},{4,12},{5,13},{6,2},{7,3},{8,0},{9,1},{10,... | collective-permute-start | bytes 1572872 | tf_op jit(solution)/shard_map/ppermute | solution.py:809
  139.5 20.0 %collective-permute-start.23 = (bf16[64,4096]{1,0:T(8,128)(2,1)}, bf16[64,4096]{1,0:T(8,128)(2,1)}, u32[]{:S(2)}, u32[]{:S(2)}) collective-permute-start(bf16[64,4096]{1,0:T(8,128)(2,1)} %collective-permute-done.19.refs_0_), channel_id=1, source_target_pairs={{0,2},{2,0},{1,3},{3,1},{4,6},{6,4},{5,7},{7,5},{8,10},{10,8},{9,1... | collective-permute-start | bytes 1572872 | tf_op jit(solution)/shard_map/ppermute | solution.py:800
  141.5 14.9 %collective-permute-start.24 = (bf16[256,1024]{1,0:T(8,128)(2,1)}, bf16[256,1024]{1,0:T(8,128)(2,1)}, u32[]{:S(2)}, u32[]{:S(2)}) collective-permute-start(bf16[256,1024]{1,0:T(8,128)(2,1)} %constant_dynamic-slice_fusion.1), channel_id=1, source_target_pairs={{0,1},{1,0},{2,3},{3,2},{4,5},{5,4},{6,7},{7,6},{8,9},{9,8},{10,11... | collective-permute-start | bytes 1572872 | tf_op jit(solution)/shard_map/ppermute | solution.py:800
  156.3 33.2 %collective-permute-start.25 = (bf16[64,4096]{1,0:T(8,128)(2,1)}, bf16[64,4096]{1,0:T(8,128)(2,1)}, u32[]{:S(2)}, u32[]{:S(2)}) collective-permute-start(bf16[64,4096]{1,0:T(8,128)(2,1)} %collective-permute-done.20.refs_1_), channel_id=1, source_target_pairs={{0,2},{2,0},{1,3},{3,1},{4,6},{6,4},{5,7},{7,5},{8,10},{10,8},{9,1... | collective-permute-start | bytes 1572872 | tf_op jit(solution)/shard_map/ppermute | solution.py:800
  156.4 36.1 %collective-permute-start.27 = (bf16[256,1024]{1,0:T(8,128)(2,1)}, bf16[256,1024]{1,0:T(8,128)(2,1)}, u32[]{:S(2)}, u32[]{:S(2)}) collective-permute-start(bf16[256,1024]{1,0:T(8,128)(2,1)} %collective-permute-done.24.refs_0_), channel_id=1, source_target_pairs={{0,4},{1,5},{2,10},{3,11},{4,0},{5,1},{6,14},{7,15},{8,12},{9,13},... | collective-permute-start | bytes 1572872 | tf_op jit(solution)/shard_map/ppermute | solution.py:809
  157.6 35.2 %collective-permute-start.28 = (bf16[256,1024]{1,0:T(8,128)(2,1)}, bf16[256,1024]{1,0:T(8,128)(2,1)}, u32[]{:S(2)}, u32[]{:S(2)}) collective-permute-start(bf16[256,1024]{1,0:T(8,128)(2,1)} %collective-permute-done.24.refs_0_), channel_id=1, source_target_pairs={{0,8},{1,9},{2,6},{3,7},{4,12},{5,13},{6,2},{7,3},{8,0},{9,1},{10,... | collective-permute-start | bytes 1572872 | tf_op jit(solution)/shard_map/ppermute | solution.py:809
  159.5 33.3 %collective-permute-start.29 = (bf16[256,1024]{1,0:T(8,128)(2,1)}, bf16[256,1024]{1,0:T(8,128)(2,1)}, u32[]{:S(2)}, u32[]{:S(2)}) collective-permute-start(bf16[256,1024]{1,0:T(8,128)(2,1)} %collective-permute-done.24.refs_0_), channel_id=1, source_target_pairs={{0,2},{2,0},{1,3},{3,1},{4,6},{6,4},{5,7},{7,5},{8,10},{10,8},{9,1... | collective-permute-start | bytes 1572872 | tf_op jit(solution)/shard_map/ppermute | solution.py:800
  165.4 27.1 %collective-permute-start.26 = (bf16[64,4096]{1,0:T(8,128)(2,1)}, bf16[64,4096]{1,0:T(8,128)(2,1)}, u32[]{:S(2)}, u32[]{:S(2)}) collective-permute-start(bf16[64,4096]{1,0:T(8,128)(2,1)} %collective-permute-done.22.refs_2_), channel_id=1, source_target_pairs={{0,2},{2,0},{1,3},{3,1},{4,6},{6,4},{5,7},{7,5},{8,10},{10,8},{9,1... | collective-permute-start | bytes 1572872 | tf_op jit(solution)/shard_map/ppermute | solution.py:800
  189.5 19.1 %collective-permute-start.30 = (bf16[64,4096]{1,0:T(8,128)(2,1)}, bf16[64,4096]{1,0:T(8,128)(2,1)}, u32[]{:S(2)}, u32[]{:S(2)}) collective-permute-start(bf16[64,4096]{1,0:T(8,128)(2,1)} %collective-permute-done.21.refs_3_), channel_id=1, source_target_pairs={{0,2},{2,0},{1,3},{3,1},{4,6},{6,4},{5,7},{7,5},{8,10},{10,8},{9,1... | collective-permute-start | bytes 1572872 | tf_op jit(solution)/shard_map/ppermute | solution.py:800
  192.5 24.9 %collective-permute-start.31 = (bf16[256,1024]{1,0:T(8,128)(2,1)}, bf16[256,1024]{1,0:T(8,128)(2,1)S(1)}, u32[]{:S(2)}, u32[]{:S(2)}) collective-permute-start(bf16[256,1024]{1,0:T(8,128)(2,1)} %collective-permute-done.27.refs_1_), channel_id=1, source_target_pairs={{0,8},{1,9},{2,6},{3,7},{4,12},{5,13},{6,2},{7,3},{8,0},{9,1},{10,... | collective-permute-start | bytes 1572872 | tf_op jit(solution)/shard_map/ppermute | solution.py:809
  192.5 27.0 %collective-permute-start.32 = (bf16[256,1024]{1,0:T(8,128)(2,1)}, bf16[256,1024]{1,0:T(8,128)(2,1)}, u32[]{:S(2)}, u32[]{:S(2)}) collective-permute-start(bf16[256,1024]{1,0:T(8,128)(2,1)} %collective-permute-done.27.refs_1_), channel_id=1, source_target_pairs={{0,2},{2,0},{1,3},{3,1},{4,6},{6,4},{5,7},{7,5},{8,10},{10,8},{9,1... | collective-permute-start | bytes 1572872 | tf_op jit(solution)/shard_map/ppermute | solution.py:800
  291.0 28.3 %collective-permute-start.37 = (bf16[1,1024,1024]{2,1,0:T(8,128)(2,1)}, bf16[1,1024,1024]{2,1,0:T(8,128)(2,1)}, u32[]{:S(2)}, u32[]{:S(2)}) collective-permute-start(bf16[1,1024,1024]{2,1,0:T(8,128)(2,1)} %get-tuple-element.194), channel_id=1, source_target_pairs={{0,4},{1,5},{2,3},{3,2},{4,0},{5,1},{6,7},{7,6},{8,12},{9,13},{10,... | collective-permute-start | bytes 6291464 | tf_op jit(solution)/shard_map/ppermute | solution.py:809
  319.2 31.0 %collective-permute-start.38 = (bf16[1,1024,1024]{2,1,0:T(8,128)(2,1)}, bf16[1,1024,1024]{2,1,0:T(8,128)(2,1)}, u32[]{:S(2)}, u32[]{:S(2)}) collective-permute-start(bf16[1,1024,1024]{2,1,0:T(8,128)(2,1)} %get-tuple-element.199), channel_id=1, source_target_pairs={{0,4},{1,5},{2,3},{3,2},{4,0},{5,1},{6,7},{7,6},{8,12},{9,13},{10,... | collective-permute-start | bytes 6291464 | tf_op jit(solution)/shard_map/ppermute | solution.py:809
  358.2 42.5 %collective-permute-start.40 = (bf16[2,512,1024]{2,1,0:T(8,128)(2,1)}, bf16[2,512,1024]{2,1,0:T(8,128)(2,1)}, u32[]{:S(2)}, u32[]{:S(2)}) collective-permute-start(bf16[2,512,1024]{2,1,0:T(8,128)(2,1)} %get-tuple-element.207), channel_id=1, source_target_pairs={{0,1},{1,0},{2,10},{3,11},{4,5},{5,4},{6,14},{7,15},{8,9},{9,8},{1... | collective-permute-start | bytes 6291464 | tf_op jit(solution)/shard_map/ppermute | solution.py:809
  374.9 23.5 %collective-permute-start.41 = (bf16[1,128,5120]{2,1,0:T(8,128)(2,1)}, bf16[1,128,5120]{2,1,0:T(8,128)(2,1)}, u32[]{:S(2)}, u32[]{:S(2)}) collective-permute-start(bf16[1,128,5120]{2,1,0:T(8,128)(2,1)} %get-tuple-element.211), channel_id=1, source_target_pairs={{0,8},{1,9},{2,6},{3,7},{4,12},{5,13},{6,2},{7,3},{8,0},{9,1},{10,... | collective-permute-start | bytes 3932168 | tf_op jit(solution)/shard_map/ppermute | solution.py:809
  398.3 32.3 %collective-permute-start.43 = (bf16[1,128,5120]{2,1,0:T(8,128)(2,1)}, bf16[1,128,5120]{2,1,0:T(8,128)(2,1)}, u32[]{:S(2)}, u32[]{:S(2)}) collective-permute-start(bf16[1,128,5120]{2,1,0:T(8,128)(2,1)} %get-tuple-element.220), channel_id=1, source_target_pairs={{0,8},{1,9},{2,6},{3,7},{4,12},{5,13},{6,2},{7,3},{8,0},{9,1},{10,... | collective-permute-start | bytes 3932168 | tf_op jit(solution)/shard_map/ppermute | solution.py:809
  404.9 22.6 %collective-permute-start.42 = (bf16[1,512,1024]{2,1,0:T(8,128)(2,1)}, bf16[1,512,1024]{2,1,0:T(8,128)(2,1)}, u32[]{:S(2)}, u32[]{:S(2)}) collective-permute-start(bf16[1,512,1024]{2,1,0:T(8,128)(2,1)} %get-tuple-element.218), channel_id=1, source_target_pairs={{0,8},{1,9},{2,6},{3,7},{4,12},{5,13},{6,2},{7,3},{8,0},{9,1},{10,... | collective-permute-start | bytes 3145736 | tf_op jit(solution)/shard_map/ppermute | solution.py:809
  438.4 26.9 %collective-permute-start.45 = (bf16[1,256,1024]{2,1,0:T(8,128)(2,1)}, bf16[1,256,1024]{2,1,0:T(8,128)(2,1)}, u32[]{:S(2)}, u32[]{:S(2)}) collective-permute-start(bf16[1,256,1024]{2,1,0:T(8,128)(2,1)} %get-tuple-element.226), channel_id=1, source_target_pairs={{0,16},{16,0},{1,17},{17,1},{2,18},{18,2},{3,19},{19,3},{4,20},{20... | collective-permute-start | bytes 1572872 | tf_op jit(solution)/shard_map/ppermute | solution.py:800
  441.0 36.4 %collective-permute-start.47 = (bf16[2,64,5120]{2,1,0:T(8,128)(2,1)}, bf16[2,64,5120]{2,1,0:T(8,128)(2,1)}, u32[]{:S(2)}, u32[]{:S(2)}) collective-permute-start(bf16[2,64,5120]{2,1,0:T(8,128)(2,1)} %get-tuple-element.229), channel_id=1, source_target_pairs={{0,1},{1,0},{2,10},{3,11},{4,5},{5,4},{6,14},{7,15},{8,9},{9,8},{1... | collective-permute-start | bytes 3932168 | tf_op jit(solution)/shard_map/ppermute | solution.py:809
  466.7 25.9 %collective-permute-start.48 = (bf16[256,1024]{1,0:T(8,128)(2,1)S(1)}, bf16[256,1024]{1,0:T(8,128)(2,1)}, u32[]{:S(2)}, u32[]{:S(2)}) collective-permute-start(bf16[256,1024]{1,0:T(8,128)(2,1)S(1)} %fusion.56.refs_0_), channel_id=1, source_target_pairs={{0,16},{16,0},{1,17},{17,1},{2,18},{18,2},{3,19},{19,3},{4,20},{20... | collective-permute-start | bytes 1572872 | tf_op jit(solution)/shard_map/ppermute | solution.py:800
  466.8 39.2 %collective-permute-start.50 = (bf16[2,128,3072]{2,1,0:T(8,128)(2,1)}, bf16[2,128,3072]{2,1,0:T(8,128)(2,1)}, u32[]{:S(2)}, u32[]{:S(2)}) collective-permute-start(bf16[2,128,3072]{2,1,0:T(8,128)(2,1)} %get-tuple-element.233), channel_id=1, source_target_pairs={{0,1},{1,0},{2,10},{3,11},{4,5},{5,4},{6,14},{7,15},{8,9},{9,8},{1... | collective-permute-start | bytes 4718600 | tf_op jit(solution)/shard_map/ppermute | solution.py:809
  495.4 15.1 %collective-permute-start.51 = (bf16[512,1024]{1,0:T(8,128)(2,1)}, bf16[512,1024]{1,0:T(8,128)(2,1)}, u32[]{:S(2)}, u32[]{:S(2)}) collective-permute-start(bf16[512,1024]{1,0:T(8,128)(2,1)} %shard_map.504.refs_0_), channel_id=1, source_target_pairs={{0,8},{1,9},{2,6},{3,7},{4,12},{5,13},{6,2},{7,3},{8,0},{9,1},{10,... | collective-permute-start | bytes 3145736 | tf_op jit(solution)/shard_map/ppermute | solution.py:809
  514.2 52.8 %collective-permute-start.53 = (bf16[1024,1024]{1,0:T(8,128)(2,1)}, bf16[1024,1024]{1,0:T(8,128)(2,1)}, u32[]{:S(2)}, u32[]{:S(2)}) collective-permute-start(bf16[1024,1024]{1,0:T(8,128)(2,1)} %shard_map.506.refs_0_), channel_id=1, source_target_pairs={{0,4},{1,5},{2,10},{3,11},{4,0},{5,1},{6,14},{7,15},{8,12},{9,13},... | collective-permute-start | bytes 6291464 | tf_op jit(solution)/shard_map/ppermute | solution.py:809
  518.3 28.9 %collective-permute-start.46 = (bf16[512,1024]{1,0:T(8,128)(2,1)}, bf16[512,1024]{1,0:T(8,128)(2,1)}, u32[]{:S(2)}, u32[]{:S(2)}) collective-permute-start(bf16[512,1024]{1,0:T(8,128)(2,1)} %slice.285), channel_id=1, source_target_pairs={{1,0},{3,2},{5,4},{7,6},{9,8},{11,10},{13,12},{15,14},{17,16},{19,... | collective-permute-start | bytes 3145736 | tf_op jit(solution)/shard_map/ppermute | solution.py:1313
  523.5 39.9 %collective-permute-start.52 = (bf16[1,64,5120]{2,1,0:T(8,128)(2,1)S(1)}, bf16[1,64,5120]{2,1,0:T(8,128)(2,1)S(1)}, u32[]{:S(2)}, u32[]{:S(2)}) collective-permute-start(bf16[1,64,5120]{2,1,0:T(8,128)(2,1)S(1)} %copy-done.65), channel_id=1, source_target_pairs={{0,4},{1,5},{2,3},{3,2},{4,0},{5,1},{6,7},{7,6},{8,12},{9,13},{10,... | collective-permute-start | bytes 1966088 | tf_op jit(solution)/shard_map/ppermute | solution.py:809
  572.6 16.7 %collective-permute-start.55 = (bf16[2048,1024]{1,0:T(8,128)(2,1)}, bf16[2048,1024]{1,0:T(8,128)(2,1)}, u32[]{:S(2)}, u32[]{:S(2)}) collective-permute-start(bf16[2048,1024]{1,0:T(8,128)(2,1)} %shard_map.509.own_ref), channel_id=1, source_target_pairs={{0,2},{2,0},{1,3},{3,1},{4,6},{6,4},{5,7},{7,5},{8,10},{10,8},{9,1... | collective-permute-start | bytes 12582920 | tf_op jit(solution)/shard_map/ppermute | solution.py:800
  573.7 30.3 %collective-permute-start.56 = (bf16[1,32,5120]{2,1,0:T(8,128)(2,1)S(1)}, bf16[1,32,5120]{2,1,0:T(8,128)(2,1)S(1)}, u32[]{:S(2)}, u32[]{:S(2)}) collective-permute-start(bf16[1,32,5120]{2,1,0:T(8,128)(2,1)S(1)} %copy-done.66), channel_id=1, source_target_pairs={{0,16},{16,0},{1,17},{17,1},{2,18},{18,2},{3,19},{19,3},{4,20},{20... | collective-permute-start | bytes 983048 | tf_op jit(solution)/shard_map/ppermute | solution.py:800
  588.6 17.0 %collective-permute-start.57 = (bf16[1,64,3072]{2,1,0:T(8,128)(2,1)}, bf16[1,64,3072]{2,1,0:T(8,128)(2,1)S(1)}, u32[]{:S(2)}, u32[]{:S(2)}) collective-permute-start(bf16[1,64,3072]{2,1,0:T(8,128)(2,1)} %get-tuple-element.257), channel_id=1, source_target_pairs={{0,8},{1,9},{2,6},{3,7},{4,12},{5,13},{6,2},{7,3},{8,0},{9,1},{10,... | collective-permute-start | bytes 1179656 | tf_op jit(solution)/shard_map/ppermute | solution.py:809
  604.1 21.6 %collective-permute-start.58 = (bf16[32,5120]{1,0:T(8,128)(2,1)S(1)}, bf16[32,5120]{1,0:T(8,128)(2,1)S(1)}, u32[]{:S(2)}, u32[]{:S(2)}) collective-permute-start(bf16[32,5120]{1,0:T(8,128)(2,1)S(1)} %fusion.57.refs_0_), channel_id=1, source_target_pairs={{0,16},{16,0},{1,17},{17,1},{2,18},{18,2},{3,19},{19,3},{4,20},{20... | collective-permute-start | bytes 983048 | tf_op jit(solution)/shard_map/ppermute | solution.py:800
  609.0 21.2 %collective-permute-start.59 = (bf16[1,32,3072]{2,1,0:T(8,128)(2,1)}, bf16[1,32,3072]{2,1,0:T(8,128)(2,1)S(1)}, u32[]{:S(2)}, u32[]{:S(2)}) collective-permute-start(bf16[1,32,3072]{2,1,0:T(8,128)(2,1)} %get-tuple-element.263), channel_id=1, source_target_pairs={{0,16},{16,0},{1,17},{17,1},{2,18},{18,2},{3,19},{19,3},{4,20},{20... | collective-permute-start | bytes 589832 | tf_op jit(solution)/shard_map/ppermute | solution.py:800
  643.8 21.9 %collective-permute-start.62 = (bf16[128,5120]{1,0:T(8,128)(2,1)}, bf16[128,5120]{1,0:T(8,128)(2,1)S(1)}, u32[]{:S(2)}, u32[]{:S(2)}) collective-permute-start(bf16[128,5120]{1,0:T(8,128)(2,1)} %shard_map.514.refs_0_), channel_id=1, source_target_pairs={{0,8},{1,9},{2,6},{3,7},{4,12},{5,13},{6,2},{7,3},{8,0},{9,1},{10,... | collective-permute-start | bytes 3932168 | tf_op jit(solution)/shard_map/ppermute | solution.py:809
  643.8 18.2 %collective-permute-start.61 = (bf16[32,3072]{1,0:T(8,128)(2,1)S(1)}, bf16[32,3072]{1,0:T(8,128)(2,1)S(1)}, u32[]{:S(2)}, u32[]{:S(2)}) collective-permute-start(bf16[32,3072]{1,0:T(8,128)(2,1)S(1)} %fusion.58.refs_0_), channel_id=1, source_target_pairs={{0,16},{16,0},{1,17},{17,1},{2,18},{18,2},{3,19},{19,3},{4,20},{20... | collective-permute-start | bytes 589832 | tf_op jit(solution)/shard_map/ppermute | solution.py:800
  671.6 39.5 %collective-permute-start.66 = (bf16[256,5120]{1,0:T(8,128)(2,1)}, bf16[256,5120]{1,0:T(8,128)(2,1)}, u32[]{:S(2)}, u32[]{:S(2)}) collective-permute-start(bf16[256,5120]{1,0:T(8,128)(2,1)} %shard_map.516.own_ref), channel_id=1, source_target_pairs={{0,2},{2,0},{1,3},{3,1},{4,6},{6,4},{5,7},{7,5},{8,10},{10,8},{9,1... | collective-permute-start | bytes 7864328 | tf_op jit(solution)/shard_map/ppermute | solution.py:800
  699.9 33.9 %collective-permute-start.71 = (bf16[256,3072]{1,0:T(8,128)(2,1)}, bf16[256,3072]{1,0:T(8,128)(2,1)}, u32[]{:S(2)}, u32[]{:S(2)}) collective-permute-start(bf16[256,3072]{1,0:T(8,128)(2,1)} %shard_map.518.own_ref), channel_id=1, source_target_pairs={{0,2},{2,0},{1,3},{3,1},{4,6},{6,4},{5,7},{7,5},{8,10},{10,8},{9,1... | collective-permute-start | bytes 4718600 | tf_op jit(solution)/shard_map/ppermute | solution.py:800
  702.7 27.3 %collective-permute-start.49 = (bf16[544,1024]{1,0:T(8,128)(2,1)}, bf16[544,1024]{1,0:T(8,128)(2,1)}, u32[]{:S(2)}, u32[]{:S(2)}) collective-permute-start(bf16[544,1024]{1,0:T(8,128)(2,1)} %slice.284), channel_id=1, source_target_pairs={{0,1},{1,0},{2,3},{3,2},{4,5},{5,4},{6,7},{7,6},{8,9},{9,8},{10,11... | collective-permute-start | bytes 3342344 | tf_op jit(solution)/shard_map/ppermute | solution.py:800
  (91 other events, 982.5 us)

commit v5 on v3

--- a/solution.py
+++ b/solution.py
@@ -1300,7 +1300,7 @@
     if two:
         sent = total_last.advance(normed_terms)
         for total in (total_mid, total_ffn):
-            sent = sent + total.advance(sent[0])
+            sent = sent + total.advance(*sent)
         grad_patch_keys = after(grad_patch_keys, *sent)
     patch_terms = dot_back(grad_patch_keys, whole_cross[:, :width]) + dot_back(
         grad_patch_values, whole_cross[:, width : 2 * width]
@@ -1337,7 +1337,7 @@
     if two:
         late = total_last.advance(patch_terms)
         for total in (total_mid, total_ffn):
-            late = late + total.advance(late[0])
+            late = late + total.advance(*late)
         norm_pairs = ((after(token_values, *late), grad_normed),) + norm_pairs[1:]
     sums = row_sums(norm_pairs, plain)
     vector_sums = jnp.concatenate([sums, column_inner.reshape(-1, width)])
@@ -1348,7 +1348,7 @@
             ahead = total_last.advance(*late)
             late = ahead
             for total in totals[:-1]:
-                late = late + total.advance(*ahead)
+                late = late + total.advance(*late)
         vector_total = VectorTotal(after(vector_sums, *late))
         grad_outer, grad_ffn_in = total_ffn.result(2, *late)
         late = vector_total.advance(grad_outer)

time: 724 us -> 720 us (level)
  starting transfers between devices: 101 us -> 78.8 us
  waiting for transfers between devices: 142 us -> 164 us
    ppermute x29, waiting for transfers between devices: 68.3 us -> 114 us  [exchange(): lax.ppermute(values, square, [(i, i ^ flip[i // 2 % 2]) for i in range(16)])]
    ppermute x41, starting transfers between devices: 60.2 us -> 38.5 us  [swap(): return lax.ppermute(values, axis_name, [(0, 1), (1, 0)])]
    ppermute x41, waiting for transfers between devices: 64.8 us -> 44.2 us  [swap(): return lax.ppermute(values, axis_name, [(0, 1), (1, 0)])]
    unnamed x166 -> x164, local copies, waits for them, and re-layouts: 15.6 us -> 17.2 us
  transfers between devices with their start and end apart: 72 -> 72, of which waited for: 21 -> 19; matrix products, arithmetic and copies ran while one was open for 19% -> 18% of each run, Pallas kernels for 34% -> 34%
where the time goes in v5:
time: 720 us; the launch traced here: 714 us
  Pallas kernels  320 us (44%)
  waiting for transfers between devices  164 us (23%)
  starting transfers between devices  78.8 us (11%)
  matrix products  71.9 us (10%)
  local copies, waits for them, and re-layouts  38.8 us (5%)
  other arithmetic  36.6 us (5%)
    ppermute x29, waiting for transfers between devices, exchange(): lax.ppermute(values, square, [(i, i ^ flip[i // 2 % 2]) for i in range(16)])  114 us
    pallas_call x3, Pallas kernels, attend(): pl.pallas_call(skip_refs(functools.partial(attend_kernel, plan), 5, len(i...  47.4 us
    ppermute x41, waiting for transfers between devices, swap(): return lax.ppermute(values, axis_name, [(0, 1), (1, 0)])  44.2 us
    pallas_call x11, Pallas kernels, join(): pl.pallas_call(functools.partial(join_kernel, count), grid_spec=pltpu.Pre...  42 us
    pallas_call x2, Pallas kernels, attend_back(): pl.pallas_call(skip_refs(functools.partial(attend_back_kernel, plan), 8,...  41.8 us
    pallas_call x1, Pallas kernels, ffn_both_ways(): pl.pallas_call(functools.partial(ffn_kernel, half_steps), grid_spec=pltpu...  40.5 us
    dot_general x8, matrix products, dot_nt(): lax.dot_general(left_side, right_side, (((1,), (1,)), ((), ())), preferre...  39.9 us
    ppermute x41, starting transfers between devices, swap(): return lax.ppermute(values, axis_name, [(0, 1), (1, 0)])  38.5 us
  transfers between devices with their start and end apart: 72, of which 19 were waited for; matrix products, arithmetic and copies ran while one was open for 18% of the time, Pallas kernels for 34%

profile of v5, /device:TPU:0, one launch (start us, length us, event | category | flops | bytes accessed | tf_op | source)
XLA Modules:
  0.0 713.7 jit_solution(7998064024328314242)
XLA Ops:
  8.8 9.5 %collective-permute-done.1 = bf16[68,128]{1,0:T(8,128)(2,1)S(1)} collective-permute-done((bf16[68,128]{1,0:T(8,128)(2,1)S(1)}, bf16[68,128]{1,0:T(8,128)(2,1)S(1)}, u32[]{:S(2)}, u32[]{:S(2)}) %collective-permute-start.1) | collective-permute-done | bytes 17440 | tf_op jit(solution)/shard_map/ppermute | solution.py:800
  34.8 6.3 collective-permute-done.5.refs_7_
  42.9 5.8 collective-permute-done.2
  53.1 8.7 %shard_map.484 = bf16[1024,4096]{1,0:T(8,128)(2,1)} custom-call(s32[9]{0:T(128)} %stack.366.place_ref, bf16[512,1024]{1,0:T(8,128)(2,1)} %refs_0_.2, bf16[512,1024]{1,0:T(8,128)(2,1)} %refs_1_.2, bf16[512,1024]{1,0:T(8,128)(2,1)} %refs_2_.2, bf16[512,1024]{1,0:T(8,128)(2,1)} %refs_3_.2, bf16[64,4096]{1,0:T(8,128)(2,1)} %copy-done.32, ...), custom_call_target="tpu_custom_call" | custom-call | flops 1 | bytes 1 | tf_op jit(solution)/shard_map/pallas_call | solution.py:312
  65.0 4.6 multiply_convert_fusion.1.refs_1_
  72.0 10.5 %collective-permute-done.11.refs_5_ = bf16[64,4096]{1,0:T(8,128)(2,1)} collective-permute-done((bf16[64,4096]{1,0:T(8,128)(2,1)}, bf16[64,4096]{1,0:T(8,128)(2,1)}, u32[]{:S(2)}, u32[]{:S(2)}) %collective-permute-start.11) | collective-permute-done | bytes 524320 | tf_op jit(solution)/shard_map/ppermute | solution.py:809
  85.7 8.2 %add_convert_fusion.refs_2_.refs_3_.refs_5_.refs_6_ = bf16[1024,2048]{1,0:T(8,128)(2,1)} fusion(f32[2048]{0:T(1024)S(1)} %pad_convert_fusion.1, bf16[1024,1024]{1,0:T(8,128)(2,1)S(1)} %fusion.6.refs_1_, bf16[1024,4096]{1,0:T(8,128)(2,1)} %shard_map.484), kind=kOutput, calls=%fused_computation.1 | convolution fusion | flops 4299161600 | bytes 10493952 | tf_op jit(solution)/shard_map/dot_general | solution.py:38
  94.8 16.4 %shard_map.485 = (bf16[512,1024]{1,0:T(8,128)(2,1)}, f32[8,2,512]{2,1,0:T(2,128)}) custom-call(s32[4]{0:T(128)} %pad_add_fusion.refs_0_, bf16[512,1024]{1,0:T(8,128)(2,1)} %multiply_convert_fusion.1.refs_1_, bf16[1024,2048]{1,0:T(8,128)(2,1)} %add_convert_fusion.refs_2_.refs_3_.refs_5_.refs_6_, ...), custom_call_target="tpu_custom_call" | custom-call | flops 1 | bytes 1 | tf_op jit(solution)/shard_map/pallas_call | solution.py:211
  116.9 6.5 collective-permute-start.19
  126.0 8.4 %shard_map.486 = bf16[1024,4096]{1,0:T(8,128)(2,1)} custom-call(s32[9]{0:T(128)} %stack.366.place_ref, bf16[512,1024]{1,0:T(8,128)(2,1)} %refs_0_.3, bf16[512,1024]{1,0:T(8,128)(2,1)} %refs_1_.3, bf16[512,1024]{1,0:T(8,128)(2,1)} %refs_2_.3, bf16[512,1024]{1,0:T(8,128)(2,1)} %refs_3_.3, bf16[64,4096]{1,0:T(8,128)(2,1)} %collective-permute-done.10.refs_4_, ...), custom_call_target="tpu_custom_call" | custom-call | flops 1 | bytes 1 | tf_op jit(solution)/shard_map/pallas_call | solution.py:312
  141.5 11.7 %collective-permute-done.20.refs_1_ = bf16[64,4096]{1,0:T(8,128)(2,1)} collective-permute-done((bf16[64,4096]{1,0:T(8,128)(2,1)}, bf16[64,4096]{1,0:T(8,128)(2,1)}, u32[]{:S(2)}, u32[]{:S(2)}) %collective-permute-start.20) | collective-permute-done | bytes 524320 | tf_op jit(solution)/shard_map/ppermute | solution.py:809
  159.5 5.9 collective-permute-done.21.refs_3_
  165.4 8.6 %fusion.refs_2_.refs_3_.refs_5_.refs_6_ = bf16[1088,2048]{1,0:T(8,128)(2,1)} fusion(bf16[1088,1024]{1,0:T(8,128)(2,1)S(1)} %pad_maximum_fusion.refs_1_, f32[2048]{0:T(1024)S(1)} %pad_convert_fusion, bf16[1024,4096]{1,0:T(8,128)(2,1)} %shard_map.486), kind=kOutput, calls=%fused_computation.2 | convolution fusion | flops 4567859200 | bytes 10887168 | tf_op jit(solution)/shard_map/dot_general | solution.py:38
  173.9 15.5 %shard_map.487 = (bf16[512,1024]{1,0:T(8,128)(2,1)}, f32[8,2,512]{2,1,0:T(2,128)}) custom-call(s32[4]{0:T(128)} %pad_add_fusion.refs_0_, bf16[512,1024]{1,0:T(8,128)(2,1)} %multiply_convert_fusion.refs_1_, bf16[1088,2048]{1,0:T(8,128)(2,1)} %fusion.refs_2_.refs_3_.refs_5_.refs_6_, bf16[1088,2048]{1,0:T(8,128)(2,1)} %fusion.refs_2_.refs_3_.refs_5_.refs_6_, ...), custom_call_target="tpu_custom_call" | custom-call | flops 1 | bytes 1 | tf_op jit(solution)/shard_map/pallas_call | solution.py:211
  192.8 15.5 %shard_map.488 = (bf16[512,1024]{1,0:T(8,128)(2,1)}, f32[8,2,512]{2,1,0:T(2,128)}) custom-call(s32[4]{0:T(128)} %pad_add_fusion.refs_0_, bf16[512,1024]{1,0:T(8,128)(2,1)} %multiply_convert_fusion.refs_1_, bf16[1088,2048]{1,0:T(8,128)(2,1)} %fusion.refs_2_.refs_3_.refs_5_.refs_6_, ...), custom_call_target="tpu_custom_call", output_to_operand_aliasing={{0}: (5, {}), {1}: (6, {})} | custom-call | flops 1 | bytes 1 | tf_op jit(solution)/shard_map/pallas_call | solution.py:211
  208.6 5.5 shard_map.489.refs_6_.refs_7_
  220.3 5.5 shard_map.490.refs_9_
  225.8 40.5 %shard_map.491 = (bf16[512,1024]{1,0:T(8,128)(2,1)}, f32[512,1024]{1,0:T(8,128)}, f32[1,4096]{1,0:T(1,128)}, bf16[2,1024,1024]{2,1,0:T(8,128)(2,1)}, bf16[2,1024...) custom-call(s32[20]{0:T(128)} %stack.355.place_ref, ...), custom_call_target="tpu_custom_call" | custom-call | flops 1 | bytes 1 | tf_op jit(solution)/shard_map/pallas_call | solution.py:462
  272.1 4.2 fusion.43.refs_3_
  280.0 10.9 %shard_map.492 = (bf16[2,1024,1024]{2,1,0:T(8,128)(2,1)}, bf16[1,1024,1024]{2,1,0:T(8,128)(2,1)}, bf16[1,1024,1024]{2,1,0:T(8,128)(2,1)}) custom-call(s32[4]{0:T(128)} %pad_add_fusion.1.place_ref, bf16[4,512,1024]{2,1,0:T(8,128)(2,1)} %bitcast.202, bf16[4,512,1024]{2,1,0:T(8,128)(2,1)} %collective-permute-done.35.refs_1_.refs_5_, ...), custom_call_target="tpu_custom_call" | custom-call | flops 1 | bytes 1 | tf_op jit(solution)/shard_map/pallas_call | solution.py:707
  292.4 26.8 %shard_map.493 = (bf16[512,1024]{1,0:T(8,128)(2,1)}, bf16[1088,1024]{1,0:T(8,128)(2,1)}, bf16[1088,1024]{1,0:T(8,128)(2,1)}) custom-call(s32[4]{0:T(128)} %pad_add_fusion.refs_0_, bf16[512,1024]{1,0:T(8,128)(2,1)} %multiply_convert_fusion.refs_1_, bf16[512,1024]{1,0:T(8,128)(2,1)} %get-tuple-element.181.refs_2_, bf16[512,1024]{1,0:T(8,128)(2,1)} %fusion.43.refs_3_, ...), custom_call_target="tpu_custom_call" | custom-call | flops 1 | bytes 1 | tf_op jit(solution)/shard_map/pallas_call | solution.py:235
  326.7 4.2 fusion.40.refs_3_
  331.0 19.3 %shard_map.494 = (bf16[2,256,5120]{2,1,0:T(8,128)(2,1)}, bf16[2,256,5120]{2,1,0:T(8,128)(2,1)}) custom-call(s32[2]{0:T(128)} %pad_add_fusion.3.place_ref, bf16[512,1024]{1,0:T(8,128)(2,1)} %add_convert_fusion.2.refs_0_, bf16[1088,1024]{1,0:T(8,128)(2,1)} %copy-done.12, bf16[512,1024]{1,0:T(8,128)(2,1)} %get-tuple-element.181.refs_2_, ...), custom_call_target="tpu_custom_call" | custom-call | flops 1 | bytes 1 | tf_op jit(solution)/shard_map/pallas_call | solution.py:570
  350.2 7.9 %shard_map.495 = (bf16[2,512,1024]{2,1,0:T(8,128)(2,1)}, bf16[2,512,1024]{2,1,0:T(8,128)(2,1)}) custom-call(s32[8]{0:T(128)} %stack.399.place_ref, bf16[4,512,1024]{2,1,0:T(8,128)(2,1)} %bitcast.200, bf16[2,512,1024]{2,1,0:T(8,128)(2,1)} %bitcast.54.refs_1_.refs_4_, bf16[2,512,1024]{2,1,0:T(8,128)(2,1)} %bitcast.55.refs_2_.refs_5_, ...), custom_call_target="tpu_custom_call" | custom-call | flops 1 | bytes 1 | tf_op jit(solution)/shard_map/pallas_call | solution.py:660
  359.0 8.2 %collective-permute-done.39.came_a.came_b = bf16[4,128,5120]{2,1,0:T(8,128)(2,1)} collective-permute-done((bf16[4,128,5120]{2,1,0:T(8,128)(2,1)}, bf16[4,128,5120]{2,1,0:T(8,128)(2,1)}, u32[]{:S(2)}, u32[]{:S(2)}) %collective-permute-start.39) | collective-permute-done | bytes 5242912 | tf_op jit(solution)/shard_map/ppermute | solution.py:800
  367.1 7.7 %shard_map.496 = (bf16[2,128,5120]{2,1,0:T(8,128)(2,1)}, bf16[1,128,5120]{2,1,0:T(8,128)(2,1)}, bf16[1,128,5120]{2,1,0:T(8,128)(2,1)}) custom-call(s32[4]{0:T(128)} %pad_add_fusion.2.place_ref, bf16[4,128,5120]{2,1,0:T(8,128)(2,1)} %bitcast.198, bf16[4,128,5120]{2,1,0:T(8,128)(2,1)} %collective-permute-done.39.came_a.came_b, ...), custom_call_target="tpu_custom_call" | custom-call | flops 1 | bytes 1 | tf_op jit(solution)/shard_map/pallas_call | solution.py:623
  376.7 15.0 %shard_map.497 = (bf16[512,1024]{1,0:T(8,128)(2,1)}, bf16[1024,1024]{1,0:T(8,128)(2,1)}, bf16[1024,1024]{1,0:T(8,128)(2,1)}) custom-call(s32[4]{0:T(128)} %pad_add_fusion.refs_0_, bf16[512,1024]{1,0:T(8,128)(2,1)} %multiply_convert_fusion.1.refs_1_, bf16[512,1024]{1,0:T(8,128)(2,1)} %get-tuple-element.162.refs_3_.refs_2_, bf16[512,1024]{1,0:T(8,128)(2,1)} %fusion.40.refs_3_, ...), custom_call_target="tpu_custom_call" | custom-call | flops 1 | bytes 1 | tf_op jit(solution)/shard_map/pallas_call | solution.py:235
  391.7 6.5 collective-permute-done.41
  407.4 12.8 %shard_map.499 = (bf16[2,256,3072]{2,1,0:T(8,128)(2,1)}, bf16[2,256,3072]{2,1,0:T(8,128)(2,1)}) custom-call(s32[2]{0:T(128)} %pad_add_fusion.3.place_ref, bf16[512,1024]{1,0:T(8,128)(2,1)} %slice.184.refs_0_, bf16[1024,1024]{1,0:T(8,128)(2,1)} %copy-done.6, bf16[512,1024]{1,0:T(8,128)(2,1)} %get-tuple-element.228.refs_2_.refs_6_, ...), custom_call_target="tpu_custom_call" | custom-call | flops 1 | bytes 1 | tf_op jit(solution)/shard_map/pallas_call | solution.py:570
  420.2 7.3 %collective-permute-done.42 = bf16[1,512,1024]{2,1,0:T(8,128)(2,1)} collective-permute-done((bf16[1,512,1024]{2,1,0:T(8,128)(2,1)}, bf16[1,512,1024]{2,1,0:T(8,128)(2,1)}, u32[]{:S(2)}, u32[]{:S(2)}) %collective-permute-start.42) | collective-permute-done | bytes 1048608 | tf_op jit(solution)/shard_map/ppermute | solution.py:809
  430.6 5.8 shard_map.501
  458.9 6.0 shard_map.502
  468.5 6.2 fusion.13
  479.5 8.2 %convolution_add_fusion.1 = f32[1088,1024]{1,0:T(8,128)} fusion(f32[1088,1024]{1,0:T(8,128)} %fusion.13, bf16[1088,1024]{1,0:T(8,128)(2,1)} %get-tuple-element.237.refs_5_, bf16[1024,4096]{1,0:T(8,128)(2,1)} %shard_map.486), kind=kOutput, calls=%fused_computation.7 | convolution fusion | flops 2282815488 | bytes 13238272 | tf_op jit(solution)/shard_map/dot_general | solution.py:32
  487.7 26.9 %collective-permute-done.49 = bf16[2,128,3072]{2,1,0:T(8,128)(2,1)} collective-permute-done((bf16[2,128,3072]{2,1,0:T(8,128)(2,1)}, bf16[2,128,3072]{2,1,0:T(8,128)(2,1)}, u32[]{:S(2)}, u32[]{:S(2)}) %collective-permute-start.49) | collective-permute-done | bytes 1572896 | tf_op jit(solution)/shard_map/ppermute | solution.py:809
  522.1 5.4 multiply_reduce_fusion.6
  532.7 9.6 %shard_map.507 = f32[16,1024]{1,0:T(8,128)} custom-call(f32[512,1024]{1,0:T(8,128)} %bitcast_convert_fusion.refs_0_, f32[512,1024]{1,0:T(8,128)} %get-tuple-element.320.refs_1_, f32[512,1024]{1,0:T(8,128)} %copy-done.3, f32[512,1024]{1,0:T(8,128)} %copy-done.16, f32[512,1024]{1,0:T(8,128)} %copy-done, f32[512,1024]{1,0:T(8,128)} %get-tuple-element.185.refs_5_, ...), custom_call_target="tpu_custom_call" | custom-call | flops 1 | bytes 1 | tf_op jit(solution)/shard_map/pallas_call | solution.py:352
  558.4 15.3 %collective-permute-done.55 = bf16[1,64,3072]{2,1,0:T(8,128)(2,1)S(1)} collective-permute-done((bf16[1,64,3072]{2,1,0:T(8,128)(2,1)}, bf16[1,64,3072]{2,1,0:T(8,128)(2,1)S(1)}, u32[]{:S(2)}, u32[]{:S(2)}) %collective-permute-start.55) | collective-permute-done | bytes 393248 | tf_op jit(solution)/shard_map/ppermute | solution.py:809
  584.2 5.5 shard_map.517.own_ref
  589.7 11.2 %collective-permute-start.64 = (bf16[2048,1024]{1,0:T(8,128)(2,1)}, bf16[2048,1024]{1,0:T(8,128)(2,1)}, u32[]{:S(2)}, u32[]{:S(2)}) collective-permute-start(bf16[2048,1024]{1,0:T(8,128)(2,1)} %shard_map.517.own_ref), channel_id=1, source_target_pairs={{0,2},{2,0},{1,3},{3,1},{4,6},{6,4},{5,7},{7,5},{8,10},{10,8},{9,1... | collective-permute-start | bytes 12582920 | tf_op jit(solution)/shard_map/ppermute | solution.py:800
  607.7 18.2 %collective-permute-done.59.refs_1_ = bf16[32,3072]{1,0:T(8,128)(2,1)S(1)} collective-permute-done((bf16[32,3072]{1,0:T(8,128)(2,1)S(1)}, bf16[32,3072]{1,0:T(8,128)(2,1)S(1)}, u32[]{:S(2)}, u32[]{:S(2)}) %collective-permute-start.59) | collective-permute-done | bytes 196640 | tf_op jit(solution)/shard_map/ppermute | solution.py:800
  630.0 4.7 shard_map.514.own_ref
  636.8 5.8 collective-permute-done.61.refs_1_
  646.7 11.6 %collective-permute-done.62.refs_1_ = bf16[128,3072]{1,0:T(8,128)(2,1)S(1)} collective-permute-done((bf16[128,3072]{1,0:T(8,128)(2,1)}, bf16[128,3072]{1,0:T(8,128)(2,1)S(1)}, u32[]{:S(2)}, u32[]{:S(2)}) %collective-permute-start.62) | collective-permute-done | bytes 786464 | tf_op jit(solution)/shard_map/ppermute | solution.py:809
  669.7 14.7 %shard_map.518 = (f32[2048,1024]{1,0:T(8,128)}, f32[512,4096]{1,0:T(8,128)}) custom-call(s32[2]{0:T(128)} %pad_add_fusion.3.place_ref, bf16[2048,1024]{1,0:T(8,128)(2,1)} %shard_map.517.own_ref, bf16[2048,1024]{1,0:T(8,128)(2,1)} %collective-permute-done.64.other_ref), custom_call_target="tpu_custom_call" | custom-call | flops 1 | bytes 1 | tf_op jit(solution)/shard_map/pallas_call | solution.py:754
  684.5 8.1 %shard_map.519 = (f32[512,1024]{1,0:T(8,128)}, f32[512,1024]{1,0:T(8,128)}, f32[512,1024]{1,0:T(8,128)}, f32[512,1024]{1,0:T(8,128)}, f32[512,1024]{1,0:T(8,128)}) custom-call(s32[2]{0:T(128)} %pad_add_fusion.3.place_ref, bf16[256,5120]{1,0:T(8,128)(2,1)} %shard_map.514.own_ref, bf16[256,5120]{1,0:T(8,128)(2,1)} %collective-permute-done.66.other_ref), custom_call_target="tpu_custom_call" | custom-call | flops 1 | bytes 1 | tf_op jit(solution)/shard_map/pallas_call | solution.py:754
  692.7 4.6 collective-permute-done.68
  705.9 6.0 shard_map.520
  (399 shorter events, 212.5 us)
Async XLA Ops:
  24.4 24.4 %collective-permute-start.2 = (bf16[512,1024]{1,0:T(8,128)(2,1)S(1)}, bf16[512,1024]{1,0:T(8,128)(2,1)S(1)}, u32[]{:S(2)}, u32[]{:S(2)}) collective-permute-start(bf16[512,1024]{1,0:T(8,128)(2,1)S(1)} %bitcast.194), channel_id=1, source_target_pairs={{0,1},{2,3},{4,5},{6,7},{8,9},{10,11},{12,13},{14,15},{16,17},{18,... | collective-permute-start | bytes 3145736 | tf_op jit(solution)/shard_map/ppermute | solution.py:1113
  34.1 17.1 %collective-permute-start.6 = (bf16[64,4096]{1,0:T(8,128)(2,1)S(1)}, bf16[64,4096]{1,0:T(8,128)(2,1)S(1)}, u32[]{:S(2)}, u32[]{:S(2)}) collective-permute-start(bf16[64,4096]{1,0:T(8,128)(2,1)S(1)} %collective-permute-done.refs_4_), channel_id=1, source_target_pairs={{0,2},{2,0},{1,3},{3,1},{4,6},{6,4},{5,7},{7,5},{8,10},{10,8},{9,1... | collective-permute-start | bytes 1572872 | tf_op jit(solution)/shard_map/ppermute | solution.py:800
  34.2 17.0 %collective-permute-start.7 = (bf16[64,4096]{1,0:T(8,128)(2,1)S(1)}, bf16[64,4096]{1,0:T(8,128)(2,1)S(1)}, u32[]{:S(2)}, u32[]{:S(2)}) collective-permute-start(bf16[64,4096]{1,0:T(8,128)(2,1)S(1)} %collective-permute-done.3.refs_5_), channel_id=1, source_target_pairs={{0,2},{2,0},{1,3},{3,1},{4,6},{6,4},{5,7},{7,5},{8,10},{10,8},{9,1... | collective-permute-start | bytes 1572872 | tf_op jit(solution)/shard_map/ppermute | solution.py:800
  48.8 20.8 %collective-permute-start.10 = (bf16[64,4096]{1,0:T(8,128)(2,1)}, bf16[64,4096]{1,0:T(8,128)(2,1)}, u32[]{:S(2)}, u32[]{:S(2)}) collective-permute-start(bf16[64,4096]{1,0:T(8,128)(2,1)} %pad_maximum_fusion.3), channel_id=1, source_target_pairs={{0,1},{1,0},{2,3},{3,2},{4,5},{5,4},{6,7},{7,6},{8,9},{9,8},{10,11... | collective-permute-start | bytes 1572872 | tf_op jit(solution)/shard_map/ppermute | solution.py:800
  71.8 39.6 %collective-permute-start.14 = (bf16[544,1024]{1,0:T(8,128)(2,1)}, bf16[544,1024]{1,0:T(8,128)(2,1)}, u32[]{:S(2)}, u32[]{:S(2)}) collective-permute-start(bf16[544,1024]{1,0:T(8,128)(2,1)} %bitcast.224), channel_id=1, source_target_pairs={{0,1},{1,0},{2,3},{3,2},{4,5},{5,4},{6,7},{7,6},{8,9},{9,8},{10,11... | collective-permute-start | bytes 3342344 | tf_op jit(solution)/shard_map/ppermute | solution.py:800
  71.9 22.0 %collective-permute-start.13 = (bf16[64,4096]{1,0:T(8,128)(2,1)}, bf16[64,4096]{1,0:T(8,128)(2,1)S(1)}, u32[]{:S(2)}, u32[]{:S(2)}) collective-permute-start(bf16[64,4096]{1,0:T(8,128)(2,1)} %collective-permute-done.10.refs_4_), channel_id=1, source_target_pairs={{0,2},{2,0},{1,3},{3,1},{4,6},{6,4},{5,7},{7,5},{8,10},{10,8},{9,1... | collective-permute-start | bytes 1572872 | tf_op jit(solution)/shard_map/ppermute | solution.py:800
  82.5 28.7 %collective-permute-start.15 = (bf16[64,4096]{1,0:T(8,128)(2,1)}, bf16[64,4096]{1,0:T(8,128)(2,1)}, u32[]{:S(2)}, u32[]{:S(2)}) collective-permute-start(bf16[64,4096]{1,0:T(8,128)(2,1)} %collective-permute-done.11.refs_5_), channel_id=1, source_target_pairs={{0,8},{1,9},{2,6},{3,7},{4,12},{5,13},{6,2},{7,3},{8,0},{9,1},{10,... | collective-permute-start | bytes 1572872 | tf_op jit(solution)/shard_map/ppermute | solution.py:809
  85.2 26.2 %collective-permute-start.16 = (bf16[64,4096]{1,0:T(8,128)(2,1)}, bf16[64,4096]{1,0:T(8,128)(2,1)}, u32[]{:S(2)}, u32[]{:S(2)}) collective-permute-start(bf16[64,4096]{1,0:T(8,128)(2,1)} %collective-permute-done.11.refs_5_), channel_id=1, source_target_pairs={{0,2},{2,0},{1,3},{3,1},{4,6},{6,4},{5,7},{7,5},{8,10},{10,8},{9,1... | collective-permute-start | bytes 1572872 | tf_op jit(solution)/shard_map/ppermute | solution.py:800
  85.2 26.2 %collective-permute-start.17 = (bf16[64,4096]{1,0:T(8,128)(2,1)}, bf16[64,4096]{1,0:T(8,128)(2,1)}, u32[]{:S(2)}, u32[]{:S(2)}) collective-permute-start(bf16[64,4096]{1,0:T(8,128)(2,1)} %collective-permute-done.12.refs_6_), channel_id=1, source_target_pairs={{0,2},{2,0},{1,3},{3,1},{4,6},{6,4},{5,7},{7,5},{8,10},{10,8},{9,1... | collective-permute-start | bytes 1572872 | tf_op jit(solution)/shard_map/ppermute | solution.py:800
  116.9 21.7 %collective-permute-start.19 = (bf16[64,4096]{1,0:T(8,128)(2,1)}, bf16[64,4096]{1,0:T(8,128)(2,1)}, u32[]{:S(2)}, u32[]{:S(2)}) collective-permute-start(bf16[64,4096]{1,0:T(8,128)(2,1)} %constant_dynamic-slice_fusion.2), channel_id=1, source_target_pairs={{0,1},{1,0},{2,3},{3,2},{4,5},{5,4},{6,7},{7,6},{8,9},{9,8},{10,11... | collective-permute-start | bytes 1572872 | tf_op jit(solution)/shard_map/ppermute | solution.py:800
  139.4 18.2 %collective-permute-start.22 = (bf16[64,4096]{1,0:T(8,128)(2,1)}, bf16[64,4096]{1,0:T(8,128)(2,1)}, u32[]{:S(2)}, u32[]{:S(2)}) collective-permute-start(bf16[64,4096]{1,0:T(8,128)(2,1)} %collective-permute-done.19.refs_0_), channel_id=1, source_target_pairs={{0,8},{1,9},{2,6},{3,7},{4,12},{5,13},{6,2},{7,3},{8,0},{9,1},{10,... | collective-permute-start | bytes 1572872 | tf_op jit(solution)/shard_map/ppermute | solution.py:809
  139.5 20.0 %collective-permute-start.23 = (bf16[64,4096]{1,0:T(8,128)(2,1)}, bf16[64,4096]{1,0:T(8,128)(2,1)}, u32[]{:S(2)}, u32[]{:S(2)}) collective-permute-start(bf16[64,4096]{1,0:T(8,128)(2,1)} %collective-permute-done.19.refs_0_), channel_id=1, source_target_pairs={{0,2},{2,0},{1,3},{3,1},{4,6},{6,4},{5,7},{7,5},{8,10},{10,8},{9,1... | collective-permute-start | bytes 1572872 | tf_op jit(solution)/shard_map/ppermute | solution.py:800
  156.3 33.2 %collective-permute-start.25 = (bf16[64,4096]{1,0:T(8,128)(2,1)}, bf16[64,4096]{1,0:T(8,128)(2,1)}, u32[]{:S(2)}, u32[]{:S(2)}) collective-permute-start(bf16[64,4096]{1,0:T(8,128)(2,1)} %collective-permute-done.20.refs_1_), channel_id=1, source_target_pairs={{0,2},{2,0},{1,3},{3,1},{4,6},{6,4},{5,7},{7,5},{8,10},{10,8},{9,1... | collective-permute-start | bytes 1572872 | tf_op jit(solution)/shard_map/ppermute | solution.py:800
  156.3 36.1 %collective-permute-start.27 = (bf16[256,1024]{1,0:T(8,128)(2,1)}, bf16[256,1024]{1,0:T(8,128)(2,1)}, u32[]{:S(2)}, u32[]{:S(2)}) collective-permute-start(bf16[256,1024]{1,0:T(8,128)(2,1)} %collective-permute-done.24.refs_0_), channel_id=1, source_target_pairs={{0,4},{1,5},{2,10},{3,11},{4,0},{5,1},{6,14},{7,15},{8,12},{9,13},... | collective-permute-start | bytes 1572872 | tf_op jit(solution)/shard_map/ppermute | solution.py:809
  157.5 35.2 %collective-permute-start.28 = (bf16[256,1024]{1,0:T(8,128)(2,1)}, bf16[256,1024]{1,0:T(8,128)(2,1)}, u32[]{:S(2)}, u32[]{:S(2)}) collective-permute-start(bf16[256,1024]{1,0:T(8,128)(2,1)} %collective-permute-done.24.refs_0_), channel_id=1, source_target_pairs={{0,8},{1,9},{2,6},{3,7},{4,12},{5,13},{6,2},{7,3},{8,0},{9,1},{10,... | collective-permute-start | bytes 1572872 | tf_op jit(solution)/shard_map/ppermute | solution.py:809
  159.5 33.3 %collective-permute-start.29 = (bf16[256,1024]{1,0:T(8,128)(2,1)}, bf16[256,1024]{1,0:T(8,128)(2,1)}, u32[]{:S(2)}, u32[]{:S(2)}) collective-permute-start(bf16[256,1024]{1,0:T(8,128)(2,1)} %collective-permute-done.24.refs_0_), channel_id=1, source_target_pairs={{0,2},{2,0},{1,3},{3,1},{4,6},{6,4},{5,7},{7,5},{8,10},{10,8},{9,1... | collective-permute-start | bytes 1572872 | tf_op jit(solution)/shard_map/ppermute | solution.py:800
  165.4 27.1 %collective-permute-start.26 = (bf16[64,4096]{1,0:T(8,128)(2,1)}, bf16[64,4096]{1,0:T(8,128)(2,1)}, u32[]{:S(2)}, u32[]{:S(2)}) collective-permute-start(bf16[64,4096]{1,0:T(8,128)(2,1)} %collective-permute-done.22.refs_2_), channel_id=1, source_target_pairs={{0,2},{2,0},{1,3},{3,1},{4,6},{6,4},{5,7},{7,5},{8,10},{10,8},{9,1... | collective-permute-start | bytes 1572872 | tf_op jit(solution)/shard_map/ppermute | solution.py:800
  189.4 19.1 %collective-permute-start.30 = (bf16[64,4096]{1,0:T(8,128)(2,1)}, bf16[64,4096]{1,0:T(8,128)(2,1)}, u32[]{:S(2)}, u32[]{:S(2)}) collective-permute-start(bf16[64,4096]{1,0:T(8,128)(2,1)} %collective-permute-done.21.refs_3_), channel_id=1, source_target_pairs={{0,2},{2,0},{1,3},{3,1},{4,6},{6,4},{5,7},{7,5},{8,10},{10,8},{9,1... | collective-permute-start | bytes 1572872 | tf_op jit(solution)/shard_map/ppermute | solution.py:800
  192.4 24.9 %collective-permute-start.31 = (bf16[256,1024]{1,0:T(8,128)(2,1)}, bf16[256,1024]{1,0:T(8,128)(2,1)S(1)}, u32[]{:S(2)}, u32[]{:S(2)}) collective-permute-start(bf16[256,1024]{1,0:T(8,128)(2,1)} %collective-permute-done.27.refs_1_), channel_id=1, source_target_pairs={{0,8},{1,9},{2,6},{3,7},{4,12},{5,13},{6,2},{7,3},{8,0},{9,1},{10,... | collective-permute-start | bytes 1572872 | tf_op jit(solution)/shard_map/ppermute | solution.py:809
  192.4 27.0 %collective-permute-start.32 = (bf16[256,1024]{1,0:T(8,128)(2,1)}, bf16[256,1024]{1,0:T(8,128)(2,1)}, u32[]{:S(2)}, u32[]{:S(2)}) collective-permute-start(bf16[256,1024]{1,0:T(8,128)(2,1)} %collective-permute-done.27.refs_1_), channel_id=1, source_target_pairs={{0,2},{2,0},{1,3},{3,1},{4,6},{6,4},{5,7},{7,5},{8,10},{10,8},{9,1... | collective-permute-start | bytes 1572872 | tf_op jit(solution)/shard_map/ppermute | solution.py:800
  290.9 28.3 %collective-permute-start.37 = (bf16[1,1024,1024]{2,1,0:T(8,128)(2,1)}, bf16[1,1024,1024]{2,1,0:T(8,128)(2,1)}, u32[]{:S(2)}, u32[]{:S(2)}) collective-permute-start(bf16[1,1024,1024]{2,1,0:T(8,128)(2,1)} %get-tuple-element.191), channel_id=1, source_target_pairs={{0,4},{1,5},{2,3},{3,2},{4,0},{5,1},{6,7},{7,6},{8,12},{9,13},{10,... | collective-permute-start | bytes 6291464 | tf_op jit(solution)/shard_map/ppermute | solution.py:809
  319.2 31.0 %collective-permute-start.38 = (bf16[1,1024,1024]{2,1,0:T(8,128)(2,1)}, bf16[1,1024,1024]{2,1,0:T(8,128)(2,1)}, u32[]{:S(2)}, u32[]{:S(2)}) collective-permute-start(bf16[1,1024,1024]{2,1,0:T(8,128)(2,1)} %get-tuple-element.196), channel_id=1, source_target_pairs={{0,4},{1,5},{2,3},{3,2},{4,0},{5,1},{6,7},{7,6},{8,12},{9,13},{10,... | collective-permute-start | bytes 6291464 | tf_op jit(solution)/shard_map/ppermute | solution.py:809
  358.1 42.5 %collective-permute-start.40 = (bf16[2,512,1024]{2,1,0:T(8,128)(2,1)}, bf16[2,512,1024]{2,1,0:T(8,128)(2,1)}, u32[]{:S(2)}, u32[]{:S(2)}) collective-permute-start(bf16[2,512,1024]{2,1,0:T(8,128)(2,1)} %get-tuple-element.204), channel_id=1, source_target_pairs={{0,1},{1,0},{2,10},{3,11},{4,5},{5,4},{6,14},{7,15},{8,9},{9,8},{1... | collective-permute-start | bytes 6291464 | tf_op jit(solution)/shard_map/ppermute | solution.py:809
  374.8 23.5 %collective-permute-start.41 = (bf16[1,128,5120]{2,1,0:T(8,128)(2,1)}, bf16[1,128,5120]{2,1,0:T(8,128)(2,1)}, u32[]{:S(2)}, u32[]{:S(2)}) collective-permute-start(bf16[1,128,5120]{2,1,0:T(8,128)(2,1)} %get-tuple-element.208), channel_id=1, source_target_pairs={{0,8},{1,9},{2,6},{3,7},{4,12},{5,13},{6,2},{7,3},{8,0},{9,1},{10,... | collective-permute-start | bytes 3932168 | tf_op jit(solution)/shard_map/ppermute | solution.py:809
  398.3 32.3 %collective-permute-start.43 = (bf16[1,128,5120]{2,1,0:T(8,128)(2,1)}, bf16[1,128,5120]{2,1,0:T(8,128)(2,1)}, u32[]{:S(2)}, u32[]{:S(2)}) collective-permute-start(bf16[1,128,5120]{2,1,0:T(8,128)(2,1)} %get-tuple-element.218), channel_id=1, source_target_pairs={{0,8},{1,9},{2,6},{3,7},{4,12},{5,13},{6,2},{7,3},{8,0},{9,1},{10,... | collective-permute-start | bytes 3932168 | tf_op jit(solution)/shard_map/ppermute | solution.py:809
  404.8 22.6 %collective-permute-start.42 = (bf16[1,512,1024]{2,1,0:T(8,128)(2,1)}, bf16[1,512,1024]{2,1,0:T(8,128)(2,1)}, u32[]{:S(2)}, u32[]{:S(2)}) collective-permute-start(bf16[1,512,1024]{2,1,0:T(8,128)(2,1)} %get-tuple-element.216), channel_id=1, source_target_pairs={{0,8},{1,9},{2,6},{3,7},{4,12},{5,13},{6,2},{7,3},{8,0},{9,1},{10,... | collective-permute-start | bytes 3145736 | tf_op jit(solution)/shard_map/ppermute | solution.py:809
  436.4 22.5 %collective-permute-start.45 = (bf16[4,128,3072]{2,1,0:T(8,128)(2,1)}, bf16[4,128,3072]{2,1,0:T(8,128)(2,1)}, u32[]{:S(2)}, u32[]{:S(2)}) collective-permute-start(bf16[4,128,3072]{2,1,0:T(8,128)(2,1)} %bitcast.266), channel_id=1, source_target_pairs={{0,2},{2,0},{1,3},{3,1},{4,6},{6,4},{5,7},{7,5},{8,10},{10,8},{9,1... | collective-permute-start | bytes 9437192 | tf_op jit(solution)/shard_map/ppermute | solution.py:800
  445.8 28.9 %collective-permute-start.47 = (bf16[1,256,1024]{2,1,0:T(8,128)(2,1)}, bf16[1,256,1024]{2,1,0:T(8,128)(2,1)S(1)}, u32[]{:S(2)}, u32[]{:S(2)}) collective-permute-start(bf16[1,256,1024]{2,1,0:T(8,128)(2,1)} %get-tuple-element.223), channel_id=1, source_target_pairs={{0,16},{16,0},{1,17},{17,1},{2,18},{18,2},{3,19},{19,3},{4,20},{20... | collective-permute-start | bytes 1572872 | tf_op jit(solution)/shard_map/ppermute | solution.py:800
  448.5 27.7 %collective-permute-start.46 = (bf16[2,64,5120]{2,1,0:T(8,128)(2,1)}, bf16[2,64,5120]{2,1,0:T(8,128)(2,1)}, u32[]{:S(2)}, u32[]{:S(2)}) collective-permute-start(bf16[2,64,5120]{2,1,0:T(8,128)(2,1)} %get-tuple-element.226), channel_id=1, source_target_pairs={{0,1},{1,0},{2,10},{3,11},{4,5},{5,4},{6,14},{7,15},{8,9},{9,8},{1... | collective-permute-start | bytes 3932168 | tf_op jit(solution)/shard_map/ppermute | solution.py:809
  457.6 64.5 %collective-permute-start.44 = (bf16[512,1024]{1,0:T(8,128)(2,1)}, bf16[512,1024]{1,0:T(8,128)(2,1)}, u32[]{:S(2)}, u32[]{:S(2)}) collective-permute-start(bf16[512,1024]{1,0:T(8,128)(2,1)} %slice.285), channel_id=1, source_target_pairs={{1,0},{3,2},{5,4},{7,6},{9,8},{11,10},{13,12},{15,14},{17,16},{19,... | collective-permute-start | bytes 3145736 | tf_op jit(solution)/shard_map/ppermute | solution.py:1310
  464.9 49.7 %collective-permute-start.49 = (bf16[2,128,3072]{2,1,0:T(8,128)(2,1)}, bf16[2,128,3072]{2,1,0:T(8,128)(2,1)}, u32[]{:S(2)}, u32[]{:S(2)}) collective-permute-start(bf16[2,128,3072]{2,1,0:T(8,128)(2,1)} %get-tuple-element.232), channel_id=1, source_target_pairs={{0,1},{1,0},{2,10},{3,11},{4,5},{5,4},{6,14},{7,15},{8,9},{9,8},{1... | collective-permute-start | bytes 4718600 | tf_op jit(solution)/shard_map/ppermute | solution.py:809
  474.9 53.1 %collective-permute-start.51 = (bf16[256,1024]{1,0:T(8,128)(2,1)S(1)}, bf16[256,1024]{1,0:T(8,128)(2,1)S(1)}, u32[]{:S(2)}, u32[]{:S(2)}) collective-permute-start(bf16[256,1024]{1,0:T(8,128)(2,1)S(1)} %fusion.56.refs_0_), channel_id=1, source_target_pairs={{0,16},{16,0},{1,17},{17,1},{2,18},{18,2},{3,19},{19,3},{4,20},{20... | collective-permute-start | bytes 1572872 | tf_op jit(solution)/shard_map/ppermute | solution.py:800
  479.5 38.6 %collective-permute-start.50 = (bf16[1,64,5120]{2,1,0:T(8,128)(2,1)}, bf16[1,64,5120]{2,1,0:T(8,128)(2,1)S(1)}, u32[]{:S(2)}, u32[]{:S(2)}) collective-permute-start(bf16[1,64,5120]{2,1,0:T(8,128)(2,1)} %get-tuple-element.235), channel_id=1, source_target_pairs={{0,4},{1,5},{2,3},{3,2},{4,0},{5,1},{6,7},{7,6},{8,12},{9,13},{10,... | collective-permute-start | bytes 1966088 | tf_op jit(solution)/shard_map/ppermute | solution.py:809
  521.8 21.4 %collective-permute-start.53 = (bf16[1,32,5120]{2,1,0:T(8,128)(2,1)}, bf16[1,32,5120]{2,1,0:T(8,128)(2,1)}, u32[]{:S(2)}, u32[]{:S(2)}) collective-permute-start(bf16[1,32,5120]{2,1,0:T(8,128)(2,1)} %get-tuple-element.243), channel_id=1, source_target_pairs={{0,16},{16,0},{1,17},{17,1},{2,18},{18,2},{3,19},{19,3},{4,20},{20... | collective-permute-start | bytes 983048 | tf_op jit(solution)/shard_map/ppermute | solution.py:800
  527.5 19.5 %collective-permute-start.52 = (bf16[2,64,3072]{2,1,0:T(8,128)(2,1)}, bf16[2,64,3072]{2,1,0:T(8,128)(2,1)S(1)}, u32[]{:S(2)}, u32[]{:S(2)}) collective-permute-start(bf16[2,64,3072]{2,1,0:T(8,128)(2,1)} %get-tuple-element.240), channel_id=1, source_target_pairs={{0,4},{1,5},{2,3},{3,2},{4,0},{5,1},{6,7},{7,6},{8,12},{9,13},{10,... | collective-permute-start | bytes 2359304 | tf_op jit(solution)/shard_map/ppermute | solution.py:809
  531.8 19.1 %collective-permute-start.54 = (bf16[512,1024]{1,0:T(8,128)(2,1)}, bf16[512,1024]{1,0:T(8,128)(2,1)S(1)}, u32[]{:S(2)}, u32[]{:S(2)}) collective-permute-start(bf16[512,1024]{1,0:T(8,128)(2,1)} %shard_map.506.refs_0_), channel_id=1, source_target_pairs={{0,8},{1,9},{2,6},{3,7},{4,12},{5,13},{6,2},{7,3},{8,0},{9,1},{10,... | collective-permute-start | bytes 3145736 | tf_op jit(solution)/shard_map/ppermute | solution.py:809
  555.5 27.4 %collective-permute-start.63 = (bf16[1024,1024]{1,0:T(8,128)(2,1)}, bf16[1024,1024]{1,0:T(8,128)(2,1)S(1)}, u32[]{:S(2)}, u32[]{:S(2)}) collective-permute-start(bf16[1024,1024]{1,0:T(8,128)(2,1)} %shard_map.509.refs_0_), channel_id=1, source_target_pairs={{0,4},{1,5},{2,10},{3,11},{4,0},{5,1},{6,14},{7,15},{8,12},{9,13},... | collective-permute-start | bytes 6291464 | tf_op jit(solution)/shard_map/ppermute | solution.py:809
  555.8 17.9 %collective-permute-start.55 = (bf16[1,64,3072]{2,1,0:T(8,128)(2,1)}, bf16[1,64,3072]{2,1,0:T(8,128)(2,1)S(1)}, u32[]{:S(2)}, u32[]{:S(2)}) collective-permute-start(bf16[1,64,3072]{2,1,0:T(8,128)(2,1)} %get-tuple-element.250), channel_id=1, source_target_pairs={{0,8},{1,9},{2,6},{3,7},{4,12},{5,13},{6,2},{7,3},{8,0},{9,1},{10,... | collective-permute-start | bytes 1179656 | tf_op jit(solution)/shard_map/ppermute | solution.py:809
  557.2 21.3 %collective-permute-start.57 = (bf16[32,5120]{1,0:T(8,128)(2,1)S(1)}, bf16[32,5120]{1,0:T(8,128)(2,1)}, u32[]{:S(2)}, u32[]{:S(2)}) collective-permute-start(bf16[32,5120]{1,0:T(8,128)(2,1)S(1)} %fusion.57.refs_0_), channel_id=1, source_target_pairs={{0,16},{16,0},{1,17},{17,1},{2,18},{18,2},{3,19},{19,3},{4,20},{20... | collective-permute-start | bytes 983048 | tf_op jit(solution)/shard_map/ppermute | solution.py:800
  577.1 23.8 %collective-permute-start.56 = (bf16[1,32,3072]{2,1,0:T(8,128)(2,1)}, bf16[1,32,3072]{2,1,0:T(8,128)(2,1)}, u32[]{:S(2)}, u32[]{:S(2)}) collective-permute-start(bf16[1,32,3072]{2,1,0:T(8,128)(2,1)} %get-tuple-element.255), channel_id=1, source_target_pairs={{0,16},{16,0},{1,17},{17,1},{2,18},{18,2},{3,19},{19,3},{4,20},{20... | collective-permute-start | bytes 589832 | tf_op jit(solution)/shard_map/ppermute | solution.py:800
  581.2 20.9 %collective-permute-start.58 = (bf16[64,5120]{1,0:T(8,128)(2,1)}, bf16[64,5120]{1,0:T(8,128)(2,1)S(1)}, u32[]{:S(2)}, u32[]{:S(2)}) collective-permute-start(bf16[64,5120]{1,0:T(8,128)(2,1)} %shard_map.511.refs_0_), channel_id=1, source_target_pairs={{0,4},{1,5},{2,10},{3,11},{4,0},{5,1},{6,14},{7,15},{8,12},{9,13},... | collective-permute-start | bytes 1966088 | tf_op jit(solution)/shard_map/ppermute | solution.py:809
  589.7 79.9 %collective-permute-start.64 = (bf16[2048,1024]{1,0:T(8,128)(2,1)}, bf16[2048,1024]{1,0:T(8,128)(2,1)}, u32[]{:S(2)}, u32[]{:S(2)}) collective-permute-start(bf16[2048,1024]{1,0:T(8,128)(2,1)} %shard_map.517.own_ref), channel_id=1, source_target_pairs={{0,2},{2,0},{1,3},{3,1},{4,6},{6,4},{5,7},{7,5},{8,10},{10,8},{9,1... | collective-permute-start | bytes 12582920 | tf_op jit(solution)/shard_map/ppermute | solution.py:800
  606.0 23.0 %collective-permute-start.60 = (bf16[128,5120]{1,0:T(8,128)(2,1)}, bf16[128,5120]{1,0:T(8,128)(2,1)S(1)}, u32[]{:S(2)}, u32[]{:S(2)}) collective-permute-start(bf16[128,5120]{1,0:T(8,128)(2,1)} %shard_map.512.refs_0_), channel_id=1, source_target_pairs={{0,8},{1,9},{2,6},{3,7},{4,12},{5,13},{6,2},{7,3},{8,0},{9,1},{10,... | collective-permute-start | bytes 3932168 | tf_op jit(solution)/shard_map/ppermute | solution.py:809
  606.3 19.6 %collective-permute-start.59 = (bf16[32,3072]{1,0:T(8,128)(2,1)S(1)}, bf16[32,3072]{1,0:T(8,128)(2,1)S(1)}, u32[]{:S(2)}, u32[]{:S(2)}) collective-permute-start(bf16[32,3072]{1,0:T(8,128)(2,1)S(1)} %fusion.58.refs_0_), channel_id=1, source_target_pairs={{0,16},{16,0},{1,17},{17,1},{2,18},{18,2},{3,19},{19,3},{4,20},{20... | collective-permute-start | bytes 589832 | tf_op jit(solution)/shard_map/ppermute | solution.py:800
  634.8 49.7 %collective-permute-start.66 = (bf16[256,5120]{1,0:T(8,128)(2,1)}, bf16[256,5120]{1,0:T(8,128)(2,1)}, u32[]{:S(2)}, u32[]{:S(2)}) collective-permute-start(bf16[256,5120]{1,0:T(8,128)(2,1)} %shard_map.514.own_ref), channel_id=1, source_target_pairs={{0,2},{2,0},{1,3},{3,1},{4,6},{6,4},{5,7},{7,5},{8,10},{10,8},{9,1... | collective-permute-start | bytes 7864328 | tf_op jit(solution)/shard_map/ppermute | solution.py:800
  662.4 43.4 %collective-permute-start.71 = (bf16[256,3072]{1,0:T(8,128)(2,1)}, bf16[256,3072]{1,0:T(8,128)(2,1)}, u32[]{:S(2)}, u32[]{:S(2)}) collective-permute-start(bf16[256,3072]{1,0:T(8,128)(2,1)} %shard_map.516.own_ref), channel_id=1, source_target_pairs={{0,2},{2,0},{1,3},{3,1},{4,6},{6,4},{5,7},{7,5},{8,10},{10,8},{9,1... | collective-permute-start | bytes 4718600 | tf_op jit(solution)/shard_map/ppermute | solution.py:800
  665.2 36.9 %collective-permute-start.48 = (bf16[544,1024]{1,0:T(8,128)(2,1)}, bf16[544,1024]{1,0:T(8,128)(2,1)}, u32[]{:S(2)}, u32[]{:S(2)}) collective-permute-start(bf16[544,1024]{1,0:T(8,128)(2,1)} %slice.284), channel_id=1, source_target_pairs={{0,1},{1,0},{2,3},{3,2},{4,5},{5,4},{6,7},{7,6},{8,9},{9,8},{10,11... | collective-permute-start | bytes 3342344 | tf_op jit(solution)/shard_map/ppermute | solution.py:800
  666.3 18.1 %collective-permute-start.65 = (f32[20,1024]{1,0:T(8,128)S(1)}, f32[20,1024]{1,0:T(8,128)S(1)}, u32[]{:S(2)}, u32[]{:S(2)}) collective-permute-start(f32[20,1024]{1,0:T(8,128)S(1)} %pad_maximum_fusion.4), channel_id=1, source_target_pairs={{0,16},{16,0},{1,17},{17,1},{2,18},{18,2},{3,19},{19,3},{4,20},{20... | collective-permute-start | bytes 245768 | tf_op jit(solution)/shard_map/ppermute | solution.py:800
  (91 other events, 912.3 us)
